TPU v7x, 512 devices: a whole 4x8x8 slice. The times are simulated.
512 devices in a mesh: fsdp: 32 (over y, z_lo), col: 16 (over x, z_hi, core).
Axes of the slice: x: 4, y: 8, z: 8 (z_hi: 2, z_lo: 4; z = z_hi * 4 + z_lo), core: 2. Of those that a mesh axis runs over, the one named last changes fastest.
Arguments:
- joined_gradient: bfloat16 [6144, 18432], P('fsdp', 'col'), may hold values from -6 to 6
- output_gradient: bfloat16 [6144, 6144], P('fsdp', 'col'), may hold values from -6 to 6
- joined_left_basis: bfloat16 [6144, 512], P('fsdp', 'col'), may hold values from -0.078125 to 0.078125
- joined_right_basis: bfloat16 [18432, 512], P('col', 'fsdp'), may hold values from -0.046875 to 0.046875
- output_left_basis: bfloat16 [6144, 512], P('fsdp', 'col'), may hold values from -0.078125 to 0.078125
- output_right_basis: bfloat16 [6144, 512], P('col', 'fsdp'), may hold values from -0.078125 to 0.078125
- joined_left_eigen: float32 [512], replicated, may hold values from 0.05 to 20
- joined_right_eigen: float32 [512], replicated, may hold values from 0.05 to 20
- output_left_eigen: float32 [512], replicated, may hold values from 0.05 to 20
- output_right_eigen: float32 [512], replicated, may hold values from 0.05 to 20
- damping: float32 [1], replicated, may hold values from 0.5 to 1
Outputs:
- joined_update: float32 [6144, 18432], P('fsdp', 'col')
- output_update: float32 [6144, 6144], P('fsdp', 'col')
All inputs are finite; a program needn't handle non-finite values.
Results may differ from a plain program's by a relative error of at most 0.0003.
Values may be sent and summed in bfloat16 or wider, within the bound.
No kernel may reach another device: no remote copies, remote signals or barrier semaphores. Data moves between devices by JAX's collectives and lax.ppermute only.
A program may use at most 64 MiB of HBM per device.

v0:
```python
import jax
import jax.numpy as jnp
from jax import lax
from jax.sharding import PartitionSpec as P


def shifted(eigen, damp):
    return 1.0 / (eigen + damp) - 1.0 / damp


def row_partial(left_basis, gradient):
    return jnp.einsum("rk,rc->kc", left_basis, gradient, preferred_element_type=jnp.float32)


def apply_left(matrix, left_wide, left_shift, row_sums, damp):
    return matrix / damp + jnp.dot(
        left_wide, left_shift[:, None] * row_sums, precision=lax.Precision.HIGHEST
    )


def apply_right(matrix, right_wide, right_shift, col_sums, damp):
    return matrix / damp + jnp.einsum(
        "rk,ck->rc", col_sums * right_shift[None, :], right_wide, precision=lax.Precision.HIGHEST
    )


def col_partial_wide(matrix, right_wide):
    return jnp.dot(matrix, right_wide, precision=lax.Precision.HIGHEST)


def local(
    joined_gradient,
    output_gradient,
    joined_left_basis,
    joined_right_basis,
    output_left_basis,
    output_right_basis,
    joined_left_eigen,
    joined_right_eigen,
    output_left_eigen,
    output_right_eigen,
    damping,
):
    damp = damping[0]
    joined_lshift = shifted(joined_left_eigen, damp)
    joined_rshift = shifted(joined_right_eigen, damp)
    output_lshift = shifted(output_left_eigen, damp)
    output_rshift = shifted(output_right_eigen, damp)
    joined_left, output_left = (
        lax.all_gather(joined_left_basis, "col", axis=1, tiled=True),
        lax.all_gather(output_left_basis, "col", axis=1, tiled=True),
    )
    joined_right, output_right = (
        lax.all_gather(joined_right_basis, "fsdp", axis=1, tiled=True),
        lax.all_gather(output_right_basis, "fsdp", axis=1, tiled=True),
    )
    joined_lwide = joined_left.astype(jnp.float32)
    output_lwide = output_left.astype(jnp.float32)
    joined_rwide = joined_right.astype(jnp.float32)
    output_rwide = output_right.astype(jnp.float32)
    joined_grad32 = joined_gradient.astype(jnp.float32)
    output_grad32 = output_gradient.astype(jnp.float32)
    joined_rows, output_rows = lax.psum(
        (row_partial(joined_left, joined_gradient), row_partial(output_left, output_gradient)),
        "fsdp",
    )
    joined_applied = apply_left(joined_grad32, joined_lwide, joined_lshift, joined_rows, damp)
    output_applied = apply_left(output_grad32, output_lwide, output_lshift, output_rows, damp)
    joined_cols, output_cols = lax.psum(
        (
            col_partial_wide(joined_applied, joined_rwide),
            col_partial_wide(output_applied, output_rwide),
        ),
        "col",
    )
    joined_update = apply_right(joined_applied, joined_rwide, joined_rshift, joined_cols, damp)
    output_update = apply_right(output_applied, output_rwide, output_rshift, output_cols, damp)
    return (joined_update, output_update)


def solution(mesh):
    placed = (
        P("fsdp", "col"),
        P("fsdp", "col"),
        P("fsdp", "col"),
        P("col", "fsdp"),
        P("fsdp", "col"),
        P("col", "fsdp"),
        P(),
        P(),
        P(),
        P(),
        P(),
    )
    return jax.shard_map(
        local,
        mesh=mesh,
        in_specs=placed,
        out_specs=(P("fsdp", "col"), P("fsdp", "col")),
        check_vma=False,
    )
```

profile of v0, /device:TPU:1, one launch (start us, length us, event | category | flops | bytes accessed | tf_op | source)
XLA Modules:
  0.0 754.6 jit_solution(9532364815103568934)
XLA Ops:
  7.2 0.0 copy-start.2
  7.2 0.0 all-reduce.5.cloned.1.call-start
  7.2 37.6 %all_gather.12 = bf16[192,512]{0,1:T(8,128)(2,1)S(1)} all-gather(bf16[192,32]{0,1:T(8,128)(2,1)} %param.13), channel_id=1, replica_groups=mesh['fsdp'=32,'col'=16] {'col'}, dimensions={1}, use_global_device_ids=true | all-gather | bytes 208896 | tf_op jit(solution)/shard_map/all_gather | solution.py:50
  44.8 25.3 %all_gather.14 = bf16[192,512]{0,1:T(8,128)(2,1)S(1)} all-gather(bf16[192,32]{0,1:T(8,128)(2,1)} %param.15), channel_id=1, replica_groups=mesh['fsdp'=32,'col'=16] {'col'}, dimensions={1}, use_global_device_ids=true | all-gather | bytes 208896 | tf_op jit(solution)/shard_map/all_gather | solution.py:51
  70.1 2.9 fusion.10
  73.1 0.0 copy-done.2
  73.1 0.0 copy-start.3
  73.1 0.0 copy-start.4
  73.1 0.0 copy-start.5
  73.1 1.2 fusion.12
  74.2 0.0 all-reduce.5.cloned.1.call-update
  74.3 0.0 copy-start.1
  74.3 0.0 all-gather.2.cloned.1.call-start
  74.3 0.7 all-gather.2.cloned.1.call-update
  75.0 0.0 all-reduce.7.cloned.1.call-start
  75.8 0.0 copy-done.3
  75.8 69.5 %all_gather.15 = bf16[384,512]{0,1:T(8,128)(2,1)S(1)} all-gather(bf16[384,16]{0,1:T(8,128)(2,1)S(1)} %copy-done.3), channel_id=1, replica_groups=mesh['fsdp'=32,'col'=16] {'fsdp'}, dimensions={1}, use_global_device_ids=true | all-gather | bytes 405504 | tf_op jit(solution)/shard_map/all_gather | solution.py:55
  145.2 0.0 copy-done.4
  145.2 0.0 copy-done.5
  145.3 232.6 %all-reduce.5.cloned.1.call-done = (f32[512,1152]{1,0:T(8,128)}, f32[512,384]{1,0:T(8,128)}) async-done(((f32[512,1152]{1,0:T(8,128)}, f32[512,384]{1,0:T(8,128)}), (f32[512,1152]{1,0:T(8,128)}, f32[512,384]{1,0:T(8,128)})) %all-reduce.5.cloned.1.call-update) | async-done | bytes 3145744 | tf_op jit(solution)/shard_map/psum | solution.py:63
  377.9 0.0 copy-start.8
  377.9 2.0 fusion.3
  379.8 1.3 fusion.13
  381.2 0.0 copy-done.1
  381.2 0.0 copy-done.8
  381.2 1.4 fusion
  382.6 0.0 copy-start.6
  382.6 0.0 copy-start.7
  382.6 149.5 %all-gather.2.cloned.1.call-done = bf16[1152,512]{0,1:T(8,128)(2,1)} async-done(((bf16[1152,16]{0,1:T(8,128)(2,1)}), bf16[1152,512]{0,1:T(8,128)(2,1)}) %all-gather.2.cloned.1.call-update) | async-done | bytes 1179664 | tf_op jit(solution)/shard_map/all_gather | solution.py:54
  532.0 0.0 copy-start
  532.0 3.5 fusion.11
  535.5 0.0 all-reduce.7.cloned.1.call-update
  535.5 0.0 copy-done.6
  535.5 0.0 copy-done.7
  535.6 207.4 %all-reduce.7.cloned.1.call-done = (f32[192,512]{1,0:T(8,128)}, f32[192,512]{1,0:T(8,128)}) async-done(((f32[192,512]{1,0:T(8,128)}, f32[192,512]{1,0:T(8,128)}), (f32[192,512]{1,0:T(8,128)}, f32[192,512]{1,0:T(8,128)})) %all-reduce.7.cloned.1.call-update) | async-done | bytes 786448 | tf_op jit(solution)/shard_map/psum | solution.py:69
  743.0 2.2 convolution_add_fusion.1
  745.2 0.0 copy-done
  745.2 2.9 convolution_add_fusion
  (3 shorter events, 0.0 us)
Async XLA Ops:
  7.2 65.9 %copy-start.2 = (bf16[192,384]{1,0:T(8,128)(2,1)S(1)}, bf16[192,384]{1,0:T(8,128)(2,1)}, u32[]{:S(2)}) copy-start(bf16[192,384]{1,0:T(8,128)(2,1)} %param.12) | copy-start | bytes 442372
  7.2 370.7 %all-reduce.5.cloned.1.call-start = ((), (), s32[]{:S(2)}) async-start(), calls=%async_computation.1 | async-start | bytes 6291456 | tf_op jit(solution)/shard_map/psum | solution.py:63
  73.1 2.7 copy-start.3
  73.1 72.2 %copy-start.4 = (f32[512]{0:T(512)S(1)}, f32[512]{0:T(512)}, u32[]{:S(2)}) copy-start(f32[512]{0:T(512)} %param.19) | copy-start | bytes 6148
  73.1 72.2 %copy-start.5 = (f32[512]{0:T(512)S(1)}, f32[512]{0:T(512)}, u32[]{:S(2)}) copy-start(f32[512]{0:T(512)} %param.17) | copy-start | bytes 6148
  74.3 306.9 %copy-start.1 = (bf16[192,1152]{1,0:T(8,128)(2,1)S(1)}, bf16[192,1152]{1,0:T(8,128)(2,1)}, u32[]{:S(2)}) copy-start(bf16[192,1152]{1,0:T(8,128)(2,1)} %param.11) | copy-start | bytes 1327108
  74.3 457.8 %all-gather.2.cloned.1.call-start = ((), (), s32[]{:S(2)}) async-start(), calls=%async_computation | async-start | bytes 1216512 | tf_op jit(solution)/shard_map/all_gather | solution.py:54
  75.0 668.0 %all-reduce.7.cloned.1.call-start = ((), (), s32[]{:S(2)}) async-start(), calls=%async_computation.2 | async-start | bytes 1572864 | tf_op jit(solution)/shard_map/psum | solution.py:69
  377.9 3.3 copy-start.8
  382.6 153.0 %copy-start.6 = (f32[512]{0:T(512)S(1)}, f32[512]{0:T(512)}, u32[]{:S(2)}) copy-start(f32[512]{0:T(512)} %param.20) | copy-start | bytes 6148
  382.6 153.0 %copy-start.7 = (f32[512]{0:T(512)S(1)}, f32[512]{0:T(512)}, u32[]{:S(2)}) copy-start(f32[512]{0:T(512)} %param.18) | copy-start | bytes 6148
  532.0 213.1 %copy-start = (bf16[1152,512]{0,1:T(8,128)(2,1)S(1)}, bf16[1152,512]{0,1:T(8,128)(2,1)}, u32[]{:S(2)}) copy-start(bf16[1152,512]{0,1:T(8,128)(2,1)} %all-gather.2.cloned.1.call-done) | copy-start | bytes 3538948
Sparse Core Ops, SparseCore 0:
  74.4 303.4 all-reduce.4
  380.1 151.8 all-gather.1
  535.8 207.0 all-reduce.6
where the time goes:
time: 755 us
  waiting for transfers between devices  590 us (78%)
  blocking collectives  132 us (17%)
  matrix products  17.3 us (2%)
  between operations  14.5 us (2%)
    psum x1, waiting for transfers between devices, local(): lax.psum((row_partial(joined_left, joined_gradient), row_partial(output_l...  233 us
    psum x1, waiting for transfers between devices, local(): lax.psum((col_partial_wide(joined_applied, joined_rwide), col_partial_wid...  207 us
    all_gather x1, waiting for transfers between devices, local(): lax.all_gather(joined_right_basis, 'fsdp', axis=1, tiled=True)  149 us
    all_gather x1, blocking collectives, local(): lax.all_gather(output_right_basis, 'fsdp', axis=1, tiled=True)  69.5 us
    all_gather x1, blocking collectives, local(): lax.all_gather(joined_left_basis, 'col', axis=1, tiled=True)  37.6 us
    all_gather x1, blocking collectives, local(): lax.all_gather(output_left_basis, 'col', axis=1, tiled=True)  25.3 us
  transfers between devices with their start and end apart: 3, of which 3 were waited for; matrix products, arithmetic and copies ran while one was open for 1% of the time, Pallas kernels for 0%

commit v1 on v0

v1 whole, which is shorter than its diff:
```python
import jax
import jax.numpy as jnp
from jax import lax
from jax.sharding import Mesh, PartitionSpec as P

FSDP = ("yp", "yb", "zp", "zb")
COL = ("x", "zh", "c")
QUAD = ("yb", "zb")
OCT = ("yp", "zp")
ROUND = (8, 7)


def shifted(eigen, damp):
    return 1.0 / (eigen + damp) - 1.0 / damp


def exchange(blocks, axes):
    return lax.all_to_all(blocks, axes, 0, 0, tiled=True)


def halves(wide):
    high = lax.reduce_precision(wide, *ROUND)
    return high.astype(jnp.bfloat16), (wide - high).astype(jnp.bfloat16)


def dot_wide_left(wide, narrow, dims):
    high, low = halves(wide)
    dot = lambda part: lax.dot_general(part, narrow, (dims, ((), ())), preferred_element_type=jnp.float32)
    return dot(high) + dot(low)


def dot_wide_right(narrow, wide, dims):
    high, low = halves(wide)
    dot = lambda part: lax.dot_general(narrow, part, (dims, ((), ())), preferred_element_type=jnp.float32)
    return dot(high) + dot(low)


def pack(values):
    top = jnp.max(jnp.abs(values))
    power = jnp.clip(jnp.floor(jnp.log2(jnp.maximum(top, 1e-30))), -100.0, 120.0)
    scaled = (values * jnp.exp2(14.0 - power)).astype(jnp.float16)
    tail = jnp.broadcast_to(power.astype(jnp.float16), values.shape[:-2] + (8, values.shape[-1]))
    return jnp.concatenate([scaled, tail], axis=-2)


def unpack(packed):
    rows = packed.shape[-2] - 8
    power = packed[..., rows : rows + 1, :].astype(jnp.float32)
    return packed[..., :rows, :].astype(jnp.float32) * jnp.exp2(power - 14.0)


def swap(values, axis):
    return lax.ppermute(values, axis, [(0, 1), (1, 0)])


def around(values, axis, size, step):
    return lax.ppermute(values, axis, [(i, (i + step) % size) for i in range(size)])


def quad_sum(values, quad):
    first = lax.ppermute(values, QUAD, [(0, 1), (1, 2), (2, 0)])
    second = lax.ppermute(values, QUAD, [(0, 2), (1, 0), (2, 1)])
    return values + first + second


def col_sum(values):
    values = values + swap(values, "c")
    values = values + swap(values, "zh")
    return values + around(values, "x", 4, 1) + around(values, "x", 4, 2) + around(values, "x", 4, 3)


def core_part(values, core, own):
    half = values.shape[0] // 2
    return lax.dynamic_slice_in_dim(values, (core if own else 1 - core) * half, half, 0)


def joined_pair(mine, other, place):
    first = jnp.where(place == 0, mine, other)
    second = jnp.where(place == 0, other, mine)
    return jnp.concatenate([first, second], axis=0)


def local(
    joined_gradient,
    output_gradient,
    joined_left_basis,
    joined_right_basis,
    output_left_basis,
    output_right_basis,
    joined_left_eigen,
    joined_right_eigen,
    output_left_eigen,
    output_right_eigen,
    damping,
):
    damp = damping[0]
    quad = lax.axis_index("yb") * 2 + lax.axis_index("zb")
    octant = lax.axis_index("yp") * 2 + lax.axis_index("zp")
    core, high = lax.axis_index("c"), lax.axis_index("zh")
    is_output = quad == 3
    left_shift = shifted(jnp.where(is_output, output_left_eigen, joined_left_eigen), damp)
    right_shift = shifted(jnp.where(is_output, output_right_eigen, joined_right_eigen), damp)
    left_shift = left_shift.reshape(8, 2, 32).transpose(1, 0, 2).reshape(512)
    own_shift = lax.dynamic_slice_in_dim(left_shift, octant * 64, 64, 0)

    gradient = jnp.stack(
        [joined_gradient[:, :384], joined_gradient[:, 384:768], joined_gradient[:, 768:], output_gradient]
    )
    gradient = exchange(gradient, QUAD)

    left_j, left_o = joined_left_basis.T, output_left_basis.T
    left = jnp.stack([left_j, left_j, left_j, left_o])
    left = jnp.broadcast_to(left[:, None], (4, 8, 32, 192)).reshape(32, 32, 192)
    left = exchange(left, QUAD + ("x", "zh")).reshape(4, 256, 192)
    left = lax.all_gather(left, "c", axis=1, tiled=True)

    right = jnp.stack(
        [joined_right_basis.T[:, :384], joined_right_basis.T[:, 384:768], joined_right_basis.T[:, 768:], output_right_basis.T]
    )
    right = jnp.broadcast_to(right.reshape(1, 2, 1, 2, 16, 384), (4, 2, 2, 2, 16, 384)).reshape(32, 16, 384)
    right = exchange(right, FSDP).reshape(512, 384)

    rows = sum(
        jnp.dot(left[q], gradient[q], preferred_element_type=jnp.float32) for q in range(4)
    )
    rows = exchange(pack(rows.reshape(8, 64, 384)), OCT)
    rows = jnp.sum(unpack(rows), axis=0)

    core_sum = dot_wide_left(rows, right, ((1,), (1,)))
    core_sum = quad_sum(col_sum(core_sum), quad)
    mixed = rows / damp + dot_wide_left(core_sum * right_shift[None, :], right, ((1,), (0,)))
    mixed = mixed * own_shift[:, None]
    packed = pack(mixed)
    mixed = unpack(exchange(jnp.broadcast_to(packed[None], (8, 72, 384)), OCT)).reshape(512, 384)

    whole = gradient.reshape(768, 384)
    cols = lax.dot_general(whole, right, (((1,), (1,)), ((), ())), preferred_element_type=jnp.float32)
    cols = core_part(cols, core, True) + swap(core_part(cols, core, False), "c")
    cols = jnp.sum(exchange(cols.reshape(4, 96, 512), ("x",)), axis=0)
    cols = core_part(cols, high, True) + swap(core_part(cols, high, False), "zh")
    cols = quad_sum(cols, quad)
    cols = joined_pair(cols, swap(cols, "zh"), high)
    cols = exchange(jnp.broadcast_to(cols[None], (4, 96, 512)), ("x",)).reshape(384, 512)
    cols = joined_pair(cols, swap(cols, "c"), core)

    part = dot_wide_left(cols * (right_shift / damp)[None, :], right, ((1,), (0,))).reshape(4, 192, 384)
    high_mixed, low_mixed = halves(mixed)
    pieces = []
    for q in range(4):
        dot = lambda m: lax.dot_general(left[q], m, (((0,), (0,)), ((), ())), preferred_element_type=jnp.float32)
        pieces.append(part[q] + dot(high_mixed) + dot(low_mixed))
    update = unpack(exchange(pack(jnp.stack(pieces)), QUAD))
    square = damp * damp
    joined_update = jnp.concatenate([update[0], update[1], update[2]], axis=1) + joined_gradient.astype(jnp.float32) / damp / damp
    output_update = update[3] + output_gradient.astype(jnp.float32) / damp / damp
    return joined_update, output_update


def solution(mesh):
    fine = Mesh(mesh.devices.reshape(4, 2, 2, 2, 4, 2, 2), ("yp", "yb", "zp", "zb", "x", "zh", "c"))
    placed = (
        P(FSDP, COL),
        P(FSDP, COL),
        P(FSDP, COL),
        P(COL, FSDP),
        P(FSDP, COL),
        P(COL, FSDP),
        P(),
        P(),
        P(),
        P(),
        P(),
    )
    return jax.shard_map(
        local,
        mesh=fine,
        in_specs=placed,
        out_specs=(P(FSDP, COL), P(FSDP, COL)),
        check_vma=False,
    )
```

time: 755 us -> 220 us (0.29)
  waiting for transfers between devices: 590 us -> 64.8 us
  blocking collectives: 132 us -> 4.26 us
  starting transfers between devices: 0.12 us -> 108 us
  other arithmetic: 0.02 us -> 15 us
  local copies, waits for them, and re-layouts: 0.04 us -> 13.3 us
  between operations: 14.5 us -> 4.19 us
  matrix products: 17.3 us -> 9.03 us
    psum x2 -> x0, waiting for transfers between devices: 440 us -> none  [the longest x1 233 us: local(): lax.psum((row_partial(joined_left, joined_gradient), row_partial(output_l...]
    all_gather x1 -> x0, waiting for transfers between devices: 149 us -> none  [local(): lax.all_gather(joined_right_basis, 'fsdp', axis=1, tiled=True)]
    all_gather x3 -> x1, blocking collectives: 132 us -> 4.26 us  [local(): left = lax.all_gather(left, 'c', axis=1, tiled=True)]
    ppermute x0 -> x13, starting transfers between devices: none -> 55.6 us  [the longest x6 35.8 us: swap(): return lax.ppermute(values, axis, [(0, 1), (1, 0)])]
    all_to_all x0 -> x8, starting transfers between devices: none -> 52.1 us  [exchange(): return lax.all_to_all(blocks, axes, 0, 0, tiled=True)]
    all_to_all x0 -> x8, waiting for transfers between devices: none -> 43.7 us  [exchange(): return lax.all_to_all(blocks, axes, 0, 0, tiled=True)]
    ppermute x0 -> x13, waiting for transfers between devices: none -> 21.1 us  [the longest x6 17.9 us: swap(): return lax.ppermute(values, axis, [(0, 1), (1, 0)])]
    add x0 -> x8, other arithmetic: none -> 8.36 us  [the longest x1 2.16 us: local(): cols = core_part(cols, core, True) + swap(core_part(cols, core, False), 'c')]
  transfers between devices with their start and end apart: 3 -> 21, of which waited for: 3 -> 14; matrix products, arithmetic and copies ran while one was open for 1% -> 12% of each run, Pallas kernels for 0% -> 0%
where the time goes in v1:
time: 220 us; the launch traced here: 218 us
  starting transfers between devices  108 us (49%)
  waiting for transfers between devices  64.8 us (29%)
  other arithmetic  15 us (7%)
  local copies, waits for them, and re-layouts  13.3 us (6%)
  matrix products  9.03 us (4%)
  blocking collectives  4.26 us (2%)
  between operations  4.19 us (2%)
    all_to_all x8, starting transfers between devices, exchange(): return lax.all_to_all(blocks, axes, 0, 0, tiled=True)  52.1 us
    all_to_all x8, waiting for transfers between devices, exchange(): return lax.all_to_all(blocks, axes, 0, 0, tiled=True)  43.7 us
    ppermute x6, starting transfers between devices, swap(): return lax.ppermute(values, axis, [(0, 1), (1, 0)])  35.8 us
    ppermute x6, waiting for transfers between devices, swap(): return lax.ppermute(values, axis, [(0, 1), (1, 0)])  17.9 us
    ppermute x3, starting transfers between devices, around(): lax.ppermute(values, axis, [(i, (i + step) % size) for i in range(size)])  9 us
    ppermute x2, starting transfers between devices, quad_sum(): second = lax.ppermute(values, QUAD, [(0, 2), (1, 0), (2, 1)])  5.64 us
    ppermute x2, starting transfers between devices, quad_sum(): first = lax.ppermute(values, QUAD, [(0, 1), (1, 2), (2, 0)])  5.16 us
  transfers between devices with their start and end apart: 21, of which 14 were waited for; matrix products, arithmetic and copies ran while one was open for 12% of the time, Pallas kernels for 0%

profile of v1, /device:TPU:1, one launch (start us, length us, event | category | flops | bytes accessed | tf_op | source)
XLA Modules:
  0.0 218.3 jit_solution(13634699337015016761)
XLA Ops:
  0.6 0.8 pad_maximum_fusion.3
  1.5 0.8 broadcast_in_dim.13
  2.4 14.7 %all-to-all-start.4 = ((bf16[32,32,192]{2,1,0:T(8,128)(2,1)}), bf16[32,32,192]{2,1,0:T(8,128)(2,1)S(1)}, u32[]{:S(2)}, u32[]{:S(2)}) async-start(bf16[32,32,192]{2,1,0:T(8,128)(2,1)} %bitcast.21), calls=%async_computation.4 | async-start | bytes 1048576 | tf_op jit(solution)/shard_map/all_to_all | solution.py:18
  17.2 0.9 pad_maximum_fusion.1
  18.1 12.2 %all-to-all-done.4 = bf16[32,32,192]{2,1,0:T(8,128)(2,1)S(1)} async-done(((bf16[32,32,192]{2,1,0:T(8,128)(2,1)}), bf16[32,32,192]{2,1,0:T(8,128)(2,1)S(1)}, u32[]{:S(2)}, u32[]{:S(2)}) %all-to-all-start.4) | async-done | bytes 393248 | tf_op jit(solution)/shard_map/all_to_all | solution.py:18
  30.3 7.3 %all-to-all-start = ((bf16[4,192,384]{2,1,0:T(8,128)(2,1)}), bf16[4,192,384]{2,1,0:T(8,128)(2,1)S(1)}, u32[]{:S(2)}, u32[]{:S(2)}) async-start(bf16[4,192,384]{2,1,0:T(8,128)(2,1)} %pad_maximum_fusion.1), calls=%async_computation | async-start | bytes 1179648 | tf_op jit(solution)/shard_map/all_to_all | solution.py:18
  37.6 4.3 %all_gather.3 = bf16[4,512,192]{2,1,0:T(8,128)(2,1)S(1)} all-gather(bf16[4,256,192]{2,1,0:T(8,128)(2,1)S(1)} %bitcast.139), channel_id=1, replica_groups=mesh['yp'=4,'yb'=2,'zp'=2,'zb'=2,'x'=4,'zh'=2,'c'=2] {'c'}, dimensions={1}, use_global_device_ids=true | all-gather | bytes 1179648 | tf_op jit(solution)/shard_map/all_gather | solution.py:115
  41.9 2.5 %all-to-all-done = bf16[4,192,384]{2,1,0:T(8,128)(2,1)S(1)} async-done(((bf16[4,192,384]{2,1,0:T(8,128)(2,1)}), bf16[4,192,384]{2,1,0:T(8,128)(2,1)S(1)}, u32[]{:S(2)}, u32[]{:S(2)}) %all-to-all-start) | async-done | bytes 589856 | tf_op jit(solution)/shard_map/all_to_all | solution.py:18
  44.4 0.8 broadcast_in_dim.11
  45.2 11.1 %all-to-all-start.1 = ((bf16[32,16,384]{2,1,0:T(8,128)(2,1)}), bf16[32,16,384]{2,1,0:T(8,128)(2,1)S(1)}, u32[]{:S(2)}, u32[]{:S(2)}) async-start(bf16[32,16,384]{2,1,0:T(8,128)(2,1)} %bitcast.12), calls=%async_computation.1 | async-start | bytes 786432 | tf_op jit(solution)/shard_map/all_to_all | solution.py:18
  57.2 0.9 abs_reduce_fusion.1
  59.0 0.9 concatenate.20
  59.8 9.8 %all-to-all-done.1 = bf16[32,16,384]{2,1,0:T(8,128)(2,1)S(1)} async-done(((bf16[32,16,384]{2,1,0:T(8,128)(2,1)}), bf16[32,16,384]{2,1,0:T(8,128)(2,1)S(1)}, u32[]{:S(2)}, u32[]{:S(2)}) %all-to-all-start.1) | async-done | bytes 393248 | tf_op jit(solution)/shard_map/all_to_all | solution.py:18
  69.7 4.2 %all-to-all-start.5 = ((f16[8,72,384]{2,1,0:T(8,128)(2,1)}), f16[8,72,384]{2,1,0:T(8,128)(2,1)}, u32[]{:S(2)}, u32[]{:S(2)}) async-start(f16[8,72,384]{2,1,0:T(8,128)(2,1)} %concatenate.20), calls=%async_computation.5 | async-start | bytes 884736 | tf_op jit(solution)/shard_map/all_to_all | solution.py:18
  73.9 1.7 fusion.29
  75.5 0.9 constant_dynamic-slice_fusion.1
  76.5 5.3 %collective-permute-start = (f32[384,512]{1,0:T(8,128)}, f32[384,512]{1,0:T(8,128)}, u32[]{:S(2)}, u32[]{:S(2)}) collective-permute-start(f32[384,512]{1,0:T(8,128)} %constant_dynamic-slice_fusion.1), channel_id=1, source_target_pairs={{0,1},{1,0},{2,3},{3,2},{4,5},{5,4},{6,7},{7,6},{8,9},{9,8},{10,11... | collective-permute-start | bytes 2359304 | tf_op jit(solution)/shard_map/ppermute | solution.py:53
  81.8 2.4 %all-to-all-done.5 = f16[8,72,384]{2,1,0:T(8,128)(2,1)} async-done(((f16[8,72,384]{2,1,0:T(8,128)(2,1)}), f16[8,72,384]{2,1,0:T(8,128)(2,1)}, u32[]{:S(2)}, u32[]{:S(2)}) %all-to-all-start.5) | async-done | bytes 442400 | tf_op jit(solution)/shard_map/all_to_all | solution.py:18
  84.2 0.8 slice.137
  85.1 1.1 multiply_reduce_fusion
  86.4 0.9 convolution_add_fusion.8
  87.3 7.5 %collective-permute-start.6 = (f32[64,512]{1,0:T(8,128)}, f32[64,512]{1,0:T(8,128)}, u32[]{:S(2)}, u32[]{:S(2)}) collective-permute-start(f32[64,512]{1,0:T(8,128)} %convolution_add_fusion.8), channel_id=1, source_target_pairs={{0,1},{1,0},{2,3},{3,2},{4,5},{5,4},{6,7},{7,6},{8,9},{9,8},{10,11... | collective-permute-start | bytes 393224 | tf_op jit(solution)/shard_map/ppermute | solution.py:53
  96.1 1.6 add.140
  97.7 4.1 %collective-permute-start.7 = (f32[64,512]{1,0:T(8,128)}, f32[64,512]{1,0:T(8,128)}, u32[]{:S(2)}, u32[]{:S(2)}) collective-permute-start(f32[64,512]{1,0:T(8,128)} %add.140), channel_id=1, source_target_pairs={{0,2},{2,0},{1,3},{3,1},{4,6},{6,4},{5,7},{7,5},{8,10},{10,8},{9,1... | collective-permute-start | bytes 393224 | tf_op jit(solution)/shard_map/ppermute | solution.py:53
  101.9 1.3 divide_subtract_fusion
  103.1 1.3 reshape.68
  104.5 1.3 copy.20
  105.8 1.4 reshape.69
  107.1 1.2 dynamic_slice.19
  108.3 3.3 %collective-permute-done.7 = f32[64,512]{1,0:T(8,128)} collective-permute-done((f32[64,512]{1,0:T(8,128)}, f32[64,512]{1,0:T(8,128)}, u32[]{:S(2)}, u32[]{:S(2)}) %collective-permute-start.7) | collective-permute-done | bytes 131104 | tf_op jit(solution)/shard_map/ppermute | solution.py:53
  111.6 1.6 add.141
  113.2 1.9 collective-permute-start.10
  115.2 3.4 %collective-permute-start.8 = (f32[64,512]{1,0:T(8,128)}, f32[64,512]{1,0:T(8,128)}, u32[]{:S(2)}, u32[]{:S(2)}) collective-permute-start(f32[64,512]{1,0:T(8,128)} %add.141), channel_id=1, source_target_pairs={{0,4},{4,8},{8,12},{12,0},{1,5},{5,9},{9,13},{13,1},{2,6},{6,10},{... | collective-permute-start | bytes 393224 | tf_op jit(solution)/shard_map/ppermute | solution.py:57
  118.5 3.7 %collective-permute-start.9 = (f32[64,512]{1,0:T(8,128)}, f32[64,512]{1,0:T(8,128)}, u32[]{:S(2)}, u32[]{:S(2)}) collective-permute-start(f32[64,512]{1,0:T(8,128)} %add.141), channel_id=1, source_target_pairs={{0,8},{4,12},{8,0},{12,4},{1,9},{5,13},{9,1},{13,5},{2,10},{6,14},... | collective-permute-start | bytes 393224 | tf_op jit(solution)/shard_map/ppermute | solution.py:57
  122.3 2.2 dynamic-slice_add_fusion
  124.4 3.6 %all-to-all-start.2 = ((f32[4,96,512]{2,1,0:T(8,128)}), f32[4,96,512]{2,1,0:T(8,128)S(1)}, u32[]{:S(2)}, u32[]{:S(2)}) async-start(f32[4,96,512]{2,1,0:T(8,128)} %bitcast.137), calls=%async_computation.2 | async-start | bytes 1572864 | tf_op jit(solution)/shard_map/all_to_all | solution.py:18
  128.1 1.1 add_add_fusion
  129.3 1.9 collective-permute-start.11
  131.2 3.4 %collective-permute-start.12 = (f32[64,512]{1,0:T(8,128)S(1)}, f32[64,512]{1,0:T(8,128)S(1)}, u32[]{:S(2)}, u32[]{:S(2)}) collective-permute-start(f32[64,512]{1,0:T(8,128)S(1)} %add_add_fusion), channel_id=1, source_target_pairs={{0,64},{16,0},{64,16},{1,65},{17,1},{65,17},{2,66},{18,2},{66,18},... | collective-permute-start | bytes 393224 | tf_op jit(solution)/shard_map/ppermute | solution.py:62
  134.6 0.7 collective-permute-done.11
  135.3 2.5 %collective-permute-done.12 = f32[64,512]{1,0:T(8,128)S(1)} collective-permute-done((f32[64,512]{1,0:T(8,128)S(1)}, f32[64,512]{1,0:T(8,128)S(1)}, u32[]{:S(2)}, u32[]{:S(2)}) %collective-permute-start.12) | collective-permute-done | bytes 131104 | tf_op jit(solution)/shard_map/ppermute | solution.py:62
  138.0 1.0 all-to-all-done.2
  139.1 2.6 %collective-permute-start.1 = (f32[48,512]{1,0:T(8,128)S(1)}, f32[48,512]{1,0:T(8,128)S(1)}, u32[]{:S(2)}, u32[]{:S(2)}) collective-permute-start(f32[48,512]{1,0:T(8,128)S(1)} %constant_dynamic-slice_fusion), channel_id=1, source_target_pairs={{0,2},{2,0},{1,3},{3,1},{4,6},{6,4},{5,7},{7,5},{8,10},{10,8},{9,1... | collective-permute-start | bytes 294920 | tf_op jit(solution)/shard_map/ppermute | solution.py:53
  141.7 0.8 abs_reduce_fusion.2
  143.3 5.2 %collective-permute-done.1 = f32[48,512]{1,0:T(8,128)S(1)} collective-permute-done((f32[48,512]{1,0:T(8,128)S(1)}, f32[48,512]{1,0:T(8,128)S(1)}, u32[]{:S(2)}, u32[]{:S(2)}) %collective-permute-start.1) | collective-permute-done | bytes 98336 | tf_op jit(solution)/shard_map/ppermute | solution.py:53
  148.5 3.2 %collective-permute-start.2 = (f32[48,512]{1,0:T(8,128)S(1)}, f32[48,512]{1,0:T(8,128)S(1)}, u32[]{:S(2)}, u32[]{:S(2)}) collective-permute-start(f32[48,512]{1,0:T(8,128)S(1)} %dynamic-slice_add_fusion.1), channel_id=1, source_target_pairs={{0,16},{16,64},{64,0},{1,17},{17,65},{65,1},{2,18},{18,66},{66,2},... | collective-permute-start | bytes 294920 | tf_op jit(solution)/shard_map/ppermute | solution.py:61
  151.7 2.3 %collective-permute-start.3 = (f32[48,512]{1,0:T(8,128)S(1)}, f32[48,512]{1,0:T(8,128)S(1)}, u32[]{:S(2)}, u32[]{:S(2)}) collective-permute-start(f32[48,512]{1,0:T(8,128)S(1)} %dynamic-slice_add_fusion.1), channel_id=1, source_target_pairs={{0,64},{16,0},{64,16},{1,65},{17,1},{65,17},{2,66},{18,2},{66,18},... | collective-permute-start | bytes 294920 | tf_op jit(solution)/shard_map/ppermute | solution.py:62
  154.1 0.8 broadcast_in_dim.14
  154.9 4.1 %all-to-all-start.6 = ((f16[8,72,384]{2,1,0:T(8,128)(2,1)}), f16[8,72,384]{2,1,0:T(8,128)(2,1)S(1)}, u32[]{:S(2)}, u32[]{:S(2)}) async-start(f16[8,72,384]{2,1,0:T(8,128)(2,1)} %broadcast_in_dim.14), calls=%async_computation.6 | async-start | bytes 884736 | tf_op jit(solution)/shard_map/all_to_all | solution.py:18
  159.0 4.2 %collective-permute-start.4 = (f32[48,512]{1,0:T(8,128)S(1)}, f32[48,512]{1,0:T(8,128)S(1)}, u32[]{:S(2)}, u32[]{:S(2)}) collective-permute-start(f32[48,512]{1,0:T(8,128)S(1)} %add_add_fusion.1), channel_id=1, source_target_pairs={{0,2},{2,0},{1,3},{3,1},{4,6},{6,4},{5,7},{7,5},{8,10},{10,8},{9,1... | collective-permute-start | bytes 294920 | tf_op jit(solution)/shard_map/ppermute | solution.py:53
  163.3 8.2 %collective-permute-done.4 = f32[48,512]{1,0:T(8,128)S(1)} collective-permute-done((f32[48,512]{1,0:T(8,128)S(1)}, f32[48,512]{1,0:T(8,128)S(1)}, u32[]{:S(2)}, u32[]{:S(2)}) %collective-permute-start.4) | collective-permute-done | bytes 98336 | tf_op jit(solution)/shard_map/ppermute | solution.py:53
  171.5 1.0 broadcast_in_dim.12
  172.5 3.5 %all-to-all-start.3 = ((f32[4,96,512]{2,1,0:T(8,128)}), f32[4,96,512]{2,1,0:T(8,128)S(1)}, u32[]{:S(2)}, u32[]{:S(2)}) async-start(f32[4,96,512]{2,1,0:T(8,128)} %broadcast_in_dim.12), calls=%async_computation.3 | async-start | bytes 1572864 | tf_op jit(solution)/shard_map/all_to_all | solution.py:18
  176.1 1.2 reduce-precision_convert_fusion.1
  177.3 7.1 %all-to-all-done.3 = f32[4,96,512]{2,1,0:T(8,128)S(1)} async-done(((f32[4,96,512]{2,1,0:T(8,128)}), f32[4,96,512]{2,1,0:T(8,128)S(1)}, u32[]{:S(2)}, u32[]{:S(2)}) %all-to-all-start.3) | async-done | bytes 786464 | tf_op jit(solution)/shard_map/all_to_all | solution.py:18
  184.3 12.0 %collective-permute-start.5 = (f32[384,512]{1,0:T(8,128)S(1)}, f32[384,512]{1,0:T(8,128)S(1)}, u32[]{:S(2)}, u32[]{:S(2)}) collective-permute-start(f32[384,512]{1,0:T(8,128)S(1)} %bitcast.138), channel_id=1, source_target_pairs={{0,1},{1,0},{2,3},{3,2},{4,5},{5,4},{6,7},{7,6},{8,9},{9,8},{10,11... | collective-permute-start | bytes 2359304 | tf_op jit(solution)/shard_map/ppermute | solution.py:53
  197.6 0.7 collective-permute-done.5
  200.9 0.7 abs_reduce_fusion
  202.4 0.9 concatenate.22
  203.4 3.5 %all-to-all-start.7 = ((f16[4,200,384]{2,1,0:T(8,128)(2,1)}), f16[4,200,384]{2,1,0:T(8,128)(2,1)S(1)}, u32[]{:S(2)}, u32[]{:S(2)}) async-start(f16[4,200,384]{2,1,0:T(8,128)(2,1)} %concatenate.22), calls=%async_computation.7 | async-start | bytes 1228800 | tf_op jit(solution)/shard_map/all_to_all | solution.py:18
  206.9 8.7 %all-to-all-done.7 = f16[4,200,384]{2,1,0:T(8,128)(2,1)S(1)} async-done(((f16[4,200,384]{2,1,0:T(8,128)(2,1)}), f16[4,200,384]{2,1,0:T(8,128)(2,1)S(1)}, u32[]{:S(2)}, u32[]{:S(2)}) %all-to-all-start.7) | async-done | bytes 614432 | tf_op jit(solution)/shard_map/all_to_all | solution.py:18
  215.8 0.8 copy-done.4
  216.6 0.7 fusion.12
  217.3 1.0 maximum_add_fusion
  (65 shorter events, 6.3 us)
Async XLA Ops:
  0.6 16.4 %copy-start.1 = (bf16[192,1152]{1,0:T(8,128)(2,1)S(1)}, bf16[192,1152]{1,0:T(8,128)(2,1)}, u32[]{:S(2)}) copy-start(bf16[192,1152]{1,0:T(8,128)(2,1)} %param.11) | copy-start | bytes 1327108
  1.5 15.6 %copy-start.3 = (bf16[192,384]{1,0:T(8,128)(2,1)S(1)}, bf16[192,384]{1,0:T(8,128)(2,1)}, u32[]{:S(2)}) copy-start(bf16[192,384]{1,0:T(8,128)(2,1)} %param.12) | copy-start | bytes 442372
  2.4 27.9 %all-to-all-start.4 = ((bf16[32,32,192]{2,1,0:T(8,128)(2,1)}), bf16[32,32,192]{2,1,0:T(8,128)(2,1)S(1)}, u32[]{:S(2)}, u32[]{:S(2)}) async-start(bf16[32,32,192]{2,1,0:T(8,128)(2,1)} %bitcast.21), calls=%async_computation.4 | async-start | bytes 1048576 | tf_op jit(solution)/shard_map/all_to_all | solution.py:18
  17.1 20.5 %copy-start.5 = (bf16[1152,16]{0,1:T(8,128)(2,1)S(1)}, bf16[1152,16]{0,1:T(8,128)(2,1)}, u32[]{:S(2)}) copy-start(bf16[1152,16]{0,1:T(8,128)(2,1)} %param.14) | copy-start | bytes 110596
  17.2 20.5 %copy-start.6 = (bf16[384,16]{0,1:T(8,128)(2,1)S(1)}, bf16[384,16]{0,1:T(8,128)(2,1)}, u32[]{:S(2)}) copy-start(bf16[384,16]{0,1:T(8,128)(2,1)} %param.16) | copy-start | bytes 36868
  30.3 14.1 %all-to-all-start = ((bf16[4,192,384]{2,1,0:T(8,128)(2,1)}), bf16[4,192,384]{2,1,0:T(8,128)(2,1)S(1)}, u32[]{:S(2)}, u32[]{:S(2)}) async-start(bf16[4,192,384]{2,1,0:T(8,128)(2,1)} %pad_maximum_fusion.1), calls=%async_computation | async-start | bytes 1179648 | tf_op jit(solution)/shard_map/all_to_all | solution.py:18
  44.4 12.9 %copy-start = (bf16[4,192,384]{2,1,0:T(8,128)(2,1)}, bf16[4,192,384]{2,1,0:T(8,128)(2,1)S(1)}, u32[]{:S(2)}) copy-start(bf16[4,192,384]{2,1,0:T(8,128)(2,1)S(1)} %all-to-all-done) | copy-start | bytes 1769476
  45.2 24.4 %all-to-all-start.1 = ((bf16[32,16,384]{2,1,0:T(8,128)(2,1)}), bf16[32,16,384]{2,1,0:T(8,128)(2,1)S(1)}, u32[]{:S(2)}, u32[]{:S(2)}) async-start(bf16[32,16,384]{2,1,0:T(8,128)(2,1)} %bitcast.12), calls=%async_computation.1 | async-start | bytes 786432 | tf_op jit(solution)/shard_map/all_to_all | solution.py:18
  69.7 14.6 %all-to-all-start.5 = ((f16[8,72,384]{2,1,0:T(8,128)(2,1)}), f16[8,72,384]{2,1,0:T(8,128)(2,1)}, u32[]{:S(2)}, u32[]{:S(2)}) async-start(f16[8,72,384]{2,1,0:T(8,128)(2,1)} %concatenate.20), calls=%async_computation.5 | async-start | bytes 884736 | tf_op jit(solution)/shard_map/all_to_all | solution.py:18
  76.5 45.8 %collective-permute-start = (f32[384,512]{1,0:T(8,128)}, f32[384,512]{1,0:T(8,128)}, u32[]{:S(2)}, u32[]{:S(2)}) collective-permute-start(f32[384,512]{1,0:T(8,128)} %constant_dynamic-slice_fusion.1), channel_id=1, source_target_pairs={{0,1},{1,0},{2,3},{3,2},{4,5},{5,4},{6,7},{7,6},{8,9},{9,8},{10,11... | collective-permute-start | bytes 2359304 | tf_op jit(solution)/shard_map/ppermute | solution.py:53
  87.3 8.8 %collective-permute-start.6 = (f32[64,512]{1,0:T(8,128)}, f32[64,512]{1,0:T(8,128)}, u32[]{:S(2)}, u32[]{:S(2)}) collective-permute-start(f32[64,512]{1,0:T(8,128)} %convolution_add_fusion.8), channel_id=1, source_target_pairs={{0,1},{1,0},{2,3},{3,2},{4,5},{5,4},{6,7},{7,6},{8,9},{9,8},{10,11... | collective-permute-start | bytes 393224 | tf_op jit(solution)/shard_map/ppermute | solution.py:53
  97.7 13.9 %collective-permute-start.7 = (f32[64,512]{1,0:T(8,128)}, f32[64,512]{1,0:T(8,128)}, u32[]{:S(2)}, u32[]{:S(2)}) collective-permute-start(f32[64,512]{1,0:T(8,128)} %add.140), channel_id=1, source_target_pairs={{0,2},{2,0},{1,3},{3,1},{4,6},{6,4},{5,7},{7,5},{8,10},{10,8},{9,1... | collective-permute-start | bytes 393224 | tf_op jit(solution)/shard_map/ppermute | solution.py:53
  113.2 14.8 %collective-permute-start.10 = (f32[64,512]{1,0:T(8,128)}, f32[64,512]{1,0:T(8,128)}, u32[]{:S(2)}, u32[]{:S(2)}) collective-permute-start(f32[64,512]{1,0:T(8,128)} %add.141), channel_id=1, source_target_pairs={{0,12},{4,0},{8,4},{12,8},{1,13},{5,1},{9,5},{13,9},{2,14},{6,2},{... | collective-permute-start | bytes 393224 | tf_op jit(solution)/shard_map/ppermute | solution.py:57
  115.2 12.9 %collective-permute-start.8 = (f32[64,512]{1,0:T(8,128)}, f32[64,512]{1,0:T(8,128)}, u32[]{:S(2)}, u32[]{:S(2)}) collective-permute-start(f32[64,512]{1,0:T(8,128)} %add.141), channel_id=1, source_target_pairs={{0,4},{4,8},{8,12},{12,0},{1,5},{5,9},{9,13},{13,1},{2,6},{6,10},{... | collective-permute-start | bytes 393224 | tf_op jit(solution)/shard_map/ppermute | solution.py:57
  118.5 9.6 %collective-permute-start.9 = (f32[64,512]{1,0:T(8,128)}, f32[64,512]{1,0:T(8,128)}, u32[]{:S(2)}, u32[]{:S(2)}) collective-permute-start(f32[64,512]{1,0:T(8,128)} %add.141), channel_id=1, source_target_pairs={{0,8},{4,12},{8,0},{12,4},{1,9},{5,13},{9,1},{13,5},{2,10},{6,14},... | collective-permute-start | bytes 393224 | tf_op jit(solution)/shard_map/ppermute | solution.py:57
  124.4 10.1 %copy-start.7 = (f32[512]{0:T(512)S(1)}, f32[512]{0:T(512)}, u32[]{:S(2)}) copy-start(f32[512]{0:T(512)} %param.20) | copy-start | bytes 6148
  124.4 10.1 %copy-start.8 = (f32[512]{0:T(512)S(1)}, f32[512]{0:T(512)}, u32[]{:S(2)}) copy-start(f32[512]{0:T(512)} %param.18) | copy-start | bytes 6148
  124.4 14.6 %all-to-all-start.2 = ((f32[4,96,512]{2,1,0:T(8,128)}), f32[4,96,512]{2,1,0:T(8,128)S(1)}, u32[]{:S(2)}, u32[]{:S(2)}) async-start(f32[4,96,512]{2,1,0:T(8,128)} %bitcast.137), calls=%async_computation.2 | async-start | bytes 1572864 | tf_op jit(solution)/shard_map/all_to_all | solution.py:18
  129.2 12.5 %copy-start.9 = (f32[64]{0:T(128)S(1)}, f32[64]{0:T(128)}, u32[]{:S(2)}) copy-start(f32[64]{0:T(128)} %dynamic_slice.19) | copy-start | bytes 772
  129.3 6.0 %collective-permute-start.11 = (f32[64,512]{1,0:T(8,128)S(1)}, f32[64,512]{1,0:T(8,128)S(1)}, u32[]{:S(2)}, u32[]{:S(2)}) collective-permute-start(f32[64,512]{1,0:T(8,128)S(1)} %add_add_fusion), channel_id=1, source_target_pairs={{0,16},{16,64},{64,0},{1,17},{17,65},{65,1},{2,18},{18,66},{66,2},... | collective-permute-start | bytes 393224 | tf_op jit(solution)/shard_map/ppermute | solution.py:61
  131.2 6.6 %collective-permute-start.12 = (f32[64,512]{1,0:T(8,128)S(1)}, f32[64,512]{1,0:T(8,128)S(1)}, u32[]{:S(2)}, u32[]{:S(2)}) collective-permute-start(f32[64,512]{1,0:T(8,128)S(1)} %add_add_fusion), channel_id=1, source_target_pairs={{0,64},{16,0},{64,16},{1,65},{17,1},{65,17},{2,66},{18,2},{66,18},... | collective-permute-start | bytes 393224 | tf_op jit(solution)/shard_map/ppermute | solution.py:62
  139.1 9.4 %collective-permute-start.1 = (f32[48,512]{1,0:T(8,128)S(1)}, f32[48,512]{1,0:T(8,128)S(1)}, u32[]{:S(2)}, u32[]{:S(2)}) collective-permute-start(f32[48,512]{1,0:T(8,128)S(1)} %constant_dynamic-slice_fusion), channel_id=1, source_target_pairs={{0,2},{2,0},{1,3},{3,1},{4,6},{6,4},{5,7},{7,5},{8,10},{10,8},{9,1... | collective-permute-start | bytes 294920 | tf_op jit(solution)/shard_map/ppermute | solution.py:53
  148.5 10.5 %collective-permute-start.2 = (f32[48,512]{1,0:T(8,128)S(1)}, f32[48,512]{1,0:T(8,128)S(1)}, u32[]{:S(2)}, u32[]{:S(2)}) collective-permute-start(f32[48,512]{1,0:T(8,128)S(1)} %dynamic-slice_add_fusion.1), channel_id=1, source_target_pairs={{0,16},{16,64},{64,0},{1,17},{17,65},{65,1},{2,18},{18,66},{66,2},... | collective-permute-start | bytes 294920 | tf_op jit(solution)/shard_map/ppermute | solution.py:61
  151.7 7.3 %collective-permute-start.3 = (f32[48,512]{1,0:T(8,128)S(1)}, f32[48,512]{1,0:T(8,128)S(1)}, u32[]{:S(2)}, u32[]{:S(2)}) collective-permute-start(f32[48,512]{1,0:T(8,128)S(1)} %dynamic-slice_add_fusion.1), channel_id=1, source_target_pairs={{0,64},{16,0},{64,16},{1,65},{17,1},{65,17},{2,66},{18,2},{66,18},... | collective-permute-start | bytes 294920 | tf_op jit(solution)/shard_map/ppermute | solution.py:62
  154.9 16.6 %all-to-all-start.6 = ((f16[8,72,384]{2,1,0:T(8,128)(2,1)}), f16[8,72,384]{2,1,0:T(8,128)(2,1)S(1)}, u32[]{:S(2)}, u32[]{:S(2)}) async-start(f16[8,72,384]{2,1,0:T(8,128)(2,1)} %broadcast_in_dim.14), calls=%async_computation.6 | async-start | bytes 884736 | tf_op jit(solution)/shard_map/all_to_all | solution.py:18
  159.0 12.4 %collective-permute-start.4 = (f32[48,512]{1,0:T(8,128)S(1)}, f32[48,512]{1,0:T(8,128)S(1)}, u32[]{:S(2)}, u32[]{:S(2)}) collective-permute-start(f32[48,512]{1,0:T(8,128)S(1)} %add_add_fusion.1), channel_id=1, source_target_pairs={{0,2},{2,0},{1,3},{3,1},{4,6},{6,4},{5,7},{7,5},{8,10},{10,8},{9,1... | collective-permute-start | bytes 294920 | tf_op jit(solution)/shard_map/ppermute | solution.py:53
  171.5 4.5 %copy-start.2 = (f16[8,72,384]{2,1,0:T(8,128)(2,1)}, f16[8,72,384]{2,1,0:T(8,128)(2,1)S(1)}, u32[]{:S(2)}) copy-start(f16[8,72,384]{2,1,0:T(8,128)(2,1)S(1)} %all-to-all-done.6) | copy-start | bytes 1327108
  172.5 11.8 %all-to-all-start.3 = ((f32[4,96,512]{2,1,0:T(8,128)}), f32[4,96,512]{2,1,0:T(8,128)S(1)}, u32[]{:S(2)}, u32[]{:S(2)}) async-start(f32[4,96,512]{2,1,0:T(8,128)} %broadcast_in_dim.12), calls=%async_computation.3 | async-start | bytes 1572864 | tf_op jit(solution)/shard_map/all_to_all | solution.py:18
  184.3 13.9 %collective-permute-start.5 = (f32[384,512]{1,0:T(8,128)S(1)}, f32[384,512]{1,0:T(8,128)S(1)}, u32[]{:S(2)}, u32[]{:S(2)}) collective-permute-start(f32[384,512]{1,0:T(8,128)S(1)} %bitcast.138), channel_id=1, source_target_pairs={{0,1},{1,0},{2,3},{3,2},{4,5},{5,4},{6,7},{7,6},{8,9},{9,8},{10,11... | collective-permute-start | bytes 2359304 | tf_op jit(solution)/shard_map/ppermute | solution.py:53
  203.4 12.2 %all-to-all-start.7 = ((f16[4,200,384]{2,1,0:T(8,128)(2,1)}), f16[4,200,384]{2,1,0:T(8,128)(2,1)S(1)}, u32[]{:S(2)}, u32[]{:S(2)}) async-start(f16[4,200,384]{2,1,0:T(8,128)(2,1)} %concatenate.22), calls=%async_computation.7 | async-start | bytes 1228800 | tf_op jit(solution)/shard_map/all_to_all | solution.py:18
  215.7 0.9 copy-start.4

commit v2 on v1

--- a/solution.py
+++ b/solution.py
@@ -101,28 +101,28 @@
     left_shift = shifted(jnp.where(is_output, output_left_eigen, joined_left_eigen), damp)
     right_shift = shifted(jnp.where(is_output, output_right_eigen, joined_right_eigen), damp)
     left_shift = left_shift.reshape(8, 2, 32).transpose(1, 0, 2).reshape(512)
+    right_shift = right_shift.reshape(4, 2, 2, 2, 16).transpose(0, 2, 1, 3, 4).reshape(512)
     own_shift = lax.dynamic_slice_in_dim(left_shift, octant * 64, 64, 0)
 
-    gradient = jnp.stack(
-        [joined_gradient[:, :384], joined_gradient[:, 384:768], joined_gradient[:, 768:], output_gradient]
-    )
-    gradient = exchange(gradient, QUAD)
+    left_j, left_o = joined_left_basis.T, output_left_basis.T
+    right_j, right_o = joined_right_basis.T, output_right_basis.T
+    gradients = (joined_gradient[:, :384], joined_gradient[:, 384:768], joined_gradient[:, 768:], output_gradient)
+    rights = (right_j[:, :384], right_j[:, 384:768], right_j[:, 768:], right_o)
+    lefts = [jnp.concatenate([left[:16], left[16:]], axis=1) for left in (left_j, left_o)]
+    lefts = (lefts[0], lefts[0], lefts[0], lefts[1])
+    sent = jnp.stack([jnp.concatenate(three, axis=0) for three in zip(gradients, rights, lefts)])
+    got = exchange(sent, QUAD)
+    gradient = got[:, :192].reshape(768, 384)
 
-    left_j, left_o = joined_left_basis.T, output_left_basis.T
-    left = jnp.stack([left_j, left_j, left_j, left_o])
-    left = jnp.broadcast_to(left[:, None], (4, 8, 32, 192)).reshape(32, 32, 192)
-    left = exchange(left, QUAD + ("x", "zh")).reshape(4, 256, 192)
-    left = lax.all_gather(left, "c", axis=1, tiled=True)
+    left = jnp.concatenate([got[:, 208:, :192], got[:, 208:, 192:]], axis=1)
+    left = left.transpose(1, 0, 2).reshape(32, 768)
+    left = exchange(jnp.broadcast_to(left[None], (8, 32, 768)), ("x", "zh")).reshape(256, 768)
+    left = lax.all_gather(left, "c", axis=0, tiled=True)
 
-    right = jnp.stack(
-        [joined_right_basis.T[:, :384], joined_right_basis.T[:, 384:768], joined_right_basis.T[:, 768:], output_right_basis.T]
-    )
-    right = jnp.broadcast_to(right.reshape(1, 2, 1, 2, 16, 384), (4, 2, 2, 2, 16, 384)).reshape(32, 16, 384)
-    right = exchange(right, FSDP).reshape(512, 384)
+    right = got[:, 192:208].reshape(64, 384)
+    right = exchange(jnp.broadcast_to(right[None], (8, 64, 384)), OCT).reshape(512, 384)
 
-    rows = sum(
-        jnp.dot(left[q], gradient[q], preferred_element_type=jnp.float32) for q in range(4)
-    )
+    rows = jnp.dot(left, gradient, preferred_element_type=jnp.float32)
     rows = exchange(pack(rows.reshape(8, 64, 384)), OCT)
     rows = jnp.sum(unpack(rows), axis=0)
 
@@ -133,8 +133,7 @@
     packed = pack(mixed)
     mixed = unpack(exchange(jnp.broadcast_to(packed[None], (8, 72, 384)), OCT)).reshape(512, 384)
 
-    whole = gradient.reshape(768, 384)
-    cols = lax.dot_general(whole, right, (((1,), (1,)), ((), ())), preferred_element_type=jnp.float32)
+    cols = lax.dot_general(gradient, right, (((1,), (1,)), ((), ())), preferred_element_type=jnp.float32)
     cols = core_part(cols, core, True) + swap(core_part(cols, core, False), "c")
     cols = jnp.sum(exchange(cols.reshape(4, 96, 512), ("x",)), axis=0)
     cols = core_part(cols, high, True) + swap(core_part(cols, high, False), "zh")
@@ -143,14 +142,9 @@
     cols = exchange(jnp.broadcast_to(cols[None], (4, 96, 512)), ("x",)).reshape(384, 512)
     cols = joined_pair(cols, swap(cols, "c"), core)
 
-    part = dot_wide_left(cols * (right_shift / damp)[None, :], right, ((1,), (0,))).reshape(4, 192, 384)
-    high_mixed, low_mixed = halves(mixed)
-    pieces = []
-    for q in range(4):
-        dot = lambda m: lax.dot_general(left[q], m, (((0,), (0,)), ((), ())), preferred_element_type=jnp.float32)
-        pieces.append(part[q] + dot(high_mixed) + dot(low_mixed))
-    update = unpack(exchange(pack(jnp.stack(pieces)), QUAD))
-    square = damp * damp
+    part = dot_wide_left(cols * (right_shift / damp)[None, :], right, ((1,), (0,)))
+    update = part + dot_wide_right(left, mixed, ((0,), (0,)))
+    update = unpack(exchange(pack(update.reshape(4, 192, 384)), QUAD))
     joined_update = jnp.concatenate([update[0], update[1], update[2]], axis=1) + joined_gradient.astype(jnp.float32) / damp / damp
     output_update = update[3] + output_gradient.astype(jnp.float32) / damp / damp
     return joined_update, output_update

time: 220 us -> 212 us (0.964)
  blocking collectives: 4.26 us -> 15.7 us
  other arithmetic: 15 us -> 7.07 us
  starting transfers between devices: 108 us -> 104 us
  waiting for transfers between devices: 64.8 us -> 61.3 us
  matrix products: 9.03 us -> 6.27 us
    all_to_all x0 -> x1, blocking collectives: none -> 12.1 us  [exchange(): return lax.all_to_all(blocks, axes, 0, 0, tiled=True)]
    all_to_all x8 -> x7, waiting for transfers between devices: 43.7 us -> 33.5 us  [exchange(): return lax.all_to_all(blocks, axes, 0, 0, tiled=True)]
    ppermute x6, waiting for transfers between devices: 17.9 us -> 24.9 us  [swap(): return lax.ppermute(values, axis, [(0, 1), (1, 0)])]
    ppermute x6, starting transfers between devices: 35.8 us -> 31.3 us  [swap(): return lax.ppermute(values, axis, [(0, 1), (1, 0)])]
    slice x0 -> x7, local copies, waits for them, and re-layouts: none -> 3.43 us  [the longest x2 1.44 us: local(): left[:16]]
    all_to_all x8 -> x7, starting transfers between devices: 52.1 us -> 55.1 us  [exchange(): return lax.all_to_all(blocks, axes, 0, 0, tiled=True)]
    dot_general x13 -> x4, matrix products: 5.73 us -> 2.99 us  [the longest x2 1.2 us: dot_wide_right(): lax.dot_general(narrow, part, (dims, ((), ())), preferred_element_type=jn...]
    reshape x2, local copies, waits for them, and re-layouts: 2.69 us -> 0.16 us  [local(): left_shift = left_shift.reshape(8, 2, 32).transpose(1, 0, 2).reshape(512)]
  transfers between devices with their start and end apart: 21 -> 20, of which waited for: 14 -> 11; matrix products, arithmetic and copies ran while one was open for 12% -> 6% of each run, Pallas kernels for 0% -> 0%
where the time goes in v2:
time: 212 us; the launch traced here: 211 us
  starting transfers between devices  104 us (49%)
  waiting for transfers between devices  61.3 us (29%)
  blocking collectives  15.7 us (7%)
  local copies, waits for them, and re-layouts  11.9 us (6%)
  other arithmetic  7.07 us (3%)
  matrix products  6.27 us (3%)
  between operations  4.07 us (2%)
    all_to_all x7, starting transfers between devices, exchange(): return lax.all_to_all(blocks, axes, 0, 0, tiled=True)  55.1 us
    all_to_all x7, waiting for transfers between devices, exchange(): return lax.all_to_all(blocks, axes, 0, 0, tiled=True)  33.5 us
    ppermute x6, starting transfers between devices, swap(): return lax.ppermute(values, axis, [(0, 1), (1, 0)])  31.3 us
    ppermute x6, waiting for transfers between devices, swap(): return lax.ppermute(values, axis, [(0, 1), (1, 0)])  24.9 us
    all_to_all x1, blocking collectives, exchange(): return lax.all_to_all(blocks, axes, 0, 0, tiled=True)  12.1 us
    ppermute x3, starting transfers between devices, around(): lax.ppermute(values, axis, [(i, (i + step) % size) for i in range(size)])  7.34 us
    ppermute x2, starting transfers between devices, quad_sum(): second = lax.ppermute(values, QUAD, [(0, 2), (1, 0), (2, 1)])  5.78 us
    ppermute x2, starting transfers between devices, quad_sum(): first = lax.ppermute(values, QUAD, [(0, 1), (1, 2), (2, 0)])  4.78 us
  transfers between devices with their start and end apart: 20, of which 11 were waited for; matrix products, arithmetic and copies ran while one was open for 6% of the time, Pallas kernels for 0%

profile of v2, /device:TPU:1, one launch (start us, length us, event | category | flops | bytes accessed | tf_op | source)
XLA Modules:
  0.0 210.7 jit_solution(7089977954285638540)
XLA Ops:
  0.6 0.7 fusion.28
  1.3 0.7 fusion.27
  2.1 1.1 fusion.26
  3.2 0.7 fusion.29
  3.9 1.0 maximum_bitcast_fusion
  4.9 0.1 pad_maximum_fusion
  5.0 12.1 %all_to_all.40 = bf16[4,224,384]{2,1,0:T(8,128)(2,1)S(1)} all-to-all(bf16[4,224,384]{2,1,0:T(8,128)(2,1)S(1)} %pad_maximum_fusion), channel_id=1, replica_groups=mesh['yp'=4,'yb'=2,'zp'=2,'zb'=2,'x'=4,'zh'=2,'c'=2] {'yb','zb'}, dimensions={0} | all-to-all | bytes 1376256 | tf_op jit(solution)/shard_map/all_to_all | solution.py:18
  17.4 0.8 broadcast_in_dim.16
  18.2 14.0 %all-to-all-start.4 = ((bf16[8,32,768]{2,1,0:T(8,128)(2,1)}), bf16[8,32,768]{2,1,0:T(8,128)(2,1)S(1)}, u32[]{:S(2)}, u32[]{:S(2)}) async-start(bf16[8,32,768]{2,1,0:T(8,128)(2,1)} %broadcast_in_dim.16), calls=%async_computation.4 | async-start | bytes 786432 | tf_op jit(solution)/shard_map/all_to_all | solution.py:18
  32.3 10.8 %all-to-all-done.4 = bf16[8,32,768]{2,1,0:T(8,128)(2,1)S(1)} async-done(((bf16[8,32,768]{2,1,0:T(8,128)(2,1)}), bf16[8,32,768]{2,1,0:T(8,128)(2,1)S(1)}, u32[]{:S(2)}, u32[]{:S(2)}) %all-to-all-start.4) | async-done | bytes 393248 | tf_op jit(solution)/shard_map/all_to_all | solution.py:18
  43.0 0.8 broadcast_in_dim.13
  43.8 13.3 %all-to-all-start.1 = ((bf16[8,64,384]{2,1,0:T(8,128)(2,1)}), bf16[8,64,384]{2,1,0:T(8,128)(2,1)S(1)}, u32[]{:S(2)}, u32[]{:S(2)}) async-start(bf16[8,64,384]{2,1,0:T(8,128)(2,1)} %broadcast_in_dim.13), calls=%async_computation.1 | async-start | bytes 786432 | tf_op jit(solution)/shard_map/all_to_all | solution.py:18
  57.1 3.6 %all_gather.3 = bf16[512,768]{1,0:T(8,128)(2,1)S(1)} all-gather(bf16[256,768]{1,0:T(8,128)(2,1)S(1)} %bitcast.81), channel_id=1, replica_groups=mesh['yp'=4,'yb'=2,'zp'=2,'zb'=2,'x'=4,'zh'=2,'c'=2] {'c'}, dimensions={0}, use_global_device_ids=true | all-gather | bytes 1179648 | tf_op jit(solution)/shard_map/all_gather | solution.py:120
  60.7 1.2 abs_reduce_fusion.1
  62.7 0.9 concatenate.48
  63.6 2.9 %all-to-all-done.1 = bf16[8,64,384]{2,1,0:T(8,128)(2,1)S(1)} async-done(((bf16[8,64,384]{2,1,0:T(8,128)(2,1)}), bf16[8,64,384]{2,1,0:T(8,128)(2,1)S(1)}, u32[]{:S(2)}, u32[]{:S(2)}) %all-to-all-start.1) | async-done | bytes 393248 | tf_op jit(solution)/shard_map/all_to_all | solution.py:18
  66.5 6.4 %all-to-all-start.5 = ((f16[8,72,384]{2,1,0:T(8,128)(2,1)}), f16[8,72,384]{2,1,0:T(8,128)(2,1)}, u32[]{:S(2)}, u32[]{:S(2)}) async-start(f16[8,72,384]{2,1,0:T(8,128)(2,1)} %concatenate.48), calls=%async_computation.5 | async-start | bytes 884736 | tf_op jit(solution)/shard_map/all_to_all | solution.py:18
  72.9 0.6 fusion.30
  73.5 0.9 constant_dynamic-slice_fusion.1
  74.5 5.3 %collective-permute-start = (f32[384,512]{1,0:T(8,128)}, f32[384,512]{1,0:T(8,128)}, u32[]{:S(2)}, u32[]{:S(2)}) collective-permute-start(f32[384,512]{1,0:T(8,128)} %constant_dynamic-slice_fusion.1), channel_id=1, source_target_pairs={{0,1},{1,0},{2,3},{3,2},{4,5},{5,4},{6,7},{7,6},{8,9},{9,8},{10,11... | collective-permute-start | bytes 2359304 | tf_op jit(solution)/shard_map/ppermute | solution.py:53
  79.8 2.9 %all-to-all-done.5 = f16[8,72,384]{2,1,0:T(8,128)(2,1)} async-done(((f16[8,72,384]{2,1,0:T(8,128)(2,1)}), f16[8,72,384]{2,1,0:T(8,128)(2,1)}, u32[]{:S(2)}, u32[]{:S(2)}) %all-to-all-start.5) | async-done | bytes 442400 | tf_op jit(solution)/shard_map/all_to_all | solution.py:18
  82.7 0.8 slice.108
  83.5 1.1 multiply_reduce_fusion
  84.6 0.2 fusion.19
  84.9 0.2 convolution_add_fusion.2
  85.1 9.3 %collective-permute-start.6 = (f32[64,512]{1,0:T(8,128)S(1)}, f32[64,512]{1,0:T(8,128)S(1)}, u32[]{:S(2)}, u32[]{:S(2)}) collective-permute-start(f32[64,512]{1,0:T(8,128)S(1)} %convolution_add_fusion.2), channel_id=1, source_target_pairs={{0,1},{1,0},{2,3},{3,2},{4,5},{5,4},{6,7},{7,6},{8,9},{9,8},{10,11... | collective-permute-start | bytes 393224 | tf_op jit(solution)/shard_map/ppermute | solution.py:53
  94.4 1.0 collective-permute-done.6
  95.4 1.9 collective-permute-start.7
  98.0 7.9 %collective-permute-done.7 = f32[64,512]{1,0:T(8,128)S(1)} collective-permute-done((f32[64,512]{1,0:T(8,128)S(1)}, f32[64,512]{1,0:T(8,128)S(1)}, u32[]{:S(2)}, u32[]{:S(2)}) %collective-permute-start.7) | collective-permute-done | bytes 131104 | tf_op jit(solution)/shard_map/ppermute | solution.py:53
  105.9 2.4 %collective-permute-start.10 = (f32[64,512]{1,0:T(8,128)S(1)}, f32[64,512]{1,0:T(8,128)S(1)}, u32[]{:S(2)}, u32[]{:S(2)}) collective-permute-start(f32[64,512]{1,0:T(8,128)S(1)} %add.111), channel_id=1, source_target_pairs={{0,12},{4,0},{8,4},{12,8},{1,13},{5,1},{9,5},{13,9},{2,14},{6,2},{... | collective-permute-start | bytes 393224 | tf_op jit(solution)/shard_map/ppermute | solution.py:57
  108.4 2.2 %collective-permute-start.9 = (f32[64,512]{1,0:T(8,128)S(1)}, f32[64,512]{1,0:T(8,128)S(1)}, u32[]{:S(2)}, u32[]{:S(2)}) collective-permute-start(f32[64,512]{1,0:T(8,128)S(1)} %add.111), channel_id=1, source_target_pairs={{0,8},{4,12},{8,0},{12,4},{1,9},{5,13},{9,1},{13,5},{2,10},{6,14},... | collective-permute-start | bytes 393224 | tf_op jit(solution)/shard_map/ppermute | solution.py:57
  110.5 2.8 %collective-permute-start.8 = (f32[64,512]{1,0:T(8,128)S(1)}, f32[64,512]{1,0:T(8,128)S(1)}, u32[]{:S(2)}, u32[]{:S(2)}) collective-permute-start(f32[64,512]{1,0:T(8,128)S(1)} %add.111), channel_id=1, source_target_pairs={{0,4},{4,8},{8,12},{12,0},{1,5},{5,9},{9,13},{13,1},{2,6},{6,10},{... | collective-permute-start | bytes 393224 | tf_op jit(solution)/shard_map/ppermute | solution.py:57
  113.3 2.2 %dynamic-slice_add_fusion = f32[384,512]{1,0:T(8,128)} fusion(f32[384,512]{1,0:T(8,128)} %collective-permute-done, f32[768,512]{1,0:T(8,128)S(1)} %fusion.30, s32[]{:T(128)S(6)} %select_n.53), kind=kLoop, calls=%fused_computation.25 | loop fusion | flops 196608 | bytes 2359300 | tf_op jit(solution)/shard_map/add | solution.py:137
  115.5 4.8 %all-to-all-start.2 = ((f32[4,96,512]{2,1,0:T(8,128)}), f32[4,96,512]{2,1,0:T(8,128)S(1)}, u32[]{:S(2)}, u32[]{:S(2)}) async-start(f32[4,96,512]{2,1,0:T(8,128)} %bitcast.11), calls=%async_computation.2 | async-start | bytes 1572864 | tf_op jit(solution)/shard_map/all_to_all | solution.py:18
  120.4 2.7 %collective-permute-start.12 = (f32[64,512]{1,0:T(8,128)S(1)}, f32[64,512]{1,0:T(8,128)S(1)}, u32[]{:S(2)}, u32[]{:S(2)}) collective-permute-start(f32[64,512]{1,0:T(8,128)S(1)} %add_add_fusion), channel_id=1, source_target_pairs={{0,64},{16,0},{64,16},{1,65},{17,1},{65,17},{2,66},{18,2},{66,18},... | collective-permute-start | bytes 393224 | tf_op jit(solution)/shard_map/ppermute | solution.py:62
  123.1 2.6 %collective-permute-start.11 = (f32[64,512]{1,0:T(8,128)S(1)}, f32[64,512]{1,0:T(8,128)S(1)}, u32[]{:S(2)}, u32[]{:S(2)}) collective-permute-start(f32[64,512]{1,0:T(8,128)S(1)} %add_add_fusion), channel_id=1, source_target_pairs={{0,16},{16,64},{64,0},{1,17},{17,65},{65,1},{2,18},{18,66},{66,2},... | collective-permute-start | bytes 393224 | tf_op jit(solution)/shard_map/ppermute | solution.py:61
  126.2 2.9 %collective-permute-done.11 = f32[64,512]{1,0:T(8,128)S(1)} collective-permute-done((f32[64,512]{1,0:T(8,128)S(1)}, f32[64,512]{1,0:T(8,128)S(1)}, u32[]{:S(2)}, u32[]{:S(2)}) %collective-permute-start.11) | collective-permute-done | bytes 131104 | tf_op jit(solution)/shard_map/ppermute | solution.py:61
  129.1 0.2 fusion.16
  129.4 3.5 %collective-permute-start.1 = (f32[48,512]{1,0:T(8,128)S(1)}, f32[48,512]{1,0:T(8,128)S(1)}, u32[]{:S(2)}, u32[]{:S(2)}) collective-permute-start(f32[48,512]{1,0:T(8,128)S(1)} %constant_dynamic-slice_fusion), channel_id=1, source_target_pairs={{0,2},{2,0},{1,3},{3,1},{4,6},{6,4},{5,7},{7,5},{8,10},{10,8},{9,1... | collective-permute-start | bytes 294920 | tf_op jit(solution)/shard_map/ppermute | solution.py:53
  132.9 0.8 abs_reduce_fusion.2
  134.5 4.2 %collective-permute-done.1 = f32[48,512]{1,0:T(8,128)S(1)} collective-permute-done((f32[48,512]{1,0:T(8,128)S(1)}, f32[48,512]{1,0:T(8,128)S(1)}, u32[]{:S(2)}, u32[]{:S(2)}) %collective-permute-start.1) | collective-permute-done | bytes 98336 | tf_op jit(solution)/shard_map/ppermute | solution.py:53
  138.7 3.1 %collective-permute-start.3 = (f32[48,512]{1,0:T(8,128)S(1)}, f32[48,512]{1,0:T(8,128)S(1)}, u32[]{:S(2)}, u32[]{:S(2)}) collective-permute-start(f32[48,512]{1,0:T(8,128)S(1)} %dynamic-slice_add_fusion.1), channel_id=1, source_target_pairs={{0,64},{16,0},{64,16},{1,65},{17,1},{65,17},{2,66},{18,2},{66,18},... | collective-permute-start | bytes 294920 | tf_op jit(solution)/shard_map/ppermute | solution.py:62
  141.8 2.2 %collective-permute-start.2 = (f32[48,512]{1,0:T(8,128)S(1)}, f32[48,512]{1,0:T(8,128)S(1)}, u32[]{:S(2)}, u32[]{:S(2)}) collective-permute-start(f32[48,512]{1,0:T(8,128)S(1)} %dynamic-slice_add_fusion.1), channel_id=1, source_target_pairs={{0,16},{16,64},{64,0},{1,17},{17,65},{65,1},{2,18},{18,66},{66,2},... | collective-permute-start | bytes 294920 | tf_op jit(solution)/shard_map/ppermute | solution.py:61
  144.0 0.8 broadcast_in_dim.17
  144.8 9.0 %all-to-all-start.6 = ((f16[8,72,384]{2,1,0:T(8,128)(2,1)}), f16[8,72,384]{2,1,0:T(8,128)(2,1)S(1)}, u32[]{:S(2)}, u32[]{:S(2)}) async-start(f16[8,72,384]{2,1,0:T(8,128)(2,1)} %broadcast_in_dim.17), calls=%async_computation.6 | async-start | bytes 884736 | tf_op jit(solution)/shard_map/all_to_all | solution.py:18
  153.9 2.1 collective-permute-start.4
  156.0 11.3 %collective-permute-done.4 = f32[48,512]{1,0:T(8,128)S(1)} collective-permute-done((f32[48,512]{1,0:T(8,128)S(1)}, f32[48,512]{1,0:T(8,128)S(1)}, u32[]{:S(2)}, u32[]{:S(2)}) %collective-permute-start.4) | collective-permute-done | bytes 98336 | tf_op jit(solution)/shard_map/ppermute | solution.py:53
  167.3 1.0 broadcast_in_dim.14
  168.3 4.1 %all-to-all-start.3 = ((f32[4,96,512]{2,1,0:T(8,128)}), f32[4,96,512]{2,1,0:T(8,128)S(1)}, u32[]{:S(2)}, u32[]{:S(2)}) async-start(f32[4,96,512]{2,1,0:T(8,128)} %broadcast_in_dim.14), calls=%async_computation.3 | async-start | bytes 1572864 | tf_op jit(solution)/shard_map/all_to_all | solution.py:18
  172.5 8.2 %all-to-all-done.3 = f32[4,96,512]{2,1,0:T(8,128)S(1)} async-done(((f32[4,96,512]{2,1,0:T(8,128)}), f32[4,96,512]{2,1,0:T(8,128)S(1)}, u32[]{:S(2)}, u32[]{:S(2)}) %all-to-all-start.3) | async-done | bytes 786464 | tf_op jit(solution)/shard_map/all_to_all | solution.py:18
  180.7 9.3 %collective-permute-start.5 = (f32[384,512]{1,0:T(8,128)S(1)}, f32[384,512]{1,0:T(8,128)S(1)}, u32[]{:S(2)}, u32[]{:S(2)}) collective-permute-start(f32[384,512]{1,0:T(8,128)S(1)} %bitcast.79), channel_id=1, source_target_pairs={{0,1},{1,0},{2,3},{3,2},{4,5},{5,4},{6,7},{7,6},{8,9},{9,8},{10,11... | collective-permute-start | bytes 2359304 | tf_op jit(solution)/shard_map/ppermute | solution.py:53
  190.1 0.6 fusion.31
  190.7 0.6 convolution_add_fusion
  191.3 0.6 collective-permute-done.5
  191.9 0.2 broadcast_select_fusion.1
  192.1 0.6 fusion.5
  192.7 1.2 abs_reduce_fusion
  194.6 0.1 multiply_convert_fusion
  194.8 0.9 concatenate.50
  195.7 3.5 %all-to-all-start.7 = ((f16[4,200,384]{2,1,0:T(8,128)(2,1)}), f16[4,200,384]{2,1,0:T(8,128)(2,1)S(1)}, u32[]{:S(2)}, u32[]{:S(2)}) async-start(f16[4,200,384]{2,1,0:T(8,128)(2,1)} %concatenate.50), calls=%async_computation.7 | async-start | bytes 1228800 | tf_op jit(solution)/shard_map/all_to_all | solution.py:18
  199.2 8.7 %all-to-all-done.7 = f16[4,200,384]{2,1,0:T(8,128)(2,1)S(1)} async-done(((f16[4,200,384]{2,1,0:T(8,128)(2,1)}), f16[4,200,384]{2,1,0:T(8,128)(2,1)S(1)}, u32[]{:S(2)}, u32[]{:S(2)}) %all-to-all-start.7) | async-done | bytes 614432 | tf_op jit(solution)/shard_map/all_to_all | solution.py:18
  208.1 0.8 copy-done.1
  208.9 0.7 fusion.9
  209.7 1.0 maximum_add_fusion
  (57 shorter events, 1.5 us)
Async XLA Ops:
  18.2 24.8 %all-to-all-start.4 = ((bf16[8,32,768]{2,1,0:T(8,128)(2,1)}), bf16[8,32,768]{2,1,0:T(8,128)(2,1)S(1)}, u32[]{:S(2)}, u32[]{:S(2)}) async-start(bf16[8,32,768]{2,1,0:T(8,128)(2,1)} %broadcast_in_dim.16), calls=%async_computation.4 | async-start | bytes 786432 | tf_op jit(solution)/shard_map/all_to_all | solution.py:18
  43.8 22.7 %all-to-all-start.1 = ((bf16[8,64,384]{2,1,0:T(8,128)(2,1)}), bf16[8,64,384]{2,1,0:T(8,128)(2,1)S(1)}, u32[]{:S(2)}, u32[]{:S(2)}) async-start(bf16[8,64,384]{2,1,0:T(8,128)(2,1)} %broadcast_in_dim.13), calls=%async_computation.1 | async-start | bytes 786432 | tf_op jit(solution)/shard_map/all_to_all | solution.py:18
  66.5 16.2 %all-to-all-start.5 = ((f16[8,72,384]{2,1,0:T(8,128)(2,1)}), f16[8,72,384]{2,1,0:T(8,128)(2,1)}, u32[]{:S(2)}, u32[]{:S(2)}) async-start(f16[8,72,384]{2,1,0:T(8,128)(2,1)} %concatenate.48), calls=%async_computation.5 | async-start | bytes 884736 | tf_op jit(solution)/shard_map/all_to_all | solution.py:18
  74.5 38.8 %collective-permute-start = (f32[384,512]{1,0:T(8,128)}, f32[384,512]{1,0:T(8,128)}, u32[]{:S(2)}, u32[]{:S(2)}) collective-permute-start(f32[384,512]{1,0:T(8,128)} %constant_dynamic-slice_fusion.1), channel_id=1, source_target_pairs={{0,1},{1,0},{2,3},{3,2},{4,5},{5,4},{6,7},{7,6},{8,9},{9,8},{10,11... | collective-permute-start | bytes 2359304 | tf_op jit(solution)/shard_map/ppermute | solution.py:53
  85.1 10.2 %collective-permute-start.6 = (f32[64,512]{1,0:T(8,128)S(1)}, f32[64,512]{1,0:T(8,128)S(1)}, u32[]{:S(2)}, u32[]{:S(2)}) collective-permute-start(f32[64,512]{1,0:T(8,128)S(1)} %convolution_add_fusion.2), channel_id=1, source_target_pairs={{0,1},{1,0},{2,3},{3,2},{4,5},{5,4},{6,7},{7,6},{8,9},{9,8},{10,11... | collective-permute-start | bytes 393224 | tf_op jit(solution)/shard_map/ppermute | solution.py:53
  95.4 10.5 %collective-permute-start.7 = (f32[64,512]{1,0:T(8,128)S(1)}, f32[64,512]{1,0:T(8,128)S(1)}, u32[]{:S(2)}, u32[]{:S(2)}) collective-permute-start(f32[64,512]{1,0:T(8,128)S(1)} %add.110), channel_id=1, source_target_pairs={{0,2},{2,0},{1,3},{3,1},{4,6},{6,4},{5,7},{7,5},{8,10},{10,8},{9,1... | collective-permute-start | bytes 393224 | tf_op jit(solution)/shard_map/ppermute | solution.py:53
  105.9 14.4 %collective-permute-start.10 = (f32[64,512]{1,0:T(8,128)S(1)}, f32[64,512]{1,0:T(8,128)S(1)}, u32[]{:S(2)}, u32[]{:S(2)}) collective-permute-start(f32[64,512]{1,0:T(8,128)S(1)} %add.111), channel_id=1, source_target_pairs={{0,12},{4,0},{8,4},{12,8},{1,13},{5,1},{9,5},{13,9},{2,14},{6,2},{... | collective-permute-start | bytes 393224 | tf_op jit(solution)/shard_map/ppermute | solution.py:57
  108.4 12.0 %collective-permute-start.9 = (f32[64,512]{1,0:T(8,128)S(1)}, f32[64,512]{1,0:T(8,128)S(1)}, u32[]{:S(2)}, u32[]{:S(2)}) collective-permute-start(f32[64,512]{1,0:T(8,128)S(1)} %add.111), channel_id=1, source_target_pairs={{0,8},{4,12},{8,0},{12,4},{1,9},{5,13},{9,1},{13,5},{2,10},{6,14},... | collective-permute-start | bytes 393224 | tf_op jit(solution)/shard_map/ppermute | solution.py:57
  110.5 9.8 %collective-permute-start.8 = (f32[64,512]{1,0:T(8,128)S(1)}, f32[64,512]{1,0:T(8,128)S(1)}, u32[]{:S(2)}, u32[]{:S(2)}) collective-permute-start(f32[64,512]{1,0:T(8,128)S(1)} %add.111), channel_id=1, source_target_pairs={{0,4},{4,8},{8,12},{12,0},{1,5},{5,9},{9,13},{13,1},{2,6},{6,10},{... | collective-permute-start | bytes 393224 | tf_op jit(solution)/shard_map/ppermute | solution.py:57
  115.5 10.2 %copy-start.2 = (f32[512]{0:T(512)S(1)}, f32[512]{0:T(512)}, u32[]{:S(2)}) copy-start(f32[512]{0:T(512)} %param.19) | copy-start | bytes 6148
  115.5 10.2 %copy-start.3 = (f32[512]{0:T(512)S(1)}, f32[512]{0:T(512)}, u32[]{:S(2)}) copy-start(f32[512]{0:T(512)} %param.17) | copy-start | bytes 6148
  115.5 10.2 %copy-start.4 = (f32[512]{0:T(512)S(1)}, f32[512]{0:T(512)}, u32[]{:S(2)}) copy-start(f32[512]{0:T(512)} %param.20) | copy-start | bytes 6148
  115.5 10.2 %copy-start.5 = (f32[512]{0:T(512)S(1)}, f32[512]{0:T(512)}, u32[]{:S(2)}) copy-start(f32[512]{0:T(512)} %param.18) | copy-start | bytes 6148
  115.5 13.8 %all-to-all-start.2 = ((f32[4,96,512]{2,1,0:T(8,128)}), f32[4,96,512]{2,1,0:T(8,128)S(1)}, u32[]{:S(2)}, u32[]{:S(2)}) async-start(f32[4,96,512]{2,1,0:T(8,128)} %bitcast.11), calls=%async_computation.2 | async-start | bytes 1572864 | tf_op jit(solution)/shard_map/all_to_all | solution.py:18
  120.4 5.8 %collective-permute-start.12 = (f32[64,512]{1,0:T(8,128)S(1)}, f32[64,512]{1,0:T(8,128)S(1)}, u32[]{:S(2)}, u32[]{:S(2)}) collective-permute-start(f32[64,512]{1,0:T(8,128)S(1)} %add_add_fusion), channel_id=1, source_target_pairs={{0,64},{16,0},{64,16},{1,65},{17,1},{65,17},{2,66},{18,2},{66,18},... | collective-permute-start | bytes 393224 | tf_op jit(solution)/shard_map/ppermute | solution.py:62
  123.1 6.0 %collective-permute-start.11 = (f32[64,512]{1,0:T(8,128)S(1)}, f32[64,512]{1,0:T(8,128)S(1)}, u32[]{:S(2)}, u32[]{:S(2)}) collective-permute-start(f32[64,512]{1,0:T(8,128)S(1)} %add_add_fusion), channel_id=1, source_target_pairs={{0,16},{16,64},{64,0},{1,17},{17,65},{65,1},{2,18},{18,66},{66,2},... | collective-permute-start | bytes 393224 | tf_op jit(solution)/shard_map/ppermute | solution.py:61
  129.4 9.3 %collective-permute-start.1 = (f32[48,512]{1,0:T(8,128)S(1)}, f32[48,512]{1,0:T(8,128)S(1)}, u32[]{:S(2)}, u32[]{:S(2)}) collective-permute-start(f32[48,512]{1,0:T(8,128)S(1)} %constant_dynamic-slice_fusion), channel_id=1, source_target_pairs={{0,2},{2,0},{1,3},{3,1},{4,6},{6,4},{5,7},{7,5},{8,10},{10,8},{9,1... | collective-permute-start | bytes 294920 | tf_op jit(solution)/shard_map/ppermute | solution.py:53
  138.7 15.1 %collective-permute-start.3 = (f32[48,512]{1,0:T(8,128)S(1)}, f32[48,512]{1,0:T(8,128)S(1)}, u32[]{:S(2)}, u32[]{:S(2)}) collective-permute-start(f32[48,512]{1,0:T(8,128)S(1)} %dynamic-slice_add_fusion.1), channel_id=1, source_target_pairs={{0,64},{16,0},{64,16},{1,65},{17,1},{65,17},{2,66},{18,2},{66,18},... | collective-permute-start | bytes 294920 | tf_op jit(solution)/shard_map/ppermute | solution.py:62
  141.8 12.0 %collective-permute-start.2 = (f32[48,512]{1,0:T(8,128)S(1)}, f32[48,512]{1,0:T(8,128)S(1)}, u32[]{:S(2)}, u32[]{:S(2)}) collective-permute-start(f32[48,512]{1,0:T(8,128)S(1)} %dynamic-slice_add_fusion.1), channel_id=1, source_target_pairs={{0,16},{16,64},{64,0},{1,17},{17,65},{65,1},{2,18},{18,66},{66,2},... | collective-permute-start | bytes 294920 | tf_op jit(solution)/shard_map/ppermute | solution.py:61
  144.8 22.4 %all-to-all-start.6 = ((f16[8,72,384]{2,1,0:T(8,128)(2,1)}), f16[8,72,384]{2,1,0:T(8,128)(2,1)S(1)}, u32[]{:S(2)}, u32[]{:S(2)}) async-start(f16[8,72,384]{2,1,0:T(8,128)(2,1)} %broadcast_in_dim.17), calls=%async_computation.6 | async-start | bytes 884736 | tf_op jit(solution)/shard_map/all_to_all | solution.py:18
  153.9 13.4 %collective-permute-start.4 = (f32[48,512]{1,0:T(8,128)S(1)}, f32[48,512]{1,0:T(8,128)S(1)}, u32[]{:S(2)}, u32[]{:S(2)}) collective-permute-start(f32[48,512]{1,0:T(8,128)S(1)} %add_add_fusion.1), channel_id=1, source_target_pairs={{0,2},{2,0},{1,3},{3,1},{4,6},{6,4},{5,7},{7,5},{8,10},{10,8},{9,1... | collective-permute-start | bytes 294920 | tf_op jit(solution)/shard_map/ppermute | solution.py:53
  168.3 12.5 %all-to-all-start.3 = ((f32[4,96,512]{2,1,0:T(8,128)}), f32[4,96,512]{2,1,0:T(8,128)S(1)}, u32[]{:S(2)}, u32[]{:S(2)}) async-start(f32[4,96,512]{2,1,0:T(8,128)} %broadcast_in_dim.14), calls=%async_computation.3 | async-start | bytes 1572864 | tf_op jit(solution)/shard_map/all_to_all | solution.py:18
  180.7 11.2 %collective-permute-start.5 = (f32[384,512]{1,0:T(8,128)S(1)}, f32[384,512]{1,0:T(8,128)S(1)}, u32[]{:S(2)}, u32[]{:S(2)}) collective-permute-start(f32[384,512]{1,0:T(8,128)S(1)} %bitcast.79), channel_id=1, source_target_pairs={{0,1},{1,0},{2,3},{3,2},{4,5},{5,4},{6,7},{7,6},{8,9},{9,8},{10,11... | collective-permute-start | bytes 2359304 | tf_op jit(solution)/shard_map/ppermute | solution.py:53
  195.7 12.2 %all-to-all-start.7 = ((f16[4,200,384]{2,1,0:T(8,128)(2,1)}), f16[4,200,384]{2,1,0:T(8,128)(2,1)S(1)}, u32[]{:S(2)}, u32[]{:S(2)}) async-start(f16[4,200,384]{2,1,0:T(8,128)(2,1)} %concatenate.50), calls=%async_computation.7 | async-start | bytes 1228800 | tf_op jit(solution)/shard_map/all_to_all | solution.py:18
  208.0 0.9 copy-start.1
  208.0 1.7 copy-start

commit v3 on v2

--- a/solution.py
+++ b/solution.py
@@ -63,10 +63,17 @@
     return values + first + second
 
 
-def col_sum(values):
-    values = values + swap(values, "c")
-    values = values + swap(values, "zh")
-    return values + around(values, "x", 4, 1) + around(values, "x", 4, 2) + around(values, "x", 4, 3)
+def ring_parts(values, place):
+    total = lax.dynamic_index_in_dim(values, place, 0, False)
+    for step in (1, 2, 3):
+        block = lax.dynamic_index_in_dim(values, (place + step) % 4, 0, False)
+        total = total + around(block, "x", 4, step)
+    return total
+
+
+def ring_gather(values, place):
+    held = jnp.stack([values] + [around(values, "x", 4, step) for step in (1, 2, 3)])
+    return jnp.concatenate([lax.dynamic_index_in_dim(held, (place - j) % 4, 0, False) for j in range(4)], axis=0)
 
 
 def core_part(values, core, own):
@@ -96,12 +103,15 @@
     damp = damping[0]
     quad = lax.axis_index("yb") * 2 + lax.axis_index("zb")
     octant = lax.axis_index("yp") * 2 + lax.axis_index("zp")
-    core, high = lax.axis_index("c"), lax.axis_index("zh")
+    core, high, place = lax.axis_index("c"), lax.axis_index("zh"), lax.axis_index("x")
     is_output = quad == 3
     left_shift = shifted(jnp.where(is_output, output_left_eigen, joined_left_eigen), damp)
     right_shift = shifted(jnp.where(is_output, output_right_eigen, joined_right_eigen), damp)
     left_shift = left_shift.reshape(8, 2, 32).transpose(1, 0, 2).reshape(512)
-    right_shift = right_shift.reshape(4, 2, 2, 2, 16).transpose(0, 2, 1, 3, 4).reshape(512)
+    right_shift = right_shift.reshape(4, 2, 2, 2, 16).transpose(0, 2, 1, 3, 4).reshape(4, 2, 64)[::-1]
+    right_shift = jnp.where(lax.axis_index("zp") == 1, right_shift[:, ::-1], right_shift)
+    right_shift = jnp.concatenate([right_shift, right_shift], axis=0)
+    right_shift = lax.dynamic_slice_in_dim(right_shift, 3 - lax.axis_index("yp"), 4, 0).reshape(512)
     own_shift = lax.dynamic_slice_in_dim(left_shift, octant * 64, 64, 0)
 
     left_j, left_o = joined_left_basis.T, output_left_basis.T
@@ -120,26 +130,32 @@
     left = lax.all_gather(left, "c", axis=0, tiled=True)
 
     right = got[:, 192:208].reshape(64, 384)
-    right = exchange(jnp.broadcast_to(right[None], (8, 64, 384)), OCT).reshape(512, 384)
+    right = jnp.concatenate([right, swap(right, "zp")], axis=0)
+    right = jnp.concatenate([right] + [around(right, "yp", 4, step) for step in (1, 2, 3)], axis=0)
 
     rows = jnp.dot(left, gradient, preferred_element_type=jnp.float32)
     rows = exchange(pack(rows.reshape(8, 64, 384)), OCT)
     rows = jnp.sum(unpack(rows), axis=0)
 
+    cols = lax.dot_general(gradient, right, (((1,), (1,)), ((), ())), preferred_element_type=jnp.float32)
+    cols = core_part(cols, core, True) + swap(core_part(cols, core, False), "c")
+    cols = ring_parts(cols.reshape(4, 96, 512), place)
+
     core_sum = dot_wide_left(rows, right, ((1,), (1,)))
-    core_sum = quad_sum(col_sum(core_sum), quad)
+    core_sum = core_sum + swap(core_sum, "c")
+    both = swap(jnp.concatenate([core_sum, core_part(cols, high, False)], axis=0), "zh")
+    core_sum = core_sum + both[:64]
+    cols = core_part(cols, high, True) + both[64:]
+    core_sum = core_sum + around(core_sum, "x", 4, 1) + around(core_sum, "x", 4, 2) + around(core_sum, "x", 4, 3)
+    both = quad_sum(jnp.concatenate([core_sum, cols], axis=0), quad)
+    core_sum, cols = both[:64], both[64:]
     mixed = rows / damp + dot_wide_left(core_sum * right_shift[None, :], right, ((1,), (0,)))
     mixed = mixed * own_shift[:, None]
     packed = pack(mixed)
     mixed = unpack(exchange(jnp.broadcast_to(packed[None], (8, 72, 384)), OCT)).reshape(512, 384)
 
-    cols = lax.dot_general(gradient, right, (((1,), (1,)), ((), ())), preferred_element_type=jnp.float32)
-    cols = core_part(cols, core, True) + swap(core_part(cols, core, False), "c")
-    cols = jnp.sum(exchange(cols.reshape(4, 96, 512), ("x",)), axis=0)
-    cols = core_part(cols, high, True) + swap(core_part(cols, high, False), "zh")
-    cols = quad_sum(cols, quad)
     cols = joined_pair(cols, swap(cols, "zh"), high)
-    cols = exchange(jnp.broadcast_to(cols[None], (4, 96, 512)), ("x",)).reshape(384, 512)
+    cols = ring_gather(cols, place)
     cols = joined_pair(cols, swap(cols, "c"), core)
 
     part = dot_wide_left(cols * (right_shift / damp)[None, :], right, ((1,), (0,)))

time: 212 us -> 202 us (0.953)
  blocking collectives: 15.7 us -> 2.65 us
  starting transfers between devices: 104 us -> 113 us
  waiting for transfers between devices: 61.3 us -> 53.2 us
  other arithmetic: 7.07 us -> 10.4 us
    ppermute x3 -> x12, starting transfers between devices: 7.34 us -> 41.6 us  [around(): lax.ppermute(values, axis, [(i, (i + step) % size) for i in range(size)])]
    all_to_all x7 -> x5, starting transfers between devices: 55.1 us -> 26.8 us  [exchange(): return lax.all_to_all(blocks, axes, 0, 0, tiled=True)]
    ppermute x3 -> x12, waiting for transfers between devices: 0.01 us -> 22.3 us  [around(): lax.ppermute(values, axis, [(i, (i + step) % size) for i in range(size)])]
    ppermute x6, waiting for transfers between devices: 24.9 us -> 5.93 us  [swap(): return lax.ppermute(values, axis, [(0, 1), (1, 0)])]
    all_to_all x7 -> x5, waiting for transfers between devices: 33.5 us -> 16 us  [exchange(): return lax.all_to_all(blocks, axes, 0, 0, tiled=True)]
    all_to_all x1 -> x0, blocking collectives: 12.1 us -> none  [exchange(): return lax.all_to_all(blocks, axes, 0, 0, tiled=True)]
    ppermute x6, starting transfers between devices: 31.3 us -> 35.8 us  [swap(): return lax.ppermute(values, axis, [(0, 1), (1, 0)])]
    ppermute x2 -> x1, waiting for transfers between devices: 2.87 us -> 6.72 us  [quad_sum(): first = lax.ppermute(values, QUAD, [(0, 1), (1, 2), (2, 0)])]
  transfers between devices with their start and end apart: 20 -> 25, of which waited for: 11 -> 13; matrix products, arithmetic and copies ran while one was open for 6% -> 7% of each run, Pallas kernels for 0% -> 0%
where the time goes in v3:
time: 202 us; the launch traced here: 201 us
  starting transfers between devices  113 us (56%)
  waiting for transfers between devices  53.2 us (26%)
  local copies, waits for them, and re-layouts  10.4 us (5%)
  other arithmetic  10.4 us (5%)
  matrix products  7.16 us (4%)
  between operations  4.33 us (2%)
  blocking collectives  2.65 us (1%)
    ppermute x12, starting transfers between devices, around(): lax.ppermute(values, axis, [(i, (i + step) % size) for i in range(size)])  41.6 us
    ppermute x6, starting transfers between devices, swap(): return lax.ppermute(values, axis, [(0, 1), (1, 0)])  35.8 us
    all_to_all x5, starting transfers between devices, exchange(): return lax.all_to_all(blocks, axes, 0, 0, tiled=True)  26.8 us
    ppermute x12, waiting for transfers between devices, around(): lax.ppermute(values, axis, [(i, (i + step) % size) for i in range(size)])  22.3 us
    all_to_all x5, waiting for transfers between devices, exchange(): return lax.all_to_all(blocks, axes, 0, 0, tiled=True)  16 us
    ppermute x1, waiting for transfers between devices, quad_sum(): first = lax.ppermute(values, QUAD, [(0, 1), (1, 2), (2, 0)])  6.72 us
    ppermute x1, starting transfers between devices, quad_sum(): first = lax.ppermute(values, QUAD, [(0, 1), (1, 2), (2, 0)])  6.05 us
    ppermute x6, waiting for transfers between devices, swap(): return lax.ppermute(values, axis, [(0, 1), (1, 0)])  5.93 us
  transfers between devices with their start and end apart: 25, of which 13 were waited for; matrix products, arithmetic and copies ran while one was open for 7% of the time, Pallas kernels for 0%

profile of v3, /device:TPU:1, one launch (start us, length us, event | category | flops | bytes accessed | tf_op | source)
XLA Modules:
  0.0 200.8 jit_solution(6125513445782236110)
XLA Ops:
  0.6 0.7 fusion.34
  1.3 0.7 fusion.33
  2.1 1.1 fusion.32
  3.2 0.7 fusion.35
  3.9 1.0 maximum_bitcast_fusion
  4.9 1.0 pad_maximum_fusion.2
  5.9 5.2 %all-to-all-start = ((bf16[4,224,384]{2,1,0:T(8,128)(2,1)}), bf16[4,224,384]{2,1,0:T(8,128)(2,1)S(1)}, u32[]{:S(2)}, u32[]{:S(2)}) async-start(bf16[4,224,384]{2,1,0:T(8,128)(2,1)} %pad_maximum_fusion.2), calls=%async_computation | async-start | bytes 1376256 | tf_op jit(solution)/shard_map/all_to_all | solution.py:18
  11.1 6.4 %all-to-all-done = bf16[4,224,384]{2,1,0:T(8,128)(2,1)S(1)} async-done(((bf16[4,224,384]{2,1,0:T(8,128)(2,1)}), bf16[4,224,384]{2,1,0:T(8,128)(2,1)S(1)}, u32[]{:S(2)}, u32[]{:S(2)}) %all-to-all-start) | async-done | bytes 688160 | tf_op jit(solution)/shard_map/all_to_all | solution.py:18
  17.4 8.7 %collective-permute-start = (bf16[64,384]{1,0:T(8,128)(2,1)S(1)}, bf16[64,384]{1,0:T(8,128)(2,1)S(1)}, u32[]{:S(2)}, u32[]{:S(2)}) collective-permute-start(bf16[64,384]{1,0:T(8,128)(2,1)S(1)} %bitcast.96), channel_id=1, source_target_pairs={{0,32},{32,0},{1,33},{33,1},{2,34},{34,2},{3,35},{35,3},{4,36},{36... | collective-permute-start | bytes 147464 | tf_op jit(solution)/shard_map/ppermute | solution.py:53
  26.4 0.8 broadcast_in_dim.7
  27.2 9.8 %all-to-all-start.1 = ((bf16[8,32,768]{2,1,0:T(8,128)(2,1)}), bf16[8,32,768]{2,1,0:T(8,128)(2,1)}, u32[]{:S(2)}, u32[]{:S(2)}) async-start(bf16[8,32,768]{2,1,0:T(8,128)(2,1)} %broadcast_in_dim.7), calls=%async_computation.1 | async-start | bytes 786432 | tf_op jit(solution)/shard_map/all_to_all | solution.py:18
  37.1 4.2 %collective-permute-start.1 = (bf16[128,384]{1,0:T(8,128)(2,1)S(1)}, bf16[128,384]{1,0:T(8,128)(2,1)S(1)}, u32[]{:S(2)}, u32[]{:S(2)}) collective-permute-start(bf16[128,384]{1,0:T(8,128)(2,1)S(1)} %pad_maximum_fusion.7), channel_id=1, source_target_pairs={{0,128},{128,256},{256,384},{384,0},{1,129},{129,257},{257,385},{3... | collective-permute-start | bytes 294920 | tf_op jit(solution)/shard_map/ppermute | solution.py:57
  41.3 5.7 %collective-permute-start.2 = (bf16[128,384]{1,0:T(8,128)(2,1)S(1)}, bf16[128,384]{1,0:T(8,128)(2,1)S(1)}, u32[]{:S(2)}, u32[]{:S(2)}) collective-permute-start(bf16[128,384]{1,0:T(8,128)(2,1)S(1)} %pad_maximum_fusion.7), channel_id=1, source_target_pairs={{0,256},{128,384},{256,0},{384,128},{1,257},{129,385},{257,1},{385... | collective-permute-start | bytes 294920 | tf_op jit(solution)/shard_map/ppermute | solution.py:57
  47.0 5.0 %collective-permute-start.3 = (bf16[128,384]{1,0:T(8,128)(2,1)S(1)}, bf16[128,384]{1,0:T(8,128)(2,1)S(1)}, u32[]{:S(2)}, u32[]{:S(2)}) collective-permute-start(bf16[128,384]{1,0:T(8,128)(2,1)S(1)} %pad_maximum_fusion.7), channel_id=1, source_target_pairs={{0,384},{128,0},{256,128},{384,256},{1,385},{129,1},{257,129},{385... | collective-permute-start | bytes 294920 | tf_op jit(solution)/shard_map/ppermute | solution.py:57
  52.1 6.3 %collective-permute-done.3 = bf16[128,384]{1,0:T(8,128)(2,1)S(1)} collective-permute-done((bf16[128,384]{1,0:T(8,128)(2,1)S(1)}, bf16[128,384]{1,0:T(8,128)(2,1)S(1)}, u32[]{:S(2)}, u32[]{:S(2)}) %collective-permute-start.3) | collective-permute-done | bytes 98336 | tf_op jit(solution)/shard_map/ppermute | solution.py:57
  58.4 0.6 fusion.36
  59.0 0.9 constant_dynamic-slice_fusion.1
  59.9 2.9 %collective-permute-start.5 = (f32[384,512]{1,0:T(8,128)}, f32[384,512]{1,0:T(8,128)}, u32[]{:S(2)}, u32[]{:S(2)}) collective-permute-start(f32[384,512]{1,0:T(8,128)} %constant_dynamic-slice_fusion.1), channel_id=1, source_target_pairs={{0,1},{1,0},{2,3},{3,2},{4,5},{5,4},{6,7},{7,6},{8,9},{9,8},{10,11... | collective-permute-start | bytes 2359304 | tf_op jit(solution)/shard_map/ppermute | solution.py:53
  62.9 2.7 %all_gather.3 = bf16[512,768]{1,0:T(8,128)(2,1)S(1)} all-gather(bf16[256,768]{1,0:T(8,128)(2,1)} %bitcast.9), channel_id=1, replica_groups=mesh['yp'=4,'yb'=2,'zp'=2,'zb'=2,'x'=4,'zh'=2,'c'=2] {'c'}, dimensions={0}, use_global_device_ids=true | all-gather | bytes 1179648 | tf_op jit(solution)/shard_map/all_gather | solution.py:130
  65.5 2.1 %abs_reduce_fusion.1 = (f32[]{:T(128)}, f32[8,64,384]{2,1,0:T(8,128)}) fusion(bf16[8,64,768]{2,1,0:T(8,128)(2,1)S(1)} %bitcast.90, bf16[768,384,1]{1,0,2:T(8,128)(2,1)S(1)} %bitcast.92), kind=kOutput, calls=%fused_computation.27 | convolution fusion | flops 302383104 | bytes 2162692 | tf_op jit(solution)/shard_map/dot_general | solution.py:136
  68.3 1.2 multiply_convert_fusion.1
  69.5 0.9 concatenate.65
  70.4 4.8 %all-to-all-start.2 = ((f16[8,72,384]{2,1,0:T(8,128)(2,1)}), f16[8,72,384]{2,1,0:T(8,128)(2,1)}, u32[]{:S(2)}, u32[]{:S(2)}) async-start(f16[8,72,384]{2,1,0:T(8,128)(2,1)} %concatenate.65), calls=%async_computation.2 | async-start | bytes 884736 | tf_op jit(solution)/shard_map/all_to_all | solution.py:18
  75.2 1.3 dynamic-slice_add_fusion
  76.5 5.3 %collective-permute-start.8 = (f32[96,512]{1,0:T(8,128)S(1)}, f32[96,512]{1,0:T(8,128)S(1)}, u32[]{:S(2)}, u32[]{:S(2)}) collective-permute-start(f32[96,512]{1,0:T(8,128)S(1)} %get-tuple-element.14), channel_id=1, source_target_pairs={{0,12},{4,0},{8,4},{12,8},{1,13},{5,1},{9,5},{13,9},{2,14},{6,2},{... | collective-permute-start | bytes 589832 | tf_op jit(solution)/shard_map/ppermute | solution.py:57
  81.8 2.5 %collective-permute-start.7 = (f32[96,512]{1,0:T(8,128)S(1)}, f32[96,512]{1,0:T(8,128)S(1)}, u32[]{:S(2)}, u32[]{:S(2)}) collective-permute-start(f32[96,512]{1,0:T(8,128)S(1)} %get-tuple-element.15), channel_id=1, source_target_pairs={{0,8},{4,12},{8,0},{12,4},{1,9},{5,13},{9,1},{13,5},{2,10},{6,14},... | collective-permute-start | bytes 589832 | tf_op jit(solution)/shard_map/ppermute | solution.py:57
  84.3 2.5 %collective-permute-start.6 = (f32[96,512]{1,0:T(8,128)S(1)}, f32[96,512]{1,0:T(8,128)}, u32[]{:S(2)}, u32[]{:S(2)}) collective-permute-start(f32[96,512]{1,0:T(8,128)S(1)} %get-tuple-element.13), channel_id=1, source_target_pairs={{0,4},{4,8},{8,12},{12,0},{1,5},{5,9},{9,13},{13,1},{2,6},{6,10},{... | collective-permute-start | bytes 589832 | tf_op jit(solution)/shard_map/ppermute | solution.py:57
  86.8 0.8 slice.123
  87.7 1.1 multiply_reduce_fusion
  89.3 4.7 %collective-permute-start.4 = (f32[64,512]{1,0:T(8,128)S(1)}, f32[64,512]{1,0:T(8,128)S(1)}, u32[]{:S(2)}, u32[]{:S(2)}) collective-permute-start(f32[64,512]{1,0:T(8,128)S(1)} %convolution_add_fusion.2), channel_id=1, source_target_pairs={{0,1},{1,0},{2,3},{3,2},{4,5},{5,4},{6,7},{7,6},{8,9},{9,8},{10,11... | collective-permute-start | bytes 393224 | tf_op jit(solution)/shard_map/ppermute | solution.py:53
  94.1 1.8 collective-permute-done.6
  95.8 1.0 fusion.11
  96.9 8.2 %collective-permute-start.9 = (f32[112,512]{1,0:T(8,128)S(1)}, f32[112,512]{1,0:T(8,128)S(1)}, u32[]{:S(2)}, u32[]{:S(2)}) collective-permute-start(f32[112,512]{1,0:T(8,128)S(1)} %pad_maximum_fusion.3), channel_id=1, source_target_pairs={{0,2},{2,0},{1,3},{3,1},{4,6},{6,4},{5,7},{7,5},{8,10},{10,8},{9,1... | collective-permute-start | bytes 688136 | tf_op jit(solution)/shard_map/ppermute | solution.py:53
  106.4 5.3 %collective-permute-done.9 = f32[112,512]{1,0:T(8,128)S(1)} collective-permute-done((f32[112,512]{1,0:T(8,128)S(1)}, f32[112,512]{1,0:T(8,128)S(1)}, u32[]{:S(2)}, u32[]{:S(2)}) %collective-permute-start.9) | collective-permute-done | bytes 229408 | tf_op jit(solution)/shard_map/ppermute | solution.py:53
  111.7 4.3 %collective-permute-start.12 = (f32[64,512]{1,0:T(8,128)S(1)}, f32[64,512]{1,0:T(8,128)S(1)}, u32[]{:S(2)}, u32[]{:S(2)}) collective-permute-start(f32[64,512]{1,0:T(8,128)S(1)} %slice_add_fusion), channel_id=1, source_target_pairs={{0,12},{4,0},{8,4},{12,8},{1,13},{5,1},{9,5},{13,9},{2,14},{6,2},{... | collective-permute-start | bytes 393224 | tf_op jit(solution)/shard_map/ppermute | solution.py:57
  116.1 2.5 %collective-permute-start.11 = (f32[64,512]{1,0:T(8,128)S(1)}, f32[64,512]{1,0:T(8,128)S(1)}, u32[]{:S(2)}, u32[]{:S(2)}) collective-permute-start(f32[64,512]{1,0:T(8,128)S(1)} %slice_add_fusion), channel_id=1, source_target_pairs={{0,8},{4,12},{8,0},{12,4},{1,9},{5,13},{9,1},{13,5},{2,10},{6,14},... | collective-permute-start | bytes 393224 | tf_op jit(solution)/shard_map/ppermute | solution.py:57
  118.6 2.5 %collective-permute-start.10 = (f32[64,512]{1,0:T(8,128)S(1)}, f32[64,512]{1,0:T(8,128)S(1)}, u32[]{:S(2)}, u32[]{:S(2)}) collective-permute-start(f32[64,512]{1,0:T(8,128)S(1)} %slice_add_fusion), channel_id=1, source_target_pairs={{0,4},{4,8},{8,12},{12,0},{1,5},{5,9},{9,13},{13,1},{2,6},{6,10},{... | collective-permute-start | bytes 393224 | tf_op jit(solution)/shard_map/ppermute | solution.py:57
  121.1 2.2 %collective-permute-done.11 = f32[64,512]{1,0:T(8,128)S(1)} collective-permute-done((f32[64,512]{1,0:T(8,128)S(1)}, f32[64,512]{1,0:T(8,128)S(1)}, u32[]{:S(2)}, u32[]{:S(2)}) %collective-permute-start.11) | collective-permute-done | bytes 131104 | tf_op jit(solution)/shard_map/ppermute | solution.py:57
  123.3 4.0 %collective-permute-done.10 = f32[64,512]{1,0:T(8,128)S(1)} collective-permute-done((f32[64,512]{1,0:T(8,128)S(1)}, f32[64,512]{1,0:T(8,128)S(1)}, u32[]{:S(2)}, u32[]{:S(2)}) %collective-permute-start.10) | collective-permute-done | bytes 131104 | tf_op jit(solution)/shard_map/ppermute | solution.py:57
  127.4 2.3 %collective-permute-start.14 = (f32[112,512]{1,0:T(8,128)S(1)}, f32[112,512]{1,0:T(8,128)S(1)}, u32[]{:S(2)}, u32[]{:S(2)}) collective-permute-start(f32[112,512]{1,0:T(8,128)S(1)} %pad_maximum_fusion.4), channel_id=1, source_target_pairs={{0,64},{16,0},{64,16},{1,65},{17,1},{65,17},{2,66},{18,2},{66,18},... | collective-permute-start | bytes 688136 | tf_op jit(solution)/shard_map/ppermute | solution.py:62
  129.7 6.1 %collective-permute-start.13 = (f32[112,512]{1,0:T(8,128)S(1)}, f32[112,512]{1,0:T(8,128)S(1)}, u32[]{:S(2)}, u32[]{:S(2)}) collective-permute-start(f32[112,512]{1,0:T(8,128)S(1)} %pad_maximum_fusion.4), channel_id=1, source_target_pairs={{0,16},{16,64},{64,0},{1,17},{17,65},{65,1},{2,18},{18,66},{66,2},... | collective-permute-start | bytes 688136 | tf_op jit(solution)/shard_map/ppermute | solution.py:61
  136.0 2.3 %collective-permute-done.14 = f32[112,512]{1,0:T(8,128)S(1)} collective-permute-done((f32[112,512]{1,0:T(8,128)S(1)}, f32[112,512]{1,0:T(8,128)S(1)}, u32[]{:S(2)}, u32[]{:S(2)}) %collective-permute-start.14) | collective-permute-done | bytes 229408 | tf_op jit(solution)/shard_map/ppermute | solution.py:62
  138.2 6.7 %collective-permute-done.13 = f32[112,512]{1,0:T(8,128)S(1)} collective-permute-done((f32[112,512]{1,0:T(8,128)S(1)}, f32[112,512]{1,0:T(8,128)S(1)}, u32[]{:S(2)}, u32[]{:S(2)}) %collective-permute-start.13) | collective-permute-done | bytes 229408 | tf_op jit(solution)/shard_map/ppermute | solution.py:61
  145.2 0.8 abs_reduce_fusion.2
  146.8 7.0 %collective-permute-start.15 = (f32[48,512]{1,0:T(8,128)S(1)}, f32[48,512]{1,0:T(8,128)S(1)}, u32[]{:S(2)}, u32[]{:S(2)}) collective-permute-start(f32[48,512]{1,0:T(8,128)S(1)} %slice.127), channel_id=1, source_target_pairs={{0,2},{2,0},{1,3},{3,1},{4,6},{6,4},{5,7},{7,5},{8,10},{10,8},{9,1... | collective-permute-start | bytes 294920 | tf_op jit(solution)/shard_map/ppermute | solution.py:53
  153.8 0.8 broadcast_in_dim.8
  154.7 3.5 %all-to-all-start.3 = ((f16[8,72,384]{2,1,0:T(8,128)(2,1)}), f16[8,72,384]{2,1,0:T(8,128)(2,1)S(1)}, u32[]{:S(2)}, u32[]{:S(2)}) async-start(f16[8,72,384]{2,1,0:T(8,128)(2,1)} %broadcast_in_dim.8), calls=%async_computation.3 | async-start | bytes 884736 | tf_op jit(solution)/shard_map/all_to_all | solution.py:18
  158.3 2.3 %collective-permute-start.18 = (f32[96,512]{1,0:T(8,128)S(1)}, f32[96,512]{1,0:T(8,128)S(1)}, u32[]{:S(2)}, u32[]{:S(2)}) collective-permute-start(f32[96,512]{1,0:T(8,128)S(1)} %get-tuple-element.24), channel_id=1, source_target_pairs={{0,12},{4,0},{8,4},{12,8},{1,13},{5,1},{9,5},{13,9},{2,14},{6,2},{... | collective-permute-start | bytes 589832 | tf_op jit(solution)/shard_map/ppermute | solution.py:57
  160.6 2.1 %collective-permute-start.17 = (f32[96,512]{1,0:T(8,128)S(1)}, f32[96,512]{1,0:T(8,128)S(1)}, u32[]{:S(2)}, u32[]{:S(2)}) collective-permute-start(f32[96,512]{1,0:T(8,128)S(1)} %get-tuple-element.24), channel_id=1, source_target_pairs={{0,8},{4,12},{8,0},{12,4},{1,9},{5,13},{9,1},{13,5},{2,10},{6,14},... | collective-permute-start | bytes 589832 | tf_op jit(solution)/shard_map/ppermute | solution.py:57
  162.7 2.8 %collective-permute-start.16 = (f32[96,512]{1,0:T(8,128)S(1)}, f32[96,512]{1,0:T(8,128)S(1)}, u32[]{:S(2)}, u32[]{:S(2)}) collective-permute-start(f32[96,512]{1,0:T(8,128)S(1)} %get-tuple-element.24), channel_id=1, source_target_pairs={{0,4},{4,8},{8,12},{12,0},{1,5},{5,9},{9,13},{13,1},{2,6},{6,10},{... | collective-permute-start | bytes 589832 | tf_op jit(solution)/shard_map/ppermute | solution.py:57
  165.5 3.3 %collective-permute-done.17 = f32[96,512]{1,0:T(8,128)S(1)} collective-permute-done((f32[96,512]{1,0:T(8,128)S(1)}, f32[96,512]{1,0:T(8,128)S(1)}, u32[]{:S(2)}, u32[]{:S(2)}) %collective-permute-start.17) | collective-permute-done | bytes 196640 | tf_op jit(solution)/shard_map/ppermute | solution.py:57
  168.8 4.7 %collective-permute-done.16 = f32[96,512]{1,0:T(8,128)S(1)} collective-permute-done((f32[96,512]{1,0:T(8,128)S(1)}, f32[96,512]{1,0:T(8,128)S(1)}, u32[]{:S(2)}, u32[]{:S(2)}) %collective-permute-start.16) | collective-permute-done | bytes 196640 | tf_op jit(solution)/shard_map/ppermute | solution.py:57
  173.7 4.3 %collective-permute-start.19 = (f32[384,512]{1,0:T(8,128)S(1)}, f32[384,512]{1,0:T(8,128)}, u32[]{:S(2)}, u32[]{:S(2)}) collective-permute-start(f32[384,512]{1,0:T(8,128)S(1)} %pad_maximum_fusion.1), channel_id=1, source_target_pairs={{0,1},{1,0},{2,3},{3,2},{4,5},{5,4},{6,7},{7,6},{8,9},{9,8},{10,11... | collective-permute-start | bytes 2359304 | tf_op jit(solution)/shard_map/ppermute | solution.py:53
  178.2 0.6 fusion.37
  178.8 0.6 convolution_add_fusion
  179.9 1.3 broadcast_select_fusion.1
  181.2 0.6 fusion.5
  181.8 1.2 abs_reduce_fusion
  183.9 0.9 concatenate.75
  184.9 3.5 %all-to-all-start.4 = ((f16[4,200,384]{2,1,0:T(8,128)(2,1)}), f16[4,200,384]{2,1,0:T(8,128)(2,1)S(1)}, u32[]{:S(2)}, u32[]{:S(2)}) async-start(f16[4,200,384]{2,1,0:T(8,128)(2,1)} %concatenate.75), calls=%async_computation.4 | async-start | bytes 1228800 | tf_op jit(solution)/shard_map/all_to_all | solution.py:18
  188.4 9.7 %all-to-all-done.4 = f16[4,200,384]{2,1,0:T(8,128)(2,1)S(1)} async-done(((f16[4,200,384]{2,1,0:T(8,128)(2,1)}), f16[4,200,384]{2,1,0:T(8,128)(2,1)S(1)}, u32[]{:S(2)}, u32[]{:S(2)}) %all-to-all-start.4) | async-done | bytes 614432 | tf_op jit(solution)/shard_map/all_to_all | solution.py:18
  198.2 0.8 copy-done.1
  199.1 0.7 fusion.9
  199.8 1.0 maximum_add_fusion
  (80 shorter events, 3.4 us)
Async XLA Ops:
  5.9 11.6 %all-to-all-start = ((bf16[4,224,384]{2,1,0:T(8,128)(2,1)}), bf16[4,224,384]{2,1,0:T(8,128)(2,1)S(1)}, u32[]{:S(2)}, u32[]{:S(2)}) async-start(bf16[4,224,384]{2,1,0:T(8,128)(2,1)} %pad_maximum_fusion.2), calls=%async_computation | async-start | bytes 1376256 | tf_op jit(solution)/shard_map/all_to_all | solution.py:18
  17.4 19.6 %collective-permute-start = (bf16[64,384]{1,0:T(8,128)(2,1)S(1)}, bf16[64,384]{1,0:T(8,128)(2,1)S(1)}, u32[]{:S(2)}, u32[]{:S(2)}) collective-permute-start(bf16[64,384]{1,0:T(8,128)(2,1)S(1)} %bitcast.96), channel_id=1, source_target_pairs={{0,32},{32,0},{1,33},{33,1},{2,34},{34,2},{3,35},{35,3},{4,36},{36... | collective-permute-start | bytes 147464 | tf_op jit(solution)/shard_map/ppermute | solution.py:53
  27.2 35.7 %all-to-all-start.1 = ((bf16[8,32,768]{2,1,0:T(8,128)(2,1)}), bf16[8,32,768]{2,1,0:T(8,128)(2,1)}, u32[]{:S(2)}, u32[]{:S(2)}) async-start(bf16[8,32,768]{2,1,0:T(8,128)(2,1)} %broadcast_in_dim.7), calls=%async_computation.1 | async-start | bytes 786432 | tf_op jit(solution)/shard_map/all_to_all | solution.py:18
  37.1 14.9 %collective-permute-start.1 = (bf16[128,384]{1,0:T(8,128)(2,1)S(1)}, bf16[128,384]{1,0:T(8,128)(2,1)S(1)}, u32[]{:S(2)}, u32[]{:S(2)}) collective-permute-start(bf16[128,384]{1,0:T(8,128)(2,1)S(1)} %pad_maximum_fusion.7), channel_id=1, source_target_pairs={{0,128},{128,256},{256,384},{384,0},{1,129},{129,257},{257,385},{3... | collective-permute-start | bytes 294920 | tf_op jit(solution)/shard_map/ppermute | solution.py:57
  41.3 10.8 %collective-permute-start.2 = (bf16[128,384]{1,0:T(8,128)(2,1)S(1)}, bf16[128,384]{1,0:T(8,128)(2,1)S(1)}, u32[]{:S(2)}, u32[]{:S(2)}) collective-permute-start(bf16[128,384]{1,0:T(8,128)(2,1)S(1)} %pad_maximum_fusion.7), channel_id=1, source_target_pairs={{0,256},{128,384},{256,0},{384,128},{1,257},{129,385},{257,1},{385... | collective-permute-start | bytes 294920 | tf_op jit(solution)/shard_map/ppermute | solution.py:57
  47.0 11.4 %collective-permute-start.3 = (bf16[128,384]{1,0:T(8,128)(2,1)S(1)}, bf16[128,384]{1,0:T(8,128)(2,1)S(1)}, u32[]{:S(2)}, u32[]{:S(2)}) collective-permute-start(bf16[128,384]{1,0:T(8,128)(2,1)S(1)} %pad_maximum_fusion.7), channel_id=1, source_target_pairs={{0,384},{128,0},{256,128},{384,256},{1,385},{129,1},{257,129},{385... | collective-permute-start | bytes 294920 | tf_op jit(solution)/shard_map/ppermute | solution.py:57
  59.9 15.2 %collective-permute-start.5 = (f32[384,512]{1,0:T(8,128)}, f32[384,512]{1,0:T(8,128)}, u32[]{:S(2)}, u32[]{:S(2)}) collective-permute-start(f32[384,512]{1,0:T(8,128)} %constant_dynamic-slice_fusion.1), channel_id=1, source_target_pairs={{0,1},{1,0},{2,3},{3,2},{4,5},{5,4},{6,7},{7,6},{8,9},{9,8},{10,11... | collective-permute-start | bytes 2359304 | tf_op jit(solution)/shard_map/ppermute | solution.py:53
  70.4 16.4 %all-to-all-start.2 = ((f16[8,72,384]{2,1,0:T(8,128)(2,1)}), f16[8,72,384]{2,1,0:T(8,128)(2,1)}, u32[]{:S(2)}, u32[]{:S(2)}) async-start(f16[8,72,384]{2,1,0:T(8,128)(2,1)} %concatenate.65), calls=%async_computation.2 | async-start | bytes 884736 | tf_op jit(solution)/shard_map/all_to_all | solution.py:18
  76.5 17.5 %collective-permute-start.8 = (f32[96,512]{1,0:T(8,128)S(1)}, f32[96,512]{1,0:T(8,128)S(1)}, u32[]{:S(2)}, u32[]{:S(2)}) collective-permute-start(f32[96,512]{1,0:T(8,128)S(1)} %get-tuple-element.14), channel_id=1, source_target_pairs={{0,12},{4,0},{8,4},{12,8},{1,13},{5,1},{9,5},{13,9},{2,14},{6,2},{... | collective-permute-start | bytes 589832 | tf_op jit(solution)/shard_map/ppermute | solution.py:57
  81.8 12.2 %collective-permute-start.7 = (f32[96,512]{1,0:T(8,128)S(1)}, f32[96,512]{1,0:T(8,128)S(1)}, u32[]{:S(2)}, u32[]{:S(2)}) collective-permute-start(f32[96,512]{1,0:T(8,128)S(1)} %get-tuple-element.15), channel_id=1, source_target_pairs={{0,8},{4,12},{8,0},{12,4},{1,9},{5,13},{9,1},{13,5},{2,10},{6,14},... | collective-permute-start | bytes 589832 | tf_op jit(solution)/shard_map/ppermute | solution.py:57
  84.3 11.5 %collective-permute-start.6 = (f32[96,512]{1,0:T(8,128)S(1)}, f32[96,512]{1,0:T(8,128)}, u32[]{:S(2)}, u32[]{:S(2)}) collective-permute-start(f32[96,512]{1,0:T(8,128)S(1)} %get-tuple-element.13), channel_id=1, source_target_pairs={{0,4},{4,8},{8,12},{12,0},{1,5},{5,9},{9,13},{13,1},{2,6},{6,10},{... | collective-permute-start | bytes 589832 | tf_op jit(solution)/shard_map/ppermute | solution.py:57
  89.2 16.7 %copy-start.2 = (f32[512]{0:T(512)S(1)}, f32[512]{0:T(512)}, u32[]{:S(2)}) copy-start(f32[512]{0:T(512)} %param.19) | copy-start | bytes 6148
  89.3 16.7 %copy-start.3 = (f32[512]{0:T(512)S(1)}, f32[512]{0:T(512)}, u32[]{:S(2)}) copy-start(f32[512]{0:T(512)} %param.17) | copy-start | bytes 6148
  89.3 16.7 %copy-start.4 = (f32[512]{0:T(512)S(1)}, f32[512]{0:T(512)}, u32[]{:S(2)}) copy-start(f32[512]{0:T(512)} %param.20) | copy-start | bytes 6148
  89.3 16.7 %copy-start.5 = (f32[512]{0:T(512)S(1)}, f32[512]{0:T(512)}, u32[]{:S(2)}) copy-start(f32[512]{0:T(512)} %param.18) | copy-start | bytes 6148
  89.3 7.6 %collective-permute-start.4 = (f32[64,512]{1,0:T(8,128)S(1)}, f32[64,512]{1,0:T(8,128)S(1)}, u32[]{:S(2)}, u32[]{:S(2)}) collective-permute-start(f32[64,512]{1,0:T(8,128)S(1)} %convolution_add_fusion.2), channel_id=1, source_target_pairs={{0,1},{1,0},{2,3},{3,2},{4,5},{5,4},{6,7},{7,6},{8,9},{9,8},{10,11... | collective-permute-start | bytes 393224 | tf_op jit(solution)/shard_map/ppermute | solution.py:53
  96.9 14.8 %collective-permute-start.9 = (f32[112,512]{1,0:T(8,128)S(1)}, f32[112,512]{1,0:T(8,128)S(1)}, u32[]{:S(2)}, u32[]{:S(2)}) collective-permute-start(f32[112,512]{1,0:T(8,128)S(1)} %pad_maximum_fusion.3), channel_id=1, source_target_pairs={{0,2},{2,0},{1,3},{3,1},{4,6},{6,4},{5,7},{7,5},{8,10},{10,8},{9,1... | collective-permute-start | bytes 688136 | tf_op jit(solution)/shard_map/ppermute | solution.py:53
  111.7 9.4 %collective-permute-start.12 = (f32[64,512]{1,0:T(8,128)S(1)}, f32[64,512]{1,0:T(8,128)S(1)}, u32[]{:S(2)}, u32[]{:S(2)}) collective-permute-start(f32[64,512]{1,0:T(8,128)S(1)} %slice_add_fusion), channel_id=1, source_target_pairs={{0,12},{4,0},{8,4},{12,8},{1,13},{5,1},{9,5},{13,9},{2,14},{6,2},{... | collective-permute-start | bytes 393224 | tf_op jit(solution)/shard_map/ppermute | solution.py:57
  116.1 7.2 %collective-permute-start.11 = (f32[64,512]{1,0:T(8,128)S(1)}, f32[64,512]{1,0:T(8,128)S(1)}, u32[]{:S(2)}, u32[]{:S(2)}) collective-permute-start(f32[64,512]{1,0:T(8,128)S(1)} %slice_add_fusion), channel_id=1, source_target_pairs={{0,8},{4,12},{8,0},{12,4},{1,9},{5,13},{9,1},{13,5},{2,10},{6,14},... | collective-permute-start | bytes 393224 | tf_op jit(solution)/shard_map/ppermute | solution.py:57
  118.6 8.7 %collective-permute-start.10 = (f32[64,512]{1,0:T(8,128)S(1)}, f32[64,512]{1,0:T(8,128)S(1)}, u32[]{:S(2)}, u32[]{:S(2)}) collective-permute-start(f32[64,512]{1,0:T(8,128)S(1)} %slice_add_fusion), channel_id=1, source_target_pairs={{0,4},{4,8},{8,12},{12,0},{1,5},{5,9},{9,13},{13,1},{2,6},{6,10},{... | collective-permute-start | bytes 393224 | tf_op jit(solution)/shard_map/ppermute | solution.py:57
  127.4 10.9 %collective-permute-start.14 = (f32[112,512]{1,0:T(8,128)S(1)}, f32[112,512]{1,0:T(8,128)S(1)}, u32[]{:S(2)}, u32[]{:S(2)}) collective-permute-start(f32[112,512]{1,0:T(8,128)S(1)} %pad_maximum_fusion.4), channel_id=1, source_target_pairs={{0,64},{16,0},{64,16},{1,65},{17,1},{65,17},{2,66},{18,2},{66,18},... | collective-permute-start | bytes 688136 | tf_op jit(solution)/shard_map/ppermute | solution.py:62
  129.7 15.2 %collective-permute-start.13 = (f32[112,512]{1,0:T(8,128)S(1)}, f32[112,512]{1,0:T(8,128)S(1)}, u32[]{:S(2)}, u32[]{:S(2)}) collective-permute-start(f32[112,512]{1,0:T(8,128)S(1)} %pad_maximum_fusion.4), channel_id=1, source_target_pairs={{0,16},{16,64},{64,0},{1,17},{17,65},{65,1},{2,18},{18,66},{66,2},... | collective-permute-start | bytes 688136 | tf_op jit(solution)/shard_map/ppermute | solution.py:61
  146.8 11.4 %collective-permute-start.15 = (f32[48,512]{1,0:T(8,128)S(1)}, f32[48,512]{1,0:T(8,128)S(1)}, u32[]{:S(2)}, u32[]{:S(2)}) collective-permute-start(f32[48,512]{1,0:T(8,128)S(1)} %slice.127), channel_id=1, source_target_pairs={{0,2},{2,0},{1,3},{3,1},{4,6},{6,4},{5,7},{7,5},{8,10},{10,8},{9,1... | collective-permute-start | bytes 294920 | tf_op jit(solution)/shard_map/ppermute | solution.py:53
  154.7 23.3 %all-to-all-start.3 = ((f16[8,72,384]{2,1,0:T(8,128)(2,1)}), f16[8,72,384]{2,1,0:T(8,128)(2,1)S(1)}, u32[]{:S(2)}, u32[]{:S(2)}) async-start(f16[8,72,384]{2,1,0:T(8,128)(2,1)} %broadcast_in_dim.8), calls=%async_computation.3 | async-start | bytes 884736 | tf_op jit(solution)/shard_map/all_to_all | solution.py:18
  158.3 7.2 %collective-permute-start.18 = (f32[96,512]{1,0:T(8,128)S(1)}, f32[96,512]{1,0:T(8,128)S(1)}, u32[]{:S(2)}, u32[]{:S(2)}) collective-permute-start(f32[96,512]{1,0:T(8,128)S(1)} %get-tuple-element.24), channel_id=1, source_target_pairs={{0,12},{4,0},{8,4},{12,8},{1,13},{5,1},{9,5},{13,9},{2,14},{6,2},{... | collective-permute-start | bytes 589832 | tf_op jit(solution)/shard_map/ppermute | solution.py:57
  160.6 8.2 %collective-permute-start.17 = (f32[96,512]{1,0:T(8,128)S(1)}, f32[96,512]{1,0:T(8,128)S(1)}, u32[]{:S(2)}, u32[]{:S(2)}) collective-permute-start(f32[96,512]{1,0:T(8,128)S(1)} %get-tuple-element.24), channel_id=1, source_target_pairs={{0,8},{4,12},{8,0},{12,4},{1,9},{5,13},{9,1},{13,5},{2,10},{6,14},... | collective-permute-start | bytes 589832 | tf_op jit(solution)/shard_map/ppermute | solution.py:57
  162.7 10.8 %collective-permute-start.16 = (f32[96,512]{1,0:T(8,128)S(1)}, f32[96,512]{1,0:T(8,128)S(1)}, u32[]{:S(2)}, u32[]{:S(2)}) collective-permute-start(f32[96,512]{1,0:T(8,128)S(1)} %get-tuple-element.24), channel_id=1, source_target_pairs={{0,4},{4,8},{8,12},{12,0},{1,5},{5,9},{9,13},{13,1},{2,6},{6,10},{... | collective-permute-start | bytes 589832 | tf_op jit(solution)/shard_map/ppermute | solution.py:57
  173.7 6.3 %collective-permute-start.19 = (f32[384,512]{1,0:T(8,128)S(1)}, f32[384,512]{1,0:T(8,128)}, u32[]{:S(2)}, u32[]{:S(2)}) collective-permute-start(f32[384,512]{1,0:T(8,128)S(1)} %pad_maximum_fusion.1), channel_id=1, source_target_pairs={{0,1},{1,0},{2,3},{3,2},{4,5},{5,4},{6,7},{7,6},{8,9},{9,8},{10,11... | collective-permute-start | bytes 2359304 | tf_op jit(solution)/shard_map/ppermute | solution.py:53
  184.9 13.2 %all-to-all-start.4 = ((f16[4,200,384]{2,1,0:T(8,128)(2,1)}), f16[4,200,384]{2,1,0:T(8,128)(2,1)S(1)}, u32[]{:S(2)}, u32[]{:S(2)}) async-start(f16[4,200,384]{2,1,0:T(8,128)(2,1)} %concatenate.75), calls=%async_computation.4 | async-start | bytes 1228800 | tf_op jit(solution)/shard_map/all_to_all | solution.py:18
  198.2 0.9 copy-start.1
  198.2 1.7 copy-start

commit v4 on v3

--- a/solution.py
+++ b/solution.py
@@ -63,14 +63,6 @@
     return values + first + second
 
 
-def ring_parts(values, place):
-    total = lax.dynamic_index_in_dim(values, place, 0, False)
-    for step in (1, 2, 3):
-        block = lax.dynamic_index_in_dim(values, (place + step) % 4, 0, False)
-        total = total + around(block, "x", 4, step)
-    return total
-
-
 def ring_gather(values, place):
     held = jnp.stack([values] + [around(values, "x", 4, step) for step in (1, 2, 3)])
     return jnp.concatenate([lax.dynamic_index_in_dim(held, (place - j) % 4, 0, False) for j in range(4)], axis=0)
@@ -103,7 +95,7 @@
     damp = damping[0]
     quad = lax.axis_index("yb") * 2 + lax.axis_index("zb")
     octant = lax.axis_index("yp") * 2 + lax.axis_index("zp")
-    core, high, place = lax.axis_index("c"), lax.axis_index("zh"), lax.axis_index("x")
+    core, place = lax.axis_index("c"), lax.axis_index("x")
     is_output = quad == 3
     left_shift = shifted(jnp.where(is_output, output_left_eigen, joined_left_eigen), damp)
     right_shift = shifted(jnp.where(is_output, output_right_eigen, joined_right_eigen), damp)
@@ -115,46 +107,51 @@
     own_shift = lax.dynamic_slice_in_dim(left_shift, octant * 64, 64, 0)
 
     left_j, left_o = joined_left_basis.T, output_left_basis.T
+    left = jnp.stack([left_j, left_j, left_j, left_o])
+    left = jnp.broadcast_to(left[:, None], (4, 8, 32, 192)).reshape(32, 32, 192)
+    left = exchange(left, QUAD + ("x", "zh")).reshape(4, 256, 192)
+    left = jnp.concatenate([left[0], left[1], left[2], left[3]], axis=1)
+    left = lax.all_gather(left, "c", axis=0, tiled=True)
+
     right_j, right_o = joined_right_basis.T, output_right_basis.T
     gradients = (joined_gradient[:, :384], joined_gradient[:, 384:768], joined_gradient[:, 768:], output_gradient)
     rights = (right_j[:, :384], right_j[:, 384:768], right_j[:, 768:], right_o)
-    lefts = [jnp.concatenate([left[:16], left[16:]], axis=1) for left in (left_j, left_o)]
-    lefts = (lefts[0], lefts[0], lefts[0], lefts[1])
-    sent = jnp.stack([jnp.concatenate(three, axis=0) for three in zip(gradients, rights, lefts)])
-    got = exchange(sent, QUAD)
+    sent = jnp.stack([jnp.concatenate(pair, axis=0) for pair in zip(gradients, rights)])
+    got = [lax.dynamic_index_in_dim(sent, quad, 0, False)]
+    for mask in (1, 2, 3):
+        block = lax.dynamic_index_in_dim(sent, quad ^ mask, 0, False)
+        got.append(lax.ppermute(block, QUAD, [(i, i ^ mask) for i in range(4)]))
+    got = jnp.stack(got)
+    got = jnp.stack([lax.dynamic_index_in_dim(got, quad ^ j, 0, False) for j in range(4)])
     gradient = got[:, :192].reshape(768, 384)
-
-    left = jnp.concatenate([got[:, 208:, :192], got[:, 208:, 192:]], axis=1)
-    left = left.transpose(1, 0, 2).reshape(32, 768)
-    left = exchange(jnp.broadcast_to(left[None], (8, 32, 768)), ("x", "zh")).reshape(256, 768)
-    left = lax.all_gather(left, "c", axis=0, tiled=True)
-
-    right = got[:, 192:208].reshape(64, 384)
+    right = got[:, 192:].reshape(64, 384)
     right = jnp.concatenate([right, swap(right, "zp")], axis=0)
-    right = jnp.concatenate([right] + [around(right, "yp", 4, step) for step in (1, 2, 3)], axis=0)
 
     rows = jnp.dot(left, gradient, preferred_element_type=jnp.float32)
-    rows = exchange(pack(rows.reshape(8, 64, 384)), OCT)
-    rows = jnp.sum(unpack(rows), axis=0)
+    rows = pack(rows.reshape(8, 64, 384))
+    right = right + (rows[0, 0, :1] * 0).astype(jnp.bfloat16)
+    rows = jnp.sum(unpack(exchange(rows, OCT)), axis=0)
+    right = jnp.concatenate([right] + [around(right, "yp", 4, step) for step in (1, 2, 3)], axis=0)
 
     cols = lax.dot_general(gradient, right, (((1,), (1,)), ((), ())), preferred_element_type=jnp.float32)
     cols = core_part(cols, core, True) + swap(core_part(cols, core, False), "c")
-    cols = ring_parts(cols.reshape(4, 96, 512), place)
+    cols = cols.reshape(4, 96, 512)
 
-    core_sum = dot_wide_left(rows, right, ((1,), (1,)))
-    core_sum = core_sum + swap(core_sum, "c")
-    both = swap(jnp.concatenate([core_sum, core_part(cols, high, False)], axis=0), "zh")
-    core_sum = core_sum + both[:64]
-    cols = core_part(cols, high, True) + both[64:]
-    core_sum = core_sum + around(core_sum, "x", 4, 1) + around(core_sum, "x", 4, 2) + around(core_sum, "x", 4, 3)
-    both = quad_sum(jnp.concatenate([core_sum, cols], axis=0), quad)
-    core_sum, cols = both[:64], both[64:]
-    mixed = rows / damp + dot_wide_left(core_sum * right_shift[None, :], right, ((1,), (0,)))
+    mid = dot_wide_left(rows, right, ((1,), (1,)))
+    mid = core_part(mid, core, True) + swap(core_part(mid, core, False), "c")
+    both = jnp.concatenate([mid, lax.dynamic_index_in_dim(cols, place, 0, False)], axis=0)
+    for step in (1, 2, 3):
+        block = lax.dynamic_index_in_dim(cols, (place + step) % 4, 0, False)
+        both = both + around(jnp.concatenate([mid, block], axis=0), "x", 4, step)
+    both = both + swap(both, "zh")
+    both = quad_sum(both, quad)
+    mid = lax.all_gather(both[:32], "c", axis=0, tiled=True)
+    cols = both[32:]
+    mixed = rows / damp + dot_wide_left(mid * right_shift[None, :], right, ((1,), (0,)))
     mixed = mixed * own_shift[:, None]
     packed = pack(mixed)
     mixed = unpack(exchange(jnp.broadcast_to(packed[None], (8, 72, 384)), OCT)).reshape(512, 384)
 
-    cols = joined_pair(cols, swap(cols, "zh"), high)
     cols = ring_gather(cols, place)
     cols = joined_pair(cols, swap(cols, "c"), core)
 

time: 202 us -> 216 us (1.069)
  waiting for transfers between devices: 53.2 us -> 77.9 us
  starting transfers between devices: 113 us -> 93.5 us
  matrix products: 7.16 us -> 13.3 us
  blocking collectives: 2.65 us -> 7.21 us
    ppermute x6 -> x5, waiting for transfers between devices: 5.93 us -> 23.6 us  [swap(): return lax.ppermute(values, axis, [(0, 1), (1, 0)])]
    ppermute x6 -> x5, starting transfers between devices: 35.8 us -> 18.6 us  [swap(): return lax.ppermute(values, axis, [(0, 1), (1, 0)])]
    ppermute x12 -> x9, starting transfers between devices: 41.6 us -> 30 us  [around(): lax.ppermute(values, axis, [(i, (i + step) % size) for i in range(size)])]
    ppermute x0 -> x3, waiting for transfers between devices: none -> 10.9 us  [local(): got.append(lax.ppermute(block, QUAD, [(i, i ^ mask) for i in range(4)]))]
    ppermute x0 -> x3, starting transfers between devices: none -> 8.37 us  [local(): got.append(lax.ppermute(block, QUAD, [(i, i ^ mask) for i in range(4)]))]
    all_to_all x5 -> x4, waiting for transfers between devices: 16 us -> 8.7 us  [exchange(): return lax.all_to_all(blocks, axes, 0, 0, tiled=True)]
    dot_general x6, matrix products: 3.29 us -> 9.31 us  [dot_wide_left(): lax.dot_general(part, narrow, (dims, ((), ())), preferred_element_type=jn...]
    ppermute x1, starting transfers between devices: 6.05 us -> 1.92 us  [quad_sum(): first = lax.ppermute(values, QUAD, [(0, 1), (1, 2), (2, 0)])]
  transfers between devices with their start and end apart: 25 -> 23, of which waited for: 13 -> 17; matrix products, arithmetic and copies ran while one was open for 7% -> 5% of each run, Pallas kernels for 0% -> 0%
where the time goes in v4:
time: 216 us; the launch traced here: 214 us
  starting transfers between devices  93.5 us (43%)
  waiting for transfers between devices  77.9 us (36%)
  matrix products  13.3 us (6%)
  other arithmetic  8.6 us (4%)
  local copies, waits for them, and re-layouts  8.49 us (4%)
  blocking collectives  7.21 us (3%)
  between operations  5.16 us (2%)
    ppermute x9, starting transfers between devices, around(): lax.ppermute(values, axis, [(i, (i + step) % size) for i in range(size)])  30 us
    all_to_all x4, starting transfers between devices, exchange(): return lax.all_to_all(blocks, axes, 0, 0, tiled=True)  29.6 us
    ppermute x9, waiting for transfers between devices, around(): lax.ppermute(values, axis, [(i, (i + step) % size) for i in range(size)])  25.1 us
    ppermute x5, waiting for transfers between devices, swap(): return lax.ppermute(values, axis, [(0, 1), (1, 0)])  23.6 us
    ppermute x5, starting transfers between devices, swap(): return lax.ppermute(values, axis, [(0, 1), (1, 0)])  18.6 us
    ppermute x3, waiting for transfers between devices, local(): got.append(lax.ppermute(block, QUAD, [(i, i ^ mask) for i in range(4)]))  10.9 us
    dot_general x6, matrix products, dot_wide_left(): lax.dot_general(part, narrow, (dims, ((), ())), preferred_element_type=jn...  9.31 us
    all_to_all x4, waiting for transfers between devices, exchange(): return lax.all_to_all(blocks, axes, 0, 0, tiled=True)  8.7 us
  transfers between devices with their start and end apart: 23, of which 17 were waited for; matrix products, arithmetic and copies ran while one was open for 5% of the time, Pallas kernels for 0%

profile of v4, /device:TPU:1, one launch (start us, length us, event | category | flops | bytes accessed | tf_op | source)
XLA Modules:
  0.0 214.2 jit_solution(6619795508789292766)
XLA Ops:
  0.7 0.8 pad_maximum_fusion.11
  1.5 0.9 broadcast_in_dim.4
  2.4 14.7 %all-to-all-start = ((bf16[32,32,192]{2,1,0:T(8,128)(2,1)}), bf16[32,32,192]{2,1,0:T(8,128)(2,1)S(1)}, u32[]{:S(2)}, u32[]{:S(2)}) async-start(bf16[32,32,192]{2,1,0:T(8,128)(2,1)} %bitcast.4), calls=%async_computation | async-start | bytes 1048576 | tf_op jit(solution)/shard_map/all_to_all | solution.py:18
  17.5 4.1 %collective-permute-start.2 = (bf16[208,384]{1,0:T(8,128)(2,1)S(1)}, bf16[208,384]{1,0:T(8,128)(2,1)S(1)}, u32[]{:S(2)}, u32[]{:S(2)}) collective-permute-start(bf16[208,384]{1,0:T(8,128)(2,1)S(1)} %get-tuple-element.22), channel_id=1, source_target_pairs={{0,80},{16,64},{64,16},{80,0},{1,81},{17,65},{65,17},{81,1},{2,82}... | collective-permute-start | bytes 479240 | tf_op jit(solution)/shard_map/ppermute | solution.py:123
  21.6 2.2 %collective-permute-start.1 = (bf16[208,384]{1,0:T(8,128)(2,1)S(1)}, bf16[208,384]{1,0:T(8,128)(2,1)S(1)}, u32[]{:S(2)}, u32[]{:S(2)}) collective-permute-start(bf16[208,384]{1,0:T(8,128)(2,1)S(1)} %get-tuple-element.23), channel_id=1, source_target_pairs={{0,64},{16,80},{64,0},{80,16},{1,65},{17,81},{65,1},{81,17},{2,66}... | collective-permute-start | bytes 479240 | tf_op jit(solution)/shard_map/ppermute | solution.py:123
  23.8 2.1 %collective-permute-start = (bf16[208,384]{1,0:T(8,128)(2,1)S(1)}, bf16[208,384]{1,0:T(8,128)(2,1)S(1)}, u32[]{:S(2)}, u32[]{:S(2)}) collective-permute-start(bf16[208,384]{1,0:T(8,128)(2,1)S(1)} %get-tuple-element.24), channel_id=1, source_target_pairs={{0,16},{16,0},{64,80},{80,64},{1,17},{17,1},{65,81},{81,65},{2,18}... | collective-permute-start | bytes 479240 | tf_op jit(solution)/shard_map/ppermute | solution.py:123
  25.9 3.8 %collective-permute-done.2 = bf16[208,384]{1,0:T(8,128)(2,1)S(1)} collective-permute-done((bf16[208,384]{1,0:T(8,128)(2,1)S(1)}, bf16[208,384]{1,0:T(8,128)(2,1)S(1)}, u32[]{:S(2)}, u32[]{:S(2)}) %collective-permute-start.2) | collective-permute-done | bytes 159776 | tf_op jit(solution)/shard_map/ppermute | solution.py:123
  29.7 1.5 collective-permute-done.1
  31.2 5.7 %collective-permute-done = bf16[208,384]{1,0:T(8,128)(2,1)S(1)} collective-permute-done((bf16[208,384]{1,0:T(8,128)(2,1)S(1)}, bf16[208,384]{1,0:T(8,128)(2,1)S(1)}, u32[]{:S(2)}, u32[]{:S(2)}) %collective-permute-start) | collective-permute-done | bytes 159776 | tf_op jit(solution)/shard_map/ppermute | solution.py:123
  37.1 0.7 copy-done.1
  38.1 4.6 %all_gather.6 = bf16[512,768]{1,0:T(8,128)(2,1)S(1)} all-gather(bf16[256,768]{1,0:T(8,128)(2,1)S(1)} %pad_maximum_fusion.9), channel_id=1, replica_groups=mesh['yp'=4,'yb'=2,'zp'=2,'zb'=2,'x'=4,'zh'=2,'c'=2] {'c'}, dimensions={0}, use_global_device_ids=true | all-gather | bytes 1179648 | tf_op jit(solution)/shard_map/all_gather | solution.py:114
  42.7 1.2 abs_reduce_fusion.1
  44.7 0.9 concatenate.59
  45.6 6.5 %all-to-all-start.1 = ((f16[8,72,384]{2,1,0:T(8,128)(2,1)}), f16[8,72,384]{2,1,0:T(8,128)(2,1)}, u32[]{:S(2)}, u32[]{:S(2)}) async-start(f16[8,72,384]{2,1,0:T(8,128)(2,1)} %concatenate.59), calls=%async_computation.1 | async-start | bytes 884736 | tf_op jit(solution)/shard_map/all_to_all | solution.py:18
  52.1 4.3 %collective-permute-start.3 = (bf16[64,384]{1,0:T(8,128)(2,1)S(1)}, bf16[64,384]{1,0:T(8,128)(2,1)S(1)}, u32[]{:S(2)}, u32[]{:S(2)}) collective-permute-start(bf16[64,384]{1,0:T(8,128)(2,1)S(1)} %bitcast.107), channel_id=1, source_target_pairs={{0,32},{32,0},{1,33},{33,1},{2,34},{34,2},{3,35},{35,3},{4,36},{36... | collective-permute-start | bytes 147464 | tf_op jit(solution)/shard_map/ppermute | solution.py:53
  57.5 9.5 %collective-permute-done.3 = bf16[64,384]{1,0:T(8,128)(2,1)S(1)} collective-permute-done((bf16[64,384]{1,0:T(8,128)(2,1)S(1)}, bf16[64,384]{1,0:T(8,128)(2,1)S(1)}, u32[]{:S(2)}, u32[]{:S(2)}) %collective-permute-start.3) | collective-permute-done | bytes 49184 | tf_op jit(solution)/shard_map/ppermute | solution.py:53
  67.0 5.5 %collective-permute-start.6 = (bf16[128,384]{1,0:T(8,128)(2,1)S(1)}, bf16[128,384]{1,0:T(8,128)(2,1)}, u32[]{:S(2)}, u32[]{:S(2)}) collective-permute-start(bf16[128,384]{1,0:T(8,128)(2,1)S(1)} %maximum_add_fusion.1), channel_id=1, source_target_pairs={{0,384},{128,0},{256,128},{384,256},{1,385},{129,1},{257,129},{385... | collective-permute-start | bytes 294920 | tf_op jit(solution)/shard_map/ppermute | solution.py:57
  72.6 3.8 %collective-permute-start.5 = (bf16[128,384]{1,0:T(8,128)(2,1)S(1)}, bf16[128,384]{1,0:T(8,128)(2,1)}, u32[]{:S(2)}, u32[]{:S(2)}) collective-permute-start(bf16[128,384]{1,0:T(8,128)(2,1)S(1)} %maximum_add_fusion.1), channel_id=1, source_target_pairs={{0,256},{128,384},{256,0},{384,128},{1,257},{129,385},{257,1},{385... | collective-permute-start | bytes 294920 | tf_op jit(solution)/shard_map/ppermute | solution.py:57
  76.3 4.3 %collective-permute-start.4 = (bf16[128,384]{1,0:T(8,128)(2,1)S(1)}, bf16[128,384]{1,0:T(8,128)(2,1)}, u32[]{:S(2)}, u32[]{:S(2)}) collective-permute-start(bf16[128,384]{1,0:T(8,128)(2,1)S(1)} %maximum_add_fusion.1), channel_id=1, source_target_pairs={{0,128},{128,256},{256,384},{384,0},{1,129},{129,257},{257,385},{3... | collective-permute-start | bytes 294920 | tf_op jit(solution)/shard_map/ppermute | solution.py:57
  80.6 1.4 collective-permute-done.5
  82.0 2.4 %collective-permute-done.4 = bf16[128,384]{1,0:T(8,128)(2,1)} collective-permute-done((bf16[128,384]{1,0:T(8,128)(2,1)S(1)}, bf16[128,384]{1,0:T(8,128)(2,1)}, u32[]{:S(2)}, u32[]{:S(2)}) %collective-permute-start.4) | collective-permute-done | bytes 98336 | tf_op jit(solution)/shard_map/ppermute | solution.py:57
  84.3 1.6 fusion.27
  85.9 0.9 constant_dynamic-slice_fusion
  86.9 4.3 %collective-permute-start.8 = (f32[384,512]{1,0:T(8,128)}, f32[384,512]{1,0:T(8,128)}, u32[]{:S(2)}, u32[]{:S(2)}) collective-permute-start(f32[384,512]{1,0:T(8,128)} %constant_dynamic-slice_fusion), channel_id=1, source_target_pairs={{0,1},{1,0},{2,3},{3,2},{4,5},{5,4},{6,7},{7,6},{8,9},{9,8},{10,11... | collective-permute-start | bytes 2359304 | tf_op jit(solution)/shard_map/ppermute | solution.py:53
  91.2 0.8 slice.113
  92.0 1.1 multiply_reduce_fusion
  93.1 1.3 fusion.19
  94.4 1.2 convolution_add_fusion.2
  95.7 1.9 collective-permute-start.7
  97.6 1.2 collective-permute-done.7
  98.8 1.3 dynamic-slice_add_fusion
  100.3 4.3 %collective-permute-start.11 = (f32[128,512]{1,0:T(8,128)S(1)}, f32[128,512]{1,0:T(8,128)S(1)}, u32[]{:S(2)}, u32[]{:S(2)}) collective-permute-start(f32[128,512]{1,0:T(8,128)S(1)} %get-tuple-element.36), channel_id=1, source_target_pairs={{0,12},{4,0},{8,4},{12,8},{1,13},{5,1},{9,5},{13,9},{2,14},{6,2},{... | collective-permute-start | bytes 786440 | tf_op jit(solution)/shard_map/ppermute | solution.py:57
  104.6 2.5 %collective-permute-start.10 = (f32[128,512]{1,0:T(8,128)S(1)}, f32[128,512]{1,0:T(8,128)S(1)}, u32[]{:S(2)}, u32[]{:S(2)}) collective-permute-start(f32[128,512]{1,0:T(8,128)S(1)} %get-tuple-element.35), channel_id=1, source_target_pairs={{0,8},{4,12},{8,0},{12,4},{1,9},{5,13},{9,1},{13,5},{2,10},{6,14},... | collective-permute-start | bytes 786440 | tf_op jit(solution)/shard_map/ppermute | solution.py:57
  107.1 2.5 %collective-permute-start.9 = (f32[128,512]{1,0:T(8,128)S(1)}, f32[128,512]{1,0:T(8,128)S(1)}, u32[]{:S(2)}, u32[]{:S(2)}) collective-permute-start(f32[128,512]{1,0:T(8,128)S(1)} %get-tuple-element.34), channel_id=1, source_target_pairs={{0,4},{4,8},{8,12},{12,0},{1,5},{5,9},{9,13},{13,1},{2,6},{6,10},{... | collective-permute-start | bytes 786440 | tf_op jit(solution)/shard_map/ppermute | solution.py:57
  109.6 6.0 %collective-permute-done.11 = f32[128,512]{1,0:T(8,128)S(1)} collective-permute-done((f32[128,512]{1,0:T(8,128)S(1)}, f32[128,512]{1,0:T(8,128)S(1)}, u32[]{:S(2)}, u32[]{:S(2)}) %collective-permute-start.11) | collective-permute-done | bytes 262176 | tf_op jit(solution)/shard_map/ppermute | solution.py:57
  115.6 6.2 %collective-permute-done.9 = f32[128,512]{1,0:T(8,128)S(1)} collective-permute-done((f32[128,512]{1,0:T(8,128)S(1)}, f32[128,512]{1,0:T(8,128)S(1)}, u32[]{:S(2)}, u32[]{:S(2)}) %collective-permute-start.9) | collective-permute-done | bytes 262176 | tf_op jit(solution)/shard_map/ppermute | solution.py:57
  121.9 5.8 %collective-permute-start.12 = (f32[128,512]{1,0:T(8,128)S(1)}, f32[128,512]{1,0:T(8,128)S(1)}, u32[]{:S(2)}, u32[]{:S(2)}) collective-permute-start(f32[128,512]{1,0:T(8,128)S(1)} %fusion.12), channel_id=1, source_target_pairs={{0,2},{2,0},{1,3},{3,1},{4,6},{6,4},{5,7},{7,5},{8,10},{10,8},{9,1... | collective-permute-start | bytes 786440 | tf_op jit(solution)/shard_map/ppermute | solution.py:53
  128.9 12.1 %collective-permute-done.12 = f32[128,512]{1,0:T(8,128)S(1)} collective-permute-done((f32[128,512]{1,0:T(8,128)S(1)}, f32[128,512]{1,0:T(8,128)S(1)}, u32[]{:S(2)}, u32[]{:S(2)}) %collective-permute-start.12) | collective-permute-done | bytes 262176 | tf_op jit(solution)/shard_map/ppermute | solution.py:53
  141.1 5.0 %collective-permute-start.14 = (f32[128,512]{1,0:T(8,128)S(1)}, f32[128,512]{1,0:T(8,128)S(1)}, u32[]{:S(2)}, u32[]{:S(2)}) collective-permute-start(f32[128,512]{1,0:T(8,128)S(1)} %add.206), channel_id=1, source_target_pairs={{0,64},{16,0},{64,16},{1,65},{17,1},{65,17},{2,66},{18,2},{66,18},... | collective-permute-start | bytes 786440 | tf_op jit(solution)/shard_map/ppermute | solution.py:62
  146.1 1.9 collective-permute-start.13
  148.2 3.0 %collective-permute-done.14 = f32[128,512]{1,0:T(8,128)S(1)} collective-permute-done((f32[128,512]{1,0:T(8,128)S(1)}, f32[128,512]{1,0:T(8,128)S(1)}, u32[]{:S(2)}, u32[]{:S(2)}) %collective-permute-start.14) | collective-permute-done | bytes 262176 | tf_op jit(solution)/shard_map/ppermute | solution.py:62
  151.2 6.7 %collective-permute-done.13 = f32[128,512]{1,0:T(8,128)S(1)} collective-permute-done((f32[128,512]{1,0:T(8,128)S(1)}, f32[128,512]{1,0:T(8,128)S(1)}, u32[]{:S(2)}, u32[]{:S(2)}) %collective-permute-start.13) | collective-permute-done | bytes 262176 | tf_op jit(solution)/shard_map/ppermute | solution.py:61
  158.0 2.6 %all_gather.7 = f32[64,512]{1,0:T(8,128)S(1)} all-gather(f32[32,512]{1,0:T(8,128)S(1)} %slice.116), channel_id=1, replica_groups=mesh['yp'=4,'yb'=2,'zp'=2,'zb'=2,'x'=4,'zh'=2,'c'=2] {'c'}, dimensions={0}, use_global_device_ids=true | all-gather | bytes 196608 | tf_op jit(solution)/shard_map/all_gather | solution.py:148
  160.6 1.2 fusion.15
  161.8 1.8 abs_reduce_fusion.2
  164.4 0.8 broadcast_in_dim.5
  165.2 5.0 %all-to-all-start.2 = ((f16[8,72,384]{2,1,0:T(8,128)(2,1)}), f16[8,72,384]{2,1,0:T(8,128)(2,1)S(1)}, u32[]{:S(2)}, u32[]{:S(2)}) async-start(f16[8,72,384]{2,1,0:T(8,128)(2,1)} %broadcast_in_dim.5), calls=%async_computation.2 | async-start | bytes 884736 | tf_op jit(solution)/shard_map/all_to_all | solution.py:18
  170.3 1.9 collective-permute-start.17
  172.2 2.5 %collective-permute-start.16 = (f32[96,512]{1,0:T(8,128)S(1)}, f32[96,512]{1,0:T(8,128)S(1)}, u32[]{:S(2)}, u32[]{:S(2)}) collective-permute-start(f32[96,512]{1,0:T(8,128)S(1)} %get-tuple-element.33), channel_id=1, source_target_pairs={{0,8},{4,12},{8,0},{12,4},{1,9},{5,13},{9,1},{13,5},{2,10},{6,14},... | collective-permute-start | bytes 589832 | tf_op jit(solution)/shard_map/ppermute | solution.py:57
  174.7 2.8 %collective-permute-start.15 = (f32[96,512]{1,0:T(8,128)S(1)}, f32[96,512]{1,0:T(8,128)S(1)}, u32[]{:S(2)}, u32[]{:S(2)}) collective-permute-start(f32[96,512]{1,0:T(8,128)S(1)} %get-tuple-element.33), channel_id=1, source_target_pairs={{0,4},{4,8},{8,12},{12,0},{1,5},{5,9},{9,13},{13,1},{2,6},{6,10},{... | collective-permute-start | bytes 589832 | tf_op jit(solution)/shard_map/ppermute | solution.py:57
  178.0 3.4 %collective-permute-done.16 = f32[96,512]{1,0:T(8,128)S(1)} collective-permute-done((f32[96,512]{1,0:T(8,128)S(1)}, f32[96,512]{1,0:T(8,128)S(1)}, u32[]{:S(2)}, u32[]{:S(2)}) %collective-permute-start.16) | collective-permute-done | bytes 196640 | tf_op jit(solution)/shard_map/ppermute | solution.py:57
  181.4 5.2 %collective-permute-done.15 = f32[96,512]{1,0:T(8,128)S(1)} collective-permute-done((f32[96,512]{1,0:T(8,128)S(1)}, f32[96,512]{1,0:T(8,128)S(1)}, u32[]{:S(2)}, u32[]{:S(2)}) %collective-permute-start.15) | collective-permute-done | bytes 196640 | tf_op jit(solution)/shard_map/ppermute | solution.py:57
  186.7 0.9 pad_maximum_fusion.1
  187.7 2.4 %collective-permute-start.18 = (f32[384,512]{1,0:T(8,128)}, f32[384,512]{1,0:T(8,128)}, u32[]{:S(2)}, u32[]{:S(2)}) collective-permute-start(f32[384,512]{1,0:T(8,128)} %pad_maximum_fusion.1), channel_id=1, source_target_pairs={{0,1},{1,0},{2,3},{3,2},{4,5},{5,4},{6,7},{7,6},{8,9},{9,8},{10,11... | collective-permute-start | bytes 2359304 | tf_op jit(solution)/shard_map/ppermute | solution.py:53
  191.5 0.8 collective-permute-done.18
  192.3 1.3 broadcast_select_fusion.1
  193.6 1.6 fusion.5
  195.2 2.3 %abs_reduce_fusion = (f32[]{:T(128)}, f32[768,384]{1,0:T(8,128)S(1)}) fusion(f32[768,384]{1,0:T(8,128)S(1)} %convolution_add_fusion, f32[768,384]{1,0:T(8,128)S(1)} %fusion.5, bf16[128,384]{1,0:T(8,128)(2,1)} %collective-permute-done.6, bf16[128,384]{1,0:T(8,128)(2,1)} %collective-permute-done.5, bf16[128,384]{1,0:T(8,128)(2,1)} %collective-permute-done.4, ...), kind=kOutput, calls=%fused_computation.9 | convolution fusion | flops 306315264 | bytes 5507076 | tf_op jit(solution)/shard_map/dot_general | solution.py:28
  198.3 0.9 concatenate.70
  199.3 3.5 %all-to-all-start.3 = ((f16[4,200,384]{2,1,0:T(8,128)(2,1)}), f16[4,200,384]{2,1,0:T(8,128)(2,1)S(1)}, u32[]{:S(2)}, u32[]{:S(2)}) async-start(f16[4,200,384]{2,1,0:T(8,128)(2,1)} %concatenate.70), calls=%async_computation.3 | async-start | bytes 1228800 | tf_op jit(solution)/shard_map/all_to_all | solution.py:18
  202.8 8.7 %all-to-all-done.3 = f16[4,200,384]{2,1,0:T(8,128)(2,1)S(1)} async-done(((f16[4,200,384]{2,1,0:T(8,128)(2,1)}), f16[4,200,384]{2,1,0:T(8,128)(2,1)S(1)}, u32[]{:S(2)}, u32[]{:S(2)}) %all-to-all-start.3) | async-done | bytes 614432 | tf_op jit(solution)/shard_map/all_to_all | solution.py:18
  211.7 0.8 copy-done.4
  212.5 0.7 fusion.9
  213.2 1.0 maximum_add_fusion
  (85 shorter events, 4.9 us)
Async XLA Ops:
  0.6 16.5 %copy-start.7 = (bf16[1152,16]{0,1:T(8,128)(2,1)S(1)}, bf16[1152,16]{0,1:T(8,128)(2,1)}, u32[]{:S(2)}) copy-start(bf16[1152,16]{0,1:T(8,128)(2,1)} %param.14) | copy-start | bytes 110596
  0.6 16.5 %copy-start = (bf16[192,1152]{1,0:T(8,128)(2,1)S(1)}, bf16[192,1152]{1,0:T(8,128)(2,1)}, u32[]{:S(2)}) copy-start(bf16[192,1152]{1,0:T(8,128)(2,1)} %param.11) | copy-start | bytes 1327108
  1.5 15.7 %copy-start.3 = (bf16[192,384]{1,0:T(8,128)(2,1)S(1)}, bf16[192,384]{1,0:T(8,128)(2,1)}, u32[]{:S(2)}) copy-start(bf16[192,384]{1,0:T(8,128)(2,1)} %param.12) | copy-start | bytes 442372
  1.5 15.7 %copy-start.8 = (bf16[384,16]{0,1:T(8,128)(2,1)S(1)}, bf16[384,16]{0,1:T(8,128)(2,1)}, u32[]{:S(2)}) copy-start(bf16[384,16]{0,1:T(8,128)(2,1)} %param.16) | copy-start | bytes 36868
  2.4 35.5 %all-to-all-start = ((bf16[32,32,192]{2,1,0:T(8,128)(2,1)}), bf16[32,32,192]{2,1,0:T(8,128)(2,1)S(1)}, u32[]{:S(2)}, u32[]{:S(2)}) async-start(bf16[32,32,192]{2,1,0:T(8,128)(2,1)} %bitcast.4), calls=%async_computation | async-start | bytes 1048576 | tf_op jit(solution)/shard_map/all_to_all | solution.py:18
  17.5 12.2 %collective-permute-start.2 = (bf16[208,384]{1,0:T(8,128)(2,1)S(1)}, bf16[208,384]{1,0:T(8,128)(2,1)S(1)}, u32[]{:S(2)}, u32[]{:S(2)}) collective-permute-start(bf16[208,384]{1,0:T(8,128)(2,1)S(1)} %get-tuple-element.22), channel_id=1, source_target_pairs={{0,80},{16,64},{64,16},{80,0},{1,81},{17,65},{65,17},{81,1},{2,82}... | collective-permute-start | bytes 479240 | tf_op jit(solution)/shard_map/ppermute | solution.py:123
  21.6 9.5 %collective-permute-start.1 = (bf16[208,384]{1,0:T(8,128)(2,1)S(1)}, bf16[208,384]{1,0:T(8,128)(2,1)S(1)}, u32[]{:S(2)}, u32[]{:S(2)}) collective-permute-start(bf16[208,384]{1,0:T(8,128)(2,1)S(1)} %get-tuple-element.23), channel_id=1, source_target_pairs={{0,64},{16,80},{64,0},{80,16},{1,65},{17,81},{65,1},{81,17},{2,66}... | collective-permute-start | bytes 479240 | tf_op jit(solution)/shard_map/ppermute | solution.py:123
  23.8 13.0 %collective-permute-start = (bf16[208,384]{1,0:T(8,128)(2,1)S(1)}, bf16[208,384]{1,0:T(8,128)(2,1)S(1)}, u32[]{:S(2)}, u32[]{:S(2)}) collective-permute-start(bf16[208,384]{1,0:T(8,128)(2,1)S(1)} %get-tuple-element.24), channel_id=1, source_target_pairs={{0,16},{16,0},{64,80},{80,64},{1,17},{17,1},{65,81},{81,65},{2,18}... | collective-permute-start | bytes 479240 | tf_op jit(solution)/shard_map/ppermute | solution.py:123
  37.0 0.7 copy-start.1
  44.7 7.3 %copy-start.2 = (bf16[1,208,384]{2,1,0:T(8,128)(2,1)S(1)}, bf16[1,208,384]{2,1,0:T(8,128)(2,1)}, u32[]{:S(2)}) copy-start(bf16[1,208,384]{2,1,0:T(8,128)(2,1)} %copy-done.1) | copy-start | bytes 479236
  45.6 45.6 %all-to-all-start.1 = ((f16[8,72,384]{2,1,0:T(8,128)(2,1)}), f16[8,72,384]{2,1,0:T(8,128)(2,1)}, u32[]{:S(2)}, u32[]{:S(2)}) async-start(f16[8,72,384]{2,1,0:T(8,128)(2,1)} %concatenate.59), calls=%async_computation.1 | async-start | bytes 884736 | tf_op jit(solution)/shard_map/all_to_all | solution.py:18
  52.1 14.9 %collective-permute-start.3 = (bf16[64,384]{1,0:T(8,128)(2,1)S(1)}, bf16[64,384]{1,0:T(8,128)(2,1)S(1)}, u32[]{:S(2)}, u32[]{:S(2)}) collective-permute-start(bf16[64,384]{1,0:T(8,128)(2,1)S(1)} %bitcast.107), channel_id=1, source_target_pairs={{0,32},{32,0},{1,33},{33,1},{2,34},{34,2},{3,35},{35,3},{4,36},{36... | collective-permute-start | bytes 147464 | tf_op jit(solution)/shard_map/ppermute | solution.py:53
  67.0 13.6 %collective-permute-start.6 = (bf16[128,384]{1,0:T(8,128)(2,1)S(1)}, bf16[128,384]{1,0:T(8,128)(2,1)}, u32[]{:S(2)}, u32[]{:S(2)}) collective-permute-start(bf16[128,384]{1,0:T(8,128)(2,1)S(1)} %maximum_add_fusion.1), channel_id=1, source_target_pairs={{0,384},{128,0},{256,128},{384,256},{1,385},{129,1},{257,129},{385... | collective-permute-start | bytes 294920 | tf_op jit(solution)/shard_map/ppermute | solution.py:57
  72.6 9.4 %collective-permute-start.5 = (bf16[128,384]{1,0:T(8,128)(2,1)S(1)}, bf16[128,384]{1,0:T(8,128)(2,1)}, u32[]{:S(2)}, u32[]{:S(2)}) collective-permute-start(bf16[128,384]{1,0:T(8,128)(2,1)S(1)} %maximum_add_fusion.1), channel_id=1, source_target_pairs={{0,256},{128,384},{256,0},{384,128},{1,257},{129,385},{257,1},{385... | collective-permute-start | bytes 294920 | tf_op jit(solution)/shard_map/ppermute | solution.py:57
  76.3 8.0 %collective-permute-start.4 = (bf16[128,384]{1,0:T(8,128)(2,1)S(1)}, bf16[128,384]{1,0:T(8,128)(2,1)}, u32[]{:S(2)}, u32[]{:S(2)}) collective-permute-start(bf16[128,384]{1,0:T(8,128)(2,1)S(1)} %maximum_add_fusion.1), channel_id=1, source_target_pairs={{0,128},{128,256},{256,384},{384,0},{1,129},{129,257},{257,385},{3... | collective-permute-start | bytes 294920 | tf_op jit(solution)/shard_map/ppermute | solution.py:57
  86.9 12.0 %collective-permute-start.8 = (f32[384,512]{1,0:T(8,128)}, f32[384,512]{1,0:T(8,128)}, u32[]{:S(2)}, u32[]{:S(2)}) collective-permute-start(f32[384,512]{1,0:T(8,128)} %constant_dynamic-slice_fusion), channel_id=1, source_target_pairs={{0,1},{1,0},{2,3},{3,2},{4,5},{5,4},{6,7},{7,6},{8,9},{9,8},{10,11... | collective-permute-start | bytes 2359304 | tf_op jit(solution)/shard_map/ppermute | solution.py:53
  93.1 2.5 %copy-start.5 = (f32[64,384]{1,0:T(8,128)}, f32[64,384]{1,0:T(8,128)S(1)}, u32[]{:S(2)}) copy-start(f32[64,384]{1,0:T(8,128)S(1)} %multiply_reduce_fusion) | copy-start | bytes 294916
  95.7 3.1 %collective-permute-start.7 = (f32[32,512]{1,0:T(8,128)S(1)}, f32[32,512]{1,0:T(8,128)S(1)}, u32[]{:S(2)}, u32[]{:S(2)}) collective-permute-start(f32[32,512]{1,0:T(8,128)S(1)} %constant_dynamic-slice_fusion.1), channel_id=1, source_target_pairs={{0,1},{1,0},{2,3},{3,2},{4,5},{5,4},{6,7},{7,6},{8,9},{9,8},{10,11... | collective-permute-start | bytes 196616 | tf_op jit(solution)/shard_map/ppermute | solution.py:53
  100.2 28.3 %copy-start.9 = (f32[512]{0:T(512)S(1)}, f32[512]{0:T(512)}, u32[]{:S(2)}) copy-start(f32[512]{0:T(512)} %param.19) | copy-start | bytes 6148
  100.2 28.3 %copy-start.10 = (f32[512]{0:T(512)S(1)}, f32[512]{0:T(512)}, u32[]{:S(2)}) copy-start(f32[512]{0:T(512)} %param.17) | copy-start | bytes 6148
  100.2 28.3 %copy-start.11 = (f32[512]{0:T(512)S(1)}, f32[512]{0:T(512)}, u32[]{:S(2)}) copy-start(f32[512]{0:T(512)} %param.20) | copy-start | bytes 6148
  100.2 28.3 %copy-start.12 = (f32[512]{0:T(512)S(1)}, f32[512]{0:T(512)}, u32[]{:S(2)}) copy-start(f32[512]{0:T(512)} %param.18) | copy-start | bytes 6148
  100.3 15.3 %collective-permute-start.11 = (f32[128,512]{1,0:T(8,128)S(1)}, f32[128,512]{1,0:T(8,128)S(1)}, u32[]{:S(2)}, u32[]{:S(2)}) collective-permute-start(f32[128,512]{1,0:T(8,128)S(1)} %get-tuple-element.36), channel_id=1, source_target_pairs={{0,12},{4,0},{8,4},{12,8},{1,13},{5,1},{9,5},{13,9},{2,14},{6,2},{... | collective-permute-start | bytes 786440 | tf_op jit(solution)/shard_map/ppermute | solution.py:57
  104.6 11.0 %collective-permute-start.10 = (f32[128,512]{1,0:T(8,128)S(1)}, f32[128,512]{1,0:T(8,128)S(1)}, u32[]{:S(2)}, u32[]{:S(2)}) collective-permute-start(f32[128,512]{1,0:T(8,128)S(1)} %get-tuple-element.35), channel_id=1, source_target_pairs={{0,8},{4,12},{8,0},{12,4},{1,9},{5,13},{9,1},{13,5},{2,10},{6,14},... | collective-permute-start | bytes 786440 | tf_op jit(solution)/shard_map/ppermute | solution.py:57
  107.1 14.7 %collective-permute-start.9 = (f32[128,512]{1,0:T(8,128)S(1)}, f32[128,512]{1,0:T(8,128)S(1)}, u32[]{:S(2)}, u32[]{:S(2)}) collective-permute-start(f32[128,512]{1,0:T(8,128)S(1)} %get-tuple-element.34), channel_id=1, source_target_pairs={{0,4},{4,8},{8,12},{12,0},{1,5},{5,9},{9,13},{13,1},{2,6},{6,10},{... | collective-permute-start | bytes 786440 | tf_op jit(solution)/shard_map/ppermute | solution.py:57
  121.9 19.1 %collective-permute-start.12 = (f32[128,512]{1,0:T(8,128)S(1)}, f32[128,512]{1,0:T(8,128)S(1)}, u32[]{:S(2)}, u32[]{:S(2)}) collective-permute-start(f32[128,512]{1,0:T(8,128)S(1)} %fusion.12), channel_id=1, source_target_pairs={{0,2},{2,0},{1,3},{3,1},{4,6},{6,4},{5,7},{7,5},{8,10},{10,8},{9,1... | collective-permute-start | bytes 786440 | tf_op jit(solution)/shard_map/ppermute | solution.py:53
  141.1 10.1 %collective-permute-start.14 = (f32[128,512]{1,0:T(8,128)S(1)}, f32[128,512]{1,0:T(8,128)S(1)}, u32[]{:S(2)}, u32[]{:S(2)}) collective-permute-start(f32[128,512]{1,0:T(8,128)S(1)} %add.206), channel_id=1, source_target_pairs={{0,64},{16,0},{64,16},{1,65},{17,1},{65,17},{2,66},{18,2},{66,18},... | collective-permute-start | bytes 786440 | tf_op jit(solution)/shard_map/ppermute | solution.py:62
  146.1 11.8 %collective-permute-start.13 = (f32[128,512]{1,0:T(8,128)S(1)}, f32[128,512]{1,0:T(8,128)S(1)}, u32[]{:S(2)}, u32[]{:S(2)}) collective-permute-start(f32[128,512]{1,0:T(8,128)S(1)} %add.206), channel_id=1, source_target_pairs={{0,16},{16,64},{64,0},{1,17},{17,65},{65,1},{2,18},{18,66},{66,2},... | collective-permute-start | bytes 786440 | tf_op jit(solution)/shard_map/ppermute | solution.py:61
  148.2 13.6 %copy-start.6 = (f32[64,384]{1,0:T(8,128)S(1)}, f32[64,384]{1,0:T(8,128)}, u32[]{:S(2)}) copy-start(f32[64,384]{1,0:T(8,128)} %copy-done.5) | copy-start | bytes 294916
  165.2 24.9 %all-to-all-start.2 = ((f16[8,72,384]{2,1,0:T(8,128)(2,1)}), f16[8,72,384]{2,1,0:T(8,128)(2,1)S(1)}, u32[]{:S(2)}, u32[]{:S(2)}) async-start(f16[8,72,384]{2,1,0:T(8,128)(2,1)} %broadcast_in_dim.5), calls=%async_computation.2 | async-start | bytes 884736 | tf_op jit(solution)/shard_map/all_to_all | solution.py:18
  170.3 7.7 %collective-permute-start.17 = (f32[96,512]{1,0:T(8,128)S(1)}, f32[96,512]{1,0:T(8,128)S(1)}, u32[]{:S(2)}, u32[]{:S(2)}) collective-permute-start(f32[96,512]{1,0:T(8,128)S(1)} %get-tuple-element.33), channel_id=1, source_target_pairs={{0,12},{4,0},{8,4},{12,8},{1,13},{5,1},{9,5},{13,9},{2,14},{6,2},{... | collective-permute-start | bytes 589832 | tf_op jit(solution)/shard_map/ppermute | solution.py:57
  172.2 9.2 %collective-permute-start.16 = (f32[96,512]{1,0:T(8,128)S(1)}, f32[96,512]{1,0:T(8,128)S(1)}, u32[]{:S(2)}, u32[]{:S(2)}) collective-permute-start(f32[96,512]{1,0:T(8,128)S(1)} %get-tuple-element.33), channel_id=1, source_target_pairs={{0,8},{4,12},{8,0},{12,4},{1,9},{5,13},{9,1},{13,5},{2,10},{6,14},... | collective-permute-start | bytes 589832 | tf_op jit(solution)/shard_map/ppermute | solution.py:57
  174.7 11.9 %collective-permute-start.15 = (f32[96,512]{1,0:T(8,128)S(1)}, f32[96,512]{1,0:T(8,128)S(1)}, u32[]{:S(2)}, u32[]{:S(2)}) collective-permute-start(f32[96,512]{1,0:T(8,128)S(1)} %get-tuple-element.33), channel_id=1, source_target_pairs={{0,4},{4,8},{8,12},{12,0},{1,5},{5,9},{9,13},{13,1},{2,6},{6,10},{... | collective-permute-start | bytes 589832 | tf_op jit(solution)/shard_map/ppermute | solution.py:57
  187.7 4.6 %collective-permute-start.18 = (f32[384,512]{1,0:T(8,128)}, f32[384,512]{1,0:T(8,128)}, u32[]{:S(2)}, u32[]{:S(2)}) collective-permute-start(f32[384,512]{1,0:T(8,128)} %pad_maximum_fusion.1), channel_id=1, source_target_pairs={{0,1},{1,0},{2,3},{3,2},{4,5},{5,4},{6,7},{7,6},{8,9},{9,8},{10,11... | collective-permute-start | bytes 2359304 | tf_op jit(solution)/shard_map/ppermute | solution.py:53
  199.3 12.2 %all-to-all-start.3 = ((f16[4,200,384]{2,1,0:T(8,128)(2,1)}), f16[4,200,384]{2,1,0:T(8,128)(2,1)S(1)}, u32[]{:S(2)}, u32[]{:S(2)}) async-start(f16[4,200,384]{2,1,0:T(8,128)(2,1)} %concatenate.70), calls=%async_computation.3 | async-start | bytes 1228800 | tf_op jit(solution)/shard_map/all_to_all | solution.py:18
  211.6 0.9 copy-start.4

commit v5 on v4

--- a/solution.py
+++ b/solution.py
@@ -35,9 +35,7 @@
     return dot(high) + dot(low)
 
 
-def pack(values):
-    top = jnp.max(jnp.abs(values))
-    power = jnp.clip(jnp.floor(jnp.log2(jnp.maximum(top, 1e-30))), -100.0, 120.0)
+def pack(values, power):
     scaled = (values * jnp.exp2(14.0 - power)).astype(jnp.float16)
     tail = jnp.broadcast_to(power.astype(jnp.float16), values.shape[:-2] + (8, values.shape[-1]))
     return jnp.concatenate([scaled, tail], axis=-2)
@@ -49,18 +47,20 @@
     return packed[..., :rows, :].astype(jnp.float32) * jnp.exp2(power - 14.0)
 
 
+def power_of(bound):
+    return jnp.clip(jnp.floor(jnp.log2(jnp.maximum(bound, 1e-30))) + 1.0, -100.0, 120.0)
+
+
+def top(values):
+    return jnp.max(jnp.abs(values)).astype(jnp.float32)
+
+
 def swap(values, axis):
     return lax.ppermute(values, axis, [(0, 1), (1, 0)])
 
 
 def around(values, axis, size, step):
     return lax.ppermute(values, axis, [(i, (i + step) % size) for i in range(size)])
-
-
-def quad_sum(values, quad):
-    first = lax.ppermute(values, QUAD, [(0, 1), (1, 2), (2, 0)])
-    second = lax.ppermute(values, QUAD, [(0, 2), (1, 0), (2, 1)])
-    return values + first + second
 
 
 def ring_gather(values, place):
@@ -100,10 +100,8 @@
     left_shift = shifted(jnp.where(is_output, output_left_eigen, joined_left_eigen), damp)
     right_shift = shifted(jnp.where(is_output, output_right_eigen, joined_right_eigen), damp)
     left_shift = left_shift.reshape(8, 2, 32).transpose(1, 0, 2).reshape(512)
-    right_shift = right_shift.reshape(4, 2, 2, 2, 16).transpose(0, 2, 1, 3, 4).reshape(4, 2, 64)[::-1]
-    right_shift = jnp.where(lax.axis_index("zp") == 1, right_shift[:, ::-1], right_shift)
-    right_shift = jnp.concatenate([right_shift, right_shift], axis=0)
-    right_shift = lax.dynamic_slice_in_dim(right_shift, 3 - lax.axis_index("yp"), 4, 0).reshape(512)
+    right_shift = right_shift.reshape(4, 2, 2, 2, 16).transpose(0, 1, 3, 2, 4).reshape(4, 4, 2, 16)
+    right_shift = jnp.where(lax.axis_index("zp") == 1, right_shift[:, :, ::-1], right_shift).reshape(512)
     own_shift = lax.dynamic_slice_in_dim(left_shift, octant * 64, 64, 0)
 
     left_j, left_o = joined_left_basis.T, output_left_basis.T
@@ -113,10 +111,12 @@
     left = jnp.concatenate([left[0], left[1], left[2], left[3]], axis=1)
     left = lax.all_gather(left, "c", axis=0, tiled=True)
 
-    right_j, right_o = joined_right_basis.T, output_right_basis.T
+    right = jnp.concatenate([joined_right_basis.T, output_right_basis.T], axis=1)
+    right = jnp.concatenate([right, swap(right, "zp")], axis=0)
     gradients = (joined_gradient[:, :384], joined_gradient[:, 384:768], joined_gradient[:, 768:], output_gradient)
-    rights = (right_j[:, :384], right_j[:, 384:768], right_j[:, 768:], right_o)
-    sent = jnp.stack([jnp.concatenate(pair, axis=0) for pair in zip(gradients, rights)])
+    sent = jnp.stack(
+        [jnp.concatenate([block, right[:, 384 * j : 384 * j + 384]], axis=0) for j, block in enumerate(gradients)]
+    )
     got = [lax.dynamic_index_in_dim(sent, quad, 0, False)]
     for mask in (1, 2, 3):
         block = lax.dynamic_index_in_dim(sent, quad ^ mask, 0, False)
@@ -124,40 +124,48 @@
     got = jnp.stack(got)
     got = jnp.stack([lax.dynamic_index_in_dim(got, quad ^ j, 0, False) for j in range(4)])
     gradient = got[:, :192].reshape(768, 384)
-    right = got[:, 192:].reshape(64, 384)
-    right = jnp.concatenate([right, swap(right, "zp")], axis=0)
+    right = got[:, 192:].reshape(128, 384)
+    right = exchange(jnp.broadcast_to(right[None], (4, 128, 384)), "yp").reshape(512, 384)
+    most = top(gradient)
 
     rows = jnp.dot(left, gradient, preferred_element_type=jnp.float32)
-    rows = pack(rows.reshape(8, 64, 384))
-    right = right + (rows[0, 0, :1] * 0).astype(jnp.bfloat16)
+    rows = pack(rows.reshape(8, 64, 384), power_of(most * 60.0))
     rows = jnp.sum(unpack(exchange(rows, OCT)), axis=0)
-    right = jnp.concatenate([right] + [around(right, "yp", 4, step) for step in (1, 2, 3)], axis=0)
 
     cols = lax.dot_general(gradient, right, (((1,), (1,)), ((), ())), preferred_element_type=jnp.float32)
     cols = core_part(cols, core, True) + swap(core_part(cols, core, False), "c")
     cols = cols.reshape(4, 96, 512)
 
     mid = dot_wide_left(rows, right, ((1,), (1,)))
-    mid = core_part(mid, core, True) + swap(core_part(mid, core, False), "c")
-    both = jnp.concatenate([mid, lax.dynamic_index_in_dim(cols, place, 0, False)], axis=0)
-    for step in (1, 2, 3):
-        block = lax.dynamic_index_in_dim(cols, (place + step) % 4, 0, False)
-        both = both + around(jnp.concatenate([mid, block], axis=0), "x", 4, step)
-    both = both + swap(both, "zh")
-    both = quad_sum(both, quad)
-    mid = lax.all_gather(both[:32], "c", axis=0, tiled=True)
-    cols = both[32:]
+    other = jnp.concatenate([core_part(mid, core, False), jnp.broadcast_to(most, (8, 512))], axis=0)
+    other = swap(other, "c")
+    mid = (core_part(mid, core, True) + other[:32]) / 512.0
+    power = power_of(jnp.maximum(most, other[32, 0]) * 864.0)
+    both = jnp.concatenate([jnp.broadcast_to(mid[None], (4, 32, 512)), cols], axis=1)
+    both = exchange(pack(both, power), "x")
+    power = jnp.max(both[:, 128, 0]).astype(jnp.float32)
+    both = jnp.sum(unpack(both), axis=0)
+    got = swap(pack(both, power), "zh")
+    power = jnp.maximum(power, got[128, 0].astype(jnp.float32))
+    both = both + unpack(got)
+    both = exchange(jnp.broadcast_to(pack(both, power)[None], (4, 136, 512)), QUAD)
+    power = jnp.max(both[:, 128, 0]).astype(jnp.float32)
+    same = (lax.broadcasted_iota(jnp.int32, (4, 1, 1), 0) == 3) == is_output
+    both = jnp.sum(jnp.where(same, unpack(both), 0.0), axis=0)
+    mid = lax.all_gather(both[:32], "c", axis=0, tiled=True) * 512.0
+    cols = (both[32:] * jnp.exp2(14.0 - power)).astype(jnp.float16)
     mixed = rows / damp + dot_wide_left(mid * right_shift[None, :], right, ((1,), (0,)))
     mixed = mixed * own_shift[:, None]
-    packed = pack(mixed)
+    packed = pack(mixed, power_of(top(mixed)))
     mixed = unpack(exchange(jnp.broadcast_to(packed[None], (8, 72, 384)), OCT)).reshape(512, 384)
 
     cols = ring_gather(cols, place)
     cols = joined_pair(cols, swap(cols, "c"), core)
 
+    cols = cols.astype(jnp.float32) * jnp.exp2(power - 14.0)
     part = dot_wide_left(cols * (right_shift / damp)[None, :], right, ((1,), (0,)))
     update = part + dot_wide_right(left, mixed, ((0,), (0,)))
-    update = unpack(exchange(pack(update.reshape(4, 192, 384)), QUAD))
+    update = unpack(exchange(pack(update.reshape(4, 192, 384), power_of(top(update))), QUAD))
     joined_update = jnp.concatenate([update[0], update[1], update[2]], axis=1) + joined_gradient.astype(jnp.float32) / damp / damp
     output_update = update[3] + output_gradient.astype(jnp.float32) / damp / damp
     return joined_update, output_update

time: 216 us -> 205 us (0.949)
  waiting for transfers between devices: 77.9 us -> 50.9 us
  blocking collectives: 7.21 us -> 25.7 us
  matrix products: 13.3 us -> 5.65 us
  local copies, waits for them, and re-layouts: 8.49 us -> 12.1 us
  starting transfers between devices: 93.5 us -> 90.2 us
  between operations: 5.16 us -> 7.96 us
    all_to_all x4 -> x6, waiting for transfers between devices: 8.7 us -> 41.5 us  [exchange(): return lax.all_to_all(blocks, axes, 0, 0, tiled=True)]
    ppermute x9 -> x3, waiting for transfers between devices: 25.1 us -> 0.01 us  [around(): lax.ppermute(values, axis, [(i, (i + step) % size) for i in range(size)])]
    ppermute x9 -> x3, starting transfers between devices: 30 us -> 7.81 us  [around(): lax.ppermute(values, axis, [(i, (i + step) % size) for i in range(size)])]
    all_to_all x4 -> x6, starting transfers between devices: 29.6 us -> 47.2 us  [exchange(): return lax.all_to_all(blocks, axes, 0, 0, tiled=True)]
    ppermute x5, waiting for transfers between devices: 23.6 us -> 9.36 us  [swap(): return lax.ppermute(values, axis, [(0, 1), (1, 0)])]
    all_to_all x0 -> x1, blocking collectives: none -> 13 us  [exchange(): return lax.all_to_all(blocks, axes, 0, 0, tiled=True)]
    ppermute x3, waiting for transfers between devices: 10.9 us -> 0.01 us  [local(): got.append(lax.ppermute(block, QUAD, [(i, i ^ mask) for i in range(4)]))]
    ppermute x2 -> x0, waiting for transfers between devices: 9.71 us -> none  [the longest x1 6.72 us: quad_sum(): first = lax.ppermute(values, QUAD, [(0, 1), (1, 2), (2, 0)])]
  transfers between devices with their start and end apart: 23 -> 17, of which waited for: 17 -> 8; matrix products, arithmetic and copies ran while one was open for 5% -> 7% of each run, Pallas kernels for 0% -> 0%
where the time goes in v5:
time: 205 us; the launch traced here: 203 us
  starting transfers between devices  90.2 us (44%)
  waiting for transfers between devices  50.9 us (25%)
  blocking collectives  25.7 us (13%)
  local copies, waits for them, and re-layouts  12.1 us (6%)
  other arithmetic  10.7 us (5%)
  between operations  7.96 us (4%)
  matrix products  5.65 us (3%)
    all_to_all x6, starting transfers between devices, exchange(): return lax.all_to_all(blocks, axes, 0, 0, tiled=True)  47.2 us
    all_to_all x6, waiting for transfers between devices, exchange(): return lax.all_to_all(blocks, axes, 0, 0, tiled=True)  41.5 us
    ppermute x5, starting transfers between devices, swap(): return lax.ppermute(values, axis, [(0, 1), (1, 0)])  26.1 us
    all_to_all x1, blocking collectives, exchange(): return lax.all_to_all(blocks, axes, 0, 0, tiled=True)  13 us
    ppermute x5, waiting for transfers between devices, swap(): return lax.ppermute(values, axis, [(0, 1), (1, 0)])  9.36 us
    ppermute x3, starting transfers between devices, local(): got.append(lax.ppermute(block, QUAD, [(i, i ^ mask) for i in range(4)]))  9.13 us
    ppermute x3, starting transfers between devices, around(): lax.ppermute(values, axis, [(i, (i + step) % size) for i in range(size)])  7.81 us
    all_gather x1, blocking collectives, local(): left = lax.all_gather(left, 'c', axis=0, tiled=True)  7.57 us
  transfers between devices with their start and end apart: 17, of which 8 were waited for; matrix products, arithmetic and copies ran while one was open for 7% of the time, Pallas kernels for 0%

profile of v5, /device:TPU:1, one launch (start us, length us, event | category | flops | bytes accessed | tf_op | source)
XLA Modules:
  0.0 203.3 jit_solution(8981974156733480570)
XLA Ops:
  0.6 0.8 pad_maximum_fusion.12
  1.5 6.6 %collective-permute-start = (bf16[16,1536]{1,0:T(8,128)(2,1)S(1)}, bf16[16,1536]{1,0:T(8,128)(2,1)S(1)}, u32[]{:S(2)}, u32[]{:S(2)}) collective-permute-start(bf16[16,1536]{1,0:T(8,128)(2,1)S(1)} %pad_maximum_fusion.12), channel_id=1, source_target_pairs={{0,32},{32,0},{1,33},{33,1},{2,34},{34,2},{3,35},{35,3},{4,36},{36... | collective-permute-start | bytes 147464 | tf_op jit(solution)/shard_map/ppermute | solution.py:59
  8.1 1.1 fusion.39
  9.2 0.3 collective-permute-done
  9.6 0.8 pad_maximum_fusion.10
  10.7 5.0 %collective-permute-start.3 = (bf16[224,384]{1,0:T(8,128)(2,1)S(1)}, bf16[224,384]{1,0:T(8,128)(2,1)S(1)}, u32[]{:S(2)}, u32[]{:S(2)}) collective-permute-start(bf16[224,384]{1,0:T(8,128)(2,1)S(1)} %get-tuple-element.16), channel_id=1, source_target_pairs={{0,80},{16,64},{64,16},{80,0},{1,81},{17,65},{65,17},{81,1},{2,82}... | collective-permute-start | bytes 516104 | tf_op jit(solution)/shard_map/ppermute | solution.py:123
  15.7 2.1 %collective-permute-start.2 = (bf16[224,384]{1,0:T(8,128)(2,1)S(1)}, bf16[224,384]{1,0:T(8,128)(2,1)S(1)}, u32[]{:S(2)}, u32[]{:S(2)}) collective-permute-start(bf16[224,384]{1,0:T(8,128)(2,1)S(1)} %get-tuple-element.17), channel_id=1, source_target_pairs={{0,64},{16,80},{64,0},{80,16},{1,65},{17,81},{65,1},{81,17},{2,66}... | collective-permute-start | bytes 516104 | tf_op jit(solution)/shard_map/ppermute | solution.py:123
  17.8 2.0 %collective-permute-start.1 = (bf16[224,384]{1,0:T(8,128)(2,1)S(1)}, bf16[224,384]{1,0:T(8,128)(2,1)S(1)}, u32[]{:S(2)}, u32[]{:S(2)}) collective-permute-start(bf16[224,384]{1,0:T(8,128)(2,1)S(1)} %get-tuple-element.18), channel_id=1, source_target_pairs={{0,16},{16,0},{64,80},{80,64},{1,17},{17,1},{65,81},{81,65},{2,18}... | collective-permute-start | bytes 516104 | tf_op jit(solution)/shard_map/ppermute | solution.py:123
  19.9 0.9 broadcast_in_dim.21
  20.8 11.6 %all-to-all-start = ((bf16[32,32,192]{2,1,0:T(8,128)(2,1)}), bf16[32,32,192]{2,1,0:T(8,128)(2,1)S(1)}, u32[]{:S(2)}, u32[]{:S(2)}) async-start(bf16[32,32,192]{2,1,0:T(8,128)(2,1)} %bitcast.4), calls=%async_computation | async-start | bytes 1048576 | tf_op jit(solution)/shard_map/all_to_all | solution.py:18
  32.7 0.8 abs_reduce_fusion.1
  34.3 10.1 %all-to-all-done = bf16[32,32,192]{2,1,0:T(8,128)(2,1)S(1)} async-done(((bf16[32,32,192]{2,1,0:T(8,128)(2,1)}), bf16[32,32,192]{2,1,0:T(8,128)(2,1)S(1)}, u32[]{:S(2)}, u32[]{:S(2)}) %all-to-all-start) | async-done | bytes 393248 | tf_op jit(solution)/shard_map/all_to_all | solution.py:18
  44.4 0.8 broadcast_in_dim.23
  45.2 5.9 %all-to-all-start.2 = ((bf16[4,128,384]{2,1,0:T(8,128)(2,1)}), bf16[4,128,384]{2,1,0:T(8,128)(2,1)S(1)}, u32[]{:S(2)}, u32[]{:S(2)}) async-start(bf16[4,128,384]{2,1,0:T(8,128)(2,1)} %broadcast_in_dim.23), calls=%async_computation.2 | async-start | bytes 786432 | tf_op jit(solution)/shard_map/all_to_all | solution.py:18
  51.1 0.2 pad_maximum_fusion.6
  51.3 7.6 %all_gather.6 = bf16[512,768]{1,0:T(8,128)(2,1)S(1)} all-gather(bf16[256,768]{1,0:T(8,128)(2,1)S(1)} %pad_maximum_fusion.6), channel_id=1, replica_groups=mesh['yp'=4,'yb'=2,'zp'=2,'zb'=2,'x'=4,'zh'=2,'c'=2] {'c'}, dimensions={0}, use_global_device_ids=true | all-gather | bytes 1179648 | tf_op jit(solution)/shard_map/all_gather | solution.py:112
  58.9 0.6 fusion.2
  59.4 0.8 concatenate.61
  60.3 0.5 all-to-all-done.2
  60.8 13.1 %all-to-all-start.1 = ((f16[8,72,384]{2,1,0:T(8,128)(2,1)}), f16[8,72,384]{2,1,0:T(8,128)(2,1)}, u32[]{:S(2)}, u32[]{:S(2)}) async-start(f16[8,72,384]{2,1,0:T(8,128)(2,1)} %concatenate.61), calls=%async_computation.1 | async-start | bytes 884736 | tf_op jit(solution)/shard_map/all_to_all | solution.py:18
  73.9 0.6 fusion.41
  74.6 4.0 %collective-permute-start.5 = (f32[384,512]{1,0:T(8,128)S(1)}, f32[384,512]{1,0:T(8,128)}, u32[]{:S(2)}, u32[]{:S(2)}) collective-permute-start(f32[384,512]{1,0:T(8,128)S(1)} %constant_dynamic-slice_fusion), channel_id=1, source_target_pairs={{0,1},{1,0},{2,3},{3,2},{4,5},{5,4},{6,7},{7,6},{8,9},{9,8},{10,11... | collective-permute-start | bytes 2359304 | tf_op jit(solution)/shard_map/ppermute | solution.py:59
  78.6 6.5 %all-to-all-done.1 = f16[8,72,384]{2,1,0:T(8,128)(2,1)} async-done(((f16[8,72,384]{2,1,0:T(8,128)(2,1)}), f16[8,72,384]{2,1,0:T(8,128)(2,1)}, u32[]{:S(2)}, u32[]{:S(2)}) %all-to-all-start.1) | async-done | bytes 442400 | tf_op jit(solution)/shard_map/all_to_all | solution.py:18
  85.1 0.8 slice.158
  85.9 1.1 multiply_reduce_fusion.1
  87.0 0.2 fusion.23
  87.3 0.2 convolution_add_fusion.2
  87.6 0.6 concatenate.62
  88.2 5.9 %collective-permute-start.4 = (f32[40,512]{1,0:T(8,128)S(1)}, f32[40,512]{1,0:T(8,128)}, u32[]{:S(2)}, u32[]{:S(2)}) collective-permute-start(f32[40,512]{1,0:T(8,128)S(1)} %concatenate.62), channel_id=1, source_target_pairs={{0,1},{1,0},{2,3},{3,2},{4,5},{5,4},{6,7},{7,6},{8,9},{9,8},{10,11... | collective-permute-start | bytes 245768 | tf_op jit(solution)/shard_map/ppermute | solution.py:59
  94.1 1.3 dynamic-slice_add_fusion
  95.4 1.2 slice.160
  98.0 0.9 fusion.19
  99.2 13.0 %all_to_all.35 = f16[4,136,512]{2,1,0:T(8,128)(2,1)S(1)} all-to-all(f16[4,136,512]{2,1,0:T(8,128)(2,1)S(1)} %concatenate.64), channel_id=1, replica_groups=mesh['yp'=4,'yb'=2,'zp'=2,'zb'=2,'x'=4,'zh'=2,'c'=2] {'x'}, dimensions={0} | all-to-all | bytes 1114112 | tf_op jit(solution)/shard_map/all_to_all | solution.py:18
  112.2 0.6 slice_reduce_fusion.1
  113.7 0.7 concatenate.65
  114.4 3.7 %collective-permute-start.6 = (f16[136,512]{1,0:T(8,128)(2,1)S(1)}, f16[136,512]{1,0:T(8,128)(2,1)S(1)}, u32[]{:S(2)}, u32[]{:S(2)}) collective-permute-start(f16[136,512]{1,0:T(8,128)(2,1)S(1)} %concatenate.65), channel_id=1, source_target_pairs={{0,2},{2,0},{1,3},{3,1},{4,6},{6,4},{5,7},{7,5},{8,10},{10,8},{9,1... | collective-permute-start | bytes 417800 | tf_op jit(solution)/shard_map/ppermute | solution.py:59
  118.1 9.0 %collective-permute-done.6 = f16[136,512]{1,0:T(8,128)(2,1)S(1)} collective-permute-done((f16[136,512]{1,0:T(8,128)(2,1)S(1)}, f16[136,512]{1,0:T(8,128)(2,1)S(1)}, u32[]{:S(2)}, u32[]{:S(2)}) %collective-permute-start.6) | collective-permute-done | bytes 139296 | tf_op jit(solution)/shard_map/ppermute | solution.py:59
  127.1 0.5 slice.166
  128.5 0.8 broadcast_in_dim.29
  129.4 3.5 %all-to-all-start.4 = ((f16[4,136,512]{2,1,0:T(8,128)(2,1)}), f16[4,136,512]{2,1,0:T(8,128)(2,1)S(1)}, u32[]{:S(2)}, u32[]{:S(2)}) async-start(f16[4,136,512]{2,1,0:T(8,128)(2,1)} %broadcast_in_dim.29), calls=%async_computation.4 | async-start | bytes 1114112 | tf_op jit(solution)/shard_map/all_to_all | solution.py:18
  134.3 4.9 %all-to-all-done.4 = f16[4,136,512]{2,1,0:T(8,128)(2,1)S(1)} async-done(((f16[4,136,512]{2,1,0:T(8,128)(2,1)}), f16[4,136,512]{2,1,0:T(8,128)(2,1)S(1)}, u32[]{:S(2)}, u32[]{:S(2)}) %all-to-all-start.4) | async-done | bytes 557088 | tf_op jit(solution)/shard_map/all_to_all | solution.py:18
  139.1 0.6 slice_reduce_fusion
  140.5 0.2 select_reduce_fusion
  140.7 2.8 %collective-permute-start.9 = (f16[96,512]{1,0:T(8,128)(2,1)S(1)}, f16[96,512]{1,0:T(8,128)(2,1)S(1)}, u32[]{:S(2)}, u32[]{:S(2)}) collective-permute-start(f16[96,512]{1,0:T(8,128)(2,1)S(1)} %fusion.14), channel_id=1, source_target_pairs={{0,12},{4,0},{8,4},{12,8},{1,13},{5,1},{9,5},{13,9},{2,14},{6,2},{... | collective-permute-start | bytes 294920 | tf_op jit(solution)/shard_map/ppermute | solution.py:63
  143.5 3.1 %collective-permute-start.8 = (f16[96,512]{1,0:T(8,128)(2,1)S(1)}, f16[96,512]{1,0:T(8,128)(2,1)S(1)}, u32[]{:S(2)}, u32[]{:S(2)}) collective-permute-start(f16[96,512]{1,0:T(8,128)(2,1)S(1)} %fusion.14), channel_id=1, source_target_pairs={{0,8},{4,12},{8,0},{12,4},{1,9},{5,13},{9,1},{13,5},{2,10},{6,14},... | collective-permute-start | bytes 294920 | tf_op jit(solution)/shard_map/ppermute | solution.py:63
  146.6 1.9 collective-permute-start.7
  148.5 5.1 %all_gather.7 = f32[64,512]{1,0:T(8,128)S(1)} all-gather(f32[32,512]{1,0:T(8,128)S(1)} %slice.171), channel_id=1, replica_groups=mesh['yp'=4,'yb'=2,'zp'=2,'zb'=2,'x'=4,'zh'=2,'c'=2] {'c'}, dimensions={0}, use_global_device_ids=true | all-gather | bytes 196608 | tf_op jit(solution)/shard_map/all_gather | solution.py:155
  153.7 0.2 fusion.18
  154.3 5.9 %collective-permute-start.10 = (f16[384,512]{1,0:T(8,128)(2,1)S(1)}, f16[384,512]{1,0:T(8,128)(2,1)S(1)}, u32[]{:S(2)}, u32[]{:S(2)}) collective-permute-start(f16[384,512]{1,0:T(8,128)(2,1)S(1)} %pad_maximum_fusion.8), channel_id=1, source_target_pairs={{0,1},{1,0},{2,3},{3,2},{4,5},{5,4},{6,7},{7,6},{8,9},{9,8},{10,11... | collective-permute-start | bytes 1179656 | tf_op jit(solution)/shard_map/ppermute | solution.py:59
  160.2 0.8 abs_reduce_fusion.2
  161.8 0.8 broadcast_in_dim.31
  162.6 5.9 %all-to-all-start.5 = ((f16[8,72,384]{2,1,0:T(8,128)(2,1)}), f16[8,72,384]{2,1,0:T(8,128)(2,1)S(1)}, u32[]{:S(2)}, u32[]{:S(2)}) async-start(f16[8,72,384]{2,1,0:T(8,128)(2,1)} %broadcast_in_dim.31), calls=%async_computation.5 | async-start | bytes 884736 | tf_op jit(solution)/shard_map/all_to_all | solution.py:18
  168.5 0.2 broadcast_select_fusion.1
  168.8 0.6 fusion.7
  169.3 0.6 convolution_add_fusion.1
  169.9 9.9 %all-to-all-done.5 = f16[8,72,384]{2,1,0:T(8,128)(2,1)S(1)} async-done(((f16[8,72,384]{2,1,0:T(8,128)(2,1)}), f16[8,72,384]{2,1,0:T(8,128)(2,1)S(1)}, u32[]{:S(2)}, u32[]{:S(2)}) %all-to-all-start.5) | async-done | bytes 442400 | tf_op jit(solution)/shard_map/all_to_all | solution.py:18
  180.1 0.6 fusion.42
  180.7 1.2 abs_reduce_fusion
  182.8 0.9 concatenate.70
  183.7 7.2 %all-to-all-start.6 = ((f16[4,200,384]{2,1,0:T(8,128)(2,1)}), f16[4,200,384]{2,1,0:T(8,128)(2,1)S(1)}, u32[]{:S(2)}, u32[]{:S(2)}) async-start(f16[4,200,384]{2,1,0:T(8,128)(2,1)} %concatenate.70), calls=%async_computation.6 | async-start | bytes 1228800 | tf_op jit(solution)/shard_map/all_to_all | solution.py:18
  190.9 9.6 %all-to-all-done.6 = f16[4,200,384]{2,1,0:T(8,128)(2,1)S(1)} async-done(((f16[4,200,384]{2,1,0:T(8,128)(2,1)}), f16[4,200,384]{2,1,0:T(8,128)(2,1)S(1)}, u32[]{:S(2)}, u32[]{:S(2)}) %all-to-all-start.6) | async-done | bytes 614432 | tf_op jit(solution)/shard_map/all_to_all | solution.py:18
  200.7 0.8 copy-done.4
  201.6 0.7 fusion.13
  202.3 1.0 maximum_add_fusion
  (87 shorter events, 2.8 us)
Async XLA Ops:
  0.6 9.8 %copy-start.3 = (bf16[192,384]{1,0:T(8,128)(2,1)S(1)}, bf16[192,384]{1,0:T(8,128)(2,1)}, u32[]{:S(2)}) copy-start(bf16[192,384]{1,0:T(8,128)(2,1)} %param.12) | copy-start | bytes 442372
  1.5 8.1 %collective-permute-start = (bf16[16,1536]{1,0:T(8,128)(2,1)S(1)}, bf16[16,1536]{1,0:T(8,128)(2,1)S(1)}, u32[]{:S(2)}, u32[]{:S(2)}) collective-permute-start(bf16[16,1536]{1,0:T(8,128)(2,1)S(1)} %pad_maximum_fusion.12), channel_id=1, source_target_pairs={{0,32},{32,0},{1,33},{33,1},{2,34},{34,2},{3,35},{35,3},{4,36},{36... | collective-permute-start | bytes 147464 | tf_op jit(solution)/shard_map/ppermute | solution.py:59
  10.5 9.4 %copy-start.6 = (bf16[192,32]{0,1:T(8,128)(2,1)S(1)}, bf16[192,32]{0,1:T(8,128)(2,1)}, u32[]{:S(2)}) copy-start(bf16[192,32]{0,1:T(8,128)(2,1)} %param.15) | copy-start | bytes 36868
  10.5 9.4 %copy-start.7 = (bf16[192,32]{0,1:T(8,128)(2,1)S(1)}, bf16[192,32]{0,1:T(8,128)(2,1)}, u32[]{:S(2)}) copy-start(bf16[192,32]{0,1:T(8,128)(2,1)} %param.13) | copy-start | bytes 36868
  10.7 21.7 %collective-permute-start.3 = (bf16[224,384]{1,0:T(8,128)(2,1)S(1)}, bf16[224,384]{1,0:T(8,128)(2,1)S(1)}, u32[]{:S(2)}, u32[]{:S(2)}) collective-permute-start(bf16[224,384]{1,0:T(8,128)(2,1)S(1)} %get-tuple-element.16), channel_id=1, source_target_pairs={{0,80},{16,64},{64,16},{80,0},{1,81},{17,65},{65,17},{81,1},{2,82}... | collective-permute-start | bytes 516104 | tf_op jit(solution)/shard_map/ppermute | solution.py:123
  15.7 16.7 %collective-permute-start.2 = (bf16[224,384]{1,0:T(8,128)(2,1)S(1)}, bf16[224,384]{1,0:T(8,128)(2,1)S(1)}, u32[]{:S(2)}, u32[]{:S(2)}) collective-permute-start(bf16[224,384]{1,0:T(8,128)(2,1)S(1)} %get-tuple-element.17), channel_id=1, source_target_pairs={{0,64},{16,80},{64,0},{80,16},{1,65},{17,81},{65,1},{81,17},{2,66}... | collective-permute-start | bytes 516104 | tf_op jit(solution)/shard_map/ppermute | solution.py:123
  17.8 14.6 %collective-permute-start.1 = (bf16[224,384]{1,0:T(8,128)(2,1)S(1)}, bf16[224,384]{1,0:T(8,128)(2,1)S(1)}, u32[]{:S(2)}, u32[]{:S(2)}) collective-permute-start(bf16[224,384]{1,0:T(8,128)(2,1)S(1)} %get-tuple-element.18), channel_id=1, source_target_pairs={{0,16},{16,0},{64,80},{80,64},{1,17},{17,1},{65,81},{81,65},{2,18}... | collective-permute-start | bytes 516104 | tf_op jit(solution)/shard_map/ppermute | solution.py:123
  20.8 23.6 %all-to-all-start = ((bf16[32,32,192]{2,1,0:T(8,128)(2,1)}), bf16[32,32,192]{2,1,0:T(8,128)(2,1)S(1)}, u32[]{:S(2)}, u32[]{:S(2)}) async-start(bf16[32,32,192]{2,1,0:T(8,128)(2,1)} %bitcast.4), calls=%async_computation | async-start | bytes 1048576 | tf_op jit(solution)/shard_map/all_to_all | solution.py:18
  45.2 15.6 %all-to-all-start.2 = ((bf16[4,128,384]{2,1,0:T(8,128)(2,1)}), bf16[4,128,384]{2,1,0:T(8,128)(2,1)S(1)}, u32[]{:S(2)}, u32[]{:S(2)}) async-start(bf16[4,128,384]{2,1,0:T(8,128)(2,1)} %broadcast_in_dim.23), calls=%async_computation.2 | async-start | bytes 786432 | tf_op jit(solution)/shard_map/all_to_all | solution.py:18
  60.8 24.3 %all-to-all-start.1 = ((f16[8,72,384]{2,1,0:T(8,128)(2,1)}), f16[8,72,384]{2,1,0:T(8,128)(2,1)}, u32[]{:S(2)}, u32[]{:S(2)}) async-start(f16[8,72,384]{2,1,0:T(8,128)(2,1)} %concatenate.61), calls=%async_computation.1 | async-start | bytes 884736 | tf_op jit(solution)/shard_map/all_to_all | solution.py:18
  74.6 19.5 %collective-permute-start.5 = (f32[384,512]{1,0:T(8,128)S(1)}, f32[384,512]{1,0:T(8,128)}, u32[]{:S(2)}, u32[]{:S(2)}) collective-permute-start(f32[384,512]{1,0:T(8,128)S(1)} %constant_dynamic-slice_fusion), channel_id=1, source_target_pairs={{0,1},{1,0},{2,3},{3,2},{4,5},{5,4},{6,7},{7,6},{8,9},{9,8},{10,11... | collective-permute-start | bytes 2359304 | tf_op jit(solution)/shard_map/ppermute | solution.py:59
  87.0 7.1 %copy-start.1 = (f32[64,384]{1,0:T(8,128)}, f32[64,384]{1,0:T(8,128)S(1)}, u32[]{:S(2)}) copy-start(f32[64,384]{1,0:T(8,128)S(1)} %multiply_reduce_fusion.1) | copy-start | bytes 294916
  87.5 6.6 %copy-start.5 = (f32[64,512]{1,0:T(8,128)}, f32[64,512]{1,0:T(8,128)S(1)}, u32[]{:S(2)}) copy-start(f32[64,512]{1,0:T(8,128)S(1)} %convolution_add_fusion.2) | copy-start | bytes 393220
  88.2 7.2 %collective-permute-start.4 = (f32[40,512]{1,0:T(8,128)S(1)}, f32[40,512]{1,0:T(8,128)}, u32[]{:S(2)}, u32[]{:S(2)}) collective-permute-start(f32[40,512]{1,0:T(8,128)S(1)} %concatenate.62), channel_id=1, source_target_pairs={{0,1},{1,0},{2,3},{3,2},{4,5},{5,4},{6,7},{7,6},{8,9},{9,8},{10,11... | collective-permute-start | bytes 245768 | tf_op jit(solution)/shard_map/ppermute | solution.py:59
  114.4 12.8 %collective-permute-start.6 = (f16[136,512]{1,0:T(8,128)(2,1)S(1)}, f16[136,512]{1,0:T(8,128)(2,1)S(1)}, u32[]{:S(2)}, u32[]{:S(2)}) collective-permute-start(f16[136,512]{1,0:T(8,128)(2,1)S(1)} %concatenate.65), channel_id=1, source_target_pairs={{0,2},{2,0},{1,3},{3,1},{4,6},{6,4},{5,7},{7,5},{8,10},{10,8},{9,1... | collective-permute-start | bytes 417800 | tf_op jit(solution)/shard_map/ppermute | solution.py:59
  128.4 5.2 %copy-start.8 = (f32[512]{0:T(512)S(1)}, f32[512]{0:T(512)}, u32[]{:S(2)}) copy-start(f32[512]{0:T(512)} %param.19) | copy-start | bytes 6148
  128.4 5.2 %copy-start.9 = (f32[512]{0:T(512)S(1)}, f32[512]{0:T(512)}, u32[]{:S(2)}) copy-start(f32[512]{0:T(512)} %param.17) | copy-start | bytes 6148
  128.5 5.2 %copy-start.10 = (f32[512]{0:T(512)S(1)}, f32[512]{0:T(512)}, u32[]{:S(2)}) copy-start(f32[512]{0:T(512)} %param.20) | copy-start | bytes 6148
  128.5 5.2 %copy-start.11 = (f32[512]{0:T(512)S(1)}, f32[512]{0:T(512)}, u32[]{:S(2)}) copy-start(f32[512]{0:T(512)} %param.18) | copy-start | bytes 6148
  129.4 9.8 %all-to-all-start.4 = ((f16[4,136,512]{2,1,0:T(8,128)(2,1)}), f16[4,136,512]{2,1,0:T(8,128)(2,1)S(1)}, u32[]{:S(2)}, u32[]{:S(2)}) async-start(f16[4,136,512]{2,1,0:T(8,128)(2,1)} %broadcast_in_dim.29), calls=%async_computation.4 | async-start | bytes 1114112 | tf_op jit(solution)/shard_map/all_to_all | solution.py:18
  140.7 13.2 %collective-permute-start.9 = (f16[96,512]{1,0:T(8,128)(2,1)S(1)}, f16[96,512]{1,0:T(8,128)(2,1)S(1)}, u32[]{:S(2)}, u32[]{:S(2)}) collective-permute-start(f16[96,512]{1,0:T(8,128)(2,1)S(1)} %fusion.14), channel_id=1, source_target_pairs={{0,12},{4,0},{8,4},{12,8},{1,13},{5,1},{9,5},{13,9},{2,14},{6,2},{... | collective-permute-start | bytes 294920 | tf_op jit(solution)/shard_map/ppermute | solution.py:63
  143.5 10.4 %collective-permute-start.8 = (f16[96,512]{1,0:T(8,128)(2,1)S(1)}, f16[96,512]{1,0:T(8,128)(2,1)S(1)}, u32[]{:S(2)}, u32[]{:S(2)}) collective-permute-start(f16[96,512]{1,0:T(8,128)(2,1)S(1)} %fusion.14), channel_id=1, source_target_pairs={{0,8},{4,12},{8,0},{12,4},{1,9},{5,13},{9,1},{13,5},{2,10},{6,14},... | collective-permute-start | bytes 294920 | tf_op jit(solution)/shard_map/ppermute | solution.py:63
  146.6 7.3 %collective-permute-start.7 = (f16[96,512]{1,0:T(8,128)(2,1)S(1)}, f16[96,512]{1,0:T(8,128)(2,1)S(1)}, u32[]{:S(2)}, u32[]{:S(2)}) collective-permute-start(f16[96,512]{1,0:T(8,128)(2,1)S(1)} %fusion.14), channel_id=1, source_target_pairs={{0,4},{4,8},{8,12},{12,0},{1,5},{5,9},{9,13},{13,1},{2,6},{6,10},{... | collective-permute-start | bytes 294920 | tf_op jit(solution)/shard_map/ppermute | solution.py:63
  153.9 6.2 %copy-start.2 = (f32[64,384]{1,0:T(8,128)S(1)}, f32[64,384]{1,0:T(8,128)}, u32[]{:S(2)}) copy-start(f32[64,384]{1,0:T(8,128)} %copy-done.1) | copy-start | bytes 294916
  154.3 14.2 %collective-permute-start.10 = (f16[384,512]{1,0:T(8,128)(2,1)S(1)}, f16[384,512]{1,0:T(8,128)(2,1)S(1)}, u32[]{:S(2)}, u32[]{:S(2)}) collective-permute-start(f16[384,512]{1,0:T(8,128)(2,1)S(1)} %pad_maximum_fusion.8), channel_id=1, source_target_pairs={{0,1},{1,0},{2,3},{3,2},{4,5},{5,4},{6,7},{7,6},{8,9},{9,8},{10,11... | collective-permute-start | bytes 1179656 | tf_op jit(solution)/shard_map/ppermute | solution.py:59
  162.6 17.2 %all-to-all-start.5 = ((f16[8,72,384]{2,1,0:T(8,128)(2,1)}), f16[8,72,384]{2,1,0:T(8,128)(2,1)S(1)}, u32[]{:S(2)}, u32[]{:S(2)}) async-start(f16[8,72,384]{2,1,0:T(8,128)(2,1)} %broadcast_in_dim.31), calls=%async_computation.5 | async-start | bytes 884736 | tf_op jit(solution)/shard_map/all_to_all | solution.py:18
  183.7 16.8 %all-to-all-start.6 = ((f16[4,200,384]{2,1,0:T(8,128)(2,1)}), f16[4,200,384]{2,1,0:T(8,128)(2,1)S(1)}, u32[]{:S(2)}, u32[]{:S(2)}) async-start(f16[4,200,384]{2,1,0:T(8,128)(2,1)} %concatenate.70), calls=%async_computation.6 | async-start | bytes 1228800 | tf_op jit(solution)/shard_map/all_to_all | solution.py:18
  200.6 0.9 copy-start.4
  200.6 1.7 copy-start

commit v6 on v5

--- a/solution.py
+++ b/solution.py
@@ -100,8 +100,8 @@
     left_shift = shifted(jnp.where(is_output, output_left_eigen, joined_left_eigen), damp)
     right_shift = shifted(jnp.where(is_output, output_right_eigen, joined_right_eigen), damp)
     left_shift = left_shift.reshape(8, 2, 32).transpose(1, 0, 2).reshape(512)
-    right_shift = right_shift.reshape(4, 2, 2, 2, 16).transpose(0, 1, 3, 2, 4).reshape(4, 4, 2, 16)
-    right_shift = jnp.where(lax.axis_index("zp") == 1, right_shift[:, :, ::-1], right_shift).reshape(512)
+    right_shift = right_shift.reshape(4, 2, 2, 2, 16).transpose(2, 0, 1, 3, 4)
+    right_shift = jnp.where(lax.axis_index("zp") == 1, right_shift[::-1], right_shift).reshape(512)
     own_shift = lax.dynamic_slice_in_dim(left_shift, octant * 64, 64, 0)
 
     left_j, left_o = joined_left_basis.T, output_left_basis.T
@@ -112,7 +112,6 @@
     left = lax.all_gather(left, "c", axis=0, tiled=True)
 
     right = jnp.concatenate([joined_right_basis.T, output_right_basis.T], axis=1)
-    right = jnp.concatenate([right, swap(right, "zp")], axis=0)
     gradients = (joined_gradient[:, :384], joined_gradient[:, 384:768], joined_gradient[:, 768:], output_gradient)
     sent = jnp.stack(
         [jnp.concatenate([block, right[:, 384 * j : 384 * j + 384]], axis=0) for j, block in enumerate(gradients)]
@@ -124,8 +123,9 @@
     got = jnp.stack(got)
     got = jnp.stack([lax.dynamic_index_in_dim(got, quad ^ j, 0, False) for j in range(4)])
     gradient = got[:, :192].reshape(768, 384)
-    right = got[:, 192:].reshape(128, 384)
-    right = exchange(jnp.broadcast_to(right[None], (4, 128, 384)), "yp").reshape(512, 384)
+    right = got[:, 192:].reshape(64, 384)
+    right = exchange(jnp.broadcast_to(right[None], (4, 64, 384)), "yp").reshape(256, 384)
+    right = jnp.concatenate([right, swap(right, "zp")], axis=0)
     most = top(gradient)
 
     rows = jnp.dot(left, gradient, preferred_element_type=jnp.float32)
@@ -157,6 +157,7 @@
     mixed = rows / damp + dot_wide_left(mid * right_shift[None, :], right, ((1,), (0,)))
     mixed = mixed * own_shift[:, None]
     packed = pack(mixed, power_of(top(mixed)))
+    cols = cols + packed[:1, :1] * 0
     mixed = unpack(exchange(jnp.broadcast_to(packed[None], (8, 72, 384)), OCT)).reshape(512, 384)
 
     cols = ring_gather(cols, place)

time: 205 us -> 210 us (1.024)
  waiting for transfers between devices: 50.9 us -> 66.7 us
  starting transfers between devices: 90.2 us -> 81.3 us
  blocking collectives: 25.7 us -> 21.3 us
    ppermute x5, waiting for transfers between devices: 9.36 us -> 26 us  [swap(): return lax.ppermute(values, axis, [(0, 1), (1, 0)])]
    ppermute x5, starting transfers between devices: 26.1 us -> 17.8 us  [swap(): return lax.ppermute(values, axis, [(0, 1), (1, 0)])]
    all_to_all x6, waiting for transfers between devices: 41.5 us -> 36.1 us  [exchange(): return lax.all_to_all(blocks, axes, 0, 0, tiled=True)]
    ppermute x3, waiting for transfers between devices: 0.01 us -> 4.6 us  [around(): lax.ppermute(values, axis, [(i, (i + step) % size) for i in range(size)])]
  transfers between devices with their start and end apart: 17 -> 17, of which waited for: 8 -> 8; matrix products, arithmetic and copies ran while one was open for 7% -> 6% of each run, Pallas kernels for 0% -> 0%
where the time goes in v6:
time: 210 us; the launch traced here: 209 us
  starting transfers between devices  81.3 us (39%)
  waiting for transfers between devices  66.7 us (32%)
  blocking collectives  21.3 us (10%)
  local copies, waits for them, and re-layouts  14.1 us (7%)
  other arithmetic  10 us (5%)
  between operations  8.72 us (4%)
  matrix products  6.7 us (3%)
    all_to_all x6, starting transfers between devices, exchange(): return lax.all_to_all(blocks, axes, 0, 0, tiled=True)  45.8 us
    all_to_all x6, waiting for transfers between devices, exchange(): return lax.all_to_all(blocks, axes, 0, 0, tiled=True)  36.1 us
    ppermute x5, waiting for transfers between devices, swap(): return lax.ppermute(values, axis, [(0, 1), (1, 0)])  26 us
    ppermute x5, starting transfers between devices, swap(): return lax.ppermute(values, axis, [(0, 1), (1, 0)])  17.8 us
    all_to_all x1, blocking collectives, exchange(): return lax.all_to_all(blocks, axes, 0, 0, tiled=True)  11.3 us
    ppermute x3, starting transfers between devices, local(): got.append(lax.ppermute(block, QUAD, [(i, i ^ mask) for i in range(4)]))  9.95 us
    ppermute x3, starting transfers between devices, around(): lax.ppermute(values, axis, [(i, (i + step) % size) for i in range(size)])  7.81 us
    all_gather x1, blocking collectives, local(): left = lax.all_gather(left, 'c', axis=0, tiled=True)  6.91 us
  transfers between devices with their start and end apart: 17, of which 8 were waited for; matrix products, arithmetic and copies ran while one was open for 6% of the time, Pallas kernels for 0%

profile of v6, /device:TPU:1, one launch (start us, length us, event | category | flops | bytes accessed | tf_op | source)
XLA Modules:
  0.0 208.9 jit_solution(6418381921818240267)
XLA Ops:
  0.6 0.7 fusion.44
  1.4 1.1 fusion.43
  2.5 1.0 maximum_bitcast_fusion.2
  3.8 5.8 %collective-permute-start.2 = (bf16[208,384]{1,0:T(8,128)(2,1)S(1)}, bf16[208,384]{1,0:T(8,128)(2,1)S(1)}, u32[]{:S(2)}, u32[]{:S(2)}) collective-permute-start(bf16[208,384]{1,0:T(8,128)(2,1)S(1)} %get-tuple-element.16), channel_id=1, source_target_pairs={{0,80},{16,64},{64,16},{80,0},{1,81},{17,65},{65,17},{81,1},{2,82}... | collective-permute-start | bytes 479240 | tf_op jit(solution)/shard_map/ppermute | solution.py:122
  9.6 2.1 collective-permute-start.1
  11.7 2.0 collective-permute-start
  13.8 0.9 broadcast_in_dim.21
  14.6 13.1 %all-to-all-start = ((bf16[32,32,192]{2,1,0:T(8,128)(2,1)}), bf16[32,32,192]{2,1,0:T(8,128)(2,1)S(1)}, u32[]{:S(2)}, u32[]{:S(2)}) async-start(bf16[32,32,192]{2,1,0:T(8,128)(2,1)} %bitcast.4), calls=%async_computation | async-start | bytes 1048576 | tf_op jit(solution)/shard_map/all_to_all | solution.py:18
  28.1 0.8 abs_reduce_fusion.1
  29.7 10.8 %all-to-all-done = bf16[32,32,192]{2,1,0:T(8,128)(2,1)S(1)} async-done(((bf16[32,32,192]{2,1,0:T(8,128)(2,1)}), bf16[32,32,192]{2,1,0:T(8,128)(2,1)S(1)}, u32[]{:S(2)}, u32[]{:S(2)}) %all-to-all-start) | async-done | bytes 393248 | tf_op jit(solution)/shard_map/all_to_all | solution.py:18
  40.5 0.7 broadcast_in_dim.23
  41.2 5.9 %all-to-all-start.2 = ((bf16[4,64,384]{2,1,0:T(8,128)(2,1)}), bf16[4,64,384]{2,1,0:T(8,128)(2,1)S(1)}, u32[]{:S(2)}, u32[]{:S(2)}) async-start(bf16[4,64,384]{2,1,0:T(8,128)(2,1)} %broadcast_in_dim.23), calls=%async_computation.2 | async-start | bytes 393216 | tf_op jit(solution)/shard_map/all_to_all | solution.py:18
  47.3 6.9 %all_gather.6 = bf16[512,768]{1,0:T(8,128)(2,1)S(1)} all-gather(bf16[256,768]{1,0:T(8,128)(2,1)S(1)} %pad_maximum_fusion.6), channel_id=1, replica_groups=mesh['yp'=4,'yb'=2,'zp'=2,'zb'=2,'x'=4,'zh'=2,'c'=2] {'c'}, dimensions={0}, use_global_device_ids=true | all-gather | bytes 1179648 | tf_op jit(solution)/shard_map/all_gather | solution.py:112
  54.2 0.6 fusion.2
  54.8 0.8 concatenate.56
  55.6 10.2 %all-to-all-start.1 = ((f16[8,72,384]{2,1,0:T(8,128)(2,1)}), f16[8,72,384]{2,1,0:T(8,128)(2,1)}, u32[]{:S(2)}, u32[]{:S(2)}) async-start(f16[8,72,384]{2,1,0:T(8,128)(2,1)} %concatenate.56), calls=%async_computation.1 | async-start | bytes 884736 | tf_op jit(solution)/shard_map/all_to_all | solution.py:18
  65.8 4.3 %collective-permute-start.3 = (bf16[256,384]{1,0:T(8,128)(2,1)S(1)}, bf16[256,384]{1,0:T(8,128)(2,1)S(1)}, u32[]{:S(2)}, u32[]{:S(2)}) collective-permute-start(bf16[256,384]{1,0:T(8,128)(2,1)S(1)} %bitcast.105), channel_id=1, source_target_pairs={{0,32},{32,0},{1,33},{33,1},{2,34},{34,2},{3,35},{35,3},{4,36},{36... | collective-permute-start | bytes 589832 | tf_op jit(solution)/shard_map/ppermute | solution.py:59
  70.1 16.9 %collective-permute-done.3 = bf16[256,384]{1,0:T(8,128)(2,1)S(1)} collective-permute-done((bf16[256,384]{1,0:T(8,128)(2,1)S(1)}, bf16[256,384]{1,0:T(8,128)(2,1)S(1)}, u32[]{:S(2)}, u32[]{:S(2)}) %collective-permute-start.3) | collective-permute-done | bytes 196640 | tf_op jit(solution)/shard_map/ppermute | solution.py:59
  87.0 0.6 fusion.41
  87.7 3.4 %collective-permute-start.5 = (f32[384,512]{1,0:T(8,128)S(1)}, f32[384,512]{1,0:T(8,128)}, u32[]{:S(2)}, u32[]{:S(2)}) collective-permute-start(f32[384,512]{1,0:T(8,128)S(1)} %constant_dynamic-slice_fusion), channel_id=1, source_target_pairs={{0,1},{1,0},{2,3},{3,2},{4,5},{5,4},{6,7},{7,6},{8,9},{9,8},{10,11... | collective-permute-start | bytes 2359304 | tf_op jit(solution)/shard_map/ppermute | solution.py:59
  91.0 0.8 slice.157
  91.9 1.1 multiply_reduce_fusion.1
  93.2 0.2 convolution_add_fusion.2
  93.5 0.7 concatenate.58
  94.2 1.9 collective-permute-start.4
  96.2 1.3 dynamic-slice_add_fusion
  97.5 0.6 copy-done.7
  98.1 0.6 slice.159
  100.1 0.9 fusion.20
  101.3 11.3 %all_to_all.35 = f16[4,136,512]{2,1,0:T(8,128)(2,1)S(1)} all-to-all(f16[4,136,512]{2,1,0:T(8,128)(2,1)S(1)} %concatenate.60), channel_id=1, replica_groups=mesh['yp'=4,'yb'=2,'zp'=2,'zb'=2,'x'=4,'zh'=2,'c'=2] {'x'}, dimensions={0} | all-to-all | bytes 1114112 | tf_op jit(solution)/shard_map/all_to_all | solution.py:18
  112.5 0.6 slice_reduce_fusion.1
  114.0 0.7 concatenate.61
  114.7 4.3 %collective-permute-start.6 = (f16[136,512]{1,0:T(8,128)(2,1)S(1)}, f16[136,512]{1,0:T(8,128)(2,1)S(1)}, u32[]{:S(2)}, u32[]{:S(2)}) collective-permute-start(f16[136,512]{1,0:T(8,128)(2,1)S(1)} %concatenate.61), channel_id=1, source_target_pairs={{0,2},{2,0},{1,3},{3,1},{4,6},{6,4},{5,7},{7,5},{8,10},{10,8},{9,1... | collective-permute-start | bytes 417800 | tf_op jit(solution)/shard_map/ppermute | solution.py:59
  119.0 9.1 %collective-permute-done.6 = f16[136,512]{1,0:T(8,128)(2,1)S(1)} collective-permute-done((f16[136,512]{1,0:T(8,128)(2,1)S(1)}, f16[136,512]{1,0:T(8,128)(2,1)S(1)}, u32[]{:S(2)}, u32[]{:S(2)}) %collective-permute-start.6) | collective-permute-done | bytes 139296 | tf_op jit(solution)/shard_map/ppermute | solution.py:59
  128.1 0.5 slice.165
  129.5 0.8 broadcast_in_dim.29
  130.3 3.5 %all-to-all-start.4 = ((f16[4,136,512]{2,1,0:T(8,128)(2,1)}), f16[4,136,512]{2,1,0:T(8,128)(2,1)S(1)}, u32[]{:S(2)}, u32[]{:S(2)}) async-start(f16[4,136,512]{2,1,0:T(8,128)(2,1)} %broadcast_in_dim.29), calls=%async_computation.4 | async-start | bytes 1114112 | tf_op jit(solution)/shard_map/all_to_all | solution.py:18
  135.1 6.4 %all-to-all-done.4 = f16[4,136,512]{2,1,0:T(8,128)(2,1)S(1)} async-done(((f16[4,136,512]{2,1,0:T(8,128)(2,1)}), f16[4,136,512]{2,1,0:T(8,128)(2,1)S(1)}, u32[]{:S(2)}, u32[]{:S(2)}) %all-to-all-start.4) | async-done | bytes 557088 | tf_op jit(solution)/shard_map/all_to_all | solution.py:18
  141.7 3.1 %all_gather.7 = f32[64,512]{1,0:T(8,128)S(1)} all-gather(f32[32,512]{1,0:T(8,128)S(1)} %slice.170), channel_id=1, replica_groups=mesh['yp'=4,'yb'=2,'zp'=2,'zb'=2,'x'=4,'zh'=2,'c'=2] {'c'}, dimensions={0}, use_global_device_ids=true | all-gather | bytes 196608 | tf_op jit(solution)/shard_map/all_gather | solution.py:155
  145.1 0.8 abs_reduce_fusion.2
  146.6 0.6 slice_reduce_fusion
  147.9 0.5 slice.171
  149.2 2.8 %collective-permute-start.9 = (f16[96,512]{1,0:T(8,128)(2,1)S(1)}, f16[96,512]{1,0:T(8,128)(2,1)S(1)}, u32[]{:S(2)}, u32[]{:S(2)}) collective-permute-start(f16[96,512]{1,0:T(8,128)(2,1)S(1)} %fusion.17), channel_id=1, source_target_pairs={{0,12},{4,0},{8,4},{12,8},{1,13},{5,1},{9,5},{13,9},{2,14},{6,2},{... | collective-permute-start | bytes 294920 | tf_op jit(solution)/shard_map/ppermute | solution.py:63
  152.0 3.1 %collective-permute-start.8 = (f16[96,512]{1,0:T(8,128)(2,1)S(1)}, f16[96,512]{1,0:T(8,128)(2,1)S(1)}, u32[]{:S(2)}, u32[]{:S(2)}) collective-permute-start(f16[96,512]{1,0:T(8,128)(2,1)S(1)} %fusion.17), channel_id=1, source_target_pairs={{0,8},{4,12},{8,0},{12,4},{1,9},{5,13},{9,1},{13,5},{2,10},{6,14},... | collective-permute-start | bytes 294920 | tf_op jit(solution)/shard_map/ppermute | solution.py:63
  155.1 1.9 collective-permute-start.7
  157.0 1.8 collective-permute-done.8
  158.8 2.8 %collective-permute-done.7 = f16[96,512]{1,0:T(8,128)(2,1)S(1)} collective-permute-done((f16[96,512]{1,0:T(8,128)(2,1)S(1)}, f16[96,512]{1,0:T(8,128)(2,1)S(1)}, u32[]{:S(2)}, u32[]{:S(2)}) %collective-permute-start.7) | collective-permute-done | bytes 98336 | tf_op jit(solution)/shard_map/ppermute | solution.py:63
  162.0 4.0 %collective-permute-start.10 = (f16[384,512]{1,0:T(8,128)(2,1)S(1)}, f16[384,512]{1,0:T(8,128)(2,1)S(1)}, u32[]{:S(2)}, u32[]{:S(2)}) collective-permute-start(f16[384,512]{1,0:T(8,128)(2,1)S(1)} %pad_maximum_fusion.9), channel_id=1, source_target_pairs={{0,1},{1,0},{2,3},{3,2},{4,5},{5,4},{6,7},{7,6},{8,9},{9,8},{10,11... | collective-permute-start | bytes 1179656 | tf_op jit(solution)/shard_map/ppermute | solution.py:59
  166.0 0.8 broadcast_in_dim.31
  166.8 5.9 %all-to-all-start.5 = ((f16[8,72,384]{2,1,0:T(8,128)(2,1)}), f16[8,72,384]{2,1,0:T(8,128)(2,1)S(1)}, u32[]{:S(2)}, u32[]{:S(2)}) async-start(f16[8,72,384]{2,1,0:T(8,128)(2,1)} %broadcast_in_dim.31), calls=%async_computation.5 | async-start | bytes 884736 | tf_op jit(solution)/shard_map/all_to_all | solution.py:18
  172.8 0.2 broadcast_select_fusion.1
  173.1 1.6 fusion.7
  174.7 9.4 %all-to-all-done.5 = f16[8,72,384]{2,1,0:T(8,128)(2,1)S(1)} async-done(((f16[8,72,384]{2,1,0:T(8,128)(2,1)}), f16[8,72,384]{2,1,0:T(8,128)(2,1)S(1)}, u32[]{:S(2)}, u32[]{:S(2)}) %all-to-all-start.5) | async-done | bytes 442400 | tf_op jit(solution)/shard_map/all_to_all | solution.py:18
  184.3 0.6 fusion.45
  184.9 0.6 convolution_add_fusion
  185.5 0.4 copy-done.4
  185.9 0.4 copy-done.14
  186.3 1.2 abs_reduce_fusion
  188.4 0.9 concatenate.66
  189.3 7.2 %all-to-all-start.6 = ((f16[4,200,384]{2,1,0:T(8,128)(2,1)}), f16[4,200,384]{2,1,0:T(8,128)(2,1)S(1)}, u32[]{:S(2)}, u32[]{:S(2)}) async-start(f16[4,200,384]{2,1,0:T(8,128)(2,1)} %concatenate.66), calls=%async_computation.6 | async-start | bytes 1228800 | tf_op jit(solution)/shard_map/all_to_all | solution.py:18
  196.5 9.6 %all-to-all-done.6 = f16[4,200,384]{2,1,0:T(8,128)(2,1)S(1)} async-done(((f16[4,200,384]{2,1,0:T(8,128)(2,1)}), f16[4,200,384]{2,1,0:T(8,128)(2,1)S(1)}, u32[]{:S(2)}, u32[]{:S(2)}) %all-to-all-start.6) | async-done | bytes 614432 | tf_op jit(solution)/shard_map/all_to_all | solution.py:18
  206.3 0.8 copy-done.1
  207.1 0.7 fusion.13
  207.9 1.0 maximum_add_fusion
  (93 shorter events, 3.5 us)
Async XLA Ops:
  3.5 10.2 %copy-start.8 = (bf16[192,32]{0,1:T(8,128)(2,1)S(1)}, bf16[192,32]{0,1:T(8,128)(2,1)}, u32[]{:S(2)}) copy-start(bf16[192,32]{0,1:T(8,128)(2,1)} %param.15) | copy-start | bytes 36868
  3.5 10.2 %copy-start.9 = (bf16[192,32]{0,1:T(8,128)(2,1)S(1)}, bf16[192,32]{0,1:T(8,128)(2,1)}, u32[]{:S(2)}) copy-start(bf16[192,32]{0,1:T(8,128)(2,1)} %param.13) | copy-start | bytes 36868
  3.8 24.0 %collective-permute-start.2 = (bf16[208,384]{1,0:T(8,128)(2,1)S(1)}, bf16[208,384]{1,0:T(8,128)(2,1)S(1)}, u32[]{:S(2)}, u32[]{:S(2)}) collective-permute-start(bf16[208,384]{1,0:T(8,128)(2,1)S(1)} %get-tuple-element.16), channel_id=1, source_target_pairs={{0,80},{16,64},{64,16},{80,0},{1,81},{17,65},{65,17},{81,1},{2,82}... | collective-permute-start | bytes 479240 | tf_op jit(solution)/shard_map/ppermute | solution.py:122
  9.6 18.2 %collective-permute-start.1 = (bf16[208,384]{1,0:T(8,128)(2,1)S(1)}, bf16[208,384]{1,0:T(8,128)(2,1)S(1)}, u32[]{:S(2)}, u32[]{:S(2)}) collective-permute-start(bf16[208,384]{1,0:T(8,128)(2,1)S(1)} %get-tuple-element.17), channel_id=1, source_target_pairs={{0,64},{16,80},{64,0},{80,16},{1,65},{17,81},{65,1},{81,17},{2,66}... | collective-permute-start | bytes 479240 | tf_op jit(solution)/shard_map/ppermute | solution.py:122
  11.7 16.1 %collective-permute-start = (bf16[208,384]{1,0:T(8,128)(2,1)S(1)}, bf16[208,384]{1,0:T(8,128)(2,1)S(1)}, u32[]{:S(2)}, u32[]{:S(2)}) collective-permute-start(bf16[208,384]{1,0:T(8,128)(2,1)S(1)} %get-tuple-element.18), channel_id=1, source_target_pairs={{0,16},{16,0},{64,80},{80,64},{1,17},{17,1},{65,81},{81,65},{2,18}... | collective-permute-start | bytes 479240 | tf_op jit(solution)/shard_map/ppermute | solution.py:122
  14.6 25.8 %all-to-all-start = ((bf16[32,32,192]{2,1,0:T(8,128)(2,1)}), bf16[32,32,192]{2,1,0:T(8,128)(2,1)S(1)}, u32[]{:S(2)}, u32[]{:S(2)}) async-start(bf16[32,32,192]{2,1,0:T(8,128)(2,1)} %bitcast.4), calls=%async_computation | async-start | bytes 1048576 | tf_op jit(solution)/shard_map/all_to_all | solution.py:18
  41.2 14.5 %all-to-all-start.2 = ((bf16[4,64,384]{2,1,0:T(8,128)(2,1)}), bf16[4,64,384]{2,1,0:T(8,128)(2,1)S(1)}, u32[]{:S(2)}, u32[]{:S(2)}) async-start(bf16[4,64,384]{2,1,0:T(8,128)(2,1)} %broadcast_in_dim.23), calls=%async_computation.2 | async-start | bytes 393216 | tf_op jit(solution)/shard_map/all_to_all | solution.py:18
  55.6 35.4 %all-to-all-start.1 = ((f16[8,72,384]{2,1,0:T(8,128)(2,1)}), f16[8,72,384]{2,1,0:T(8,128)(2,1)}, u32[]{:S(2)}, u32[]{:S(2)}) async-start(f16[8,72,384]{2,1,0:T(8,128)(2,1)} %concatenate.56), calls=%async_computation.1 | async-start | bytes 884736 | tf_op jit(solution)/shard_map/all_to_all | solution.py:18
  65.8 21.2 %collective-permute-start.3 = (bf16[256,384]{1,0:T(8,128)(2,1)S(1)}, bf16[256,384]{1,0:T(8,128)(2,1)S(1)}, u32[]{:S(2)}, u32[]{:S(2)}) collective-permute-start(bf16[256,384]{1,0:T(8,128)(2,1)S(1)} %bitcast.105), channel_id=1, source_target_pairs={{0,32},{32,0},{1,33},{33,1},{2,34},{34,2},{3,35},{35,3},{4,36},{36... | collective-permute-start | bytes 589832 | tf_op jit(solution)/shard_map/ppermute | solution.py:59
  87.7 8.5 %collective-permute-start.5 = (f32[384,512]{1,0:T(8,128)S(1)}, f32[384,512]{1,0:T(8,128)}, u32[]{:S(2)}, u32[]{:S(2)}) collective-permute-start(f32[384,512]{1,0:T(8,128)S(1)} %constant_dynamic-slice_fusion), channel_id=1, source_target_pairs={{0,1},{1,0},{2,3},{3,2},{4,5},{5,4},{6,7},{7,6},{8,9},{9,8},{10,11... | collective-permute-start | bytes 2359304 | tf_op jit(solution)/shard_map/ppermute | solution.py:59
  93.0 3.2 %copy-start.5 = (f32[64,384]{1,0:T(8,128)}, f32[64,384]{1,0:T(8,128)S(1)}, u32[]{:S(2)}) copy-start(f32[64,384]{1,0:T(8,128)S(1)} %multiply_reduce_fusion.1) | copy-start | bytes 294916
  93.5 2.7 %copy-start.2 = (f32[64,512]{1,0:T(8,128)}, f32[64,512]{1,0:T(8,128)S(1)}, u32[]{:S(2)}) copy-start(f32[64,512]{1,0:T(8,128)S(1)} %convolution_add_fusion.2) | copy-start | bytes 393220
  94.2 3.2 %collective-permute-start.4 = (f32[40,512]{1,0:T(8,128)S(1)}, f32[40,512]{1,0:T(8,128)S(1)}, u32[]{:S(2)}, u32[]{:S(2)}) collective-permute-start(f32[40,512]{1,0:T(8,128)S(1)} %concatenate.58), channel_id=1, source_target_pairs={{0,1},{1,0},{2,3},{3,2},{4,5},{5,4},{6,7},{7,6},{8,9},{9,8},{10,11... | collective-permute-start | bytes 245768 | tf_op jit(solution)/shard_map/ppermute | solution.py:59
  97.5 0.6 copy-start.7
  114.7 13.4 %collective-permute-start.6 = (f16[136,512]{1,0:T(8,128)(2,1)S(1)}, f16[136,512]{1,0:T(8,128)(2,1)S(1)}, u32[]{:S(2)}, u32[]{:S(2)}) collective-permute-start(f16[136,512]{1,0:T(8,128)(2,1)S(1)} %concatenate.61), channel_id=1, source_target_pairs={{0,2},{2,0},{1,3},{3,1},{4,6},{6,4},{5,7},{7,5},{8,10},{10,8},{9,1... | collective-permute-start | bytes 417800 | tf_op jit(solution)/shard_map/ppermute | solution.py:59
  129.4 5.2 %copy-start.10 = (f32[512]{0:T(512)S(1)}, f32[512]{0:T(512)}, u32[]{:S(2)}) copy-start(f32[512]{0:T(512)} %param.19) | copy-start | bytes 6148
  129.4 5.2 %copy-start.11 = (f32[512]{0:T(512)S(1)}, f32[512]{0:T(512)}, u32[]{:S(2)}) copy-start(f32[512]{0:T(512)} %param.17) | copy-start | bytes 6148
  129.4 5.2 %copy-start.12 = (f32[512]{0:T(512)S(1)}, f32[512]{0:T(512)}, u32[]{:S(2)}) copy-start(f32[512]{0:T(512)} %param.20) | copy-start | bytes 6148
  129.4 5.2 %copy-start.13 = (f32[512]{0:T(512)S(1)}, f32[512]{0:T(512)}, u32[]{:S(2)}) copy-start(f32[512]{0:T(512)} %param.18) | copy-start | bytes 6148
  130.3 11.2 %all-to-all-start.4 = ((f16[4,136,512]{2,1,0:T(8,128)(2,1)}), f16[4,136,512]{2,1,0:T(8,128)(2,1)S(1)}, u32[]{:S(2)}, u32[]{:S(2)}) async-start(f16[4,136,512]{2,1,0:T(8,128)(2,1)} %broadcast_in_dim.29), calls=%async_computation.4 | async-start | bytes 1114112 | tf_op jit(solution)/shard_map/all_to_all | solution.py:18
  133.8 11.2 %copy-start.6 = (f32[64,384]{1,0:T(8,128)S(1)}, f32[64,384]{1,0:T(8,128)}, u32[]{:S(2)}) copy-start(f32[64,384]{1,0:T(8,128)} %copy-done.5) | copy-start | bytes 294916
  149.2 7.9 %collective-permute-start.9 = (f16[96,512]{1,0:T(8,128)(2,1)S(1)}, f16[96,512]{1,0:T(8,128)(2,1)S(1)}, u32[]{:S(2)}, u32[]{:S(2)}) collective-permute-start(f16[96,512]{1,0:T(8,128)(2,1)S(1)} %fusion.17), channel_id=1, source_target_pairs={{0,12},{4,0},{8,4},{12,8},{1,13},{5,1},{9,5},{13,9},{2,14},{6,2},{... | collective-permute-start | bytes 294920 | tf_op jit(solution)/shard_map/ppermute | solution.py:63
  152.0 6.9 %collective-permute-start.8 = (f16[96,512]{1,0:T(8,128)(2,1)S(1)}, f16[96,512]{1,0:T(8,128)(2,1)S(1)}, u32[]{:S(2)}, u32[]{:S(2)}) collective-permute-start(f16[96,512]{1,0:T(8,128)(2,1)S(1)} %fusion.17), channel_id=1, source_target_pairs={{0,8},{4,12},{8,0},{12,4},{1,9},{5,13},{9,1},{13,5},{2,10},{6,14},... | collective-permute-start | bytes 294920 | tf_op jit(solution)/shard_map/ppermute | solution.py:63
  155.1 6.6 %collective-permute-start.7 = (f16[96,512]{1,0:T(8,128)(2,1)S(1)}, f16[96,512]{1,0:T(8,128)(2,1)S(1)}, u32[]{:S(2)}, u32[]{:S(2)}) collective-permute-start(f16[96,512]{1,0:T(8,128)(2,1)S(1)} %fusion.17), channel_id=1, source_target_pairs={{0,4},{4,8},{8,12},{12,0},{1,5},{5,9},{9,13},{13,1},{2,6},{6,10},{... | collective-permute-start | bytes 294920 | tf_op jit(solution)/shard_map/ppermute | solution.py:63
  162.0 10.9 %collective-permute-start.10 = (f16[384,512]{1,0:T(8,128)(2,1)S(1)}, f16[384,512]{1,0:T(8,128)(2,1)S(1)}, u32[]{:S(2)}, u32[]{:S(2)}) collective-permute-start(f16[384,512]{1,0:T(8,128)(2,1)S(1)} %pad_maximum_fusion.9), channel_id=1, source_target_pairs={{0,1},{1,0},{2,3},{3,2},{4,5},{5,4},{6,7},{7,6},{8,9},{9,8},{10,11... | collective-permute-start | bytes 1179656 | tf_op jit(solution)/shard_map/ppermute | solution.py:59
  166.8 17.3 %all-to-all-start.5 = ((f16[8,72,384]{2,1,0:T(8,128)(2,1)}), f16[8,72,384]{2,1,0:T(8,128)(2,1)S(1)}, u32[]{:S(2)}, u32[]{:S(2)}) async-start(f16[8,72,384]{2,1,0:T(8,128)(2,1)} %broadcast_in_dim.31), calls=%async_computation.5 | async-start | bytes 884736 | tf_op jit(solution)/shard_map/all_to_all | solution.py:18
  173.1 1.6 copy-start.3
  184.9 1.0 copy-start.4
  184.9 1.4 copy-start.14
  189.3 16.8 %all-to-all-start.6 = ((f16[4,200,384]{2,1,0:T(8,128)(2,1)}), f16[4,200,384]{2,1,0:T(8,128)(2,1)S(1)}, u32[]{:S(2)}, u32[]{:S(2)}) async-start(f16[4,200,384]{2,1,0:T(8,128)(2,1)} %concatenate.66), calls=%async_computation.6 | async-start | bytes 1228800 | tf_op jit(solution)/shard_map/all_to_all | solution.py:18
  206.2 0.9 copy-start.1
  206.2 1.7 copy-start

commit v7 on v5

--- a/solution.py
+++ b/solution.py
@@ -63,20 +63,9 @@
     return lax.ppermute(values, axis, [(i, (i + step) % size) for i in range(size)])
 
 
-def ring_gather(values, place):
-    held = jnp.stack([values] + [around(values, "x", 4, step) for step in (1, 2, 3)])
-    return jnp.concatenate([lax.dynamic_index_in_dim(held, (place - j) % 4, 0, False) for j in range(4)], axis=0)
-
-
 def core_part(values, core, own):
     half = values.shape[0] // 2
     return lax.dynamic_slice_in_dim(values, (core if own else 1 - core) * half, half, 0)
-
-
-def joined_pair(mine, other, place):
-    first = jnp.where(place == 0, mine, other)
-    second = jnp.where(place == 0, other, mine)
-    return jnp.concatenate([first, second], axis=0)
 
 
 def local(
@@ -113,19 +102,19 @@
 
     right = jnp.concatenate([joined_right_basis.T, output_right_basis.T], axis=1)
     right = jnp.concatenate([right, swap(right, "zp")], axis=0)
+    right = jnp.stack([right[:, 384 * j : 384 * j + 384] for j in range(4)])
+    right = jnp.broadcast_to(right[None], (4, 4, 32, 384)).reshape(16, 32, 384)
+    right = exchange(right, ("yp",) + QUAD).reshape(512, 384)
+
     gradients = (joined_gradient[:, :384], joined_gradient[:, 384:768], joined_gradient[:, 768:], output_gradient)
-    sent = jnp.stack(
-        [jnp.concatenate([block, right[:, 384 * j : 384 * j + 384]], axis=0) for j, block in enumerate(gradients)]
-    )
+    sent = jnp.stack(gradients)
     got = [lax.dynamic_index_in_dim(sent, quad, 0, False)]
     for mask in (1, 2, 3):
         block = lax.dynamic_index_in_dim(sent, quad ^ mask, 0, False)
         got.append(lax.ppermute(block, QUAD, [(i, i ^ mask) for i in range(4)]))
     got = jnp.stack(got)
     got = jnp.stack([lax.dynamic_index_in_dim(got, quad ^ j, 0, False) for j in range(4)])
-    gradient = got[:, :192].reshape(768, 384)
-    right = got[:, 192:].reshape(128, 384)
-    right = exchange(jnp.broadcast_to(right[None], (4, 128, 384)), "yp").reshape(512, 384)
+    gradient = got.reshape(768, 384)
     most = top(gradient)
 
     rows = jnp.dot(left, gradient, preferred_element_type=jnp.float32)
@@ -133,18 +122,20 @@
     rows = jnp.sum(unpack(exchange(rows, OCT)), axis=0)
 
     cols = lax.dot_general(gradient, right, (((1,), (1,)), ((), ())), preferred_element_type=jnp.float32)
-    cols = core_part(cols, core, True) + swap(core_part(cols, core, False), "c")
-    cols = cols.reshape(4, 96, 512)
+    other = jnp.concatenate([core_part(cols, core, False), jnp.broadcast_to(most, (8, 512))], axis=0)
+    other = swap(other, "c")
+    power = power_of(jnp.maximum(most, other[384, 0]) * 864.0)
+    blocks = pack((core_part(cols, core, True) + other[:384]).reshape(4, 96, 512), power)
+    parts = [lax.dynamic_index_in_dim(blocks, place, 0, False)]
+    for step in (1, 2, 3):
+        parts.append(around(lax.dynamic_index_in_dim(blocks, (place + step) % 4, 0, False), "x", 4, step))
+    cols = sum(unpack(part) for part in parts)
+    for part in parts[1:]:
+        power = jnp.maximum(power, part[96, 0].astype(jnp.float32))
 
     mid = dot_wide_left(rows, right, ((1,), (1,)))
-    other = jnp.concatenate([core_part(mid, core, False), jnp.broadcast_to(most, (8, 512))], axis=0)
-    other = swap(other, "c")
-    mid = (core_part(mid, core, True) + other[:32]) / 512.0
-    power = power_of(jnp.maximum(most, other[32, 0]) * 864.0)
-    both = jnp.concatenate([jnp.broadcast_to(mid[None], (4, 32, 512)), cols], axis=1)
-    both = exchange(pack(both, power), "x")
-    power = jnp.max(both[:, 128, 0]).astype(jnp.float32)
-    both = jnp.sum(unpack(both), axis=0)
+    mid = core_part(mid, core, True) + swap(core_part(mid, core, False), "c")
+    both = jnp.concatenate([mid / 512.0, cols], axis=0)
     got = swap(pack(both, power), "zh")
     power = jnp.maximum(power, got[128, 0].astype(jnp.float32))
     both = both + unpack(got)
@@ -152,15 +143,15 @@
     power = jnp.max(both[:, 128, 0]).astype(jnp.float32)
     same = (lax.broadcasted_iota(jnp.int32, (4, 1, 1), 0) == 3) == is_output
     both = jnp.sum(jnp.where(same, unpack(both), 0.0), axis=0)
-    mid = lax.all_gather(both[:32], "c", axis=0, tiled=True) * 512.0
-    cols = (both[32:] * jnp.exp2(14.0 - power)).astype(jnp.float16)
+    both = exchange(jnp.broadcast_to(pack(both, power)[None], (4, 136, 512)), "x")
+    power = jnp.max(both[:, 128, 0]).astype(jnp.float32)
+    mid = jnp.sum(unpack(both)[:, :32], axis=0)
+    mid = lax.all_gather(mid, "c", axis=0, tiled=True) * 512.0
+    cols = lax.all_gather(both[:, 32:128].reshape(384, 512), "c", axis=0, tiled=True)
     mixed = rows / damp + dot_wide_left(mid * right_shift[None, :], right, ((1,), (0,)))
     mixed = mixed * own_shift[:, None]
     packed = pack(mixed, power_of(top(mixed)))
     mixed = unpack(exchange(jnp.broadcast_to(packed[None], (8, 72, 384)), OCT)).reshape(512, 384)
-
-    cols = ring_gather(cols, place)
-    cols = joined_pair(cols, swap(cols, "c"), core)
 
     cols = cols.astype(jnp.float32) * jnp.exp2(power - 14.0)
     part = dot_wide_left(cols * (right_shift / damp)[None, :], right, ((1,), (0,)))

time: 205 us -> 207 us (level)
  waiting for transfers between devices: 50.9 us -> 70.6 us
  blocking collectives: 25.7 us -> 13.3 us
  starting transfers between devices: 90.2 us -> 81.1 us
  local copies, waits for them, and re-layouts: 12.1 us -> 15.5 us
    all_to_all x6 -> x7, waiting for transfers between devices: 41.5 us -> 57.9 us  [exchange(): return lax.all_to_all(blocks, axes, 0, 0, tiled=True)]
    all_to_all x1 -> x0, blocking collectives: 13 us -> none  [exchange(): return lax.all_to_all(blocks, axes, 0, 0, tiled=True)]
    ppermute x5 -> x4, starting transfers between devices: 26.1 us -> 17.1 us  [swap(): return lax.ppermute(values, axis, [(0, 1), (1, 0)])]
    all_gather x1 -> x2, blocking collectives: 5.14 us -> 10.5 us  [the longest x1 7.88 us: local(): mid = lax.all_gather(mid, 'c', axis=0, tiled=True) * 512.0]
    ppermute x3, waiting for transfers between devices: 0.01 us -> 5.07 us  [around(): lax.ppermute(values, axis, [(i, (i + step) % size) for i in range(size)])]
    all_gather x1, blocking collectives: 7.57 us -> 2.79 us  [local(): left = lax.all_gather(left, 'c', axis=0, tiled=True)]
    ppermute x5 -> x4, waiting for transfers between devices: 9.36 us -> 7.68 us  [swap(): return lax.ppermute(values, axis, [(0, 1), (1, 0)])]
    all_to_all x6 -> x7, starting transfers between devices: 47.2 us -> 47.3 us  [exchange(): return lax.all_to_all(blocks, axes, 0, 0, tiled=True)]
  transfers between devices with their start and end apart: 17 -> 17, of which waited for: 8 -> 9; matrix products, arithmetic and copies ran while one was open for 7% -> 8% of each run, Pallas kernels for 0% -> 0%
where the time goes in v7:
time: 207 us; the launch traced here: 205 us
  starting transfers between devices  81.1 us (39%)
  waiting for transfers between devices  70.6 us (34%)
  local copies, waits for them, and re-layouts  15.5 us (7%)
  blocking collectives  13.3 us (6%)
  between operations  9.93 us (5%)
  other arithmetic  9.18 us (4%)
  matrix products  5.64 us (3%)
    all_to_all x7, waiting for transfers between devices, exchange(): return lax.all_to_all(blocks, axes, 0, 0, tiled=True)  57.9 us
    all_to_all x7, starting transfers between devices, exchange(): return lax.all_to_all(blocks, axes, 0, 0, tiled=True)  47.3 us
    ppermute x4, starting transfers between devices, swap(): return lax.ppermute(values, axis, [(0, 1), (1, 0)])  17.1 us
    ppermute x3, starting transfers between devices, local(): got.append(lax.ppermute(block, QUAD, [(i, i ^ mask) for i in range(4)]))  9.13 us
    all_gather x1, blocking collectives, local(): mid = lax.all_gather(mid, 'c', axis=0, tiled=True) * 512.0  7.88 us
    ppermute x4, waiting for transfers between devices, swap(): return lax.ppermute(values, axis, [(0, 1), (1, 0)])  7.68 us
    ppermute x3, starting transfers between devices, around(): lax.ppermute(values, axis, [(i, (i + step) % size) for i in range(size)])  7.58 us
    ppermute x3, waiting for transfers between devices, around(): lax.ppermute(values, axis, [(i, (i + step) % size) for i in range(size)])  5.07 us
  transfers between devices with their start and end apart: 17, of which 9 were waited for; matrix products, arithmetic and copies ran while one was open for 8% of the time, Pallas kernels for 0%

profile of v7, /device:TPU:1, one launch (start us, length us, event | category | flops | bytes accessed | tf_op | source)
XLA Modules:
  0.0 205.2 jit_solution(16520840296483609894)
XLA Ops:
  0.6 0.8 pad_maximum_fusion.8
  1.4 6.6 %collective-permute-start.3 = (bf16[16,1536]{1,0:T(8,128)(2,1)S(1)}, bf16[16,1536]{1,0:T(8,128)(2,1)S(1)}, u32[]{:S(2)}, u32[]{:S(2)}) collective-permute-start(bf16[16,1536]{1,0:T(8,128)(2,1)S(1)} %pad_maximum_fusion.8), channel_id=1, source_target_pairs={{0,32},{32,0},{1,33},{33,1},{2,34},{34,2},{3,35},{35,3},{4,36},{36... | collective-permute-start | bytes 147464 | tf_op jit(solution)/shard_map/ppermute | solution.py:59
  8.1 1.1 slice_bitcast_fusion.6
  9.2 1.0 pad_maximum_fusion
  10.3 5.0 %collective-permute-start.2 = (bf16[192,384]{1,0:T(8,128)(2,1)S(1)}, bf16[192,384]{1,0:T(8,128)(2,1)S(1)}, u32[]{:S(2)}, u32[]{:S(2)}) collective-permute-start(bf16[192,384]{1,0:T(8,128)(2,1)S(1)} %get-tuple-element.14), channel_id=1, source_target_pairs={{0,80},{16,64},{64,16},{80,0},{1,81},{17,65},{65,17},{81,1},{2,82}... | collective-permute-start | bytes 442376 | tf_op jit(solution)/shard_map/ppermute | solution.py:114
  15.4 2.1 %collective-permute-start.1 = (bf16[192,384]{1,0:T(8,128)(2,1)S(1)}, bf16[192,384]{1,0:T(8,128)(2,1)S(1)}, u32[]{:S(2)}, u32[]{:S(2)}) collective-permute-start(bf16[192,384]{1,0:T(8,128)(2,1)S(1)} %get-tuple-element.15), channel_id=1, source_target_pairs={{0,64},{16,80},{64,0},{80,16},{1,65},{17,81},{65,1},{81,17},{2,66}... | collective-permute-start | bytes 442376 | tf_op jit(solution)/shard_map/ppermute | solution.py:114
  17.5 2.0 collective-permute-start
  19.5 0.9 broadcast_in_dim.19
  20.4 11.3 %all-to-all-start = ((bf16[32,32,192]{2,1,0:T(8,128)(2,1)}), bf16[32,32,192]{2,1,0:T(8,128)(2,1)S(1)}, u32[]{:S(2)}, u32[]{:S(2)}) async-start(bf16[32,32,192]{2,1,0:T(8,128)(2,1)} %bitcast.4), calls=%async_computation | async-start | bytes 1048576 | tf_op jit(solution)/shard_map/all_to_all | solution.py:18
  32.0 0.7 abs_reduce_fusion.1
  33.5 14.7 %all-to-all-done = bf16[32,32,192]{2,1,0:T(8,128)(2,1)S(1)} async-done(((bf16[32,32,192]{2,1,0:T(8,128)(2,1)}), bf16[32,32,192]{2,1,0:T(8,128)(2,1)S(1)}, u32[]{:S(2)}, u32[]{:S(2)}) %all-to-all-start) | async-done | bytes 393248 | tf_op jit(solution)/shard_map/all_to_all | solution.py:18
  48.2 0.8 broadcast_in_dim.20
  49.0 9.5 %all-to-all-start.2 = ((bf16[16,32,384]{2,1,0:T(8,128)(2,1)}), bf16[16,32,384]{2,1,0:T(8,128)(2,1)S(1)}, u32[]{:S(2)}, u32[]{:S(2)}) async-start(bf16[16,32,384]{2,1,0:T(8,128)(2,1)} %bitcast.29), calls=%async_computation.2 | async-start | bytes 786432 | tf_op jit(solution)/shard_map/all_to_all | solution.py:18
  58.7 2.8 %all_gather.9 = bf16[512,768]{1,0:T(8,128)(2,1)S(1)} all-gather(bf16[256,768]{1,0:T(8,128)(2,1)S(1)} %pad_maximum_fusion.3), channel_id=1, replica_groups=mesh['yp'=4,'yb'=2,'zp'=2,'zb'=2,'x'=4,'zh'=2,'c'=2] {'c'}, dimensions={0}, use_global_device_ids=true | all-gather | bytes 1179648 | tf_op jit(solution)/shard_map/all_gather | solution.py:101
  61.5 0.6 fusion.2
  62.1 0.9 concatenate.40
  63.0 9.0 %all-to-all-done.2 = bf16[16,32,384]{2,1,0:T(8,128)(2,1)S(1)} async-done(((bf16[16,32,384]{2,1,0:T(8,128)(2,1)}), bf16[16,32,384]{2,1,0:T(8,128)(2,1)S(1)}, u32[]{:S(2)}, u32[]{:S(2)}) %all-to-all-start.2) | async-done | bytes 393248 | tf_op jit(solution)/shard_map/all_to_all | solution.py:18
  72.0 4.1 %all-to-all-start.1 = ((f16[8,72,384]{2,1,0:T(8,128)(2,1)}), f16[8,72,384]{2,1,0:T(8,128)(2,1)}, u32[]{:S(2)}, u32[]{:S(2)}) async-start(f16[8,72,384]{2,1,0:T(8,128)(2,1)} %concatenate.40), calls=%async_computation.1 | async-start | bytes 884736 | tf_op jit(solution)/shard_map/all_to_all | solution.py:18
  76.2 0.6 fusion.52
  76.9 1.6 concatenate.43
  78.5 3.8 %collective-permute-start.5 = (f32[392,512]{1,0:T(8,128)}, f32[392,512]{1,0:T(8,128)}, u32[]{:S(2)}, u32[]{:S(2)}) collective-permute-start(f32[392,512]{1,0:T(8,128)} %concatenate.43), channel_id=1, source_target_pairs={{0,1},{1,0},{2,3},{3,2},{4,5},{5,4},{6,7},{7,6},{8,9},{9,8},{10,11... | collective-permute-start | bytes 2408456 | tf_op jit(solution)/shard_map/ppermute | solution.py:59
  82.2 7.3 %all-to-all-done.1 = f16[8,72,384]{2,1,0:T(8,128)(2,1)} async-done(((f16[8,72,384]{2,1,0:T(8,128)(2,1)}), f16[8,72,384]{2,1,0:T(8,128)(2,1)}, u32[]{:S(2)}, u32[]{:S(2)}) %all-to-all-start.1) | async-done | bytes 442400 | tf_op jit(solution)/shard_map/all_to_all | solution.py:18
  89.5 0.8 slice.191
  90.4 1.1 multiply_reduce_fusion
  91.5 0.2 fusion.29
  91.7 0.2 convolution_add_fusion.2
  92.0 4.6 %collective-permute-start.4 = (f32[32,512]{1,0:T(8,128)S(1)}, f32[32,512]{1,0:T(8,128)S(1)}, u32[]{:S(2)}, u32[]{:S(2)}) collective-permute-start(f32[32,512]{1,0:T(8,128)S(1)} %constant_dynamic-slice_fusion.1), channel_id=1, source_target_pairs={{0,1},{1,0},{2,3},{3,2},{4,5},{5,4},{6,7},{7,6},{8,9},{9,8},{10,11... | collective-permute-start | bytes 196616 | tf_op jit(solution)/shard_map/ppermute | solution.py:59
  96.6 1.2 slice.197
  99.1 1.3 fusion.9
  100.5 2.8 %collective-permute-start.8 = (f16[104,512]{1,0:T(8,128)(2,1)S(1)}, f16[104,512]{1,0:T(8,128)(2,1)S(1)}, u32[]{:S(2)}, u32[]{:S(2)}) collective-permute-start(f16[104,512]{1,0:T(8,128)(2,1)S(1)} %get-tuple-element.26), channel_id=1, source_target_pairs={{0,12},{4,0},{8,4},{12,8},{1,13},{5,1},{9,5},{13,9},{2,14},{6,2},{... | collective-permute-start | bytes 319496 | tf_op jit(solution)/shard_map/ppermute | solution.py:63
  103.4 2.8 %collective-permute-start.7 = (f16[104,512]{1,0:T(8,128)(2,1)S(1)}, f16[104,512]{1,0:T(8,128)(2,1)S(1)}, u32[]{:S(2)}, u32[]{:S(2)}) collective-permute-start(f16[104,512]{1,0:T(8,128)(2,1)S(1)} %get-tuple-element.25), channel_id=1, source_target_pairs={{0,8},{4,12},{8,0},{12,4},{1,9},{5,13},{9,1},{13,5},{2,10},{6,14},... | collective-permute-start | bytes 319496 | tf_op jit(solution)/shard_map/ppermute | solution.py:63
  106.2 1.9 collective-permute-start.6
  108.2 5.1 %collective-permute-done.6 = f16[104,512]{1,0:T(8,128)(2,1)S(1)} collective-permute-done((f16[104,512]{1,0:T(8,128)(2,1)S(1)}, f16[104,512]{1,0:T(8,128)(2,1)S(1)}, u32[]{:S(2)}, u32[]{:S(2)}) %collective-permute-start.6) | collective-permute-done | bytes 106528 | tf_op jit(solution)/shard_map/ppermute | solution.py:63
  113.3 0.5 slice.204
  114.4 0.5 slice.205
  115.6 0.5 slice.206
  117.1 2.1 %collective-permute-start.9 = (f16[136,512]{1,0:T(8,128)(2,1)S(1)}, f16[136,512]{1,0:T(8,128)(2,1)S(1)}, u32[]{:S(2)}, u32[]{:S(2)}) collective-permute-start(f16[136,512]{1,0:T(8,128)(2,1)S(1)} %concatenate.46), channel_id=1, source_target_pairs={{0,2},{2,0},{1,3},{3,1},{4,6},{6,4},{5,7},{7,5},{8,10},{10,8},{9,1... | collective-permute-start | bytes 417800 | tf_op jit(solution)/shard_map/ppermute | solution.py:59
  119.2 7.7 %collective-permute-done.9 = f16[136,512]{1,0:T(8,128)(2,1)S(1)} collective-permute-done((f16[136,512]{1,0:T(8,128)(2,1)S(1)}, f16[136,512]{1,0:T(8,128)(2,1)S(1)}, u32[]{:S(2)}, u32[]{:S(2)}) %collective-permute-start.9) | collective-permute-done | bytes 139296 | tf_op jit(solution)/shard_map/ppermute | solution.py:59
  126.9 0.5 slice.209
  128.2 0.8 broadcast_in_dim.25
  129.1 3.6 %all-to-all-start.3 = ((f16[4,136,512]{2,1,0:T(8,128)(2,1)}), f16[4,136,512]{2,1,0:T(8,128)(2,1)S(1)}, u32[]{:S(2)}, u32[]{:S(2)}) async-start(f16[4,136,512]{2,1,0:T(8,128)(2,1)} %broadcast_in_dim.25), calls=%async_computation.3 | async-start | bytes 1114112 | tf_op jit(solution)/shard_map/all_to_all | solution.py:18
  133.4 4.9 %all-to-all-done.3 = f16[4,136,512]{2,1,0:T(8,128)(2,1)S(1)} async-done(((f16[4,136,512]{2,1,0:T(8,128)(2,1)}), f16[4,136,512]{2,1,0:T(8,128)(2,1)S(1)}, u32[]{:S(2)}, u32[]{:S(2)}) %all-to-all-start.3) | async-done | bytes 557088 | tf_op jit(solution)/shard_map/all_to_all | solution.py:18
  138.4 0.6 slice_reduce_fusion.1
  139.9 0.7 concatenate.48
  140.6 0.8 broadcast_in_dim.27
  141.5 3.5 %all-to-all-start.4 = ((f16[4,136,512]{2,1,0:T(8,128)(2,1)}), f16[4,136,512]{2,1,0:T(8,128)(2,1)S(1)}, u32[]{:S(2)}, u32[]{:S(2)}) async-start(f16[4,136,512]{2,1,0:T(8,128)(2,1)} %broadcast_in_dim.27), calls=%async_computation.4 | async-start | bytes 1114112 | tf_op jit(solution)/shard_map/all_to_all | solution.py:18
  145.6 6.4 %all-to-all-done.4 = f16[4,136,512]{2,1,0:T(8,128)(2,1)S(1)} async-done(((f16[4,136,512]{2,1,0:T(8,128)(2,1)}), f16[4,136,512]{2,1,0:T(8,128)(2,1)S(1)}, u32[]{:S(2)}, u32[]{:S(2)}) %all-to-all-start.4) | async-done | bytes 557088 | tf_op jit(solution)/shard_map/all_to_all | solution.py:18
  152.2 7.9 %all_gather.11 = f32[64,512]{1,0:T(8,128)S(1)} all-gather(f32[32,512]{1,0:T(8,128)S(1)} %multiply_reduce_fusion.1), channel_id=1, replica_groups=mesh['yp'=4,'yb'=2,'zp'=2,'zb'=2,'x'=4,'zh'=2,'c'=2] {'c'}, dimensions={0}, use_global_device_ids=true | all-gather | bytes 196608 | tf_op jit(solution)/shard_map/all_gather | solution.py:149
  160.3 0.8 abs_reduce_fusion.2
  161.8 0.6 slice_reduce_fusion
  163.2 0.8 broadcast_in_dim.28
  164.0 6.7 %all-to-all-start.5 = ((f16[8,72,384]{2,1,0:T(8,128)(2,1)}), f16[8,72,384]{2,1,0:T(8,128)(2,1)S(1)}, u32[]{:S(2)}, u32[]{:S(2)}) async-start(f16[8,72,384]{2,1,0:T(8,128)(2,1)} %broadcast_in_dim.28), calls=%async_computation.5 | async-start | bytes 884736 | tf_op jit(solution)/shard_map/all_to_all | solution.py:18
  170.8 2.6 %all_gather.10 = f16[768,512]{1,0:T(8,128)(2,1)S(1)} all-gather(f16[384,512]{1,0:T(8,128)(2,1)S(1)} %bitcast.135), channel_id=1, replica_groups=mesh['yp'=4,'yb'=2,'zp'=2,'zb'=2,'x'=4,'zh'=2,'c'=2] {'c'}, dimensions={0}, use_global_device_ids=true | all-gather | bytes 1179648 | tf_op jit(solution)/shard_map/all_gather | solution.py:150
  173.4 0.6 fusion.7
  174.0 0.6 convolution_add_fusion.1
  174.6 7.1 %all-to-all-done.5 = f16[8,72,384]{2,1,0:T(8,128)(2,1)S(1)} async-done(((f16[8,72,384]{2,1,0:T(8,128)(2,1)}), f16[8,72,384]{2,1,0:T(8,128)(2,1)S(1)}, u32[]{:S(2)}, u32[]{:S(2)}) %all-to-all-start.5) | async-done | bytes 442400 | tf_op jit(solution)/shard_map/all_to_all | solution.py:18
  181.9 0.6 fusion.53
  182.5 1.2 abs_reduce_fusion
  184.6 0.9 concatenate.50
  185.5 8.6 %all-to-all-start.6 = ((f16[4,200,384]{2,1,0:T(8,128)(2,1)}), f16[4,200,384]{2,1,0:T(8,128)(2,1)S(1)}, u32[]{:S(2)}, u32[]{:S(2)}) async-start(f16[4,200,384]{2,1,0:T(8,128)(2,1)} %concatenate.50), calls=%async_computation.6 | async-start | bytes 1228800 | tf_op jit(solution)/shard_map/all_to_all | solution.py:18
  194.1 8.3 %all-to-all-done.6 = f16[4,200,384]{2,1,0:T(8,128)(2,1)S(1)} async-done(((f16[4,200,384]{2,1,0:T(8,128)(2,1)}), f16[4,200,384]{2,1,0:T(8,128)(2,1)S(1)}, u32[]{:S(2)}, u32[]{:S(2)}) %all-to-all-start.6) | async-done | bytes 614432 | tf_op jit(solution)/shard_map/all_to_all | solution.py:18
  202.7 0.8 copy-done.1
  203.5 0.7 fusion.14
  204.2 1.0 maximum_add_fusion
  (84 shorter events, 2.8 us)
Async XLA Ops:
  1.4 30.3 %collective-permute-start.3 = (bf16[16,1536]{1,0:T(8,128)(2,1)S(1)}, bf16[16,1536]{1,0:T(8,128)(2,1)S(1)}, u32[]{:S(2)}, u32[]{:S(2)}) collective-permute-start(bf16[16,1536]{1,0:T(8,128)(2,1)S(1)} %pad_maximum_fusion.8), channel_id=1, source_target_pairs={{0,32},{32,0},{1,33},{33,1},{2,34},{34,2},{3,35},{35,3},{4,36},{36... | collective-permute-start | bytes 147464 | tf_op jit(solution)/shard_map/ppermute | solution.py:59
  9.2 10.3 %copy-start.4 = (bf16[192,32]{0,1:T(8,128)(2,1)S(1)}, bf16[192,32]{0,1:T(8,128)(2,1)}, u32[]{:S(2)}) copy-start(bf16[192,32]{0,1:T(8,128)(2,1)} %param.15) | copy-start | bytes 36868
  9.2 10.3 %copy-start.5 = (bf16[192,32]{0,1:T(8,128)(2,1)S(1)}, bf16[192,32]{0,1:T(8,128)(2,1)}, u32[]{:S(2)}) copy-start(bf16[192,32]{0,1:T(8,128)(2,1)} %param.13) | copy-start | bytes 36868
  10.2 21.5 %copy-start.2 = (bf16[1152,16]{0,1:T(8,128)(2,1)S(1)}, bf16[1152,16]{0,1:T(8,128)(2,1)}, u32[]{:S(2)}) copy-start(bf16[1152,16]{0,1:T(8,128)(2,1)} %param.14) | copy-start | bytes 110596
  10.3 21.5 %copy-start.3 = (bf16[384,16]{0,1:T(8,128)(2,1)S(1)}, bf16[384,16]{0,1:T(8,128)(2,1)}, u32[]{:S(2)}) copy-start(bf16[384,16]{0,1:T(8,128)(2,1)} %param.16) | copy-start | bytes 36868
  10.3 21.5 %collective-permute-start.2 = (bf16[192,384]{1,0:T(8,128)(2,1)S(1)}, bf16[192,384]{1,0:T(8,128)(2,1)S(1)}, u32[]{:S(2)}, u32[]{:S(2)}) collective-permute-start(bf16[192,384]{1,0:T(8,128)(2,1)S(1)} %get-tuple-element.14), channel_id=1, source_target_pairs={{0,80},{16,64},{64,16},{80,0},{1,81},{17,65},{65,17},{81,1},{2,82}... | collective-permute-start | bytes 442376 | tf_op jit(solution)/shard_map/ppermute | solution.py:114
  15.4 16.5 %collective-permute-start.1 = (bf16[192,384]{1,0:T(8,128)(2,1)S(1)}, bf16[192,384]{1,0:T(8,128)(2,1)S(1)}, u32[]{:S(2)}, u32[]{:S(2)}) collective-permute-start(bf16[192,384]{1,0:T(8,128)(2,1)S(1)} %get-tuple-element.15), channel_id=1, source_target_pairs={{0,64},{16,80},{64,0},{80,16},{1,65},{17,81},{65,1},{81,17},{2,66}... | collective-permute-start | bytes 442376 | tf_op jit(solution)/shard_map/ppermute | solution.py:114
  17.5 14.4 %collective-permute-start = (bf16[192,384]{1,0:T(8,128)(2,1)S(1)}, bf16[192,384]{1,0:T(8,128)(2,1)S(1)}, u32[]{:S(2)}, u32[]{:S(2)}) collective-permute-start(bf16[192,384]{1,0:T(8,128)(2,1)S(1)} %get-tuple-element.16), channel_id=1, source_target_pairs={{0,16},{16,0},{64,80},{80,64},{1,17},{17,1},{65,81},{81,65},{2,18}... | collective-permute-start | bytes 442376 | tf_op jit(solution)/shard_map/ppermute | solution.py:114
  20.4 27.9 %all-to-all-start = ((bf16[32,32,192]{2,1,0:T(8,128)(2,1)}), bf16[32,32,192]{2,1,0:T(8,128)(2,1)S(1)}, u32[]{:S(2)}, u32[]{:S(2)}) async-start(bf16[32,32,192]{2,1,0:T(8,128)(2,1)} %bitcast.4), calls=%async_computation | async-start | bytes 1048576 | tf_op jit(solution)/shard_map/all_to_all | solution.py:18
  49.0 23.0 %all-to-all-start.2 = ((bf16[16,32,384]{2,1,0:T(8,128)(2,1)}), bf16[16,32,384]{2,1,0:T(8,128)(2,1)S(1)}, u32[]{:S(2)}, u32[]{:S(2)}) async-start(bf16[16,32,384]{2,1,0:T(8,128)(2,1)} %bitcast.29), calls=%async_computation.2 | async-start | bytes 786432 | tf_op jit(solution)/shard_map/all_to_all | solution.py:18
  72.0 17.5 %all-to-all-start.1 = ((f16[8,72,384]{2,1,0:T(8,128)(2,1)}), f16[8,72,384]{2,1,0:T(8,128)(2,1)}, u32[]{:S(2)}, u32[]{:S(2)}) async-start(f16[8,72,384]{2,1,0:T(8,128)(2,1)} %concatenate.40), calls=%async_computation.1 | async-start | bytes 884736 | tf_op jit(solution)/shard_map/all_to_all | solution.py:18
  78.5 18.1 %collective-permute-start.5 = (f32[392,512]{1,0:T(8,128)}, f32[392,512]{1,0:T(8,128)}, u32[]{:S(2)}, u32[]{:S(2)}) collective-permute-start(f32[392,512]{1,0:T(8,128)} %concatenate.43), channel_id=1, source_target_pairs={{0,1},{1,0},{2,3},{3,2},{4,5},{5,4},{6,7},{7,6},{8,9},{9,8},{10,11... | collective-permute-start | bytes 2408456 | tf_op jit(solution)/shard_map/ppermute | solution.py:59
  92.0 16.2 %collective-permute-start.4 = (f32[32,512]{1,0:T(8,128)S(1)}, f32[32,512]{1,0:T(8,128)S(1)}, u32[]{:S(2)}, u32[]{:S(2)}) collective-permute-start(f32[32,512]{1,0:T(8,128)S(1)} %constant_dynamic-slice_fusion.1), channel_id=1, source_target_pairs={{0,1},{1,0},{2,3},{3,2},{4,5},{5,4},{6,7},{7,6},{8,9},{9,8},{10,11... | collective-permute-start | bytes 196616 | tf_op jit(solution)/shard_map/ppermute | solution.py:59
  100.5 15.1 %collective-permute-start.8 = (f16[104,512]{1,0:T(8,128)(2,1)S(1)}, f16[104,512]{1,0:T(8,128)(2,1)S(1)}, u32[]{:S(2)}, u32[]{:S(2)}) collective-permute-start(f16[104,512]{1,0:T(8,128)(2,1)S(1)} %get-tuple-element.26), channel_id=1, source_target_pairs={{0,12},{4,0},{8,4},{12,8},{1,13},{5,1},{9,5},{13,9},{2,14},{6,2},{... | collective-permute-start | bytes 319496 | tf_op jit(solution)/shard_map/ppermute | solution.py:63
  103.4 11.1 %collective-permute-start.7 = (f16[104,512]{1,0:T(8,128)(2,1)S(1)}, f16[104,512]{1,0:T(8,128)(2,1)S(1)}, u32[]{:S(2)}, u32[]{:S(2)}) collective-permute-start(f16[104,512]{1,0:T(8,128)(2,1)S(1)} %get-tuple-element.25), channel_id=1, source_target_pairs={{0,8},{4,12},{8,0},{12,4},{1,9},{5,13},{9,1},{13,5},{2,10},{6,14},... | collective-permute-start | bytes 319496 | tf_op jit(solution)/shard_map/ppermute | solution.py:63
  106.2 7.1 %collective-permute-start.6 = (f16[104,512]{1,0:T(8,128)(2,1)S(1)}, f16[104,512]{1,0:T(8,128)(2,1)S(1)}, u32[]{:S(2)}, u32[]{:S(2)}) collective-permute-start(f16[104,512]{1,0:T(8,128)(2,1)S(1)} %get-tuple-element.24), channel_id=1, source_target_pairs={{0,4},{4,8},{8,12},{12,0},{1,5},{5,9},{9,13},{13,1},{2,6},{6,10},{... | collective-permute-start | bytes 319496 | tf_op jit(solution)/shard_map/ppermute | solution.py:63
  117.1 9.8 %collective-permute-start.9 = (f16[136,512]{1,0:T(8,128)(2,1)S(1)}, f16[136,512]{1,0:T(8,128)(2,1)S(1)}, u32[]{:S(2)}, u32[]{:S(2)}) collective-permute-start(f16[136,512]{1,0:T(8,128)(2,1)S(1)} %concatenate.46), channel_id=1, source_target_pairs={{0,2},{2,0},{1,3},{3,1},{4,6},{6,4},{5,7},{7,5},{8,10},{10,8},{9,1... | collective-permute-start | bytes 417800 | tf_op jit(solution)/shard_map/ppermute | solution.py:59
  129.1 9.3 %all-to-all-start.3 = ((f16[4,136,512]{2,1,0:T(8,128)(2,1)}), f16[4,136,512]{2,1,0:T(8,128)(2,1)S(1)}, u32[]{:S(2)}, u32[]{:S(2)}) async-start(f16[4,136,512]{2,1,0:T(8,128)(2,1)} %broadcast_in_dim.25), calls=%async_computation.3 | async-start | bytes 1114112 | tf_op jit(solution)/shard_map/all_to_all | solution.py:18
  139.9 5.1 %copy-start.6 = (f32[512]{0:T(512)S(1)}, f32[512]{0:T(512)}, u32[]{:S(2)}) copy-start(f32[512]{0:T(512)} %param.19) | copy-start | bytes 6148
  139.9 5.1 %copy-start.7 = (f32[512]{0:T(512)S(1)}, f32[512]{0:T(512)}, u32[]{:S(2)}) copy-start(f32[512]{0:T(512)} %param.17) | copy-start | bytes 6148
  139.9 5.1 %copy-start.8 = (f32[512]{0:T(512)S(1)}, f32[512]{0:T(512)}, u32[]{:S(2)}) copy-start(f32[512]{0:T(512)} %param.20) | copy-start | bytes 6148
  139.9 5.1 %copy-start.9 = (f32[512]{0:T(512)S(1)}, f32[512]{0:T(512)}, u32[]{:S(2)}) copy-start(f32[512]{0:T(512)} %param.18) | copy-start | bytes 6148
  141.5 10.6 %all-to-all-start.4 = ((f16[4,136,512]{2,1,0:T(8,128)(2,1)}), f16[4,136,512]{2,1,0:T(8,128)(2,1)S(1)}, u32[]{:S(2)}, u32[]{:S(2)}) async-start(f16[4,136,512]{2,1,0:T(8,128)(2,1)} %broadcast_in_dim.27), calls=%async_computation.4 | async-start | bytes 1114112 | tf_op jit(solution)/shard_map/all_to_all | solution.py:18
  164.0 17.7 %all-to-all-start.5 = ((f16[8,72,384]{2,1,0:T(8,128)(2,1)}), f16[8,72,384]{2,1,0:T(8,128)(2,1)S(1)}, u32[]{:S(2)}, u32[]{:S(2)}) async-start(f16[8,72,384]{2,1,0:T(8,128)(2,1)} %broadcast_in_dim.28), calls=%async_computation.5 | async-start | bytes 884736 | tf_op jit(solution)/shard_map/all_to_all | solution.py:18
  185.5 16.9 %all-to-all-start.6 = ((f16[4,200,384]{2,1,0:T(8,128)(2,1)}), f16[4,200,384]{2,1,0:T(8,128)(2,1)S(1)}, u32[]{:S(2)}, u32[]{:S(2)}) async-start(f16[4,200,384]{2,1,0:T(8,128)(2,1)} %concatenate.50), calls=%async_computation.6 | async-start | bytes 1228800 | tf_op jit(solution)/shard_map/all_to_all | solution.py:18
  202.6 0.9 copy-start.1
  202.6 1.7 copy-start

commit v8 on v5

v8 whole, which is shorter than its diff:
```python
import jax
import jax.numpy as jnp
from jax import lax
from jax.sharding import Mesh, PartitionSpec as P

FSDP = ("yp", "yb", "zp", "zb")
COL = ("x", "zh", "c")
QUAD = ("yb", "zb")
OCT = ("yp", "zp")
ROUND = (8, 7)


def shifted(eigen, damp):
    return 1.0 / (eigen + damp) - 1.0 / damp


def exchange(blocks, axes):
    return lax.all_to_all(blocks, axes, 0, 0, tiled=True)


def halves(wide):
    high = lax.reduce_precision(wide, *ROUND)
    return high.astype(jnp.bfloat16), (wide - high).astype(jnp.bfloat16)


def dot_wide_left(wide, narrow, dims):
    high, low = halves(wide)
    dot = lambda part: lax.dot_general(part, narrow, (dims, ((), ())), preferred_element_type=jnp.float32)
    return dot(high) + dot(low)


def dot_wide_right(narrow, wide, dims):
    high, low = halves(wide)
    dot = lambda part: lax.dot_general(narrow, part, (dims, ((), ())), preferred_element_type=jnp.float32)
    return dot(high) + dot(low)


def pack(values, power):
    scaled = (values * jnp.exp2(14.0 - power)).astype(jnp.float16)
    tail = jnp.broadcast_to(power.astype(jnp.float16), values.shape[:-2] + (8, values.shape[-1]))
    return jnp.concatenate([scaled, tail], axis=-2)


def unpack(packed):
    rows = packed.shape[-2] - 8
    power = packed[..., rows : rows + 1, :].astype(jnp.float32)
    return packed[..., :rows, :].astype(jnp.float32) * jnp.exp2(power - 14.0)


def power_of(bound):
    return jnp.clip(jnp.floor(jnp.log2(jnp.maximum(bound, 1e-30))) + 1.0, -100.0, 120.0)


def top(values):
    return jnp.max(jnp.abs(values)).astype(jnp.float32)


def swap(values, axis):
    return lax.ppermute(values, axis, [(0, 1), (1, 0)])


def around(values, axis, size, step):
    return lax.ppermute(values, axis, [(i, (i + step) % size) for i in range(size)])


def core_part(values, core, own):
    half = values.shape[0] // 2
    return lax.dynamic_slice_in_dim(values, (core if own else 1 - core) * half, half, 0)


def local(
    joined_gradient,
    output_gradient,
    joined_left_basis,
    joined_right_basis,
    output_left_basis,
    output_right_basis,
    joined_left_eigen,
    joined_right_eigen,
    output_left_eigen,
    output_right_eigen,
    damping,
):
    damp = damping[0]
    quad = lax.axis_index("yb") * 2 + lax.axis_index("zb")
    octant = lax.axis_index("yp") * 2 + lax.axis_index("zp")
    core = lax.axis_index("c")
    is_output = quad == 3
    left_shift = shifted(jnp.where(is_output, output_left_eigen, joined_left_eigen), damp)
    right_shift = shifted(jnp.where(is_output, output_right_eigen, joined_right_eigen), damp)
    left_shift = left_shift.reshape(4, 2, 2, 32).transpose(2, 0, 1, 3)
    left_shift = jnp.where(lax.axis_index("zh") == 1, left_shift[:, :, ::-1], left_shift).reshape(512)
    own_shift = lax.dynamic_slice_in_dim(left_shift, octant * 64, 64, 0)
    right_shift = right_shift.reshape(4, 2, 2, 2, 16).transpose(0, 1, 3, 2, 4).reshape(4, 4, 2, 16)[::-1]
    right_shift = jnp.where(lax.axis_index("zp") == 1, right_shift[:, :, ::-1], right_shift).reshape(4, 128)
    right_shift = jnp.concatenate([right_shift, right_shift], axis=0)
    right_shift = lax.dynamic_slice_in_dim(right_shift, 3 - lax.axis_index("yp"), 4, 0).reshape(512)

    right = jnp.concatenate([joined_right_basis.T, output_right_basis.T], axis=1)
    right = jnp.concatenate([right, swap(right, "zp")], axis=0)
    lefts = [jnp.concatenate([basis.T[:16], basis.T[16:]], axis=1) for basis in (joined_left_basis, output_left_basis)]
    left = jnp.concatenate(lefts, axis=0)
    other = swap(left, "zh")
    lefts = [jnp.concatenate([left[rows], other[rows]], axis=0) for rows in (slice(0, 16), slice(16, 32))]
    lefts = (lefts[0], lefts[0], lefts[0], lefts[1])
    gradients = (joined_gradient[:, :384], joined_gradient[:, 384:768], joined_gradient[:, 768:], output_gradient)
    sent = jnp.stack(
        [
            jnp.concatenate([gradients[j], right[:, 384 * j : 384 * j + 384], lefts[j]], axis=0)
            for j in range(4)
        ]
    )
    got = exchange(sent, QUAD)
    gradient = got[:, :192].reshape(768, 384)
    most = top(gradient)

    left = got[:, 224:].reshape(4, 2, 16, 384)
    left = jnp.stack([left[..., :192], left[..., 192:]], axis=2).reshape(4, 64, 192)
    left = jnp.concatenate([left[0], left[1], left[2], left[3]], axis=1)
    left = exchange(jnp.broadcast_to(left[None], (4, 64, 768)), "x").reshape(256, 768)
    left = lax.all_gather(left, "c", axis=0, tiled=True)

    right = got[:, 192:224].reshape(128, 384)
    right = jnp.concatenate([right] + [around(right, "yp", 4, step) for step in (1, 2, 3)], axis=0)

    rows = jnp.dot(left, gradient, preferred_element_type=jnp.float32)
    rows = pack(rows.reshape(8, 64, 384), power_of(most * 60.0))
    rows = jnp.sum(unpack(exchange(rows, OCT)), axis=0) * own_shift[:, None]
    rows = pack(rows, power_of(top(rows)))
    rows = exchange(jnp.broadcast_to(rows[None], (8, 72, 384)), OCT)
    limit = jnp.max(rows[:, 64, 0]).astype(jnp.float32)
    limit = most / damp + 40.0 * jnp.exp2(limit)
    rows = unpack(rows).reshape(512, 384)

    lifted = dot_wide_right(left, rows, ((0,), (0,)))
    applied = gradient.astype(jnp.float32) / damp + lifted
    cols = dot_wide_left(applied, right, ((1,), (1,)))
    other = jnp.concatenate([core_part(cols, core, False), jnp.broadcast_to(limit, (8, 512))], axis=0)
    other = swap(other, "c")
    power = power_of(jnp.maximum(limit, other[384, 0]) * 864.0)
    cols = (core_part(cols, core, True) + other[:384]).reshape(4, 96, 512)
    cols = exchange(pack(cols, power), "x")
    power = jnp.max(cols[:, 96, 0]).astype(jnp.float32)
    cols = jnp.sum(unpack(cols), axis=0)
    other = swap(pack(cols, power), "zh")
    power = jnp.maximum(power, other[96, 0].astype(jnp.float32))
    cols = cols + unpack(other)
    cols = exchange(jnp.broadcast_to(pack(cols, power)[None], (4, 104, 512)), QUAD)
    power = jnp.max(cols[:, 96, 0]).astype(jnp.float32)
    same = (lax.broadcasted_iota(jnp.int32, (4, 1, 1), 0) == 3) == is_output
    cols = jnp.sum(jnp.where(same, unpack(cols), 0.0), axis=0)
    cols = (cols * jnp.exp2(14.0 - power)).astype(jnp.float16)
    cols = exchange(jnp.broadcast_to(cols[None], (4, 96, 512)), "x").reshape(384, 512)
    cols = lax.all_gather(cols, "c", axis=0, tiled=True)
    cols = cols.astype(jnp.float32) * jnp.exp2(power - 14.0)

    update = lifted / damp + dot_wide_left(cols * right_shift[None, :], right, ((1,), (0,)))
    update = unpack(exchange(pack(update.reshape(4, 192, 384), power_of(top(update))), QUAD))
    joined_update = jnp.concatenate([update[0], update[1], update[2]], axis=1) + joined_gradient.astype(jnp.float32) / damp / damp
    output_update = update[3] + output_gradient.astype(jnp.float32) / damp / damp
    return joined_update, output_update


def solution(mesh):
    fine = Mesh(mesh.devices.reshape(4, 2, 2, 2, 4, 2, 2), ("yp", "yb", "zp", "zb", "x", "zh", "c"))
    placed = (
        P(FSDP, COL),
        P(FSDP, COL),
        P(FSDP, COL),
        P(COL, FSDP),
        P(FSDP, COL),
        P(COL, FSDP),
        P(),
        P(),
        P(),
        P(),
        P(),
    )
    return jax.shard_map(
        local,
        mesh=fine,
        in_specs=placed,
        out_specs=(P(FSDP, COL), P(FSDP, COL)),
        check_vma=False,
    )
```

time: 205 us -> 190 us (0.927)
  starting transfers between devices: 90.2 us -> 69.5 us
  blocking collectives: 25.7 us -> 33.2 us
    all_to_all x6, starting transfers between devices: 47.2 us -> 32.3 us  [exchange(): return lax.all_to_all(blocks, axes, 0, 0, tiled=True)]
    all_to_all x1 -> x2, blocking collectives: 13 us -> 22.3 us  [exchange(): return lax.all_to_all(blocks, axes, 0, 0, tiled=True)]
    ppermute x3 -> x0, starting transfers between devices: 9.13 us -> none  [local(): got.append(lax.ppermute(block, QUAD, [(i, i ^ mask) for i in range(4)]))]
    ppermute x3, starting transfers between devices: 7.81 us -> 13.4 us  [around(): lax.ppermute(values, axis, [(i, (i + step) % size) for i in range(size)])]
    ppermute x5 -> x4, starting transfers between devices: 26.1 us -> 23.8 us  [swap(): return lax.ppermute(values, axis, [(0, 1), (1, 0)])]
    ppermute x5 -> x4, waiting for transfers between devices: 9.36 us -> 8.62 us  [swap(): return lax.ppermute(values, axis, [(0, 1), (1, 0)])]
  transfers between devices with their start and end apart: 17 -> 13, of which waited for: 8 -> 10; matrix products, arithmetic and copies ran while one was open for 7% -> 3% of each run, Pallas kernels for 0% -> 0%
where the time goes in v8:
time: 190 us; the launch traced here: 188 us
  starting transfers between devices  69.5 us (37%)
  waiting for transfers between devices  50.1 us (26%)
  blocking collectives  33.2 us (17%)
  local copies, waits for them, and re-layouts  11.5 us (6%)
  other arithmetic  9.31 us (5%)
  between operations  8.35 us (4%)
  matrix products  5.81 us (3%)
    all_to_all x6, waiting for transfers between devices, exchange(): return lax.all_to_all(blocks, axes, 0, 0, tiled=True)  40.8 us
    all_to_all x6, starting transfers between devices, exchange(): return lax.all_to_all(blocks, axes, 0, 0, tiled=True)  32.3 us
    ppermute x4, starting transfers between devices, swap(): return lax.ppermute(values, axis, [(0, 1), (1, 0)])  23.8 us
    all_to_all x2, blocking collectives, exchange(): return lax.all_to_all(blocks, axes, 0, 0, tiled=True)  22.3 us
    ppermute x3, starting transfers between devices, around(): lax.ppermute(values, axis, [(i, (i + step) % size) for i in range(size)])  13.4 us
    ppermute x4, waiting for transfers between devices, swap(): return lax.ppermute(values, axis, [(0, 1), (1, 0)])  8.62 us
    all_gather x1, blocking collectives, local(): left = lax.all_gather(left, 'c', axis=0, tiled=True)  7.07 us
    all_gather x1, blocking collectives, local(): cols = lax.all_gather(cols, 'c', axis=0, tiled=True)  3.83 us
  transfers between devices with their start and end apart: 13, of which 10 were waited for; matrix products, arithmetic and copies ran while one was open for 3% of the time, Pallas kernels for 0%

profile of v8, /device:TPU:1, one launch (start us, length us, event | category | flops | bytes accessed | tf_op | source)
XLA Modules:
  0.0 187.8 jit_solution(14362632741007955955)
XLA Ops:
  0.7 0.8 fusion.40
  1.5 11.5 %collective-permute-start.1 = (bf16[32,384]{1,0:T(8,128)(2,1)S(1)}, bf16[32,384]{1,0:T(8,128)(2,1)S(1)}, u32[]{:S(2)}, u32[]{:S(2)}) collective-permute-start(bf16[32,384]{1,0:T(8,128)(2,1)S(1)} %maximum_maximum_fusion), channel_id=1, source_target_pairs={{0,2},{2,0},{1,3},{3,1},{4,6},{6,4},{5,7},{7,5},{8,10},{10,8},{9,1... | collective-permute-start | bytes 73736 | tf_op jit(solution)/shard_map/ppermute | solution.py:59
  13.0 0.8 pad_maximum_fusion.8
  13.8 4.0 %collective-permute-start = (bf16[16,1536]{1,0:T(8,128)(2,1)S(1)}, bf16[16,1536]{1,0:T(8,128)(2,1)S(1)}, u32[]{:S(2)}, u32[]{:S(2)}) collective-permute-start(bf16[16,1536]{1,0:T(8,128)(2,1)S(1)} %pad_maximum_fusion.8), channel_id=1, source_target_pairs={{0,32},{32,0},{1,33},{33,1},{2,34},{34,2},{3,35},{35,3},{4,36},{36... | collective-permute-start | bytes 147464 | tf_op jit(solution)/shard_map/ppermute | solution.py:59
  17.8 1.1 fusion.37
  18.9 0.6 collective-permute-done
  19.5 0.7 pad_maximum_fusion.6
  20.4 0.1 pad_maximum_fusion
  20.5 11.9 %all_to_all.40 = bf16[4,256,384]{2,1,0:T(8,128)(2,1)S(1)} all-to-all(bf16[4,256,384]{2,1,0:T(8,128)(2,1)S(1)} %pad_maximum_fusion), channel_id=1, replica_groups=mesh['yp'=4,'yb'=2,'zp'=2,'zb'=2,'x'=4,'zh'=2,'c'=2] {'yb','zb'}, dimensions={0} | all-to-all | bytes 1572864 | tf_op jit(solution)/shard_map/all_to_all | solution.py:18
  32.6 0.1 pad_maximum_fusion.7
  32.7 0.8 broadcast_in_dim.16
  33.5 4.0 %all-to-all-start.1 = ((bf16[4,64,768]{2,1,0:T(8,128)(2,1)}), bf16[4,64,768]{2,1,0:T(8,128)(2,1)S(1)}, u32[]{:S(2)}, u32[]{:S(2)}) async-start(bf16[4,64,768]{2,1,0:T(8,128)(2,1)} %broadcast_in_dim.16), calls=%async_computation.1 | async-start | bytes 786432 | tf_op jit(solution)/shard_map/all_to_all | solution.py:18
  37.5 0.7 abs_reduce_fusion.1
  38.9 4.8 %all-to-all-done.1 = bf16[4,64,768]{2,1,0:T(8,128)(2,1)S(1)} async-done(((bf16[4,64,768]{2,1,0:T(8,128)(2,1)}), bf16[4,64,768]{2,1,0:T(8,128)(2,1)S(1)}, u32[]{:S(2)}, u32[]{:S(2)}) %all-to-all-start.1) | async-done | bytes 393248 | tf_op jit(solution)/shard_map/all_to_all | solution.py:18
  43.7 7.1 %all_gather.6 = bf16[512,768]{1,0:T(8,128)(2,1)S(1)} all-gather(bf16[256,768]{1,0:T(8,128)(2,1)S(1)} %bitcast.87), channel_id=1, replica_groups=mesh['yp'=4,'yb'=2,'zp'=2,'zb'=2,'x'=4,'zh'=2,'c'=2] {'c'}, dimensions={0}, use_global_device_ids=true | all-gather | bytes 1179648 | tf_op jit(solution)/shard_map/all_gather | solution.py:121
  50.8 0.6 fusion.2
  51.4 0.8 concatenate.74
  52.2 8.3 %all-to-all-start.2 = ((f16[8,72,384]{2,1,0:T(8,128)(2,1)}), f16[8,72,384]{2,1,0:T(8,128)(2,1)S(1)}, u32[]{:S(2)}, u32[]{:S(2)}) async-start(f16[8,72,384]{2,1,0:T(8,128)(2,1)} %concatenate.74), calls=%async_computation.2 | async-start | bytes 884736 | tf_op jit(solution)/shard_map/all_to_all | solution.py:18
  61.5 12.6 %all-to-all-done.2 = f16[8,72,384]{2,1,0:T(8,128)(2,1)S(1)} async-done(((f16[8,72,384]{2,1,0:T(8,128)(2,1)}), f16[8,72,384]{2,1,0:T(8,128)(2,1)S(1)}, u32[]{:S(2)}, u32[]{:S(2)}) %all-to-all-start.2) | async-done | bytes 442400 | tf_op jit(solution)/shard_map/all_to_all | solution.py:18
  74.2 0.7 abs_reduce_fusion.2
  75.8 0.8 broadcast_in_dim.17
  76.6 5.2 %all-to-all-start.3 = ((f16[8,72,384]{2,1,0:T(8,128)(2,1)}), f16[8,72,384]{2,1,0:T(8,128)(2,1)S(1)}, u32[]{:S(2)}, u32[]{:S(2)}) async-start(f16[8,72,384]{2,1,0:T(8,128)(2,1)} %broadcast_in_dim.17), calls=%async_computation.3 | async-start | bytes 884736 | tf_op jit(solution)/shard_map/all_to_all | solution.py:18
  81.8 5.5 %collective-permute-start.4 = (bf16[128,384]{1,0:T(8,128)(2,1)S(1)}, bf16[128,384]{1,0:T(8,128)(2,1)S(1)}, u32[]{:S(2)}, u32[]{:S(2)}) collective-permute-start(bf16[128,384]{1,0:T(8,128)(2,1)S(1)} %bitcast.88), channel_id=1, source_target_pairs={{0,384},{128,0},{256,128},{384,256},{1,385},{129,1},{257,129},{385... | collective-permute-start | bytes 294920 | tf_op jit(solution)/shard_map/ppermute | solution.py:63
  87.3 4.0 %collective-permute-start.3 = (bf16[128,384]{1,0:T(8,128)(2,1)S(1)}, bf16[128,384]{1,0:T(8,128)(2,1)S(1)}, u32[]{:S(2)}, u32[]{:S(2)}) collective-permute-start(bf16[128,384]{1,0:T(8,128)(2,1)S(1)} %bitcast.89), channel_id=1, source_target_pairs={{0,256},{128,384},{256,0},{384,128},{1,257},{129,385},{257,1},{385... | collective-permute-start | bytes 294920 | tf_op jit(solution)/shard_map/ppermute | solution.py:63
  91.3 4.0 %collective-permute-start.2 = (bf16[128,384]{1,0:T(8,128)(2,1)S(1)}, bf16[128,384]{1,0:T(8,128)(2,1)S(1)}, u32[]{:S(2)}, u32[]{:S(2)}) collective-permute-start(bf16[128,384]{1,0:T(8,128)(2,1)S(1)} %bitcast.90), channel_id=1, source_target_pairs={{0,128},{128,256},{256,384},{384,0},{1,129},{129,257},{257,385},{3... | collective-permute-start | bytes 294920 | tf_op jit(solution)/shard_map/ppermute | solution.py:63
  96.1 0.1 fusion.4
  96.2 0.6 fusion.42
  96.8 0.5 copy-done.3
  97.2 1.6 divide_add_fusion
  98.9 0.6 slice_reduce_fusion
  100.2 0.4 collective-permute-done.3
  100.6 0.3 collective-permute-done.2
  100.9 0.6 fusion.13
  101.5 0.6 convolution_add_fusion
  102.2 4.9 %collective-permute-start.5 = (f32[392,512]{1,0:T(8,128)S(1)}, f32[392,512]{1,0:T(8,128)}, u32[]{:S(2)}, u32[]{:S(2)}) collective-permute-start(f32[392,512]{1,0:T(8,128)S(1)} %concatenate.77), channel_id=1, source_target_pairs={{0,1},{1,0},{2,3},{3,2},{4,5},{5,4},{6,7},{7,6},{8,9},{9,8},{10,11... | collective-permute-start | bytes 2408456 | tf_op jit(solution)/shard_map/ppermute | solution.py:59
  107.1 2.0 %collective-permute-done.5 = f32[392,512]{1,0:T(8,128)} collective-permute-done((f32[392,512]{1,0:T(8,128)S(1)}, f32[392,512]{1,0:T(8,128)}, u32[]{:S(2)}, u32[]{:S(2)}) %collective-permute-start.5) | collective-permute-done | bytes 802848 | tf_op jit(solution)/shard_map/ppermute | solution.py:59
  109.2 1.2 slice.207
  111.1 1.3 fusion.8
  112.5 10.4 %all_to_all.41 = f16[4,104,512]{2,1,0:T(8,128)(2,1)S(1)} all-to-all(f16[4,104,512]{2,1,0:T(8,128)(2,1)S(1)} %concatenate.78), channel_id=1, replica_groups=mesh['yp'=4,'yb'=2,'zp'=2,'zb'=2,'x'=4,'zh'=2,'c'=2] {'x'}, dimensions={0} | all-to-all | bytes 851968 | tf_op jit(solution)/shard_map/all_to_all | solution.py:18
  122.9 0.6 slice_reduce_fusion.2
  124.4 0.7 concatenate.79
  125.1 3.5 %collective-permute-start.6 = (f16[104,512]{1,0:T(8,128)(2,1)S(1)}, f16[104,512]{1,0:T(8,128)(2,1)S(1)}, u32[]{:S(2)}, u32[]{:S(2)}) collective-permute-start(f16[104,512]{1,0:T(8,128)(2,1)S(1)} %concatenate.79), channel_id=1, source_target_pairs={{0,2},{2,0},{1,3},{3,1},{4,6},{6,4},{5,7},{7,5},{8,10},{10,8},{9,1... | collective-permute-start | bytes 319496 | tf_op jit(solution)/shard_map/ppermute | solution.py:59
  128.5 6.0 %collective-permute-done.6 = f16[104,512]{1,0:T(8,128)(2,1)S(1)} collective-permute-done((f16[104,512]{1,0:T(8,128)(2,1)S(1)}, f16[104,512]{1,0:T(8,128)(2,1)S(1)}, u32[]{:S(2)}, u32[]{:S(2)}) %collective-permute-start.6) | collective-permute-done | bytes 106528 | tf_op jit(solution)/shard_map/ppermute | solution.py:59
  134.5 0.5 slice.213
  135.9 0.8 broadcast_in_dim.19
  136.6 7.9 %all-to-all-start.5 = ((f16[4,104,512]{2,1,0:T(8,128)(2,1)}), f16[4,104,512]{2,1,0:T(8,128)(2,1)S(1)}, u32[]{:S(2)}, u32[]{:S(2)}) async-start(f16[4,104,512]{2,1,0:T(8,128)(2,1)} %broadcast_in_dim.19), calls=%async_computation.5 | async-start | bytes 851968 | tf_op jit(solution)/shard_map/all_to_all | solution.py:18
  144.5 0.1 reshape.82
  144.7 7.7 %all-to-all-done.5 = f16[4,104,512]{2,1,0:T(8,128)(2,1)S(1)} async-done(((f16[4,104,512]{2,1,0:T(8,128)(2,1)}), f16[4,104,512]{2,1,0:T(8,128)(2,1)S(1)}, u32[]{:S(2)}, u32[]{:S(2)}) %all-to-all-start.5) | async-done | bytes 426016 | tf_op jit(solution)/shard_map/all_to_all | solution.py:18
  152.4 0.6 slice_reduce_fusion.1
  153.8 0.1 select_reduce_fusion
  153.9 0.8 broadcast_in_dim.21
  154.7 3.5 %all-to-all-start.6 = ((f16[4,96,512]{2,1,0:T(8,128)(2,1)}), f16[4,96,512]{2,1,0:T(8,128)(2,1)S(1)}, u32[]{:S(2)}, u32[]{:S(2)}) async-start(f16[4,96,512]{2,1,0:T(8,128)(2,1)} %broadcast_in_dim.21), calls=%async_computation.6 | async-start | bytes 786432 | tf_op jit(solution)/shard_map/all_to_all | solution.py:18
  158.4 7.0 %all-to-all-done.6 = f16[4,96,512]{2,1,0:T(8,128)(2,1)S(1)} async-done(((f16[4,96,512]{2,1,0:T(8,128)(2,1)}), f16[4,96,512]{2,1,0:T(8,128)(2,1)S(1)}, u32[]{:S(2)}, u32[]{:S(2)}) %all-to-all-start.6) | async-done | bytes 393248 | tf_op jit(solution)/shard_map/all_to_all | solution.py:18
  165.3 3.8 %all_gather.7 = f16[768,512]{1,0:T(8,128)(2,1)S(1)} all-gather(f16[384,512]{1,0:T(8,128)(2,1)S(1)} %bitcast.86), channel_id=1, replica_groups=mesh['yp'=4,'yb'=2,'zp'=2,'zb'=2,'x'=4,'zh'=2,'c'=2] {'c'}, dimensions={0}, use_global_device_ids=true | all-gather | bytes 1179648 | tf_op jit(solution)/shard_map/all_gather | solution.py:154
  169.2 0.6 fusion.5
  169.7 0.7 copy-done.9
  170.4 1.2 abs_reduce_fusion
  172.4 0.1 multiply_convert_fusion
  172.5 0.9 concatenate.82
  173.5 3.5 %all-to-all-start.7 = ((f16[4,200,384]{2,1,0:T(8,128)(2,1)}), f16[4,200,384]{2,1,0:T(8,128)(2,1)S(1)}, u32[]{:S(2)}, u32[]{:S(2)}) async-start(f16[4,200,384]{2,1,0:T(8,128)(2,1)} %concatenate.82), calls=%async_computation.7 | async-start | bytes 1228800 | tf_op jit(solution)/shard_map/all_to_all | solution.py:18
  176.9 8.7 %all-to-all-done.7 = f16[4,200,384]{2,1,0:T(8,128)(2,1)S(1)} async-done(((f16[4,200,384]{2,1,0:T(8,128)(2,1)}), f16[4,200,384]{2,1,0:T(8,128)(2,1)S(1)}, u32[]{:S(2)}, u32[]{:S(2)}) %all-to-all-start.7) | async-done | bytes 614432 | tf_op jit(solution)/shard_map/all_to_all | solution.py:18
  185.8 0.7 fusion.15
  186.6 0.2 copy-done
  186.8 1.0 maximum_add_fusion
  (67 shorter events, 1.8 us)
Async XLA Ops:
  0.6 18.9 %copy-start.4 = (bf16[1152,16]{0,1:T(8,128)(2,1)S(1)}, bf16[1152,16]{0,1:T(8,128)(2,1)}, u32[]{:S(2)}) copy-start(bf16[1152,16]{0,1:T(8,128)(2,1)} %param.14) | copy-start | bytes 110596
  0.6 19.6 %copy-start.1 = (bf16[192,384]{1,0:T(8,128)(2,1)S(1)}, bf16[192,384]{1,0:T(8,128)(2,1)}, u32[]{:S(2)}) copy-start(bf16[192,384]{1,0:T(8,128)(2,1)} %param.12) | copy-start | bytes 442372
  1.5 17.4 %collective-permute-start.1 = (bf16[32,384]{1,0:T(8,128)(2,1)S(1)}, bf16[32,384]{1,0:T(8,128)(2,1)S(1)}, u32[]{:S(2)}, u32[]{:S(2)}) collective-permute-start(bf16[32,384]{1,0:T(8,128)(2,1)S(1)} %maximum_maximum_fusion), channel_id=1, source_target_pairs={{0,2},{2,0},{1,3},{3,1},{4,6},{6,4},{5,7},{7,5},{8,10},{10,8},{9,1... | collective-permute-start | bytes 73736 | tf_op jit(solution)/shard_map/ppermute | solution.py:59
  13.8 5.7 %collective-permute-start = (bf16[16,1536]{1,0:T(8,128)(2,1)S(1)}, bf16[16,1536]{1,0:T(8,128)(2,1)S(1)}, u32[]{:S(2)}, u32[]{:S(2)}) collective-permute-start(bf16[16,1536]{1,0:T(8,128)(2,1)S(1)} %pad_maximum_fusion.8), channel_id=1, source_target_pairs={{0,32},{32,0},{1,33},{33,1},{2,34},{34,2},{3,35},{35,3},{4,36},{36... | collective-permute-start | bytes 147464 | tf_op jit(solution)/shard_map/ppermute | solution.py:59
  33.5 10.2 %all-to-all-start.1 = ((bf16[4,64,768]{2,1,0:T(8,128)(2,1)}), bf16[4,64,768]{2,1,0:T(8,128)(2,1)S(1)}, u32[]{:S(2)}, u32[]{:S(2)}) async-start(bf16[4,64,768]{2,1,0:T(8,128)(2,1)} %broadcast_in_dim.16), calls=%async_computation.1 | async-start | bytes 786432 | tf_op jit(solution)/shard_map/all_to_all | solution.py:18
  38.2 13.2 %copy-start.2 = (bf16[4,192,384]{2,1,0:T(8,128)(2,1)}, bf16[4,192,384]{2,1,0:T(8,128)(2,1)S(1)}, u32[]{:S(2)}) copy-start(bf16[4,192,384]{2,1,0:T(8,128)(2,1)S(1)} %get-tuple-element.10) | copy-start | bytes 1769476
  51.4 9.8 %copy-start.5 = (f32[512]{0:T(512)S(1)}, f32[512]{0:T(512)}, u32[]{:S(2)}) copy-start(f32[512]{0:T(512)} %param.19) | copy-start | bytes 6148
  51.4 9.8 %copy-start.6 = (f32[512]{0:T(512)S(1)}, f32[512]{0:T(512)}, u32[]{:S(2)}) copy-start(f32[512]{0:T(512)} %param.17) | copy-start | bytes 6148
  52.2 21.9 %all-to-all-start.2 = ((f16[8,72,384]{2,1,0:T(8,128)(2,1)}), f16[8,72,384]{2,1,0:T(8,128)(2,1)S(1)}, u32[]{:S(2)}, u32[]{:S(2)}) async-start(f16[8,72,384]{2,1,0:T(8,128)(2,1)} %concatenate.74), calls=%async_computation.2 | async-start | bytes 884736 | tf_op jit(solution)/shard_map/all_to_all | solution.py:18
  76.6 19.3 %all-to-all-start.3 = ((f16[8,72,384]{2,1,0:T(8,128)(2,1)}), f16[8,72,384]{2,1,0:T(8,128)(2,1)S(1)}, u32[]{:S(2)}, u32[]{:S(2)}) async-start(f16[8,72,384]{2,1,0:T(8,128)(2,1)} %broadcast_in_dim.17), calls=%async_computation.3 | async-start | bytes 884736 | tf_op jit(solution)/shard_map/all_to_all | solution.py:18
  81.8 18.4 %collective-permute-start.4 = (bf16[128,384]{1,0:T(8,128)(2,1)S(1)}, bf16[128,384]{1,0:T(8,128)(2,1)S(1)}, u32[]{:S(2)}, u32[]{:S(2)}) collective-permute-start(bf16[128,384]{1,0:T(8,128)(2,1)S(1)} %bitcast.88), channel_id=1, source_target_pairs={{0,384},{128,0},{256,128},{384,256},{1,385},{129,1},{257,129},{385... | collective-permute-start | bytes 294920 | tf_op jit(solution)/shard_map/ppermute | solution.py:63
  87.3 13.3 %collective-permute-start.3 = (bf16[128,384]{1,0:T(8,128)(2,1)S(1)}, bf16[128,384]{1,0:T(8,128)(2,1)S(1)}, u32[]{:S(2)}, u32[]{:S(2)}) collective-permute-start(bf16[128,384]{1,0:T(8,128)(2,1)S(1)} %bitcast.89), channel_id=1, source_target_pairs={{0,256},{128,384},{256,0},{384,128},{1,257},{129,385},{257,1},{385... | collective-permute-start | bytes 294920 | tf_op jit(solution)/shard_map/ppermute | solution.py:63
  91.3 9.6 %collective-permute-start.2 = (bf16[128,384]{1,0:T(8,128)(2,1)S(1)}, bf16[128,384]{1,0:T(8,128)(2,1)S(1)}, u32[]{:S(2)}, u32[]{:S(2)}) collective-permute-start(bf16[128,384]{1,0:T(8,128)(2,1)S(1)} %bitcast.90), channel_id=1, source_target_pairs={{0,128},{128,256},{256,384},{384,0},{1,129},{129,257},{257,385},{3... | collective-permute-start | bytes 294920 | tf_op jit(solution)/shard_map/ppermute | solution.py:63
  96.2 1.1 copy-start.3
  102.2 6.9 %collective-permute-start.5 = (f32[392,512]{1,0:T(8,128)S(1)}, f32[392,512]{1,0:T(8,128)}, u32[]{:S(2)}, u32[]{:S(2)}) collective-permute-start(f32[392,512]{1,0:T(8,128)S(1)} %concatenate.77), channel_id=1, source_target_pairs={{0,1},{1,0},{2,3},{3,2},{4,5},{5,4},{6,7},{7,6},{8,9},{9,8},{10,11... | collective-permute-start | bytes 2408456 | tf_op jit(solution)/shard_map/ppermute | solution.py:59
  124.4 20.2 %copy-start.7 = (f32[512]{0:T(512)S(1)}, f32[512]{0:T(512)}, u32[]{:S(2)}) copy-start(f32[512]{0:T(512)} %param.20) | copy-start | bytes 6148
  124.4 20.1 %copy-start.8 = (f32[512]{0:T(512)S(1)}, f32[512]{0:T(512)}, u32[]{:S(2)}) copy-start(f32[512]{0:T(512)} %param.18) | copy-start | bytes 6148
  125.1 9.5 %collective-permute-start.6 = (f16[104,512]{1,0:T(8,128)(2,1)S(1)}, f16[104,512]{1,0:T(8,128)(2,1)S(1)}, u32[]{:S(2)}, u32[]{:S(2)}) collective-permute-start(f16[104,512]{1,0:T(8,128)(2,1)S(1)} %concatenate.79), channel_id=1, source_target_pairs={{0,2},{2,0},{1,3},{3,1},{4,6},{6,4},{5,7},{7,5},{8,10},{10,8},{9,1... | collective-permute-start | bytes 319496 | tf_op jit(solution)/shard_map/ppermute | solution.py:59
  136.6 15.8 %all-to-all-start.5 = ((f16[4,104,512]{2,1,0:T(8,128)(2,1)}), f16[4,104,512]{2,1,0:T(8,128)(2,1)S(1)}, u32[]{:S(2)}, u32[]{:S(2)}) async-start(f16[4,104,512]{2,1,0:T(8,128)(2,1)} %broadcast_in_dim.19), calls=%async_computation.5 | async-start | bytes 851968 | tf_op jit(solution)/shard_map/all_to_all | solution.py:18
  154.7 10.6 %all-to-all-start.6 = ((f16[4,96,512]{2,1,0:T(8,128)(2,1)}), f16[4,96,512]{2,1,0:T(8,128)(2,1)S(1)}, u32[]{:S(2)}, u32[]{:S(2)}) async-start(f16[4,96,512]{2,1,0:T(8,128)(2,1)} %broadcast_in_dim.21), calls=%async_computation.6 | async-start | bytes 786432 | tf_op jit(solution)/shard_map/all_to_all | solution.py:18
  169.1 1.3 copy-start.9
  173.5 12.2 %all-to-all-start.7 = ((f16[4,200,384]{2,1,0:T(8,128)(2,1)}), f16[4,200,384]{2,1,0:T(8,128)(2,1)S(1)}, u32[]{:S(2)}, u32[]{:S(2)}) async-start(f16[4,200,384]{2,1,0:T(8,128)(2,1)} %concatenate.82), calls=%async_computation.7 | async-start | bytes 1228800 | tf_op jit(solution)/shard_map/all_to_all | solution.py:18
  185.8 1.0 copy-start

commit v9 on v8

v9 whole, which is shorter than its diff:
```python
import jax
import jax.numpy as jnp
from jax import lax
from jax.sharding import Mesh, PartitionSpec as P

FSDP = ("yp", "yb", "zp", "zb")
COL = ("x", "zh", "c")
QUAD = ("yb", "zb")
OCT = ("yp", "zp")
ROUND = (8, 7)


def shifted(eigen, damp):
    return 1.0 / (eigen + damp) - 1.0 / damp


def exchange(blocks, axes):
    return lax.all_to_all(blocks, axes, 0, 0, tiled=True)


def halves(wide):
    high = lax.reduce_precision(wide, *ROUND)
    return high.astype(jnp.bfloat16), (wide - high).astype(jnp.bfloat16)


def dot_wide_left(wide, narrow, dims):
    high, low = halves(wide)
    dot = lambda part: lax.dot_general(part, narrow, (dims, ((), ())), preferred_element_type=jnp.float32)
    return dot(high) + dot(low)


def dot_wide_right(narrow, wide, dims):
    high, low = halves(wide)
    dot = lambda part: lax.dot_general(narrow, part, (dims, ((), ())), preferred_element_type=jnp.float32)
    return dot(high) + dot(low)


def pack(values):
    top = jnp.max(jnp.abs(values), axis=-2, keepdims=True)
    power = jnp.clip(jnp.floor(jnp.log2(jnp.maximum(top, 1e-30))), -100.0, 120.0)
    scaled = (values * jnp.exp2(14.0 - power)).astype(jnp.float16)
    tail = jnp.broadcast_to(power.astype(jnp.float16), values.shape[:-2] + (8, values.shape[-1]))
    return jnp.concatenate([scaled, tail], axis=-2)


def unpack(packed):
    rows = packed.shape[-2] - 8
    power = packed[..., rows : rows + 1, :].astype(jnp.float32)
    return packed[..., :rows, :].astype(jnp.float32) * jnp.exp2(power - 14.0)


def spread(values, count):
    return jnp.broadcast_to(values[None], (count,) + values.shape)


def swap(values, axis):
    return lax.ppermute(values, axis, [(0, 1), (1, 0)])


def around(values, axis, size, step):
    return lax.ppermute(values, axis, [(i, (i + step) % size) for i in range(size)])


def core_part(values, core, own):
    half = values.shape[0] // 2
    return lax.dynamic_slice_in_dim(values, (core if own else 1 - core) * half, half, 0)


def local(
    joined_gradient,
    output_gradient,
    joined_left_basis,
    joined_right_basis,
    output_left_basis,
    output_right_basis,
    joined_left_eigen,
    joined_right_eigen,
    output_left_eigen,
    output_right_eigen,
    damping,
):
    damp = damping[0]
    quad = lax.axis_index("yb") * 2 + lax.axis_index("zb")
    level = lax.axis_index("yp")
    core = lax.axis_index("c")
    is_output = quad == 3
    left_shift = shifted(jnp.where(is_output, output_left_eigen, joined_left_eigen), damp)
    right_shift = shifted(jnp.where(is_output, output_right_eigen, joined_right_eigen), damp)
    left_shift = left_shift.reshape(4, 2, 2, 32).transpose(2, 0, 1, 3)
    left_shift = jnp.where(lax.axis_index("zh") == 1, left_shift[:, :, ::-1], left_shift).reshape(512)
    own_shift = lax.dynamic_slice_in_dim(left_shift, level * 128, 128, 0)
    right_shift = right_shift.reshape(4, 2, 2, 2, 16).transpose(0, 2, 1, 3, 4).reshape(4, 2, 64)[::-1]
    right_shift = jnp.where(lax.axis_index("zp") == 1, right_shift[:, ::-1], right_shift)
    right_shift = jnp.concatenate([right_shift, right_shift], axis=0)
    right_shift = lax.dynamic_slice_in_dim(right_shift, 3 - level, 4, 0).reshape(512)

    right = jnp.concatenate([joined_right_basis.T, output_right_basis.T], axis=1)
    lefts = [jnp.concatenate([basis.T[:16], basis.T[16:]], axis=1) for basis in (joined_left_basis, output_left_basis)]
    left = jnp.concatenate(lefts, axis=0)
    other = swap(left, "zh")
    lefts = [jnp.concatenate([left[rows], other[rows]], axis=0) for rows in (slice(0, 16), slice(16, 32))]
    lefts = (lefts[0], lefts[0], lefts[0], lefts[1])
    gradients = (joined_gradient[:, :384], joined_gradient[:, 384:768], joined_gradient[:, 768:], output_gradient)
    sent = jnp.stack(
        [
            jnp.concatenate([gradients[j], right[:, 384 * j : 384 * j + 384], lefts[j]], axis=0)
            for j in range(4)
        ]
    )
    got = exchange(sent, QUAD)
    gradient = got[:, :192].reshape(768, 384)

    left = got[:, 208:].reshape(4, 2, 16, 384)
    left = jnp.stack([left[..., :192], left[..., 192:]], axis=2).reshape(4, 64, 192)
    left = jnp.concatenate([left[0], left[1], left[2], left[3]], axis=1)
    left = exchange(spread(left, 4), "x").reshape(256, 768)
    left = lax.all_gather(left, "c", axis=0, tiled=True)

    rows = jnp.dot(left, gradient, preferred_element_type=jnp.float32)
    rows = jnp.sum(unpack(exchange(pack(rows.reshape(4, 128, 384)), "yp")), axis=0)
    right = got[:, 192:208].reshape(64, 384)
    scaled = (right.astype(jnp.float32) * 2.0**19).astype(jnp.float16)
    other = swap(jnp.concatenate([pack(rows), scaled], axis=0), "zp")
    rows = (rows + unpack(other[:136])) * own_shift[:, None]
    rows = unpack(exchange(spread(pack(rows), 4), "yp")).reshape(512, 384)
    scaled = (other[136:].astype(jnp.float32) * 2.0**-19).astype(jnp.bfloat16)
    right = jnp.concatenate([right, scaled], axis=0)
    right = jnp.concatenate([right] + [around(right, "yp", 4, step) for step in (1, 2, 3)], axis=0)

    lifted = dot_wide_right(left, rows, ((0,), (0,)))
    applied = gradient.astype(jnp.float32) / damp + lifted
    cols = dot_wide_left(applied, right, ((1,), (1,)))
    cols = core_part(cols, core, True) + swap(core_part(cols, core, False), "c")
    cols = jnp.sum(unpack(exchange(pack(cols.reshape(4, 96, 512)), "x")), axis=0)
    cols = cols + unpack(swap(pack(cols), "zh"))
    cols = unpack(exchange(spread(pack(cols), 4), QUAD))
    same = (lax.broadcasted_iota(jnp.int32, (4, 1, 1), 0) == 3) == is_output
    cols = jnp.sum(jnp.where(same, cols, 0.0), axis=0)
    cols = exchange(spread(pack(cols), 4), "x")
    cols = unpack(lax.all_gather(cols, "c", axis=0, tiled=True)).reshape(768, 512)

    update = lifted / damp + dot_wide_left(cols * right_shift[None, :], right, ((1,), (0,)))
    update = unpack(exchange(pack(update.reshape(4, 192, 384)), QUAD))
    joined_update = jnp.concatenate([update[0], update[1], update[2]], axis=1) + joined_gradient.astype(jnp.float32) / damp / damp
    output_update = update[3] + output_gradient.astype(jnp.float32) / damp / damp
    return joined_update, output_update


def solution(mesh):
    fine = Mesh(mesh.devices.reshape(4, 2, 2, 2, 4, 2, 2), ("yp", "yb", "zp", "zb", "x", "zh", "c"))
    placed = (
        P(FSDP, COL),
        P(FSDP, COL),
        P(FSDP, COL),
        P(COL, FSDP),
        P(FSDP, COL),
        P(COL, FSDP),
        P(),
        P(),
        P(),
        P(),
        P(),
    )
    return jax.shard_map(
        local,
        mesh=fine,
        in_specs=placed,
        out_specs=(P(FSDP, COL), P(FSDP, COL)),
        check_vma=False,
    )
```

time: 190 us -> 181 us (0.953)
  between operations: 8.35 us -> 2.08 us
  waiting for transfers between devices: 50.1 us -> 54.5 us
  starting transfers between devices: 69.5 us -> 65.5 us
  blocking collectives: 33.2 us -> 37 us
  local copies, waits for them, and re-layouts: 11.5 us -> 8.35 us
    all_to_all x6, starting transfers between devices: 32.3 us -> 25.7 us  [exchange(): return lax.all_to_all(blocks, axes, 0, 0, tiled=True)]
    all_gather x1, blocking collectives: 3.83 us -> 8.73 us  [local(): lax.all_gather(cols, 'c', axis=0, tiled=True)]
    ppermute x3, waiting for transfers between devices: 0.7 us -> 5.15 us  [around(): lax.ppermute(values, axis, [(i, (i + step) % size) for i in range(size)])]
    all_to_all x6, waiting for transfers between devices: 40.8 us -> 37.8 us  [exchange(): return lax.all_to_all(blocks, axes, 0, 0, tiled=True)]
    ppermute x4, waiting for transfers between devices: 8.62 us -> 11.6 us  [swap(): return lax.ppermute(values, axis, [(0, 1), (1, 0)])]
    reduce_max x5 -> x7, other arithmetic: 3.28 us -> 0.38 us  [pack(): top = jnp.max(jnp.abs(values), axis=-2, keepdims=True)]
    concatenate x7 -> x1, local copies, waits for them, and re-layouts: 2.63 us -> 0.02 us  [local(): jnp.concatenate([right] + [around(right, 'yp', 4, step) for step in (1, 2...]
    ppermute x4, starting transfers between devices: 23.8 us -> 26.3 us  [swap(): return lax.ppermute(values, axis, [(0, 1), (1, 0)])]
  transfers between devices with their start and end apart: 13 -> 13, of which waited for: 10 -> 9; matrix products, arithmetic and copies ran while one was open for 3% -> 1% of each run, Pallas kernels for 0% -> 0%
where the time goes in v9:
time: 181 us; the launch traced here: 180 us
  starting transfers between devices  65.5 us (36%)
  waiting for transfers between devices  54.5 us (30%)
  blocking collectives  37 us (20%)
  local copies, waits for them, and re-layouts  8.35 us (5%)
  other arithmetic  7.48 us (4%)
  matrix products  5.21 us (3%)
  between operations  2.08 us (1%)
    all_to_all x6, waiting for transfers between devices, exchange(): return lax.all_to_all(blocks, axes, 0, 0, tiled=True)  37.8 us
    ppermute x4, starting transfers between devices, swap(): return lax.ppermute(values, axis, [(0, 1), (1, 0)])  26.3 us
    all_to_all x6, starting transfers between devices, exchange(): return lax.all_to_all(blocks, axes, 0, 0, tiled=True)  25.7 us
    all_to_all x2, blocking collectives, exchange(): return lax.all_to_all(blocks, axes, 0, 0, tiled=True)  22.1 us
    ppermute x3, starting transfers between devices, around(): lax.ppermute(values, axis, [(i, (i + step) % size) for i in range(size)])  13.5 us
    ppermute x4, waiting for transfers between devices, swap(): return lax.ppermute(values, axis, [(0, 1), (1, 0)])  11.6 us
    all_gather x1, blocking collectives, local(): lax.all_gather(cols, 'c', axis=0, tiled=True)  8.73 us
    all_gather x1, blocking collectives, local(): left = lax.all_gather(left, 'c', axis=0, tiled=True)  6.09 us
  transfers between devices with their start and end apart: 13, of which 9 were waited for; matrix products, arithmetic and copies ran while one was open for 1% of the time, Pallas kernels for 0%

profile of v9, /device:TPU:1, one launch (start us, length us, event | category | flops | bytes accessed | tf_op | source)
XLA Modules:
  0.0 180.1 jit_solution(15314547138979690842)
XLA Ops:
  0.6 0.8 fusion.49
  1.5 11.5 %collective-permute-start = (bf16[32,384]{1,0:T(8,128)(2,1)S(1)}, bf16[32,384]{1,0:T(8,128)(2,1)S(1)}, u32[]{:S(2)}, u32[]{:S(2)}) collective-permute-start(bf16[32,384]{1,0:T(8,128)(2,1)S(1)} %maximum_maximum_fusion), channel_id=1, source_target_pairs={{0,2},{2,0},{1,3},{3,1},{4,6},{6,4},{5,7},{7,5},{8,10},{10,8},{9,1... | collective-permute-start | bytes 73736 | tf_op jit(solution)/shard_map/ppermute | solution.py:57
  13.0 1.1 fusion.46
  14.1 0.8 fusion.47
  14.8 0.8 maximum_bitcast_fusion
  15.7 0.1 pad_maximum_fusion
  15.8 11.7 %all_to_all.40 = bf16[4,240,384]{2,1,0:T(8,128)(2,1)S(1)} all-to-all(bf16[4,240,384]{2,1,0:T(8,128)(2,1)S(1)} %pad_maximum_fusion), channel_id=1, replica_groups=mesh['yp'=4,'yb'=2,'zp'=2,'zb'=2,'x'=4,'zh'=2,'c'=2] {'yb','zb'}, dimensions={0} | all-to-all | bytes 1474560 | tf_op jit(solution)/shard_map/all_to_all | solution.py:18
  27.6 0.1 slice_bitcast_fusion.5
  27.7 0.1 pad_maximum_fusion.13
  27.8 0.8 broadcast_in_dim.32
  28.6 4.8 %all-to-all-start.1 = ((bf16[4,64,768]{2,1,0:T(8,128)(2,1)}), bf16[4,64,768]{2,1,0:T(8,128)(2,1)S(1)}, u32[]{:S(2)}, u32[]{:S(2)}) async-start(bf16[4,64,768]{2,1,0:T(8,128)(2,1)} %broadcast_in_dim.32), calls=%async_computation.1 | async-start | bytes 786432 | tf_op jit(solution)/shard_map/all_to_all | solution.py:18
  33.4 6.2 %all-to-all-done.1 = bf16[4,64,768]{2,1,0:T(8,128)(2,1)S(1)} async-done(((bf16[4,64,768]{2,1,0:T(8,128)(2,1)}), bf16[4,64,768]{2,1,0:T(8,128)(2,1)S(1)}, u32[]{:S(2)}, u32[]{:S(2)}) %all-to-all-start.1) | async-done | bytes 393248 | tf_op jit(solution)/shard_map/all_to_all | solution.py:18
  39.6 6.1 %all_gather.6 = bf16[512,768]{1,0:T(8,128)(2,1)S(1)} all-gather(bf16[256,768]{1,0:T(8,128)(2,1)S(1)} %bitcast.97), channel_id=1, replica_groups=mesh['yp'=4,'yb'=2,'zp'=2,'zb'=2,'x'=4,'zh'=2,'c'=2] {'c'}, dimensions={0}, use_global_device_ids=true | all-gather | bytes 1179648 | tf_op jit(solution)/shard_map/all_gather | solution.py:117
  45.7 0.6 abs_reduce_fusion.2
  46.4 0.9 pad_maximum_fusion.3
  47.3 5.9 %all-to-all-start.2 = ((f16[4,136,384]{2,1,0:T(8,128)(2,1)}), f16[4,136,384]{2,1,0:T(8,128)(2,1)S(1)}, u32[]{:S(2)}, u32[]{:S(2)}) async-start(f16[4,136,384]{2,1,0:T(8,128)(2,1)} %pad_maximum_fusion.3), calls=%async_computation.2 | async-start | bytes 835584 | tf_op jit(solution)/shard_map/all_to_all | solution.py:18
  54.0 0.1 reshape.244
  54.1 11.5 %all-to-all-done.2 = f16[4,136,384]{2,1,0:T(8,128)(2,1)S(1)} async-done(((f16[4,136,384]{2,1,0:T(8,128)(2,1)}), f16[4,136,384]{2,1,0:T(8,128)(2,1)S(1)}, u32[]{:S(2)}, u32[]{:S(2)}) %all-to-all-start.2) | async-done | bytes 417824 | tf_op jit(solution)/shard_map/all_to_all | solution.py:18
  65.9 4.0 %collective-permute-start.1 = (f16[200,384]{1,0:T(8,128)(2,1)S(1)}, f16[200,384]{1,0:T(8,128)(2,1)S(1)}, u32[]{:S(2)}, u32[]{:S(2)}) collective-permute-start(f16[200,384]{1,0:T(8,128)(2,1)S(1)} %pad_maximum_fusion.8), channel_id=1, source_target_pairs={{0,32},{32,0},{1,33},{33,1},{2,34},{34,2},{3,35},{35,3},{4,36},{36... | collective-permute-start | bytes 460808 | tf_op jit(solution)/shard_map/ppermute | solution.py:57
  69.9 0.1 reshape.245
  70.1 7.1 %collective-permute-done.1 = f16[200,384]{1,0:T(8,128)(2,1)S(1)} collective-permute-done((f16[200,384]{1,0:T(8,128)(2,1)S(1)}, f16[200,384]{1,0:T(8,128)(2,1)S(1)}, u32[]{:S(2)}, u32[]{:S(2)}) %collective-permute-start.1) | collective-permute-done | bytes 153632 | tf_op jit(solution)/shard_map/ppermute | solution.py:57
  77.2 0.1 abs_reduce_fusion.6
  77.3 0.1 multiply_convert_fusion.6
  77.5 0.8 broadcast_in_dim.36
  78.2 4.6 %all-to-all-start.3 = ((f16[4,136,384]{2,1,0:T(8,128)(2,1)}), f16[4,136,384]{2,1,0:T(8,128)(2,1)S(1)}, u32[]{:S(2)}, u32[]{:S(2)}) async-start(f16[4,136,384]{2,1,0:T(8,128)(2,1)} %broadcast_in_dim.36), calls=%async_computation.3 | async-start | bytes 835584 | tf_op jit(solution)/shard_map/all_to_all | solution.py:18
  82.9 5.5 %collective-permute-start.4 = (bf16[128,384]{1,0:T(8,128)(2,1)S(1)}, bf16[128,384]{1,0:T(8,128)(2,1)S(1)}, u32[]{:S(2)}, u32[]{:S(2)}) collective-permute-start(bf16[128,384]{1,0:T(8,128)(2,1)S(1)} %pad_maximum_fusion.14), channel_id=1, source_target_pairs={{0,384},{128,0},{256,128},{384,256},{1,385},{129,1},{257,129},{385... | collective-permute-start | bytes 294920 | tf_op jit(solution)/shard_map/ppermute | solution.py:61
  88.4 4.0 %collective-permute-start.3 = (bf16[128,384]{1,0:T(8,128)(2,1)S(1)}, bf16[128,384]{1,0:T(8,128)(2,1)S(1)}, u32[]{:S(2)}, u32[]{:S(2)}) collective-permute-start(bf16[128,384]{1,0:T(8,128)(2,1)S(1)} %pad_maximum_fusion.14), channel_id=1, source_target_pairs={{0,256},{128,384},{256,0},{384,128},{1,257},{129,385},{257,1},{385... | collective-permute-start | bytes 294920 | tf_op jit(solution)/shard_map/ppermute | solution.py:61
  92.4 4.0 %collective-permute-start.2 = (bf16[128,384]{1,0:T(8,128)(2,1)S(1)}, bf16[128,384]{1,0:T(8,128)(2,1)S(1)}, u32[]{:S(2)}, u32[]{:S(2)}) collective-permute-start(bf16[128,384]{1,0:T(8,128)(2,1)S(1)} %pad_maximum_fusion.14), channel_id=1, source_target_pairs={{0,128},{128,256},{256,384},{384,0},{1,129},{129,257},{257,385},{3... | collective-permute-start | bytes 294920 | tf_op jit(solution)/shard_map/ppermute | solution.py:61
  96.4 5.1 %collective-permute-done.2 = bf16[128,384]{1,0:T(8,128)(2,1)S(1)} collective-permute-done((bf16[128,384]{1,0:T(8,128)(2,1)S(1)}, bf16[128,384]{1,0:T(8,128)(2,1)S(1)}, u32[]{:S(2)}, u32[]{:S(2)}) %collective-permute-start.2) | collective-permute-done | bytes 98336 | tf_op jit(solution)/shard_map/ppermute | solution.py:61
  101.8 0.1 fusion.3
  101.9 0.6 fusion.51
  102.5 1.6 divide_add_fusion
  104.1 0.6 fusion.4
  104.7 0.6 convolution_add_fusion
  105.4 4.0 %collective-permute-start.5 = (f32[384,512]{1,0:T(8,128)S(1)}, f32[384,512]{1,0:T(8,128)S(1)}, u32[]{:S(2)}, u32[]{:S(2)}) collective-permute-start(f32[384,512]{1,0:T(8,128)S(1)} %constant_dynamic-slice_fusion), channel_id=1, source_target_pairs={{0,1},{1,0},{2,3},{3,2},{4,5},{5,4},{6,7},{7,6},{8,9},{9,8},{10,11... | collective-permute-start | bytes 2359304 | tf_op jit(solution)/shard_map/ppermute | solution.py:57
  109.4 1.9 %collective-permute-done.5 = f32[384,512]{1,0:T(8,128)S(1)} collective-permute-done((f32[384,512]{1,0:T(8,128)S(1)}, f32[384,512]{1,0:T(8,128)S(1)}, u32[]{:S(2)}, u32[]{:S(2)}) %collective-permute-start.5) | collective-permute-done | bytes 786464 | tf_op jit(solution)/shard_map/ppermute | solution.py:57
  111.3 0.1 dynamic-slice_add_fusion
  111.6 0.1 multiply_convert_fusion.1
  111.7 0.1 pad_maximum_fusion.2
  111.8 10.4 %all_to_all.41 = f16[4,104,512]{2,1,0:T(8,128)(2,1)S(1)} all-to-all(f16[4,104,512]{2,1,0:T(8,128)(2,1)S(1)} %pad_maximum_fusion.2), channel_id=1, replica_groups=mesh['yp'=4,'yb'=2,'zp'=2,'zb'=2,'x'=4,'zh'=2,'c'=2] {'x'}, dimensions={0} | all-to-all | bytes 851968 | tf_op jit(solution)/shard_map/all_to_all | solution.py:18
  122.4 6.8 %collective-permute-start.6 = (f16[104,512]{1,0:T(8,128)(2,1)S(1)}, f16[104,512]{1,0:T(8,128)(2,1)S(1)}, u32[]{:S(2)}, u32[]{:S(2)}) collective-permute-start(f16[104,512]{1,0:T(8,128)(2,1)S(1)} %pad_maximum_fusion.9), channel_id=1, source_target_pairs={{0,2},{2,0},{1,3},{3,1},{4,6},{6,4},{5,7},{7,5},{8,10},{10,8},{9,1... | collective-permute-start | bytes 319496 | tf_op jit(solution)/shard_map/ppermute | solution.py:57
  129.3 2.6 %collective-permute-done.6 = f16[104,512]{1,0:T(8,128)(2,1)S(1)} collective-permute-done((f16[104,512]{1,0:T(8,128)(2,1)S(1)}, f16[104,512]{1,0:T(8,128)(2,1)S(1)}, u32[]{:S(2)}, u32[]{:S(2)}) %collective-permute-start.6) | collective-permute-done | bytes 106528 | tf_op jit(solution)/shard_map/ppermute | solution.py:57
  132.1 0.8 broadcast_in_dim.45
  132.9 3.5 %all-to-all-start.5 = ((f16[4,104,512]{2,1,0:T(8,128)(2,1)}), f16[4,104,512]{2,1,0:T(8,128)(2,1)S(1)}, u32[]{:S(2)}, u32[]{:S(2)}) async-start(f16[4,104,512]{2,1,0:T(8,128)(2,1)} %broadcast_in_dim.45), calls=%async_computation.5 | async-start | bytes 851968 | tf_op jit(solution)/shard_map/all_to_all | solution.py:18
  136.3 0.1 reshape.249
  136.5 0.1 reshape.250
  136.6 5.2 %all-to-all-done.5 = f16[4,104,512]{2,1,0:T(8,128)(2,1)S(1)} async-done(((f16[4,104,512]{2,1,0:T(8,128)(2,1)}), f16[4,104,512]{2,1,0:T(8,128)(2,1)S(1)}, u32[]{:S(2)}, u32[]{:S(2)}) %all-to-all-start.5) | async-done | bytes 426016 | tf_op jit(solution)/shard_map/all_to_all | solution.py:18
  141.8 0.1 select_reduce_fusion
  142.1 0.8 broadcast_in_dim.48
  142.9 3.5 %all-to-all-start.6 = ((f16[4,104,512]{2,1,0:T(8,128)(2,1)}), f16[4,104,512]{2,1,0:T(8,128)(2,1)S(1)}, u32[]{:S(2)}, u32[]{:S(2)}) async-start(f16[4,104,512]{2,1,0:T(8,128)(2,1)} %broadcast_in_dim.48), calls=%async_computation.6 | async-start | bytes 851968 | tf_op jit(solution)/shard_map/all_to_all | solution.py:18
  146.5 6.2 %all-to-all-done.6 = f16[4,104,512]{2,1,0:T(8,128)(2,1)S(1)} async-done(((f16[4,104,512]{2,1,0:T(8,128)(2,1)}), f16[4,104,512]{2,1,0:T(8,128)(2,1)S(1)}, u32[]{:S(2)}, u32[]{:S(2)}) %all-to-all-start.6) | async-done | bytes 426016 | tf_op jit(solution)/shard_map/all_to_all | solution.py:18
  152.7 8.7 %all_gather.7 = f16[8,104,512]{2,1,0:T(8,128)(2,1)S(1)} all-gather(f16[4,104,512]{2,1,0:T(8,128)(2,1)S(1)} %all-to-all-done.6), channel_id=1, replica_groups=mesh['yp'=4,'yb'=2,'zp'=2,'zb'=2,'x'=4,'zh'=2,'c'=2] {'c'}, dimensions={0}, use_global_device_ids=true | all-gather | bytes 1277952 | tf_op jit(solution)/shard_map/all_gather | solution.py:140
  161.5 0.2 convert_multiply_fusion
  161.7 0.3 reduce-precision_convert_fusion
  162.0 0.6 fusion.52
  162.6 0.7 copy-done.7
  163.3 0.6 fusion.1
  164.0 0.1 multiply_convert_fusion
  164.1 1.0 pad_maximum_fusion.1
  165.1 3.5 %all-to-all-start.7 = ((f16[4,200,384]{2,1,0:T(8,128)(2,1)}), f16[4,200,384]{2,1,0:T(8,128)(2,1)S(1)}, u32[]{:S(2)}, u32[]{:S(2)}) async-start(f16[4,200,384]{2,1,0:T(8,128)(2,1)} %pad_maximum_fusion.1), calls=%async_computation.7 | async-start | bytes 1228800 | tf_op jit(solution)/shard_map/all_to_all | solution.py:18
  168.6 8.7 %all-to-all-done.7 = f16[4,200,384]{2,1,0:T(8,128)(2,1)S(1)} async-done(((f16[4,200,384]{2,1,0:T(8,128)(2,1)}), f16[4,200,384]{2,1,0:T(8,128)(2,1)S(1)}, u32[]{:S(2)}, u32[]{:S(2)}) %all-to-all-start.7) | async-done | bytes 614432 | tf_op jit(solution)/shard_map/all_to_all | solution.py:18
  177.5 0.8 copy-done.2
  178.3 0.7 fusion.6
  179.1 1.0 maximum_add_fusion
  (95 shorter events, 2.1 us)
Async XLA Ops:
  0.6 14.2 %copy-start.1 = (bf16[192,384]{1,0:T(8,128)(2,1)S(1)}, bf16[192,384]{1,0:T(8,128)(2,1)}, u32[]{:S(2)}) copy-start(bf16[192,384]{1,0:T(8,128)(2,1)} %param.12) | copy-start | bytes 442372
  1.5 13.3 %collective-permute-start = (bf16[32,384]{1,0:T(8,128)(2,1)S(1)}, bf16[32,384]{1,0:T(8,128)(2,1)S(1)}, u32[]{:S(2)}, u32[]{:S(2)}) collective-permute-start(bf16[32,384]{1,0:T(8,128)(2,1)S(1)} %maximum_maximum_fusion), channel_id=1, source_target_pairs={{0,2},{2,0},{1,3},{3,1},{4,6},{6,4},{5,7},{7,5},{8,10},{10,8},{9,1... | collective-permute-start | bytes 73736 | tf_op jit(solution)/shard_map/ppermute | solution.py:57
  28.6 11.0 %all-to-all-start.1 = ((bf16[4,64,768]{2,1,0:T(8,128)(2,1)}), bf16[4,64,768]{2,1,0:T(8,128)(2,1)S(1)}, u32[]{:S(2)}, u32[]{:S(2)}) async-start(bf16[4,64,768]{2,1,0:T(8,128)(2,1)} %broadcast_in_dim.32), calls=%async_computation.1 | async-start | bytes 786432 | tf_op jit(solution)/shard_map/all_to_all | solution.py:18
  46.3 7.6 %copy-start.3 = (f32[512]{0:T(512)S(1)}, f32[512]{0:T(512)}, u32[]{:S(2)}) copy-start(f32[512]{0:T(512)} %param.20) | copy-start | bytes 6148
  46.3 7.6 %copy-start.4 = (f32[512]{0:T(512)S(1)}, f32[512]{0:T(512)}, u32[]{:S(2)}) copy-start(f32[512]{0:T(512)} %param.18) | copy-start | bytes 6148
  46.3 7.6 %copy-start.5 = (f32[512]{0:T(512)S(1)}, f32[512]{0:T(512)}, u32[]{:S(2)}) copy-start(f32[512]{0:T(512)} %param.19) | copy-start | bytes 6148
  46.3 7.6 %copy-start.6 = (f32[512]{0:T(512)S(1)}, f32[512]{0:T(512)}, u32[]{:S(2)}) copy-start(f32[512]{0:T(512)} %param.17) | copy-start | bytes 6148
  47.3 18.3 %all-to-all-start.2 = ((f16[4,136,384]{2,1,0:T(8,128)(2,1)}), f16[4,136,384]{2,1,0:T(8,128)(2,1)S(1)}, u32[]{:S(2)}, u32[]{:S(2)}) async-start(f16[4,136,384]{2,1,0:T(8,128)(2,1)} %pad_maximum_fusion.3), calls=%async_computation.2 | async-start | bytes 835584 | tf_op jit(solution)/shard_map/all_to_all | solution.py:18
  65.9 11.3 %collective-permute-start.1 = (f16[200,384]{1,0:T(8,128)(2,1)S(1)}, f16[200,384]{1,0:T(8,128)(2,1)S(1)}, u32[]{:S(2)}, u32[]{:S(2)}) collective-permute-start(f16[200,384]{1,0:T(8,128)(2,1)S(1)} %pad_maximum_fusion.8), channel_id=1, source_target_pairs={{0,32},{32,0},{1,33},{33,1},{2,34},{34,2},{3,35},{35,3},{4,36},{36... | collective-permute-start | bytes 460808 | tf_op jit(solution)/shard_map/ppermute | solution.py:57
  78.2 23.4 %all-to-all-start.3 = ((f16[4,136,384]{2,1,0:T(8,128)(2,1)}), f16[4,136,384]{2,1,0:T(8,128)(2,1)S(1)}, u32[]{:S(2)}, u32[]{:S(2)}) async-start(f16[4,136,384]{2,1,0:T(8,128)(2,1)} %broadcast_in_dim.36), calls=%async_computation.3 | async-start | bytes 835584 | tf_op jit(solution)/shard_map/all_to_all | solution.py:18
  82.9 18.7 %collective-permute-start.4 = (bf16[128,384]{1,0:T(8,128)(2,1)S(1)}, bf16[128,384]{1,0:T(8,128)(2,1)S(1)}, u32[]{:S(2)}, u32[]{:S(2)}) collective-permute-start(bf16[128,384]{1,0:T(8,128)(2,1)S(1)} %pad_maximum_fusion.14), channel_id=1, source_target_pairs={{0,384},{128,0},{256,128},{384,256},{1,385},{129,1},{257,129},{385... | collective-permute-start | bytes 294920 | tf_op jit(solution)/shard_map/ppermute | solution.py:61
  88.4 13.2 %collective-permute-start.3 = (bf16[128,384]{1,0:T(8,128)(2,1)S(1)}, bf16[128,384]{1,0:T(8,128)(2,1)S(1)}, u32[]{:S(2)}, u32[]{:S(2)}) collective-permute-start(bf16[128,384]{1,0:T(8,128)(2,1)S(1)} %pad_maximum_fusion.14), channel_id=1, source_target_pairs={{0,256},{128,384},{256,0},{384,128},{1,257},{129,385},{257,1},{385... | collective-permute-start | bytes 294920 | tf_op jit(solution)/shard_map/ppermute | solution.py:61
  92.4 9.2 %collective-permute-start.2 = (bf16[128,384]{1,0:T(8,128)(2,1)S(1)}, bf16[128,384]{1,0:T(8,128)(2,1)S(1)}, u32[]{:S(2)}, u32[]{:S(2)}) collective-permute-start(bf16[128,384]{1,0:T(8,128)(2,1)S(1)} %pad_maximum_fusion.14), channel_id=1, source_target_pairs={{0,128},{128,256},{256,384},{384,0},{1,129},{129,257},{257,385},{3... | collective-permute-start | bytes 294920 | tf_op jit(solution)/shard_map/ppermute | solution.py:61
  105.4 5.9 %collective-permute-start.5 = (f32[384,512]{1,0:T(8,128)S(1)}, f32[384,512]{1,0:T(8,128)S(1)}, u32[]{:S(2)}, u32[]{:S(2)}) collective-permute-start(f32[384,512]{1,0:T(8,128)S(1)} %constant_dynamic-slice_fusion), channel_id=1, source_target_pairs={{0,1},{1,0},{2,3},{3,2},{4,5},{5,4},{6,7},{7,6},{8,9},{9,8},{10,11... | collective-permute-start | bytes 2359304 | tf_op jit(solution)/shard_map/ppermute | solution.py:57
  122.4 9.5 %collective-permute-start.6 = (f16[104,512]{1,0:T(8,128)(2,1)S(1)}, f16[104,512]{1,0:T(8,128)(2,1)S(1)}, u32[]{:S(2)}, u32[]{:S(2)}) collective-permute-start(f16[104,512]{1,0:T(8,128)(2,1)S(1)} %pad_maximum_fusion.9), channel_id=1, source_target_pairs={{0,2},{2,0},{1,3},{3,1},{4,6},{6,4},{5,7},{7,5},{8,10},{10,8},{9,1... | collective-permute-start | bytes 319496 | tf_op jit(solution)/shard_map/ppermute | solution.py:57
  132.9 8.9 %all-to-all-start.5 = ((f16[4,104,512]{2,1,0:T(8,128)(2,1)}), f16[4,104,512]{2,1,0:T(8,128)(2,1)S(1)}, u32[]{:S(2)}, u32[]{:S(2)}) async-start(f16[4,104,512]{2,1,0:T(8,128)(2,1)} %broadcast_in_dim.45), calls=%async_computation.5 | async-start | bytes 851968 | tf_op jit(solution)/shard_map/all_to_all | solution.py:18
  142.9 9.8 %all-to-all-start.6 = ((f16[4,104,512]{2,1,0:T(8,128)(2,1)}), f16[4,104,512]{2,1,0:T(8,128)(2,1)S(1)}, u32[]{:S(2)}, u32[]{:S(2)}) async-start(f16[4,104,512]{2,1,0:T(8,128)(2,1)} %broadcast_in_dim.48), calls=%async_computation.6 | async-start | bytes 851968 | tf_op jit(solution)/shard_map/all_to_all | solution.py:18
  162.0 1.3 copy-start.7
  165.1 12.2 %all-to-all-start.7 = ((f16[4,200,384]{2,1,0:T(8,128)(2,1)}), f16[4,200,384]{2,1,0:T(8,128)(2,1)S(1)}, u32[]{:S(2)}, u32[]{:S(2)}) async-start(f16[4,200,384]{2,1,0:T(8,128)(2,1)} %pad_maximum_fusion.1), calls=%async_computation.7 | async-start | bytes 1228800 | tf_op jit(solution)/shard_map/all_to_all | solution.py:18
  177.4 0.9 copy-start.2
  177.4 1.7 copy-start

commit v10 on v9

--- a/solution.py
+++ b/solution.py
@@ -57,8 +57,8 @@
     return lax.ppermute(values, axis, [(0, 1), (1, 0)])
 
 
-def around(values, axis, size, step):
-    return lax.ppermute(values, axis, [(i, (i + step) % size) for i in range(size)])
+def flip(values, mask):
+    return lax.ppermute(values, "yp", [(i, i ^ mask) for i in range(4)])
 
 
 def core_part(values, core, own):
@@ -89,10 +89,10 @@
     left_shift = left_shift.reshape(4, 2, 2, 32).transpose(2, 0, 1, 3)
     left_shift = jnp.where(lax.axis_index("zh") == 1, left_shift[:, :, ::-1], left_shift).reshape(512)
     own_shift = lax.dynamic_slice_in_dim(left_shift, level * 128, 128, 0)
-    right_shift = right_shift.reshape(4, 2, 2, 2, 16).transpose(0, 2, 1, 3, 4).reshape(4, 2, 64)[::-1]
+    right_shift = right_shift.reshape(2, 2, 2, 2, 2, 16).transpose(0, 3, 1, 2, 4, 5).reshape(2, 2, 2, 64)
+    right_shift = jnp.where(level >= 2, right_shift[::-1], right_shift)
     right_shift = jnp.where(lax.axis_index("zp") == 1, right_shift[:, ::-1], right_shift)
-    right_shift = jnp.concatenate([right_shift, right_shift], axis=0)
-    right_shift = lax.dynamic_slice_in_dim(right_shift, 3 - level, 4, 0).reshape(512)
+    right_shift = jnp.where(level % 2 == 1, right_shift[:, :, ::-1], right_shift).reshape(512)
 
     right = jnp.concatenate([joined_right_basis.T, output_right_basis.T], axis=1)
     lefts = [jnp.concatenate([basis.T[:16], basis.T[16:]], axis=1) for basis in (joined_left_basis, output_left_basis)]
@@ -119,13 +119,14 @@
     rows = jnp.dot(left, gradient, preferred_element_type=jnp.float32)
     rows = jnp.sum(unpack(exchange(pack(rows.reshape(4, 128, 384)), "yp")), axis=0)
     right = got[:, 192:208].reshape(64, 384)
+    right = jnp.concatenate([right, flip(right, 1)], axis=0)
     scaled = (right.astype(jnp.float32) * 2.0**19).astype(jnp.float16)
     other = swap(jnp.concatenate([pack(rows), scaled], axis=0), "zp")
     rows = (rows + unpack(other[:136])) * own_shift[:, None]
     rows = unpack(exchange(spread(pack(rows), 4), "yp")).reshape(512, 384)
     scaled = (other[136:].astype(jnp.float32) * 2.0**-19).astype(jnp.bfloat16)
     right = jnp.concatenate([right, scaled], axis=0)
-    right = jnp.concatenate([right] + [around(right, "yp", 4, step) for step in (1, 2, 3)], axis=0)
+    right = jnp.concatenate([right, flip(right, 2)], axis=0)
 
     lifted = dot_wide_right(left, rows, ((0,), (0,)))
     applied = gradient.astype(jnp.float32) / damp + lifted

time: 181 us -> 188 us (1.039); the launches traced: 180 us -> 185 us
  waiting for transfers between devices: 54.5 us -> 61.8 us
  starting transfers between devices: 65.5 us -> 62.5 us
    ppermute x3 -> x2, waiting for transfers between devices: 5.15 us -> 9.43 us  [flip(): return lax.ppermute(values, 'yp', [(i, i ^ mask) for i in range(4)])]
    ppermute x4, waiting for transfers between devices: 11.6 us -> 14.1 us  [swap(): return lax.ppermute(values, axis, [(0, 1), (1, 0)])]
    ppermute x3 -> x2, starting transfers between devices: 13.5 us -> 11.5 us  [flip(): return lax.ppermute(values, 'yp', [(i, i ^ mask) for i in range(4)])]
  transfers between devices with their start and end apart: 13 -> 12, of which waited for: 9 -> 9; matrix products, arithmetic and copies ran while one was open for 1% -> 3% of each run, Pallas kernels for 0% -> 0%
where the time goes in v10:
time: 188 us; the launch traced here: 185 us
  starting transfers between devices  62.5 us (33%)
  waiting for transfers between devices  61.8 us (33%)
  blocking collectives  36.9 us (20%)
  local copies, waits for them, and re-layouts  9.17 us (5%)
  other arithmetic  7.48 us (4%)
  matrix products  5.23 us (3%)
  between operations  2.01 us (1%)
    all_to_all x6, waiting for transfers between devices, exchange(): return lax.all_to_all(blocks, axes, 0, 0, tiled=True)  38.2 us
    all_to_all x6, starting transfers between devices, exchange(): return lax.all_to_all(blocks, axes, 0, 0, tiled=True)  26.2 us
    ppermute x4, starting transfers between devices, swap(): return lax.ppermute(values, axis, [(0, 1), (1, 0)])  24.7 us
    all_to_all x2, blocking collectives, exchange(): return lax.all_to_all(blocks, axes, 0, 0, tiled=True)  22.1 us
    ppermute x4, waiting for transfers between devices, swap(): return lax.ppermute(values, axis, [(0, 1), (1, 0)])  14.1 us
    ppermute x2, starting transfers between devices, flip(): return lax.ppermute(values, 'yp', [(i, i ^ mask) for i in range(4)])  11.5 us
    ppermute x2, waiting for transfers between devices, flip(): return lax.ppermute(values, 'yp', [(i, i ^ mask) for i in range(4)])  9.43 us
    all_gather x1, blocking collectives, local(): lax.all_gather(cols, 'c', axis=0, tiled=True)  8.72 us
  transfers between devices with their start and end apart: 12, of which 9 were waited for; matrix products, arithmetic and copies ran while one was open for 3% of the time, Pallas kernels for 0%

profile of v10, /device:TPU:1, one launch (start us, length us, event | category | flops | bytes accessed | tf_op | source)
XLA Modules:
  0.0 185.1 jit_solution(4176712216507491437)
XLA Ops:
  0.6 0.8 fusion.49
  1.5 11.5 %collective-permute-start = (bf16[32,384]{1,0:T(8,128)(2,1)S(1)}, bf16[32,384]{1,0:T(8,128)(2,1)S(1)}, u32[]{:S(2)}, u32[]{:S(2)}) collective-permute-start(bf16[32,384]{1,0:T(8,128)(2,1)S(1)} %maximum_maximum_fusion), channel_id=1, source_target_pairs={{0,2},{2,0},{1,3},{3,1},{4,6},{6,4},{5,7},{7,5},{8,10},{10,8},{9,1... | collective-permute-start | bytes 73736 | tf_op jit(solution)/shard_map/ppermute | solution.py:57
  13.0 1.1 fusion.46
  14.1 0.8 fusion.47
  14.8 0.8 maximum_bitcast_fusion
  15.7 0.1 pad_maximum_fusion
  15.8 11.7 %all_to_all.40 = bf16[4,240,384]{2,1,0:T(8,128)(2,1)S(1)} all-to-all(bf16[4,240,384]{2,1,0:T(8,128)(2,1)S(1)} %pad_maximum_fusion), channel_id=1, replica_groups=mesh['yp'=4,'yb'=2,'zp'=2,'zb'=2,'x'=4,'zh'=2,'c'=2] {'yb','zb'}, dimensions={0} | all-to-all | bytes 1474560 | tf_op jit(solution)/shard_map/all_to_all | solution.py:18
  27.6 0.1 slice_bitcast_fusion.5
  27.7 0.1 pad_maximum_fusion.15
  27.8 0.8 broadcast_in_dim.32
  28.6 4.8 %all-to-all-start.1 = ((bf16[4,64,768]{2,1,0:T(8,128)(2,1)}), bf16[4,64,768]{2,1,0:T(8,128)(2,1)S(1)}, u32[]{:S(2)}, u32[]{:S(2)}) async-start(bf16[4,64,768]{2,1,0:T(8,128)(2,1)} %broadcast_in_dim.32), calls=%async_computation.1 | async-start | bytes 786432 | tf_op jit(solution)/shard_map/all_to_all | solution.py:18
  33.4 6.2 %all-to-all-done.1 = bf16[4,64,768]{2,1,0:T(8,128)(2,1)S(1)} async-done(((bf16[4,64,768]{2,1,0:T(8,128)(2,1)}), bf16[4,64,768]{2,1,0:T(8,128)(2,1)S(1)}, u32[]{:S(2)}, u32[]{:S(2)}) %all-to-all-start.1) | async-done | bytes 393248 | tf_op jit(solution)/shard_map/all_to_all | solution.py:18
  39.6 6.1 %all_gather.6 = bf16[512,768]{1,0:T(8,128)(2,1)S(1)} all-gather(bf16[256,768]{1,0:T(8,128)(2,1)S(1)} %bitcast.92), channel_id=1, replica_groups=mesh['yp'=4,'yb'=2,'zp'=2,'zb'=2,'x'=4,'zh'=2,'c'=2] {'c'}, dimensions={0}, use_global_device_ids=true | all-gather | bytes 1179648 | tf_op jit(solution)/shard_map/all_gather | solution.py:117
  45.7 0.6 abs_reduce_fusion.2
  46.4 0.9 pad_maximum_fusion.3
  47.3 5.9 %all-to-all-start.2 = ((f16[4,136,384]{2,1,0:T(8,128)(2,1)}), f16[4,136,384]{2,1,0:T(8,128)(2,1)S(1)}, u32[]{:S(2)}, u32[]{:S(2)}) async-start(f16[4,136,384]{2,1,0:T(8,128)(2,1)} %pad_maximum_fusion.3), calls=%async_computation.2 | async-start | bytes 835584 | tf_op jit(solution)/shard_map/all_to_all | solution.py:18
  54.0 4.3 %collective-permute-start.1 = (bf16[64,384]{1,0:T(8,128)(2,1)S(1)}, bf16[64,384]{1,0:T(8,128)(2,1)S(1)}, u32[]{:S(2)}, u32[]{:S(2)}) collective-permute-start(bf16[64,384]{1,0:T(8,128)(2,1)S(1)} %bitcast.93), channel_id=1, source_target_pairs={{0,128},{128,0},{256,384},{384,256},{1,129},{129,1},{257,385},{385... | collective-permute-start | bytes 147464 | tf_op jit(solution)/shard_map/ppermute | solution.py:61
  58.4 9.4 %collective-permute-done.1 = bf16[64,384]{1,0:T(8,128)(2,1)S(1)} collective-permute-done((bf16[64,384]{1,0:T(8,128)(2,1)S(1)}, bf16[64,384]{1,0:T(8,128)(2,1)S(1)}, u32[]{:S(2)}, u32[]{:S(2)}) %collective-permute-start.1) | collective-permute-done | bytes 49184 | tf_op jit(solution)/shard_map/ppermute | solution.py:61
  68.1 4.0 %collective-permute-start.2 = (f16[264,384]{1,0:T(8,128)(2,1)S(1)}, f16[264,384]{1,0:T(8,128)(2,1)S(1)}, u32[]{:S(2)}, u32[]{:S(2)}) collective-permute-start(f16[264,384]{1,0:T(8,128)(2,1)S(1)} %pad_maximum_fusion.8), channel_id=1, source_target_pairs={{0,32},{32,0},{1,33},{33,1},{2,34},{34,2},{3,35},{35,3},{4,36},{36... | collective-permute-start | bytes 608264 | tf_op jit(solution)/shard_map/ppermute | solution.py:57
  72.2 0.1 reshape.245
  72.3 9.4 %collective-permute-done.2 = f16[264,384]{1,0:T(8,128)(2,1)S(1)} collective-permute-done((f16[264,384]{1,0:T(8,128)(2,1)S(1)}, f16[264,384]{1,0:T(8,128)(2,1)S(1)}, u32[]{:S(2)}, u32[]{:S(2)}) %collective-permute-start.2) | collective-permute-done | bytes 202784 | tf_op jit(solution)/shard_map/ppermute | solution.py:57
  81.8 0.1 abs_reduce_fusion.6
  81.9 0.1 multiply_convert_fusion.6
  82.1 0.8 broadcast_in_dim.36
  82.8 4.6 %all-to-all-start.3 = ((f16[4,136,384]{2,1,0:T(8,128)(2,1)}), f16[4,136,384]{2,1,0:T(8,128)(2,1)S(1)}, u32[]{:S(2)}, u32[]{:S(2)}) async-start(f16[4,136,384]{2,1,0:T(8,128)(2,1)} %broadcast_in_dim.36), calls=%async_computation.3 | async-start | bytes 835584 | tf_op jit(solution)/shard_map/all_to_all | solution.py:18
  87.5 7.3 %collective-permute-start.3 = (bf16[256,384]{1,0:T(8,128)(2,1)S(1)}, bf16[256,384]{1,0:T(8,128)(2,1)S(1)}, u32[]{:S(2)}, u32[]{:S(2)}) collective-permute-start(bf16[256,384]{1,0:T(8,128)(2,1)S(1)} %pad_maximum_fusion.9), channel_id=1, source_target_pairs={{0,256},{128,384},{256,0},{384,128},{1,257},{129,385},{257,1},{385... | collective-permute-start | bytes 589832 | tf_op jit(solution)/shard_map/ppermute | solution.py:61
  94.8 11.7 %all-to-all-done.3 = f16[4,136,384]{2,1,0:T(8,128)(2,1)S(1)} async-done(((f16[4,136,384]{2,1,0:T(8,128)(2,1)}), f16[4,136,384]{2,1,0:T(8,128)(2,1)S(1)}, u32[]{:S(2)}, u32[]{:S(2)}) %all-to-all-start.3) | async-done | bytes 417824 | tf_op jit(solution)/shard_map/all_to_all | solution.py:18
  106.5 0.1 fusion.3
  106.7 0.6 fusion.51
  107.3 1.6 divide_add_fusion
  108.9 0.6 fusion.4
  109.5 0.6 convolution_add_fusion
  110.1 0.9 constant_dynamic-slice_fusion
  111.1 2.5 %collective-permute-start.4 = (f32[384,512]{1,0:T(8,128)}, f32[384,512]{1,0:T(8,128)S(1)}, u32[]{:S(2)}, u32[]{:S(2)}) collective-permute-start(f32[384,512]{1,0:T(8,128)} %constant_dynamic-slice_fusion), channel_id=1, source_target_pairs={{0,1},{1,0},{2,3},{3,2},{4,5},{5,4},{6,7},{7,6},{8,9},{9,8},{10,11... | collective-permute-start | bytes 2359304 | tf_op jit(solution)/shard_map/ppermute | solution.py:57
  113.6 2.1 %collective-permute-done.4 = f32[384,512]{1,0:T(8,128)S(1)} collective-permute-done((f32[384,512]{1,0:T(8,128)}, f32[384,512]{1,0:T(8,128)S(1)}, u32[]{:S(2)}, u32[]{:S(2)}) %collective-permute-start.4) | collective-permute-done | bytes 786464 | tf_op jit(solution)/shard_map/ppermute | solution.py:57
  115.7 0.1 dynamic-slice_add_fusion
  115.9 0.1 multiply_convert_fusion.1
  116.0 0.1 pad_maximum_fusion.2
  116.1 10.4 %all_to_all.41 = f16[4,104,512]{2,1,0:T(8,128)(2,1)S(1)} all-to-all(f16[4,104,512]{2,1,0:T(8,128)(2,1)S(1)} %pad_maximum_fusion.2), channel_id=1, replica_groups=mesh['yp'=4,'yb'=2,'zp'=2,'zb'=2,'x'=4,'zh'=2,'c'=2] {'x'}, dimensions={0} | all-to-all | bytes 851968 | tf_op jit(solution)/shard_map/all_to_all | solution.py:18
  126.8 6.8 %collective-permute-start.5 = (f16[104,512]{1,0:T(8,128)(2,1)S(1)}, f16[104,512]{1,0:T(8,128)(2,1)S(1)}, u32[]{:S(2)}, u32[]{:S(2)}) collective-permute-start(f16[104,512]{1,0:T(8,128)(2,1)S(1)} %pad_maximum_fusion.11), channel_id=1, source_target_pairs={{0,2},{2,0},{1,3},{3,1},{4,6},{6,4},{5,7},{7,5},{8,10},{10,8},{9,1... | collective-permute-start | bytes 319496 | tf_op jit(solution)/shard_map/ppermute | solution.py:57
  133.6 2.6 %collective-permute-done.5 = f16[104,512]{1,0:T(8,128)(2,1)S(1)} collective-permute-done((f16[104,512]{1,0:T(8,128)(2,1)S(1)}, f16[104,512]{1,0:T(8,128)(2,1)S(1)}, u32[]{:S(2)}, u32[]{:S(2)}) %collective-permute-start.5) | collective-permute-done | bytes 106528 | tf_op jit(solution)/shard_map/ppermute | solution.py:57
  136.4 0.8 broadcast_in_dim.45
  137.2 4.0 %all-to-all-start.5 = ((f16[4,104,512]{2,1,0:T(8,128)(2,1)}), f16[4,104,512]{2,1,0:T(8,128)(2,1)S(1)}, u32[]{:S(2)}, u32[]{:S(2)}) async-start(f16[4,104,512]{2,1,0:T(8,128)(2,1)} %broadcast_in_dim.45), calls=%async_computation.5 | async-start | bytes 851968 | tf_op jit(solution)/shard_map/all_to_all | solution.py:18
  141.2 0.1 reshape.249
  141.3 0.1 reshape.250
  141.4 5.4 %all-to-all-done.5 = f16[4,104,512]{2,1,0:T(8,128)(2,1)S(1)} async-done(((f16[4,104,512]{2,1,0:T(8,128)(2,1)}), f16[4,104,512]{2,1,0:T(8,128)(2,1)S(1)}, u32[]{:S(2)}, u32[]{:S(2)}) %all-to-all-start.5) | async-done | bytes 426016 | tf_op jit(solution)/shard_map/all_to_all | solution.py:18
  146.9 0.1 select_reduce_fusion
  147.1 0.8 broadcast_in_dim.48
  147.9 3.5 %all-to-all-start.6 = ((f16[4,104,512]{2,1,0:T(8,128)(2,1)}), f16[4,104,512]{2,1,0:T(8,128)(2,1)S(1)}, u32[]{:S(2)}, u32[]{:S(2)}) async-start(f16[4,104,512]{2,1,0:T(8,128)(2,1)} %broadcast_in_dim.48), calls=%async_computation.6 | async-start | bytes 851968 | tf_op jit(solution)/shard_map/all_to_all | solution.py:18
  151.4 0.1 mul.231
  151.5 6.2 %all-to-all-done.6 = f16[4,104,512]{2,1,0:T(8,128)(2,1)S(1)} async-done(((f16[4,104,512]{2,1,0:T(8,128)(2,1)}), f16[4,104,512]{2,1,0:T(8,128)(2,1)S(1)}, u32[]{:S(2)}, u32[]{:S(2)}) %all-to-all-start.6) | async-done | bytes 426016 | tf_op jit(solution)/shard_map/all_to_all | solution.py:18
  157.7 8.7 %all_gather.7 = f16[8,104,512]{2,1,0:T(8,128)(2,1)S(1)} all-gather(f16[4,104,512]{2,1,0:T(8,128)(2,1)S(1)} %all-to-all-done.6), channel_id=1, replica_groups=mesh['yp'=4,'yb'=2,'zp'=2,'zb'=2,'x'=4,'zh'=2,'c'=2] {'c'}, dimensions={0}, use_global_device_ids=true | all-gather | bytes 1277952 | tf_op jit(solution)/shard_map/all_gather | solution.py:141
  166.5 0.2 convert_multiply_fusion
  166.7 0.3 reduce-precision_convert_fusion
  167.0 0.6 fusion.45
  167.6 0.7 copy-done.7
  168.3 0.6 fusion.1
  169.0 0.1 multiply_convert_fusion
  169.1 1.0 pad_maximum_fusion.1
  170.1 3.5 %all-to-all-start.7 = ((f16[4,200,384]{2,1,0:T(8,128)(2,1)}), f16[4,200,384]{2,1,0:T(8,128)(2,1)S(1)}, u32[]{:S(2)}, u32[]{:S(2)}) async-start(f16[4,200,384]{2,1,0:T(8,128)(2,1)} %pad_maximum_fusion.1), calls=%async_computation.7 | async-start | bytes 1228800 | tf_op jit(solution)/shard_map/all_to_all | solution.py:18
  173.6 8.7 %all-to-all-done.7 = f16[4,200,384]{2,1,0:T(8,128)(2,1)S(1)} async-done(((f16[4,200,384]{2,1,0:T(8,128)(2,1)}), f16[4,200,384]{2,1,0:T(8,128)(2,1)S(1)}, u32[]{:S(2)}, u32[]{:S(2)}) %all-to-all-start.7) | async-done | bytes 614432 | tf_op jit(solution)/shard_map/all_to_all | solution.py:18
  182.5 0.8 copy-done.2
  183.3 0.7 fusion.6
  184.1 1.0 maximum_add_fusion
  (88 shorter events, 2.0 us)
Async XLA Ops:
  0.6 14.2 %copy-start.1 = (bf16[192,384]{1,0:T(8,128)(2,1)S(1)}, bf16[192,384]{1,0:T(8,128)(2,1)}, u32[]{:S(2)}) copy-start(bf16[192,384]{1,0:T(8,128)(2,1)} %param.12) | copy-start | bytes 442372
  1.5 13.3 %collective-permute-start = (bf16[32,384]{1,0:T(8,128)(2,1)S(1)}, bf16[32,384]{1,0:T(8,128)(2,1)S(1)}, u32[]{:S(2)}, u32[]{:S(2)}) collective-permute-start(bf16[32,384]{1,0:T(8,128)(2,1)S(1)} %maximum_maximum_fusion), channel_id=1, source_target_pairs={{0,2},{2,0},{1,3},{3,1},{4,6},{6,4},{5,7},{7,5},{8,10},{10,8},{9,1... | collective-permute-start | bytes 73736 | tf_op jit(solution)/shard_map/ppermute | solution.py:57
  28.6 11.0 %all-to-all-start.1 = ((bf16[4,64,768]{2,1,0:T(8,128)(2,1)}), bf16[4,64,768]{2,1,0:T(8,128)(2,1)S(1)}, u32[]{:S(2)}, u32[]{:S(2)}) async-start(bf16[4,64,768]{2,1,0:T(8,128)(2,1)} %broadcast_in_dim.32), calls=%async_computation.1 | async-start | bytes 786432 | tf_op jit(solution)/shard_map/all_to_all | solution.py:18
  46.4 11.9 %copy-start.3 = (f32[512]{0:T(512)S(1)}, f32[512]{0:T(512)}, u32[]{:S(2)}) copy-start(f32[512]{0:T(512)} %param.20) | copy-start | bytes 6148
  46.4 11.9 %copy-start.4 = (f32[512]{0:T(512)S(1)}, f32[512]{0:T(512)}, u32[]{:S(2)}) copy-start(f32[512]{0:T(512)} %param.18) | copy-start | bytes 6148
  46.4 11.8 %copy-start.5 = (f32[512]{0:T(512)S(1)}, f32[512]{0:T(512)}, u32[]{:S(2)}) copy-start(f32[512]{0:T(512)} %param.19) | copy-start | bytes 6148
  46.4 11.8 %copy-start.6 = (f32[512]{0:T(512)S(1)}, f32[512]{0:T(512)}, u32[]{:S(2)}) copy-start(f32[512]{0:T(512)} %param.17) | copy-start | bytes 6148
  47.3 20.5 %all-to-all-start.2 = ((f16[4,136,384]{2,1,0:T(8,128)(2,1)}), f16[4,136,384]{2,1,0:T(8,128)(2,1)S(1)}, u32[]{:S(2)}, u32[]{:S(2)}) async-start(f16[4,136,384]{2,1,0:T(8,128)(2,1)} %pad_maximum_fusion.3), calls=%async_computation.2 | async-start | bytes 835584 | tf_op jit(solution)/shard_map/all_to_all | solution.py:18
  54.0 13.9 %collective-permute-start.1 = (bf16[64,384]{1,0:T(8,128)(2,1)S(1)}, bf16[64,384]{1,0:T(8,128)(2,1)S(1)}, u32[]{:S(2)}, u32[]{:S(2)}) collective-permute-start(bf16[64,384]{1,0:T(8,128)(2,1)S(1)} %bitcast.93), channel_id=1, source_target_pairs={{0,128},{128,0},{256,384},{384,256},{1,129},{129,1},{257,385},{385... | collective-permute-start | bytes 147464 | tf_op jit(solution)/shard_map/ppermute | solution.py:61
  68.1 13.6 %collective-permute-start.2 = (f16[264,384]{1,0:T(8,128)(2,1)S(1)}, f16[264,384]{1,0:T(8,128)(2,1)S(1)}, u32[]{:S(2)}, u32[]{:S(2)}) collective-permute-start(f16[264,384]{1,0:T(8,128)(2,1)S(1)} %pad_maximum_fusion.8), channel_id=1, source_target_pairs={{0,32},{32,0},{1,33},{33,1},{2,34},{34,2},{3,35},{35,3},{4,36},{36... | collective-permute-start | bytes 608264 | tf_op jit(solution)/shard_map/ppermute | solution.py:57
  82.8 23.6 %all-to-all-start.3 = ((f16[4,136,384]{2,1,0:T(8,128)(2,1)}), f16[4,136,384]{2,1,0:T(8,128)(2,1)S(1)}, u32[]{:S(2)}, u32[]{:S(2)}) async-start(f16[4,136,384]{2,1,0:T(8,128)(2,1)} %broadcast_in_dim.36), calls=%async_computation.3 | async-start | bytes 835584 | tf_op jit(solution)/shard_map/all_to_all | solution.py:18
  87.5 21.4 %collective-permute-start.3 = (bf16[256,384]{1,0:T(8,128)(2,1)S(1)}, bf16[256,384]{1,0:T(8,128)(2,1)S(1)}, u32[]{:S(2)}, u32[]{:S(2)}) collective-permute-start(bf16[256,384]{1,0:T(8,128)(2,1)S(1)} %pad_maximum_fusion.9), channel_id=1, source_target_pairs={{0,256},{128,384},{256,0},{384,128},{1,257},{129,385},{257,1},{385... | collective-permute-start | bytes 589832 | tf_op jit(solution)/shard_map/ppermute | solution.py:61
  111.1 4.6 %collective-permute-start.4 = (f32[384,512]{1,0:T(8,128)}, f32[384,512]{1,0:T(8,128)S(1)}, u32[]{:S(2)}, u32[]{:S(2)}) collective-permute-start(f32[384,512]{1,0:T(8,128)} %constant_dynamic-slice_fusion), channel_id=1, source_target_pairs={{0,1},{1,0},{2,3},{3,2},{4,5},{5,4},{6,7},{7,6},{8,9},{9,8},{10,11... | collective-permute-start | bytes 2359304 | tf_op jit(solution)/shard_map/ppermute | solution.py:57
  126.8 9.5 %collective-permute-start.5 = (f16[104,512]{1,0:T(8,128)(2,1)S(1)}, f16[104,512]{1,0:T(8,128)(2,1)S(1)}, u32[]{:S(2)}, u32[]{:S(2)}) collective-permute-start(f16[104,512]{1,0:T(8,128)(2,1)S(1)} %pad_maximum_fusion.11), channel_id=1, source_target_pairs={{0,2},{2,0},{1,3},{3,1},{4,6},{6,4},{5,7},{7,5},{8,10},{10,8},{9,1... | collective-permute-start | bytes 319496 | tf_op jit(solution)/shard_map/ppermute | solution.py:57
  137.2 9.6 %all-to-all-start.5 = ((f16[4,104,512]{2,1,0:T(8,128)(2,1)}), f16[4,104,512]{2,1,0:T(8,128)(2,1)S(1)}, u32[]{:S(2)}, u32[]{:S(2)}) async-start(f16[4,104,512]{2,1,0:T(8,128)(2,1)} %broadcast_in_dim.45), calls=%async_computation.5 | async-start | bytes 851968 | tf_op jit(solution)/shard_map/all_to_all | solution.py:18
  147.9 9.8 %all-to-all-start.6 = ((f16[4,104,512]{2,1,0:T(8,128)(2,1)}), f16[4,104,512]{2,1,0:T(8,128)(2,1)S(1)}, u32[]{:S(2)}, u32[]{:S(2)}) async-start(f16[4,104,512]{2,1,0:T(8,128)(2,1)} %broadcast_in_dim.48), calls=%async_computation.6 | async-start | bytes 851968 | tf_op jit(solution)/shard_map/all_to_all | solution.py:18
  167.0 1.3 copy-start.7
  170.1 12.2 %all-to-all-start.7 = ((f16[4,200,384]{2,1,0:T(8,128)(2,1)}), f16[4,200,384]{2,1,0:T(8,128)(2,1)S(1)}, u32[]{:S(2)}, u32[]{:S(2)}) async-start(f16[4,200,384]{2,1,0:T(8,128)(2,1)} %pad_maximum_fusion.1), calls=%async_computation.7 | async-start | bytes 1228800 | tf_op jit(solution)/shard_map/all_to_all | solution.py:18
  182.4 0.9 copy-start.2
  182.4 1.7 copy-start

commit v11 on v9

--- a/solution.py
+++ b/solution.py
@@ -35,11 +35,11 @@
     return dot(high) + dot(low)
 
 
-def pack(values):
+def pack(values, after=0.0):
     top = jnp.max(jnp.abs(values), axis=-2, keepdims=True)
     power = jnp.clip(jnp.floor(jnp.log2(jnp.maximum(top, 1e-30))), -100.0, 120.0)
     scaled = (values * jnp.exp2(14.0 - power)).astype(jnp.float16)
-    tail = jnp.broadcast_to(power.astype(jnp.float16), values.shape[:-2] + (8, values.shape[-1]))
+    tail = jnp.broadcast_to((power + after).astype(jnp.float16), values.shape[:-2] + (8, values.shape[-1]))
     return jnp.concatenate([scaled, tail], axis=-2)
 
 
@@ -89,10 +89,10 @@
     left_shift = left_shift.reshape(4, 2, 2, 32).transpose(2, 0, 1, 3)
     left_shift = jnp.where(lax.axis_index("zh") == 1, left_shift[:, :, ::-1], left_shift).reshape(512)
     own_shift = lax.dynamic_slice_in_dim(left_shift, level * 128, 128, 0)
-    right_shift = right_shift.reshape(4, 2, 2, 2, 16).transpose(0, 2, 1, 3, 4).reshape(4, 2, 64)[::-1]
-    right_shift = jnp.where(lax.axis_index("zp") == 1, right_shift[:, ::-1], right_shift)
-    right_shift = jnp.concatenate([right_shift, right_shift], axis=0)
-    right_shift = lax.dynamic_slice_in_dim(right_shift, 3 - level, 4, 0).reshape(512)
+    right_shift = right_shift.reshape(4, 2, 2, 2, 16).transpose(2, 0, 1, 3, 4).reshape(2, 4, 64)[:, ::-1]
+    right_shift = jnp.where(lax.axis_index("zp") == 1, right_shift[::-1], right_shift)
+    right_shift = jnp.concatenate([right_shift, right_shift], axis=1)
+    right_shift = lax.dynamic_slice_in_dim(right_shift, 3 - level, 4, 1).reshape(512)
 
     right = jnp.concatenate([joined_right_basis.T, output_right_basis.T], axis=1)
     lefts = [jnp.concatenate([basis.T[:16], basis.T[16:]], axis=1) for basis in (joined_left_basis, output_left_basis)]
@@ -116,16 +116,18 @@
     left = exchange(spread(left, 4), "x").reshape(256, 768)
     left = lax.all_gather(left, "c", axis=0, tiled=True)
 
+    right = got[:, 192:208].reshape(64, 384)
+    parts = [around(right, "yp", 4, step) for step in (1, 2, 3)]
+    here = sum(part[0, 0].astype(jnp.float32) for part in parts) * 0.0
+    right = jnp.concatenate([right] + parts, axis=0)
+    other = swap(right, "zp")
+    there = other[0, 0].astype(jnp.float32) * 0.0
+    right = jnp.concatenate([right, other], axis=0)
+
     rows = jnp.dot(left, gradient, preferred_element_type=jnp.float32)
-    rows = jnp.sum(unpack(exchange(pack(rows.reshape(4, 128, 384)), "yp")), axis=0)
-    right = got[:, 192:208].reshape(64, 384)
-    scaled = (right.astype(jnp.float32) * 2.0**19).astype(jnp.float16)
-    other = swap(jnp.concatenate([pack(rows), scaled], axis=0), "zp")
-    rows = (rows + unpack(other[:136])) * own_shift[:, None]
+    rows = jnp.sum(unpack(exchange(pack(rows.reshape(4, 128, 384), here), "yp")), axis=0)
+    rows = (rows + unpack(swap(pack(rows, there), "zp"))) * own_shift[:, None]
     rows = unpack(exchange(spread(pack(rows), 4), "yp")).reshape(512, 384)
-    scaled = (other[136:].astype(jnp.float32) * 2.0**-19).astype(jnp.bfloat16)
-    right = jnp.concatenate([right, scaled], axis=0)
-    right = jnp.concatenate([right] + [around(right, "yp", 4, step) for step in (1, 2, 3)], axis=0)
 
     lifted = dot_wide_right(left, rows, ((0,), (0,)))
     applied = gradient.astype(jnp.float32) / damp + lifted

time: 181 us -> 189 us (1.044)
  starting transfers between devices: 65.5 us -> 69.1 us
  between operations: 2.08 us -> 4.53 us
  local copies, waits for them, and re-layouts: 8.35 us -> 10.4 us
  waiting for transfers between devices: 54.5 us -> 52.5 us
    ppermute x4 -> x5, waiting for transfers between devices: 11.6 us -> 21 us  [swap(): return lax.ppermute(values, axis, [(0, 1), (1, 0)])]
    all_to_all x6, waiting for transfers between devices: 37.8 us -> 31.4 us  [exchange(): return lax.all_to_all(blocks, axes, 0, 0, tiled=True)]
    ppermute x3, waiting for transfers between devices: 5.15 us -> 0.01 us  [around(): lax.ppermute(values, axis, [(i, (i + step) % size) for i in range(size)])]
    slice x0 -> x4, local copies, waits for them, and re-layouts: none -> 2.05 us  [the longest x3 1.54 us: local(): here = sum((part[0, 0].astype(jnp.float32) for part in parts)) * 0.0]
    ppermute x4 -> x5, starting transfers between devices: 26.3 us -> 28.1 us  [swap(): return lax.ppermute(values, axis, [(0, 1), (1, 0)])]
  transfers between devices with their start and end apart: 13 -> 14, of which waited for: 9 -> 8; matrix products, arithmetic and copies ran while one was open for 1% -> 3% of each run, Pallas kernels for 0% -> 0%
where the time goes in v11:
time: 189 us; the launch traced here: 188 us
  starting transfers between devices  69.1 us (37%)
  waiting for transfers between devices  52.5 us (28%)
  blocking collectives  38.7 us (20%)
  local copies, waits for them, and re-layouts  10.4 us (6%)
  other arithmetic  7.42 us (4%)
  matrix products  5.2 us (3%)
  between operations  4.53 us (2%)
    all_to_all x6, waiting for transfers between devices, exchange(): return lax.all_to_all(blocks, axes, 0, 0, tiled=True)  31.4 us
    ppermute x5, starting transfers between devices, swap(): return lax.ppermute(values, axis, [(0, 1), (1, 0)])  28.1 us
    all_to_all x6, starting transfers between devices, exchange(): return lax.all_to_all(blocks, axes, 0, 0, tiled=True)  27.1 us
    all_to_all x2, blocking collectives, exchange(): return lax.all_to_all(blocks, axes, 0, 0, tiled=True)  23.9 us
    ppermute x5, waiting for transfers between devices, swap(): return lax.ppermute(values, axis, [(0, 1), (1, 0)])  21 us
    ppermute x3, starting transfers between devices, around(): lax.ppermute(values, axis, [(i, (i + step) % size) for i in range(size)])  14 us
    all_gather x1, blocking collectives, local(): lax.all_gather(cols, 'c', axis=0, tiled=True)  9.04 us
    all_gather x1, blocking collectives, local(): left = lax.all_gather(left, 'c', axis=0, tiled=True)  5.77 us
  transfers between devices with their start and end apart: 14, of which 8 were waited for; matrix products, arithmetic and copies ran while one was open for 3% of the time, Pallas kernels for 0%

profile of v11, /device:TPU:1, one launch (start us, length us, event | category | flops | bytes accessed | tf_op | source)
XLA Modules:
  0.0 187.9 jit_solution(10856060052398191891)
XLA Ops:
  0.6 0.8 fusion.47
  1.5 11.5 %collective-permute-start = (bf16[32,384]{1,0:T(8,128)(2,1)S(1)}, bf16[32,384]{1,0:T(8,128)(2,1)S(1)}, u32[]{:S(2)}, u32[]{:S(2)}) collective-permute-start(bf16[32,384]{1,0:T(8,128)(2,1)S(1)} %maximum_maximum_fusion), channel_id=1, source_target_pairs={{0,2},{2,0},{1,3},{3,1},{4,6},{6,4},{5,7},{7,5},{8,10},{10,8},{9,1... | collective-permute-start | bytes 73736 | tf_op jit(solution)/shard_map/ppermute | solution.py:57
  13.0 1.1 fusion.44
  14.1 0.8 fusion.45
  14.8 0.8 maximum_bitcast_fusion
  15.7 0.1 pad_maximum_fusion
  15.8 11.7 %all_to_all.40 = bf16[4,240,384]{2,1,0:T(8,128)(2,1)S(1)} all-to-all(bf16[4,240,384]{2,1,0:T(8,128)(2,1)S(1)} %pad_maximum_fusion), channel_id=1, replica_groups=mesh['yp'=4,'yb'=2,'zp'=2,'zb'=2,'x'=4,'zh'=2,'c'=2] {'yb','zb'}, dimensions={0} | all-to-all | bytes 1474560 | tf_op jit(solution)/shard_map/all_to_all | solution.py:18
  27.7 0.1 pad_maximum_fusion.14
  27.8 0.8 broadcast_in_dim.32
  28.6 4.8 %all-to-all-start.1 = ((bf16[4,64,768]{2,1,0:T(8,128)(2,1)}), bf16[4,64,768]{2,1,0:T(8,128)(2,1)S(1)}, u32[]{:S(2)}, u32[]{:S(2)}) async-start(bf16[4,64,768]{2,1,0:T(8,128)(2,1)} %broadcast_in_dim.32), calls=%async_computation.1 | async-start | bytes 786432 | tf_op jit(solution)/shard_map/all_to_all | solution.py:18
  33.4 6.6 %collective-permute-start.2 = (bf16[64,384]{1,0:T(8,128)(2,1)S(1)}, bf16[64,384]{1,0:T(8,128)(2,1)S(1)}, u32[]{:S(2)}, u32[]{:S(2)}) collective-permute-start(bf16[64,384]{1,0:T(8,128)(2,1)S(1)} %bitcast.103), channel_id=1, source_target_pairs={{0,256},{128,384},{256,0},{384,128},{1,257},{129,385},{257,1},{385... | collective-permute-start | bytes 147464 | tf_op jit(solution)/shard_map/ppermute | solution.py:61
  40.0 2.4 %collective-permute-start.1 = (bf16[64,384]{1,0:T(8,128)(2,1)S(1)}, bf16[64,384]{1,0:T(8,128)(2,1)S(1)}, u32[]{:S(2)}, u32[]{:S(2)}) collective-permute-start(bf16[64,384]{1,0:T(8,128)(2,1)S(1)} %bitcast.104), channel_id=1, source_target_pairs={{0,128},{128,256},{256,384},{384,0},{1,129},{129,257},{257,385},{3... | collective-permute-start | bytes 147464 | tf_op jit(solution)/shard_map/ppermute | solution.py:61
  42.4 5.0 %collective-permute-start.3 = (bf16[64,384]{1,0:T(8,128)(2,1)S(1)}, bf16[64,384]{1,0:T(8,128)(2,1)S(1)}, u32[]{:S(2)}, u32[]{:S(2)}) collective-permute-start(bf16[64,384]{1,0:T(8,128)(2,1)S(1)} %bitcast.105), channel_id=1, source_target_pairs={{0,384},{128,0},{256,128},{384,256},{1,385},{129,1},{257,129},{385... | collective-permute-start | bytes 147464 | tf_op jit(solution)/shard_map/ppermute | solution.py:61
  47.5 0.5 slice.205
  48.0 0.5 slice.204
  49.7 0.5 slice.206
  50.9 5.8 %all_gather.6 = bf16[512,768]{1,0:T(8,128)(2,1)S(1)} all-gather(bf16[256,768]{1,0:T(8,128)(2,1)S(1)} %bitcast.101), channel_id=1, replica_groups=mesh['yp'=4,'yb'=2,'zp'=2,'zb'=2,'x'=4,'zh'=2,'c'=2] {'c'}, dimensions={0}, use_global_device_ids=true | all-gather | bytes 1179648 | tf_op jit(solution)/shard_map/all_gather | solution.py:117
  56.7 0.6 abs_reduce_fusion.2
  57.4 0.9 pad_maximum_fusion.3
  58.3 5.4 %all-to-all-start.2 = ((f16[4,136,384]{2,1,0:T(8,128)(2,1)}), f16[4,136,384]{2,1,0:T(8,128)(2,1)S(1)}, u32[]{:S(2)}, u32[]{:S(2)}) async-start(f16[4,136,384]{2,1,0:T(8,128)(2,1)} %pad_maximum_fusion.3), calls=%async_computation.2 | async-start | bytes 835584 | tf_op jit(solution)/shard_map/all_to_all | solution.py:18
  64.4 4.0 %collective-permute-start.4 = (bf16[256,384]{1,0:T(8,128)(2,1)S(1)}, bf16[256,384]{1,0:T(8,128)(2,1)S(1)}, u32[]{:S(2)}, u32[]{:S(2)}) collective-permute-start(bf16[256,384]{1,0:T(8,128)(2,1)S(1)} %pad_maximum_fusion.7), channel_id=1, source_target_pairs={{0,32},{32,0},{1,33},{33,1},{2,34},{34,2},{3,35},{35,3},{4,36},{36... | collective-permute-start | bytes 589832 | tf_op jit(solution)/shard_map/ppermute | solution.py:57
  68.5 9.4 %collective-permute-done.4 = bf16[256,384]{1,0:T(8,128)(2,1)S(1)} collective-permute-done((bf16[256,384]{1,0:T(8,128)(2,1)S(1)}, bf16[256,384]{1,0:T(8,128)(2,1)S(1)}, u32[]{:S(2)}, u32[]{:S(2)}) %collective-permute-start.4) | collective-permute-done | bytes 196640 | tf_op jit(solution)/shard_map/ppermute | solution.py:57
  78.0 0.5 slice.209
  79.3 1.9 %collective-permute-start.5 = (f16[136,384]{1,0:T(8,128)(2,1)S(1)}, f16[136,384]{1,0:T(8,128)(2,1)S(1)}, u32[]{:S(2)}, u32[]{:S(2)}) collective-permute-start(f16[136,384]{1,0:T(8,128)(2,1)S(1)} %pad_maximum_fusion.12), channel_id=1, source_target_pairs={{0,32},{32,0},{1,33},{33,1},{2,34},{34,2},{3,35},{35,3},{4,36},{36... | collective-permute-start | bytes 313352 | tf_op jit(solution)/shard_map/ppermute | solution.py:57
  81.5 7.1 %collective-permute-done.5 = f16[136,384]{1,0:T(8,128)(2,1)S(1)} collective-permute-done((f16[136,384]{1,0:T(8,128)(2,1)S(1)}, f16[136,384]{1,0:T(8,128)(2,1)S(1)}, u32[]{:S(2)}, u32[]{:S(2)}) %collective-permute-start.5) | collective-permute-done | bytes 104480 | tf_op jit(solution)/shard_map/ppermute | solution.py:57
  88.6 0.1 abs_reduce_fusion.6
  88.7 0.1 multiply_convert_fusion.6
  88.9 0.8 broadcast_in_dim.36
  89.7 6.6 %all-to-all-start.3 = ((f16[4,136,384]{2,1,0:T(8,128)(2,1)}), f16[4,136,384]{2,1,0:T(8,128)(2,1)S(1)}, u32[]{:S(2)}, u32[]{:S(2)}) async-start(f16[4,136,384]{2,1,0:T(8,128)(2,1)} %broadcast_in_dim.36), calls=%async_computation.3 | async-start | bytes 835584 | tf_op jit(solution)/shard_map/all_to_all | solution.py:18
  96.3 11.9 %all-to-all-done.3 = f16[4,136,384]{2,1,0:T(8,128)(2,1)S(1)} async-done(((f16[4,136,384]{2,1,0:T(8,128)(2,1)}), f16[4,136,384]{2,1,0:T(8,128)(2,1)S(1)}, u32[]{:S(2)}, u32[]{:S(2)}) %all-to-all-start.3) | async-done | bytes 417824 | tf_op jit(solution)/shard_map/all_to_all | solution.py:18
  108.3 0.1 fusion.3
  108.4 0.6 fusion.49
  109.0 1.6 divide_add_fusion
  110.7 0.6 fusion.4
  111.3 0.6 convolution_add_fusion
  112.0 3.8 %collective-permute-start.6 = (f32[384,512]{1,0:T(8,128)S(1)}, f32[384,512]{1,0:T(8,128)S(1)}, u32[]{:S(2)}, u32[]{:S(2)}) collective-permute-start(f32[384,512]{1,0:T(8,128)S(1)} %constant_dynamic-slice_fusion), channel_id=1, source_target_pairs={{0,1},{1,0},{2,3},{3,2},{4,5},{5,4},{6,7},{7,6},{8,9},{9,8},{10,11... | collective-permute-start | bytes 2359304 | tf_op jit(solution)/shard_map/ppermute | solution.py:57
  115.8 1.9 %collective-permute-done.6 = f32[384,512]{1,0:T(8,128)S(1)} collective-permute-done((f32[384,512]{1,0:T(8,128)S(1)}, f32[384,512]{1,0:T(8,128)S(1)}, u32[]{:S(2)}, u32[]{:S(2)}) %collective-permute-start.6) | collective-permute-done | bytes 786464 | tf_op jit(solution)/shard_map/ppermute | solution.py:57
  117.7 0.1 dynamic-slice_add_fusion
  118.0 0.1 multiply_convert_fusion.1
  118.1 0.1 pad_maximum_fusion.2
  118.2 12.2 %all_to_all.41 = f16[4,104,512]{2,1,0:T(8,128)(2,1)S(1)} all-to-all(f16[4,104,512]{2,1,0:T(8,128)(2,1)S(1)} %pad_maximum_fusion.2), channel_id=1, replica_groups=mesh['yp'=4,'yb'=2,'zp'=2,'zb'=2,'x'=4,'zh'=2,'c'=2] {'x'}, dimensions={0} | all-to-all | bytes 851968 | tf_op jit(solution)/shard_map/all_to_all | solution.py:18
  130.6 6.8 %collective-permute-start.7 = (f16[104,512]{1,0:T(8,128)(2,1)S(1)}, f16[104,512]{1,0:T(8,128)(2,1)S(1)}, u32[]{:S(2)}, u32[]{:S(2)}) collective-permute-start(f16[104,512]{1,0:T(8,128)(2,1)S(1)} %pad_maximum_fusion.9), channel_id=1, source_target_pairs={{0,2},{2,0},{1,3},{3,1},{4,6},{6,4},{5,7},{7,5},{8,10},{10,8},{9,1... | collective-permute-start | bytes 319496 | tf_op jit(solution)/shard_map/ppermute | solution.py:57
  137.4 2.6 %collective-permute-done.7 = f16[104,512]{1,0:T(8,128)(2,1)S(1)} collective-permute-done((f16[104,512]{1,0:T(8,128)(2,1)S(1)}, f16[104,512]{1,0:T(8,128)(2,1)S(1)}, u32[]{:S(2)}, u32[]{:S(2)}) %collective-permute-start.7) | collective-permute-done | bytes 106528 | tf_op jit(solution)/shard_map/ppermute | solution.py:57
  140.2 0.8 broadcast_in_dim.45
  141.0 3.5 %all-to-all-start.5 = ((f16[4,104,512]{2,1,0:T(8,128)(2,1)}), f16[4,104,512]{2,1,0:T(8,128)(2,1)S(1)}, u32[]{:S(2)}, u32[]{:S(2)}) async-start(f16[4,104,512]{2,1,0:T(8,128)(2,1)} %broadcast_in_dim.45), calls=%async_computation.5 | async-start | bytes 851968 | tf_op jit(solution)/shard_map/all_to_all | solution.py:18
  144.6 0.1 reshape.264
  144.8 4.6 %all-to-all-done.5 = f16[4,104,512]{2,1,0:T(8,128)(2,1)S(1)} async-done(((f16[4,104,512]{2,1,0:T(8,128)(2,1)}), f16[4,104,512]{2,1,0:T(8,128)(2,1)S(1)}, u32[]{:S(2)}, u32[]{:S(2)}) %all-to-all-start.5) | async-done | bytes 426016 | tf_op jit(solution)/shard_map/all_to_all | solution.py:18
  149.4 0.1 select_reduce_fusion
  149.7 0.8 broadcast_in_dim.48
  150.4 3.5 %all-to-all-start.6 = ((f16[4,104,512]{2,1,0:T(8,128)(2,1)}), f16[4,104,512]{2,1,0:T(8,128)(2,1)S(1)}, u32[]{:S(2)}, u32[]{:S(2)}) async-start(f16[4,104,512]{2,1,0:T(8,128)(2,1)} %broadcast_in_dim.48), calls=%async_computation.6 | async-start | bytes 851968 | tf_op jit(solution)/shard_map/all_to_all | solution.py:18
  154.0 6.2 %all-to-all-done.6 = f16[4,104,512]{2,1,0:T(8,128)(2,1)S(1)} async-done(((f16[4,104,512]{2,1,0:T(8,128)(2,1)}), f16[4,104,512]{2,1,0:T(8,128)(2,1)S(1)}, u32[]{:S(2)}, u32[]{:S(2)}) %all-to-all-start.6) | async-done | bytes 426016 | tf_op jit(solution)/shard_map/all_to_all | solution.py:18
  160.3 9.0 %all_gather.7 = f16[8,104,512]{2,1,0:T(8,128)(2,1)S(1)} all-gather(f16[4,104,512]{2,1,0:T(8,128)(2,1)S(1)} %all-to-all-done.6), channel_id=1, replica_groups=mesh['yp'=4,'yb'=2,'zp'=2,'zb'=2,'x'=4,'zh'=2,'c'=2] {'c'}, dimensions={0}, use_global_device_ids=true | all-gather | bytes 1277952 | tf_op jit(solution)/shard_map/all_gather | solution.py:142
  169.4 0.2 convert_multiply_fusion
  169.6 0.3 reduce-precision_convert_fusion
  169.9 0.6 fusion.50
  170.5 0.7 copy-done.7
  171.1 0.6 fusion.1
  171.8 0.1 multiply_convert_fusion
  172.0 1.0 pad_maximum_fusion.1
  173.0 3.5 %all-to-all-start.7 = ((f16[4,200,384]{2,1,0:T(8,128)(2,1)}), f16[4,200,384]{2,1,0:T(8,128)(2,1)S(1)}, u32[]{:S(2)}, u32[]{:S(2)}) async-start(f16[4,200,384]{2,1,0:T(8,128)(2,1)} %pad_maximum_fusion.1), calls=%async_computation.7 | async-start | bytes 1228800 | tf_op jit(solution)/shard_map/all_to_all | solution.py:18
  176.5 8.7 %all-to-all-done.7 = f16[4,200,384]{2,1,0:T(8,128)(2,1)S(1)} async-done(((f16[4,200,384]{2,1,0:T(8,128)(2,1)}), f16[4,200,384]{2,1,0:T(8,128)(2,1)S(1)}, u32[]{:S(2)}, u32[]{:S(2)}) %all-to-all-start.7) | async-done | bytes 614432 | tf_op jit(solution)/shard_map/all_to_all | solution.py:18
  185.4 0.8 copy-done.2
  186.2 0.7 fusion.6
  186.9 1.0 maximum_add_fusion
  (100 shorter events, 2.5 us)
Async XLA Ops:
  0.6 14.2 %copy-start.1 = (bf16[192,384]{1,0:T(8,128)(2,1)S(1)}, bf16[192,384]{1,0:T(8,128)(2,1)}, u32[]{:S(2)}) copy-start(bf16[192,384]{1,0:T(8,128)(2,1)} %param.12) | copy-start | bytes 442372
  1.5 13.3 %collective-permute-start = (bf16[32,384]{1,0:T(8,128)(2,1)S(1)}, bf16[32,384]{1,0:T(8,128)(2,1)S(1)}, u32[]{:S(2)}, u32[]{:S(2)}) collective-permute-start(bf16[32,384]{1,0:T(8,128)(2,1)S(1)} %maximum_maximum_fusion), channel_id=1, source_target_pairs={{0,2},{2,0},{1,3},{3,1},{4,6},{6,4},{5,7},{7,5},{8,10},{10,8},{9,1... | collective-permute-start | bytes 73736 | tf_op jit(solution)/shard_map/ppermute | solution.py:57
  28.6 22.3 %all-to-all-start.1 = ((bf16[4,64,768]{2,1,0:T(8,128)(2,1)}), bf16[4,64,768]{2,1,0:T(8,128)(2,1)S(1)}, u32[]{:S(2)}, u32[]{:S(2)}) async-start(bf16[4,64,768]{2,1,0:T(8,128)(2,1)} %broadcast_in_dim.32), calls=%async_computation.1 | async-start | bytes 786432 | tf_op jit(solution)/shard_map/all_to_all | solution.py:18
  33.4 14.1 %collective-permute-start.2 = (bf16[64,384]{1,0:T(8,128)(2,1)S(1)}, bf16[64,384]{1,0:T(8,128)(2,1)S(1)}, u32[]{:S(2)}, u32[]{:S(2)}) collective-permute-start(bf16[64,384]{1,0:T(8,128)(2,1)S(1)} %bitcast.103), channel_id=1, source_target_pairs={{0,256},{128,384},{256,0},{384,128},{1,257},{129,385},{257,1},{385... | collective-permute-start | bytes 147464 | tf_op jit(solution)/shard_map/ppermute | solution.py:61
  40.0 8.0 %collective-permute-start.1 = (bf16[64,384]{1,0:T(8,128)(2,1)S(1)}, bf16[64,384]{1,0:T(8,128)(2,1)S(1)}, u32[]{:S(2)}, u32[]{:S(2)}) collective-permute-start(bf16[64,384]{1,0:T(8,128)(2,1)S(1)} %bitcast.104), channel_id=1, source_target_pairs={{0,128},{128,256},{256,384},{384,0},{1,129},{129,257},{257,385},{3... | collective-permute-start | bytes 147464 | tf_op jit(solution)/shard_map/ppermute | solution.py:61
  42.4 7.3 %collective-permute-start.3 = (bf16[64,384]{1,0:T(8,128)(2,1)S(1)}, bf16[64,384]{1,0:T(8,128)(2,1)S(1)}, u32[]{:S(2)}, u32[]{:S(2)}) collective-permute-start(bf16[64,384]{1,0:T(8,128)(2,1)S(1)} %bitcast.105), channel_id=1, source_target_pairs={{0,384},{128,0},{256,128},{384,256},{1,385},{129,1},{257,129},{385... | collective-permute-start | bytes 147464 | tf_op jit(solution)/shard_map/ppermute | solution.py:61
  57.4 11.0 %copy-start.3 = (f32[512]{0:T(512)S(1)}, f32[512]{0:T(512)}, u32[]{:S(2)}) copy-start(f32[512]{0:T(512)} %param.20) | copy-start | bytes 6148
  57.4 11.0 %copy-start.4 = (f32[512]{0:T(512)S(1)}, f32[512]{0:T(512)}, u32[]{:S(2)}) copy-start(f32[512]{0:T(512)} %param.18) | copy-start | bytes 6148
  57.4 11.0 %copy-start.5 = (f32[512]{0:T(512)S(1)}, f32[512]{0:T(512)}, u32[]{:S(2)}) copy-start(f32[512]{0:T(512)} %param.19) | copy-start | bytes 6148
  57.4 11.0 %copy-start.6 = (f32[512]{0:T(512)S(1)}, f32[512]{0:T(512)}, u32[]{:S(2)}) copy-start(f32[512]{0:T(512)} %param.17) | copy-start | bytes 6148
  58.3 20.8 %all-to-all-start.2 = ((f16[4,136,384]{2,1,0:T(8,128)(2,1)}), f16[4,136,384]{2,1,0:T(8,128)(2,1)S(1)}, u32[]{:S(2)}, u32[]{:S(2)}) async-start(f16[4,136,384]{2,1,0:T(8,128)(2,1)} %pad_maximum_fusion.3), calls=%async_computation.2 | async-start | bytes 835584 | tf_op jit(solution)/shard_map/all_to_all | solution.py:18
  64.4 13.6 %collective-permute-start.4 = (bf16[256,384]{1,0:T(8,128)(2,1)S(1)}, bf16[256,384]{1,0:T(8,128)(2,1)S(1)}, u32[]{:S(2)}, u32[]{:S(2)}) collective-permute-start(bf16[256,384]{1,0:T(8,128)(2,1)S(1)} %pad_maximum_fusion.7), channel_id=1, source_target_pairs={{0,32},{32,0},{1,33},{33,1},{2,34},{34,2},{3,35},{35,3},{4,36},{36... | collective-permute-start | bytes 589832 | tf_op jit(solution)/shard_map/ppermute | solution.py:57
  79.3 9.2 %collective-permute-start.5 = (f16[136,384]{1,0:T(8,128)(2,1)S(1)}, f16[136,384]{1,0:T(8,128)(2,1)S(1)}, u32[]{:S(2)}, u32[]{:S(2)}) collective-permute-start(f16[136,384]{1,0:T(8,128)(2,1)S(1)} %pad_maximum_fusion.12), channel_id=1, source_target_pairs={{0,32},{32,0},{1,33},{33,1},{2,34},{34,2},{3,35},{35,3},{4,36},{36... | collective-permute-start | bytes 313352 | tf_op jit(solution)/shard_map/ppermute | solution.py:57
  89.7 18.6 %all-to-all-start.3 = ((f16[4,136,384]{2,1,0:T(8,128)(2,1)}), f16[4,136,384]{2,1,0:T(8,128)(2,1)S(1)}, u32[]{:S(2)}, u32[]{:S(2)}) async-start(f16[4,136,384]{2,1,0:T(8,128)(2,1)} %broadcast_in_dim.36), calls=%async_computation.3 | async-start | bytes 835584 | tf_op jit(solution)/shard_map/all_to_all | solution.py:18
  112.0 5.7 %collective-permute-start.6 = (f32[384,512]{1,0:T(8,128)S(1)}, f32[384,512]{1,0:T(8,128)S(1)}, u32[]{:S(2)}, u32[]{:S(2)}) collective-permute-start(f32[384,512]{1,0:T(8,128)S(1)} %constant_dynamic-slice_fusion), channel_id=1, source_target_pairs={{0,1},{1,0},{2,3},{3,2},{4,5},{5,4},{6,7},{7,6},{8,9},{9,8},{10,11... | collective-permute-start | bytes 2359304 | tf_op jit(solution)/shard_map/ppermute | solution.py:57
  130.6 9.5 %collective-permute-start.7 = (f16[104,512]{1,0:T(8,128)(2,1)S(1)}, f16[104,512]{1,0:T(8,128)(2,1)S(1)}, u32[]{:S(2)}, u32[]{:S(2)}) collective-permute-start(f16[104,512]{1,0:T(8,128)(2,1)S(1)} %pad_maximum_fusion.9), channel_id=1, source_target_pairs={{0,2},{2,0},{1,3},{3,1},{4,6},{6,4},{5,7},{7,5},{8,10},{10,8},{9,1... | collective-permute-start | bytes 319496 | tf_op jit(solution)/shard_map/ppermute | solution.py:57
  141.0 8.3 %all-to-all-start.5 = ((f16[4,104,512]{2,1,0:T(8,128)(2,1)}), f16[4,104,512]{2,1,0:T(8,128)(2,1)S(1)}, u32[]{:S(2)}, u32[]{:S(2)}) async-start(f16[4,104,512]{2,1,0:T(8,128)(2,1)} %broadcast_in_dim.45), calls=%async_computation.5 | async-start | bytes 851968 | tf_op jit(solution)/shard_map/all_to_all | solution.py:18
  150.4 9.8 %all-to-all-start.6 = ((f16[4,104,512]{2,1,0:T(8,128)(2,1)}), f16[4,104,512]{2,1,0:T(8,128)(2,1)S(1)}, u32[]{:S(2)}, u32[]{:S(2)}) async-start(f16[4,104,512]{2,1,0:T(8,128)(2,1)} %broadcast_in_dim.48), calls=%async_computation.6 | async-start | bytes 851968 | tf_op jit(solution)/shard_map/all_to_all | solution.py:18
  169.9 1.3 copy-start.7
  173.0 12.2 %all-to-all-start.7 = ((f16[4,200,384]{2,1,0:T(8,128)(2,1)}), f16[4,200,384]{2,1,0:T(8,128)(2,1)S(1)}, u32[]{:S(2)}, u32[]{:S(2)}) async-start(f16[4,200,384]{2,1,0:T(8,128)(2,1)} %pad_maximum_fusion.1), calls=%async_computation.7 | async-start | bytes 1228800 | tf_op jit(solution)/shard_map/all_to_all | solution.py:18
  185.3 0.9 copy-start.2
  185.3 1.7 copy-start

commit v12 on v9

--- a/solution.py
+++ b/solution.py
@@ -35,11 +35,11 @@
     return dot(high) + dot(low)
 
 
-def pack(values):
+def pack(values, after=0.0):
     top = jnp.max(jnp.abs(values), axis=-2, keepdims=True)
     power = jnp.clip(jnp.floor(jnp.log2(jnp.maximum(top, 1e-30))), -100.0, 120.0)
     scaled = (values * jnp.exp2(14.0 - power)).astype(jnp.float16)
-    tail = jnp.broadcast_to(power.astype(jnp.float16), values.shape[:-2] + (8, values.shape[-1]))
+    tail = jnp.broadcast_to((power + after).astype(jnp.float16), values.shape[:-2] + (8, values.shape[-1]))
     return jnp.concatenate([scaled, tail], axis=-2)
 
 
@@ -116,15 +116,15 @@
     left = exchange(spread(left, 4), "x").reshape(256, 768)
     left = lax.all_gather(left, "c", axis=0, tiled=True)
 
+    right = got[:, 192:208].reshape(64, 384)
+    other = swap(right, "zp")
+    there = other[:1].astype(jnp.float32) * 0.0
+    right = jnp.concatenate([right, other], axis=0)
+
     rows = jnp.dot(left, gradient, preferred_element_type=jnp.float32)
     rows = jnp.sum(unpack(exchange(pack(rows.reshape(4, 128, 384)), "yp")), axis=0)
-    right = got[:, 192:208].reshape(64, 384)
-    scaled = (right.astype(jnp.float32) * 2.0**19).astype(jnp.float16)
-    other = swap(jnp.concatenate([pack(rows), scaled], axis=0), "zp")
-    rows = (rows + unpack(other[:136])) * own_shift[:, None]
+    rows = (rows + unpack(swap(pack(rows, there), "zp"))) * own_shift[:, None]
     rows = unpack(exchange(spread(pack(rows), 4), "yp")).reshape(512, 384)
-    scaled = (other[136:].astype(jnp.float32) * 2.0**-19).astype(jnp.bfloat16)
-    right = jnp.concatenate([right, scaled], axis=0)
     right = jnp.concatenate([right] + [around(right, "yp", 4, step) for step in (1, 2, 3)], axis=0)
 
     lifted = dot_wide_right(left, rows, ((0,), (0,)))

time: 181 us -> 178 us (0.983)
  waiting for transfers between devices: 54.5 us -> 47 us
  starting transfers between devices: 65.5 us -> 71.1 us
    all_to_all x6, waiting for transfers between devices: 37.8 us -> 33.7 us  [exchange(): return lax.all_to_all(blocks, axes, 0, 0, tiled=True)]
    ppermute x4 -> x5, starting transfers between devices: 26.3 us -> 30.2 us  [swap(): return lax.ppermute(values, axis, [(0, 1), (1, 0)])]
    ppermute x4 -> x5, waiting for transfers between devices: 11.6 us -> 7.73 us  [swap(): return lax.ppermute(values, axis, [(0, 1), (1, 0)])]
  transfers between devices with their start and end apart: 13 -> 14, of which waited for: 9 -> 9; matrix products, arithmetic and copies ran while one was open for 1% -> 2% of each run, Pallas kernels for 0% -> 0%
where the time goes in v12:
time: 178 us; the launch traced here: 177 us
  starting transfers between devices  71.1 us (40%)
  waiting for transfers between devices  47 us (26%)
  blocking collectives  35.8 us (20%)
  local copies, waits for them, and re-layouts  8.37 us (5%)
  other arithmetic  7.43 us (4%)
  matrix products  5.19 us (3%)
  between operations  2.08 us (1%)
    all_to_all x6, waiting for transfers between devices, exchange(): return lax.all_to_all(blocks, axes, 0, 0, tiled=True)  33.7 us
    ppermute x5, starting transfers between devices, swap(): return lax.ppermute(values, axis, [(0, 1), (1, 0)])  30.2 us
    all_to_all x6, starting transfers between devices, exchange(): return lax.all_to_all(blocks, axes, 0, 0, tiled=True)  27.5 us
    all_to_all x2, blocking collectives, exchange(): return lax.all_to_all(blocks, axes, 0, 0, tiled=True)  22.1 us
    ppermute x3, starting transfers between devices, around(): lax.ppermute(values, axis, [(i, (i + step) % size) for i in range(size)])  13.5 us
    ppermute x5, waiting for transfers between devices, swap(): return lax.ppermute(values, axis, [(0, 1), (1, 0)])  7.73 us
    all_gather x1, blocking collectives, local(): lax.all_gather(cols, 'c', axis=0, tiled=True)  7.59 us
    all_gather x1, blocking collectives, local(): left = lax.all_gather(left, 'c', axis=0, tiled=True)  6.09 us
  transfers between devices with their start and end apart: 14, of which 9 were waited for; matrix products, arithmetic and copies ran while one was open for 2% of the time, Pallas kernels for 0%

profile of v12, /device:TPU:1, one launch (start us, length us, event | category | flops | bytes accessed | tf_op | source)
XLA Modules:
  0.0 176.9 jit_solution(15072203772221926610)
XLA Ops:
  0.6 0.8 fusion.50
  1.5 11.5 %collective-permute-start = (bf16[32,384]{1,0:T(8,128)(2,1)S(1)}, bf16[32,384]{1,0:T(8,128)(2,1)S(1)}, u32[]{:S(2)}, u32[]{:S(2)}) collective-permute-start(bf16[32,384]{1,0:T(8,128)(2,1)S(1)} %maximum_maximum_fusion), channel_id=1, source_target_pairs={{0,2},{2,0},{1,3},{3,1},{4,6},{6,4},{5,7},{7,5},{8,10},{10,8},{9,1... | collective-permute-start | bytes 73736 | tf_op jit(solution)/shard_map/ppermute | solution.py:57
  13.0 1.1 fusion.47
  14.1 0.8 fusion.48
  14.8 0.8 maximum_bitcast_fusion
  15.7 0.1 pad_maximum_fusion
  15.8 11.7 %all_to_all.40 = bf16[4,240,384]{2,1,0:T(8,128)(2,1)S(1)} all-to-all(bf16[4,240,384]{2,1,0:T(8,128)(2,1)S(1)} %pad_maximum_fusion), channel_id=1, replica_groups=mesh['yp'=4,'yb'=2,'zp'=2,'zb'=2,'x'=4,'zh'=2,'c'=2] {'yb','zb'}, dimensions={0} | all-to-all | bytes 1474560 | tf_op jit(solution)/shard_map/all_to_all | solution.py:18
  27.6 0.1 slice_bitcast_fusion.5
  27.7 0.1 pad_maximum_fusion.13
  27.8 0.8 broadcast_in_dim.34
  28.6 4.8 %all-to-all-start.1 = ((bf16[4,64,768]{2,1,0:T(8,128)(2,1)}), bf16[4,64,768]{2,1,0:T(8,128)(2,1)S(1)}, u32[]{:S(2)}, u32[]{:S(2)}) async-start(bf16[4,64,768]{2,1,0:T(8,128)(2,1)} %broadcast_in_dim.34), calls=%async_computation.1 | async-start | bytes 786432 | tf_op jit(solution)/shard_map/all_to_all | solution.py:18
  33.4 6.2 %all-to-all-done.1 = bf16[4,64,768]{2,1,0:T(8,128)(2,1)S(1)} async-done(((bf16[4,64,768]{2,1,0:T(8,128)(2,1)}), bf16[4,64,768]{2,1,0:T(8,128)(2,1)S(1)}, u32[]{:S(2)}, u32[]{:S(2)}) %all-to-all-start.1) | async-done | bytes 393248 | tf_op jit(solution)/shard_map/all_to_all | solution.py:18
  39.6 6.1 %all_gather.6 = bf16[512,768]{1,0:T(8,128)(2,1)S(1)} all-gather(bf16[256,768]{1,0:T(8,128)(2,1)S(1)} %bitcast.96), channel_id=1, replica_groups=mesh['yp'=4,'yb'=2,'zp'=2,'zb'=2,'x'=4,'zh'=2,'c'=2] {'c'}, dimensions={0}, use_global_device_ids=true | all-gather | bytes 1179648 | tf_op jit(solution)/shard_map/all_gather | solution.py:117
  45.7 0.6 abs_reduce_fusion.2
  46.4 0.9 pad_maximum_fusion.3
  47.3 5.9 %all-to-all-start.2 = ((f16[4,136,384]{2,1,0:T(8,128)(2,1)}), f16[4,136,384]{2,1,0:T(8,128)(2,1)S(1)}, u32[]{:S(2)}, u32[]{:S(2)}) async-start(f16[4,136,384]{2,1,0:T(8,128)(2,1)} %pad_maximum_fusion.3), calls=%async_computation.2 | async-start | bytes 835584 | tf_op jit(solution)/shard_map/all_to_all | solution.py:18
  54.1 4.0 %collective-permute-start.1 = (bf16[64,384]{1,0:T(8,128)(2,1)S(1)}, bf16[64,384]{1,0:T(8,128)(2,1)S(1)}, u32[]{:S(2)}, u32[]{:S(2)}) collective-permute-start(bf16[64,384]{1,0:T(8,128)(2,1)S(1)} %bitcast.98), channel_id=1, source_target_pairs={{0,32},{32,0},{1,33},{33,1},{2,34},{34,2},{3,35},{35,3},{4,36},{36... | collective-permute-start | bytes 147464 | tf_op jit(solution)/shard_map/ppermute | solution.py:57
  58.1 7.5 %all-to-all-done.2 = f16[4,136,384]{2,1,0:T(8,128)(2,1)S(1)} async-done(((f16[4,136,384]{2,1,0:T(8,128)(2,1)}), f16[4,136,384]{2,1,0:T(8,128)(2,1)S(1)}, u32[]{:S(2)}, u32[]{:S(2)}) %all-to-all-start.2) | async-done | bytes 417824 | tf_op jit(solution)/shard_map/all_to_all | solution.py:18
  65.9 4.0 %collective-permute-start.2 = (f16[136,384]{1,0:T(8,128)(2,1)S(1)}, f16[136,384]{1,0:T(8,128)(2,1)S(1)}, u32[]{:S(2)}, u32[]{:S(2)}) collective-permute-start(f16[136,384]{1,0:T(8,128)(2,1)S(1)} %pad_maximum_fusion.11), channel_id=1, source_target_pairs={{0,32},{32,0},{1,33},{33,1},{2,34},{34,2},{3,35},{35,3},{4,36},{36... | collective-permute-start | bytes 313352 | tf_op jit(solution)/shard_map/ppermute | solution.py:57
  69.9 0.1 reshape.261
  70.1 3.2 %collective-permute-done.2 = f16[136,384]{1,0:T(8,128)(2,1)S(1)} collective-permute-done((f16[136,384]{1,0:T(8,128)(2,1)S(1)}, f16[136,384]{1,0:T(8,128)(2,1)S(1)}, u32[]{:S(2)}, u32[]{:S(2)}) %collective-permute-start.2) | collective-permute-done | bytes 104480 | tf_op jit(solution)/shard_map/ppermute | solution.py:57
  73.3 0.1 abs_reduce_fusion.6
  73.5 0.1 multiply_convert_fusion.6
  73.6 0.8 broadcast_in_dim.39
  74.4 6.4 %all-to-all-start.3 = ((f16[4,136,384]{2,1,0:T(8,128)(2,1)}), f16[4,136,384]{2,1,0:T(8,128)(2,1)S(1)}, u32[]{:S(2)}, u32[]{:S(2)}) async-start(f16[4,136,384]{2,1,0:T(8,128)(2,1)} %broadcast_in_dim.39), calls=%async_computation.3 | async-start | bytes 835584 | tf_op jit(solution)/shard_map/all_to_all | solution.py:18
  80.8 5.5 %collective-permute-start.5 = (bf16[128,384]{1,0:T(8,128)(2,1)S(1)}, bf16[128,384]{1,0:T(8,128)(2,1)S(1)}, u32[]{:S(2)}, u32[]{:S(2)}) collective-permute-start(bf16[128,384]{1,0:T(8,128)(2,1)S(1)} %pad_maximum_fusion.14), channel_id=1, source_target_pairs={{0,384},{128,0},{256,128},{384,256},{1,385},{129,1},{257,129},{385... | collective-permute-start | bytes 294920 | tf_op jit(solution)/shard_map/ppermute | solution.py:61
  86.3 4.0 %collective-permute-start.4 = (bf16[128,384]{1,0:T(8,128)(2,1)S(1)}, bf16[128,384]{1,0:T(8,128)(2,1)S(1)}, u32[]{:S(2)}, u32[]{:S(2)}) collective-permute-start(bf16[128,384]{1,0:T(8,128)(2,1)S(1)} %pad_maximum_fusion.14), channel_id=1, source_target_pairs={{0,256},{128,384},{256,0},{384,128},{1,257},{129,385},{257,1},{385... | collective-permute-start | bytes 294920 | tf_op jit(solution)/shard_map/ppermute | solution.py:61
  90.3 4.0 %collective-permute-start.3 = (bf16[128,384]{1,0:T(8,128)(2,1)S(1)}, bf16[128,384]{1,0:T(8,128)(2,1)S(1)}, u32[]{:S(2)}, u32[]{:S(2)}) collective-permute-start(bf16[128,384]{1,0:T(8,128)(2,1)S(1)} %pad_maximum_fusion.14), channel_id=1, source_target_pairs={{0,128},{128,256},{256,384},{384,0},{1,129},{129,257},{257,385},{3... | collective-permute-start | bytes 294920 | tf_op jit(solution)/shard_map/ppermute | solution.py:61
  94.3 5.5 %collective-permute-done.3 = bf16[128,384]{1,0:T(8,128)(2,1)S(1)} collective-permute-done((bf16[128,384]{1,0:T(8,128)(2,1)S(1)}, bf16[128,384]{1,0:T(8,128)(2,1)S(1)}, u32[]{:S(2)}, u32[]{:S(2)}) %collective-permute-start.3) | collective-permute-done | bytes 98336 | tf_op jit(solution)/shard_map/ppermute | solution.py:61
  100.0 0.1 fusion.3
  100.1 0.6 fusion.52
  100.8 1.6 divide_add_fusion
  102.4 0.6 fusion.4
  103.0 0.6 convolution_add_fusion
  103.7 3.8 %collective-permute-start.6 = (f32[384,512]{1,0:T(8,128)S(1)}, f32[384,512]{1,0:T(8,128)S(1)}, u32[]{:S(2)}, u32[]{:S(2)}) collective-permute-start(f32[384,512]{1,0:T(8,128)S(1)} %constant_dynamic-slice_fusion), channel_id=1, source_target_pairs={{0,1},{1,0},{2,3},{3,2},{4,5},{5,4},{6,7},{7,6},{8,9},{9,8},{10,11... | collective-permute-start | bytes 2359304 | tf_op jit(solution)/shard_map/ppermute | solution.py:57
  107.5 1.9 %collective-permute-done.6 = f32[384,512]{1,0:T(8,128)S(1)} collective-permute-done((f32[384,512]{1,0:T(8,128)S(1)}, f32[384,512]{1,0:T(8,128)S(1)}, u32[]{:S(2)}, u32[]{:S(2)}) %collective-permute-start.6) | collective-permute-done | bytes 786464 | tf_op jit(solution)/shard_map/ppermute | solution.py:57
  109.4 0.1 dynamic-slice_add_fusion
  109.7 0.1 multiply_convert_fusion.1
  109.8 0.1 pad_maximum_fusion.2
  109.9 10.4 %all_to_all.41 = f16[4,104,512]{2,1,0:T(8,128)(2,1)S(1)} all-to-all(f16[4,104,512]{2,1,0:T(8,128)(2,1)S(1)} %pad_maximum_fusion.2), channel_id=1, replica_groups=mesh['yp'=4,'yb'=2,'zp'=2,'zb'=2,'x'=4,'zh'=2,'c'=2] {'x'}, dimensions={0} | all-to-all | bytes 851968 | tf_op jit(solution)/shard_map/all_to_all | solution.py:18
  120.5 6.8 %collective-permute-start.7 = (f16[104,512]{1,0:T(8,128)(2,1)S(1)}, f16[104,512]{1,0:T(8,128)(2,1)S(1)}, u32[]{:S(2)}, u32[]{:S(2)}) collective-permute-start(f16[104,512]{1,0:T(8,128)(2,1)S(1)} %pad_maximum_fusion.8), channel_id=1, source_target_pairs={{0,2},{2,0},{1,3},{3,1},{4,6},{6,4},{5,7},{7,5},{8,10},{10,8},{9,1... | collective-permute-start | bytes 319496 | tf_op jit(solution)/shard_map/ppermute | solution.py:57
  127.4 2.6 %collective-permute-done.7 = f16[104,512]{1,0:T(8,128)(2,1)S(1)} collective-permute-done((f16[104,512]{1,0:T(8,128)(2,1)S(1)}, f16[104,512]{1,0:T(8,128)(2,1)S(1)}, u32[]{:S(2)}, u32[]{:S(2)}) %collective-permute-start.7) | collective-permute-done | bytes 106528 | tf_op jit(solution)/shard_map/ppermute | solution.py:57
  130.2 0.8 broadcast_in_dim.48
  131.0 3.5 %all-to-all-start.5 = ((f16[4,104,512]{2,1,0:T(8,128)(2,1)}), f16[4,104,512]{2,1,0:T(8,128)(2,1)S(1)}, u32[]{:S(2)}, u32[]{:S(2)}) async-start(f16[4,104,512]{2,1,0:T(8,128)(2,1)} %broadcast_in_dim.48), calls=%async_computation.5 | async-start | bytes 851968 | tf_op jit(solution)/shard_map/all_to_all | solution.py:18
  134.4 0.1 reshape.265
  134.6 0.1 reshape.266
  134.7 5.1 %all-to-all-done.5 = f16[4,104,512]{2,1,0:T(8,128)(2,1)S(1)} async-done(((f16[4,104,512]{2,1,0:T(8,128)(2,1)}), f16[4,104,512]{2,1,0:T(8,128)(2,1)S(1)}, u32[]{:S(2)}, u32[]{:S(2)}) %all-to-all-start.5) | async-done | bytes 426016 | tf_op jit(solution)/shard_map/all_to_all | solution.py:18
  139.9 0.1 select_reduce_fusion
  140.1 0.8 broadcast_in_dim.51
  140.9 3.5 %all-to-all-start.6 = ((f16[4,104,512]{2,1,0:T(8,128)(2,1)}), f16[4,104,512]{2,1,0:T(8,128)(2,1)S(1)}, u32[]{:S(2)}, u32[]{:S(2)}) async-start(f16[4,104,512]{2,1,0:T(8,128)(2,1)} %broadcast_in_dim.51), calls=%async_computation.6 | async-start | bytes 851968 | tf_op jit(solution)/shard_map/all_to_all | solution.py:18
  144.5 6.2 %all-to-all-done.6 = f16[4,104,512]{2,1,0:T(8,128)(2,1)S(1)} async-done(((f16[4,104,512]{2,1,0:T(8,128)(2,1)}), f16[4,104,512]{2,1,0:T(8,128)(2,1)S(1)}, u32[]{:S(2)}, u32[]{:S(2)}) %all-to-all-start.6) | async-done | bytes 426016 | tf_op jit(solution)/shard_map/all_to_all | solution.py:18
  150.7 7.6 %all_gather.7 = f16[8,104,512]{2,1,0:T(8,128)(2,1)S(1)} all-gather(f16[4,104,512]{2,1,0:T(8,128)(2,1)S(1)} %all-to-all-done.6), channel_id=1, replica_groups=mesh['yp'=4,'yb'=2,'zp'=2,'zb'=2,'x'=4,'zh'=2,'c'=2] {'c'}, dimensions={0}, use_global_device_ids=true | all-gather | bytes 1277952 | tf_op jit(solution)/shard_map/all_gather | solution.py:140
  158.4 0.2 convert_multiply_fusion
  158.6 0.3 reduce-precision_convert_fusion
  158.9 0.6 fusion.53
  159.5 0.7 copy-done.7
  160.1 0.6 fusion.1
  160.9 0.1 multiply_convert_fusion
  161.0 1.0 pad_maximum_fusion.1
  162.0 3.5 %all-to-all-start.7 = ((f16[4,200,384]{2,1,0:T(8,128)(2,1)}), f16[4,200,384]{2,1,0:T(8,128)(2,1)S(1)}, u32[]{:S(2)}, u32[]{:S(2)}) async-start(f16[4,200,384]{2,1,0:T(8,128)(2,1)} %pad_maximum_fusion.1), calls=%async_computation.7 | async-start | bytes 1228800 | tf_op jit(solution)/shard_map/all_to_all | solution.py:18
  165.5 8.7 %all-to-all-done.7 = f16[4,200,384]{2,1,0:T(8,128)(2,1)S(1)} async-done(((f16[4,200,384]{2,1,0:T(8,128)(2,1)}), f16[4,200,384]{2,1,0:T(8,128)(2,1)S(1)}, u32[]{:S(2)}, u32[]{:S(2)}) %all-to-all-start.7) | async-done | bytes 614432 | tf_op jit(solution)/shard_map/all_to_all | solution.py:18
  174.4 0.8 copy-done.2
  175.2 0.7 fusion.6
  175.9 1.0 maximum_add_fusion
  (96 shorter events, 2.2 us)
Async XLA Ops:
  0.6 14.2 %copy-start.1 = (bf16[192,384]{1,0:T(8,128)(2,1)S(1)}, bf16[192,384]{1,0:T(8,128)(2,1)}, u32[]{:S(2)}) copy-start(bf16[192,384]{1,0:T(8,128)(2,1)} %param.12) | copy-start | bytes 442372
  1.5 13.3 %collective-permute-start = (bf16[32,384]{1,0:T(8,128)(2,1)S(1)}, bf16[32,384]{1,0:T(8,128)(2,1)S(1)}, u32[]{:S(2)}, u32[]{:S(2)}) collective-permute-start(bf16[32,384]{1,0:T(8,128)(2,1)S(1)} %maximum_maximum_fusion), channel_id=1, source_target_pairs={{0,2},{2,0},{1,3},{3,1},{4,6},{6,4},{5,7},{7,5},{8,10},{10,8},{9,1... | collective-permute-start | bytes 73736 | tf_op jit(solution)/shard_map/ppermute | solution.py:57
  28.6 11.0 %all-to-all-start.1 = ((bf16[4,64,768]{2,1,0:T(8,128)(2,1)}), bf16[4,64,768]{2,1,0:T(8,128)(2,1)S(1)}, u32[]{:S(2)}, u32[]{:S(2)}) async-start(bf16[4,64,768]{2,1,0:T(8,128)(2,1)} %broadcast_in_dim.34), calls=%async_computation.1 | async-start | bytes 786432 | tf_op jit(solution)/shard_map/all_to_all | solution.py:18
  46.3 7.6 %copy-start.3 = (f32[512]{0:T(512)S(1)}, f32[512]{0:T(512)}, u32[]{:S(2)}) copy-start(f32[512]{0:T(512)} %param.20) | copy-start | bytes 6148
  46.3 7.6 %copy-start.4 = (f32[512]{0:T(512)S(1)}, f32[512]{0:T(512)}, u32[]{:S(2)}) copy-start(f32[512]{0:T(512)} %param.18) | copy-start | bytes 6148
  46.3 7.6 %copy-start.5 = (f32[512]{0:T(512)S(1)}, f32[512]{0:T(512)}, u32[]{:S(2)}) copy-start(f32[512]{0:T(512)} %param.19) | copy-start | bytes 6148
  46.3 7.6 %copy-start.6 = (f32[512]{0:T(512)S(1)}, f32[512]{0:T(512)}, u32[]{:S(2)}) copy-start(f32[512]{0:T(512)} %param.17) | copy-start | bytes 6148
  47.3 18.3 %all-to-all-start.2 = ((f16[4,136,384]{2,1,0:T(8,128)(2,1)}), f16[4,136,384]{2,1,0:T(8,128)(2,1)S(1)}, u32[]{:S(2)}, u32[]{:S(2)}) async-start(f16[4,136,384]{2,1,0:T(8,128)(2,1)} %pad_maximum_fusion.3), calls=%async_computation.2 | async-start | bytes 835584 | tf_op jit(solution)/shard_map/all_to_all | solution.py:18
  54.1 11.7 %collective-permute-start.1 = (bf16[64,384]{1,0:T(8,128)(2,1)S(1)}, bf16[64,384]{1,0:T(8,128)(2,1)S(1)}, u32[]{:S(2)}, u32[]{:S(2)}) collective-permute-start(bf16[64,384]{1,0:T(8,128)(2,1)S(1)} %bitcast.98), channel_id=1, source_target_pairs={{0,32},{32,0},{1,33},{33,1},{2,34},{34,2},{3,35},{35,3},{4,36},{36... | collective-permute-start | bytes 147464 | tf_op jit(solution)/shard_map/ppermute | solution.py:57
  65.9 7.4 %collective-permute-start.2 = (f16[136,384]{1,0:T(8,128)(2,1)S(1)}, f16[136,384]{1,0:T(8,128)(2,1)S(1)}, u32[]{:S(2)}, u32[]{:S(2)}) collective-permute-start(f16[136,384]{1,0:T(8,128)(2,1)S(1)} %pad_maximum_fusion.11), channel_id=1, source_target_pairs={{0,32},{32,0},{1,33},{33,1},{2,34},{34,2},{3,35},{35,3},{4,36},{36... | collective-permute-start | bytes 313352 | tf_op jit(solution)/shard_map/ppermute | solution.py:57
  74.4 25.5 %all-to-all-start.3 = ((f16[4,136,384]{2,1,0:T(8,128)(2,1)}), f16[4,136,384]{2,1,0:T(8,128)(2,1)S(1)}, u32[]{:S(2)}, u32[]{:S(2)}) async-start(f16[4,136,384]{2,1,0:T(8,128)(2,1)} %broadcast_in_dim.39), calls=%async_computation.3 | async-start | bytes 835584 | tf_op jit(solution)/shard_map/all_to_all | solution.py:18
  80.8 19.1 %collective-permute-start.5 = (bf16[128,384]{1,0:T(8,128)(2,1)S(1)}, bf16[128,384]{1,0:T(8,128)(2,1)S(1)}, u32[]{:S(2)}, u32[]{:S(2)}) collective-permute-start(bf16[128,384]{1,0:T(8,128)(2,1)S(1)} %pad_maximum_fusion.14), channel_id=1, source_target_pairs={{0,384},{128,0},{256,128},{384,256},{1,385},{129,1},{257,129},{385... | collective-permute-start | bytes 294920 | tf_op jit(solution)/shard_map/ppermute | solution.py:61
  86.3 13.6 %collective-permute-start.4 = (bf16[128,384]{1,0:T(8,128)(2,1)S(1)}, bf16[128,384]{1,0:T(8,128)(2,1)S(1)}, u32[]{:S(2)}, u32[]{:S(2)}) collective-permute-start(bf16[128,384]{1,0:T(8,128)(2,1)S(1)} %pad_maximum_fusion.14), channel_id=1, source_target_pairs={{0,256},{128,384},{256,0},{384,128},{1,257},{129,385},{257,1},{385... | collective-permute-start | bytes 294920 | tf_op jit(solution)/shard_map/ppermute | solution.py:61
  90.3 9.5 %collective-permute-start.3 = (bf16[128,384]{1,0:T(8,128)(2,1)S(1)}, bf16[128,384]{1,0:T(8,128)(2,1)S(1)}, u32[]{:S(2)}, u32[]{:S(2)}) collective-permute-start(bf16[128,384]{1,0:T(8,128)(2,1)S(1)} %pad_maximum_fusion.14), channel_id=1, source_target_pairs={{0,128},{128,256},{256,384},{384,0},{1,129},{129,257},{257,385},{3... | collective-permute-start | bytes 294920 | tf_op jit(solution)/shard_map/ppermute | solution.py:61
  103.7 5.7 %collective-permute-start.6 = (f32[384,512]{1,0:T(8,128)S(1)}, f32[384,512]{1,0:T(8,128)S(1)}, u32[]{:S(2)}, u32[]{:S(2)}) collective-permute-start(f32[384,512]{1,0:T(8,128)S(1)} %constant_dynamic-slice_fusion), channel_id=1, source_target_pairs={{0,1},{1,0},{2,3},{3,2},{4,5},{5,4},{6,7},{7,6},{8,9},{9,8},{10,11... | collective-permute-start | bytes 2359304 | tf_op jit(solution)/shard_map/ppermute | solution.py:57
  120.5 9.5 %collective-permute-start.7 = (f16[104,512]{1,0:T(8,128)(2,1)S(1)}, f16[104,512]{1,0:T(8,128)(2,1)S(1)}, u32[]{:S(2)}, u32[]{:S(2)}) collective-permute-start(f16[104,512]{1,0:T(8,128)(2,1)S(1)} %pad_maximum_fusion.8), channel_id=1, source_target_pairs={{0,2},{2,0},{1,3},{3,1},{4,6},{6,4},{5,7},{7,5},{8,10},{10,8},{9,1... | collective-permute-start | bytes 319496 | tf_op jit(solution)/shard_map/ppermute | solution.py:57
  131.0 8.8 %all-to-all-start.5 = ((f16[4,104,512]{2,1,0:T(8,128)(2,1)}), f16[4,104,512]{2,1,0:T(8,128)(2,1)S(1)}, u32[]{:S(2)}, u32[]{:S(2)}) async-start(f16[4,104,512]{2,1,0:T(8,128)(2,1)} %broadcast_in_dim.48), calls=%async_computation.5 | async-start | bytes 851968 | tf_op jit(solution)/shard_map/all_to_all | solution.py:18
  140.9 9.8 %all-to-all-start.6 = ((f16[4,104,512]{2,1,0:T(8,128)(2,1)}), f16[4,104,512]{2,1,0:T(8,128)(2,1)S(1)}, u32[]{:S(2)}, u32[]{:S(2)}) async-start(f16[4,104,512]{2,1,0:T(8,128)(2,1)} %broadcast_in_dim.51), calls=%async_computation.6 | async-start | bytes 851968 | tf_op jit(solution)/shard_map/all_to_all | solution.py:18
  158.9 1.3 copy-start.7
  162.0 12.2 %all-to-all-start.7 = ((f16[4,200,384]{2,1,0:T(8,128)(2,1)}), f16[4,200,384]{2,1,0:T(8,128)(2,1)S(1)}, u32[]{:S(2)}, u32[]{:S(2)}) async-start(f16[4,200,384]{2,1,0:T(8,128)(2,1)} %pad_maximum_fusion.1), calls=%async_computation.7 | async-start | bytes 1228800 | tf_op jit(solution)/shard_map/all_to_all | solution.py:18
  174.3 0.9 copy-start.2
  174.3 1.7 copy-start

commit v13 on v9

--- a/solution.py
+++ b/solution.py
@@ -57,10 +57,6 @@
     return lax.ppermute(values, axis, [(0, 1), (1, 0)])
 
 
-def around(values, axis, size, step):
-    return lax.ppermute(values, axis, [(i, (i + step) % size) for i in range(size)])
-
-
 def core_part(values, core, own):
     half = values.shape[0] // 2
     return lax.dynamic_slice_in_dim(values, (core if own else 1 - core) * half, half, 0)
@@ -89,10 +85,8 @@
     left_shift = left_shift.reshape(4, 2, 2, 32).transpose(2, 0, 1, 3)
     left_shift = jnp.where(lax.axis_index("zh") == 1, left_shift[:, :, ::-1], left_shift).reshape(512)
     own_shift = lax.dynamic_slice_in_dim(left_shift, level * 128, 128, 0)
-    right_shift = right_shift.reshape(4, 2, 2, 2, 16).transpose(0, 2, 1, 3, 4).reshape(4, 2, 64)[::-1]
-    right_shift = jnp.where(lax.axis_index("zp") == 1, right_shift[:, ::-1], right_shift)
-    right_shift = jnp.concatenate([right_shift, right_shift], axis=0)
-    right_shift = lax.dynamic_slice_in_dim(right_shift, 3 - level, 4, 0).reshape(512)
+    right_shift = right_shift.reshape(4, 2, 2, 2, 16).transpose(2, 0, 1, 3, 4)
+    right_shift = jnp.where(lax.axis_index("zp") == 1, right_shift[::-1], right_shift).reshape(512)
 
     right = jnp.concatenate([joined_right_basis.T, output_right_basis.T], axis=1)
     lefts = [jnp.concatenate([basis.T[:16], basis.T[16:]], axis=1) for basis in (joined_left_basis, output_left_basis)]
@@ -116,16 +110,17 @@
     left = exchange(spread(left, 4), "x").reshape(256, 768)
     left = lax.all_gather(left, "c", axis=0, tiled=True)
 
-    rows = jnp.dot(left, gradient, preferred_element_type=jnp.float32)
-    rows = jnp.sum(unpack(exchange(pack(rows.reshape(4, 128, 384)), "yp")), axis=0)
     right = got[:, 192:208].reshape(64, 384)
     scaled = (right.astype(jnp.float32) * 2.0**19).astype(jnp.float16)
-    other = swap(jnp.concatenate([pack(rows), scaled], axis=0), "zp")
-    rows = (rows + unpack(other[:136])) * own_shift[:, None]
+
+    rows = jnp.dot(left, gradient, preferred_element_type=jnp.float32)
+    rows = jnp.concatenate([pack(rows.reshape(4, 128, 384)), spread(scaled, 4)], axis=1)
+    got = exchange(rows, "yp")
+    rows = jnp.sum(unpack(got[:, :136]), axis=0)
+    rows = (rows + unpack(swap(pack(rows), "zp"))) * own_shift[:, None]
     rows = unpack(exchange(spread(pack(rows), 4), "yp")).reshape(512, 384)
-    scaled = (other[136:].astype(jnp.float32) * 2.0**-19).astype(jnp.bfloat16)
-    right = jnp.concatenate([right, scaled], axis=0)
-    right = jnp.concatenate([right] + [around(right, "yp", 4, step) for step in (1, 2, 3)], axis=0)
+    right = (got[:, 136:].reshape(256, 384).astype(jnp.float32) * 2.0**-19).astype(jnp.bfloat16)
+    right = jnp.concatenate([right, swap(right, "zp")], axis=0)
 
     lifted = dot_wide_right(left, rows, ((0,), (0,)))
     applied = gradient.astype(jnp.float32) / damp + lifted

time: 181 us -> 175 us (0.967)
  starting transfers between devices: 65.5 us -> 58.3 us
  waiting for transfers between devices: 54.5 us -> 56.5 us
    ppermute x3 -> x0, starting transfers between devices: 13.5 us -> none  [around(): lax.ppermute(values, axis, [(i, (i + step) % size) for i in range(size)])]
    all_to_all x6, waiting for transfers between devices: 37.8 us -> 48.8 us  [exchange(): return lax.all_to_all(blocks, axes, 0, 0, tiled=True)]
    ppermute x3 -> x0, waiting for transfers between devices: 5.15 us -> none  [around(): lax.ppermute(values, axis, [(i, (i + step) % size) for i in range(size)])]
    ppermute x4 -> x5, waiting for transfers between devices: 11.6 us -> 7.7 us  [swap(): return lax.ppermute(values, axis, [(0, 1), (1, 0)])]
    all_to_all x6, starting transfers between devices: 25.7 us -> 29.5 us  [exchange(): return lax.all_to_all(blocks, axes, 0, 0, tiled=True)]
    ppermute x4 -> x5, starting transfers between devices: 26.3 us -> 28.8 us  [swap(): return lax.ppermute(values, axis, [(0, 1), (1, 0)])]
  transfers between devices with their start and end apart: 13 -> 11, of which waited for: 9 -> 10; matrix products, arithmetic and copies ran while one was open for 1% -> 3% of each run, Pallas kernels for 0% -> 0%
where the time goes in v13:
time: 175 us; the launch traced here: 174 us
  starting transfers between devices  58.3 us (33%)
  waiting for transfers between devices  56.5 us (32%)
  blocking collectives  36.1 us (21%)
  local copies, waits for them, and re-layouts  8.19 us (5%)
  other arithmetic  7.57 us (4%)
  matrix products  5.23 us (3%)
  between operations  2.01 us (1%)
    all_to_all x6, waiting for transfers between devices, exchange(): return lax.all_to_all(blocks, axes, 0, 0, tiled=True)  48.8 us
    all_to_all x6, starting transfers between devices, exchange(): return lax.all_to_all(blocks, axes, 0, 0, tiled=True)  29.5 us
    ppermute x5, starting transfers between devices, swap(): return lax.ppermute(values, axis, [(0, 1), (1, 0)])  28.8 us
    all_to_all x2, blocking collectives, exchange(): return lax.all_to_all(blocks, axes, 0, 0, tiled=True)  22.1 us
    all_gather x1, blocking collectives, local(): lax.all_gather(cols, 'c', axis=0, tiled=True)  7.88 us
    ppermute x5, waiting for transfers between devices, swap(): return lax.ppermute(values, axis, [(0, 1), (1, 0)])  7.7 us
    all_gather x1, blocking collectives, local(): left = lax.all_gather(left, 'c', axis=0, tiled=True)  6.09 us
  transfers between devices with their start and end apart: 11, of which 10 were waited for; matrix products, arithmetic and copies ran while one was open for 3% of the time, Pallas kernels for 0%

profile of v13, /device:TPU:1, one launch (start us, length us, event | category | flops | bytes accessed | tf_op | source)
XLA Modules:
  0.0 173.8 jit_solution(16419256087640813020)
XLA Ops:
  0.6 0.8 fusion.49
  1.5 11.5 %collective-permute-start = (bf16[32,384]{1,0:T(8,128)(2,1)S(1)}, bf16[32,384]{1,0:T(8,128)(2,1)S(1)}, u32[]{:S(2)}, u32[]{:S(2)}) collective-permute-start(bf16[32,384]{1,0:T(8,128)(2,1)S(1)} %maximum_maximum_fusion), channel_id=1, source_target_pairs={{0,2},{2,0},{1,3},{3,1},{4,6},{6,4},{5,7},{7,5},{8,10},{10,8},{9,1... | collective-permute-start | bytes 73736 | tf_op jit(solution)/shard_map/ppermute | solution.py:57
  13.0 1.1 fusion.46
  14.1 0.8 fusion.47
  14.8 0.8 maximum_bitcast_fusion
  15.7 0.1 pad_maximum_fusion
  15.8 11.7 %all_to_all.40 = bf16[4,240,384]{2,1,0:T(8,128)(2,1)S(1)} all-to-all(bf16[4,240,384]{2,1,0:T(8,128)(2,1)S(1)} %pad_maximum_fusion), channel_id=1, replica_groups=mesh['yp'=4,'yb'=2,'zp'=2,'zb'=2,'x'=4,'zh'=2,'c'=2] {'yb','zb'}, dimensions={0} | all-to-all | bytes 1474560 | tf_op jit(solution)/shard_map/all_to_all | solution.py:18
  27.6 0.1 slice_bitcast_fusion.5
  27.7 0.1 pad_maximum_fusion.14
  27.8 0.8 broadcast_in_dim.34
  28.6 4.8 %all-to-all-start.1 = ((bf16[4,64,768]{2,1,0:T(8,128)(2,1)}), bf16[4,64,768]{2,1,0:T(8,128)(2,1)S(1)}, u32[]{:S(2)}, u32[]{:S(2)}) async-start(bf16[4,64,768]{2,1,0:T(8,128)(2,1)} %broadcast_in_dim.34), calls=%async_computation.1 | async-start | bytes 786432 | tf_op jit(solution)/shard_map/all_to_all | solution.py:18
  33.4 6.1 %all-to-all-done.1 = bf16[4,64,768]{2,1,0:T(8,128)(2,1)S(1)} async-done(((bf16[4,64,768]{2,1,0:T(8,128)(2,1)}), bf16[4,64,768]{2,1,0:T(8,128)(2,1)S(1)}, u32[]{:S(2)}, u32[]{:S(2)}) %all-to-all-start.1) | async-done | bytes 393248 | tf_op jit(solution)/shard_map/all_to_all | solution.py:18
  39.6 6.1 %all_gather.6 = bf16[512,768]{1,0:T(8,128)(2,1)S(1)} all-gather(bf16[256,768]{1,0:T(8,128)(2,1)S(1)} %bitcast.98), channel_id=1, replica_groups=mesh['yp'=4,'yb'=2,'zp'=2,'zb'=2,'x'=4,'zh'=2,'c'=2] {'c'}, dimensions={0}, use_global_device_ids=true | all-gather | bytes 1179648 | tf_op jit(solution)/shard_map/all_gather | solution.py:111
  45.7 0.6 abs_reduce_fusion.2
  46.5 1.0 pad_maximum_fusion.1
  47.5 5.9 %all-to-all-start.2 = ((f16[4,200,384]{2,1,0:T(8,128)(2,1)}), f16[4,200,384]{2,1,0:T(8,128)(2,1)S(1)}, u32[]{:S(2)}, u32[]{:S(2)}) async-start(f16[4,200,384]{2,1,0:T(8,128)(2,1)} %pad_maximum_fusion.1), calls=%async_computation.2 | async-start | bytes 1228800 | tf_op jit(solution)/shard_map/all_to_all | solution.py:18
  54.2 0.1 reshape.254
  54.3 14.9 %all-to-all-done.2 = f16[4,200,384]{2,1,0:T(8,128)(2,1)S(1)} async-done(((f16[4,200,384]{2,1,0:T(8,128)(2,1)}), f16[4,200,384]{2,1,0:T(8,128)(2,1)S(1)}, u32[]{:S(2)}, u32[]{:S(2)}) %all-to-all-start.2) | async-done | bytes 614432 | tf_op jit(solution)/shard_map/all_to_all | solution.py:18
  69.4 4.0 %collective-permute-start.1 = (f16[136,384]{1,0:T(8,128)(2,1)S(1)}, f16[136,384]{1,0:T(8,128)(2,1)S(1)}, u32[]{:S(2)}, u32[]{:S(2)}) collective-permute-start(f16[136,384]{1,0:T(8,128)(2,1)S(1)} %pad_maximum_fusion.12), channel_id=1, source_target_pairs={{0,32},{32,0},{1,33},{33,1},{2,34},{34,2},{3,35},{35,3},{4,36},{36... | collective-permute-start | bytes 313352 | tf_op jit(solution)/shard_map/ppermute | solution.py:57
  73.5 0.1 reshape.255
  73.7 2.1 %collective-permute-done.1 = f16[136,384]{1,0:T(8,128)(2,1)S(1)} collective-permute-done((f16[136,384]{1,0:T(8,128)(2,1)S(1)}, f16[136,384]{1,0:T(8,128)(2,1)S(1)}, u32[]{:S(2)}, u32[]{:S(2)}) %collective-permute-start.1) | collective-permute-done | bytes 104480 | tf_op jit(solution)/shard_map/ppermute | solution.py:57
  75.8 0.1 abs_reduce_fusion.6
  75.9 0.1 multiply_convert_fusion.7
  76.1 0.8 broadcast_in_dim.39
  76.9 8.4 %all-to-all-start.3 = ((f16[4,136,384]{2,1,0:T(8,128)(2,1)}), f16[4,136,384]{2,1,0:T(8,128)(2,1)S(1)}, u32[]{:S(2)}, u32[]{:S(2)}) async-start(f16[4,136,384]{2,1,0:T(8,128)(2,1)} %broadcast_in_dim.39), calls=%async_computation.3 | async-start | bytes 835584 | tf_op jit(solution)/shard_map/all_to_all | solution.py:18
  85.3 1.9 %collective-permute-start.2 = (bf16[256,384]{1,0:T(8,128)(2,1)S(1)}, bf16[256,384]{1,0:T(8,128)(2,1)S(1)}, u32[]{:S(2)}, u32[]{:S(2)}) collective-permute-start(bf16[256,384]{1,0:T(8,128)(2,1)S(1)} %bitcast.92), channel_id=1, source_target_pairs={{0,32},{32,0},{1,33},{33,1},{2,34},{34,2},{3,35},{35,3},{4,36},{36... | collective-permute-start | bytes 589832 | tf_op jit(solution)/shard_map/ppermute | solution.py:57
  87.2 8.0 %all-to-all-done.3 = f16[4,136,384]{2,1,0:T(8,128)(2,1)S(1)} async-done(((f16[4,136,384]{2,1,0:T(8,128)(2,1)}), f16[4,136,384]{2,1,0:T(8,128)(2,1)S(1)}, u32[]{:S(2)}, u32[]{:S(2)}) %all-to-all-start.3) | async-done | bytes 417824 | tf_op jit(solution)/shard_map/all_to_all | solution.py:18
  95.3 0.1 fusion.3
  95.4 0.6 fusion.51
  96.0 1.6 divide_add_fusion
  97.7 1.1 collective-permute-done.2
  98.8 0.6 fusion.4
  99.4 0.6 convolution_add_fusion
  100.1 4.5 %collective-permute-start.3 = (f32[384,512]{1,0:T(8,128)S(1)}, f32[384,512]{1,0:T(8,128)S(1)}, u32[]{:S(2)}, u32[]{:S(2)}) collective-permute-start(f32[384,512]{1,0:T(8,128)S(1)} %constant_dynamic-slice_fusion), channel_id=1, source_target_pairs={{0,1},{1,0},{2,3},{3,2},{4,5},{5,4},{6,7},{7,6},{8,9},{9,8},{10,11... | collective-permute-start | bytes 2359304 | tf_op jit(solution)/shard_map/ppermute | solution.py:57
  104.6 1.9 %collective-permute-done.3 = f32[384,512]{1,0:T(8,128)S(1)} collective-permute-done((f32[384,512]{1,0:T(8,128)S(1)}, f32[384,512]{1,0:T(8,128)S(1)}, u32[]{:S(2)}, u32[]{:S(2)}) %collective-permute-start.3) | collective-permute-done | bytes 786464 | tf_op jit(solution)/shard_map/ppermute | solution.py:57
  106.5 0.1 dynamic-slice_add_fusion
  106.8 0.1 multiply_convert_fusion.1
  106.9 0.1 pad_maximum_fusion.3
  107.0 10.4 %all_to_all.41 = f16[4,104,512]{2,1,0:T(8,128)(2,1)S(1)} all-to-all(f16[4,104,512]{2,1,0:T(8,128)(2,1)S(1)} %pad_maximum_fusion.3), channel_id=1, replica_groups=mesh['yp'=4,'yb'=2,'zp'=2,'zb'=2,'x'=4,'zh'=2,'c'=2] {'x'}, dimensions={0} | all-to-all | bytes 851968 | tf_op jit(solution)/shard_map/all_to_all | solution.py:18
  117.6 6.8 %collective-permute-start.4 = (f16[104,512]{1,0:T(8,128)(2,1)S(1)}, f16[104,512]{1,0:T(8,128)(2,1)S(1)}, u32[]{:S(2)}, u32[]{:S(2)}) collective-permute-start(f16[104,512]{1,0:T(8,128)(2,1)S(1)} %pad_maximum_fusion.9), channel_id=1, source_target_pairs={{0,2},{2,0},{1,3},{3,1},{4,6},{6,4},{5,7},{7,5},{8,10},{10,8},{9,1... | collective-permute-start | bytes 319496 | tf_op jit(solution)/shard_map/ppermute | solution.py:57
  124.5 2.6 %collective-permute-done.4 = f16[104,512]{1,0:T(8,128)(2,1)S(1)} collective-permute-done((f16[104,512]{1,0:T(8,128)(2,1)S(1)}, f16[104,512]{1,0:T(8,128)(2,1)S(1)}, u32[]{:S(2)}, u32[]{:S(2)}) %collective-permute-start.4) | collective-permute-done | bytes 106528 | tf_op jit(solution)/shard_map/ppermute | solution.py:57
  127.3 0.8 broadcast_in_dim.44
  128.1 3.5 %all-to-all-start.5 = ((f16[4,104,512]{2,1,0:T(8,128)(2,1)}), f16[4,104,512]{2,1,0:T(8,128)(2,1)S(1)}, u32[]{:S(2)}, u32[]{:S(2)}) async-start(f16[4,104,512]{2,1,0:T(8,128)(2,1)} %broadcast_in_dim.44), calls=%async_computation.5 | async-start | bytes 851968 | tf_op jit(solution)/shard_map/all_to_all | solution.py:18
  131.6 4.9 %all-to-all-done.5 = f16[4,104,512]{2,1,0:T(8,128)(2,1)S(1)} async-done(((f16[4,104,512]{2,1,0:T(8,128)(2,1)}), f16[4,104,512]{2,1,0:T(8,128)(2,1)S(1)}, u32[]{:S(2)}, u32[]{:S(2)}) %all-to-all-start.5) | async-done | bytes 426016 | tf_op jit(solution)/shard_map/all_to_all | solution.py:18
  136.4 0.1 select_reduce_fusion
  136.7 0.8 broadcast_in_dim.51
  137.5 3.5 %all-to-all-start.6 = ((f16[4,104,512]{2,1,0:T(8,128)(2,1)}), f16[4,104,512]{2,1,0:T(8,128)(2,1)S(1)}, u32[]{:S(2)}, u32[]{:S(2)}) async-start(f16[4,104,512]{2,1,0:T(8,128)(2,1)} %broadcast_in_dim.51), calls=%async_computation.6 | async-start | bytes 851968 | tf_op jit(solution)/shard_map/all_to_all | solution.py:18
  141.0 0.1 reshape.259
  141.1 0.1 mul.237
  141.2 6.2 %all-to-all-done.6 = f16[4,104,512]{2,1,0:T(8,128)(2,1)S(1)} async-done(((f16[4,104,512]{2,1,0:T(8,128)(2,1)}), f16[4,104,512]{2,1,0:T(8,128)(2,1)S(1)}, u32[]{:S(2)}, u32[]{:S(2)}) %all-to-all-start.6) | async-done | bytes 426016 | tf_op jit(solution)/shard_map/all_to_all | solution.py:18
  147.3 7.9 %all_gather.7 = f16[8,104,512]{2,1,0:T(8,128)(2,1)S(1)} all-gather(f16[4,104,512]{2,1,0:T(8,128)(2,1)S(1)} %all-to-all-done.6), channel_id=1, replica_groups=mesh['yp'=4,'yb'=2,'zp'=2,'zb'=2,'x'=4,'zh'=2,'c'=2] {'c'}, dimensions={0}, use_global_device_ids=true | all-gather | bytes 1277952 | tf_op jit(solution)/shard_map/all_gather | solution.py:135
  155.3 0.2 convert_multiply_fusion
  155.5 0.3 reduce-precision_convert_fusion
  155.8 0.6 fusion.45
  156.4 0.7 copy-done.7
  157.0 0.6 fusion.1
  157.7 0.1 multiply_convert_fusion
  157.9 1.0 pad_maximum_fusion.2
  158.9 3.5 %all-to-all-start.7 = ((f16[4,200,384]{2,1,0:T(8,128)(2,1)}), f16[4,200,384]{2,1,0:T(8,128)(2,1)S(1)}, u32[]{:S(2)}, u32[]{:S(2)}) async-start(f16[4,200,384]{2,1,0:T(8,128)(2,1)} %pad_maximum_fusion.2), calls=%async_computation.7 | async-start | bytes 1228800 | tf_op jit(solution)/shard_map/all_to_all | solution.py:18
  162.4 8.7 %all-to-all-done.7 = f16[4,200,384]{2,1,0:T(8,128)(2,1)S(1)} async-done(((f16[4,200,384]{2,1,0:T(8,128)(2,1)}), f16[4,200,384]{2,1,0:T(8,128)(2,1)S(1)}, u32[]{:S(2)}, u32[]{:S(2)}) %all-to-all-start.7) | async-done | bytes 614432 | tf_op jit(solution)/shard_map/all_to_all | solution.py:18
  171.1 0.1 convert_multiply_fusion.1
  171.3 0.8 copy-done.2
  172.1 0.7 fusion.6
  172.8 1.0 maximum_add_fusion
  (82 shorter events, 1.8 us)
Async XLA Ops:
  0.6 14.2 %copy-start.1 = (bf16[192,384]{1,0:T(8,128)(2,1)S(1)}, bf16[192,384]{1,0:T(8,128)(2,1)}, u32[]{:S(2)}) copy-start(bf16[192,384]{1,0:T(8,128)(2,1)} %param.12) | copy-start | bytes 442372
  1.5 13.3 %collective-permute-start = (bf16[32,384]{1,0:T(8,128)(2,1)S(1)}, bf16[32,384]{1,0:T(8,128)(2,1)S(1)}, u32[]{:S(2)}, u32[]{:S(2)}) collective-permute-start(bf16[32,384]{1,0:T(8,128)(2,1)S(1)} %maximum_maximum_fusion), channel_id=1, source_target_pairs={{0,2},{2,0},{1,3},{3,1},{4,6},{6,4},{5,7},{7,5},{8,10},{10,8},{9,1... | collective-permute-start | bytes 73736 | tf_op jit(solution)/shard_map/ppermute | solution.py:57
  28.6 11.0 %all-to-all-start.1 = ((bf16[4,64,768]{2,1,0:T(8,128)(2,1)}), bf16[4,64,768]{2,1,0:T(8,128)(2,1)S(1)}, u32[]{:S(2)}, u32[]{:S(2)}) async-start(bf16[4,64,768]{2,1,0:T(8,128)(2,1)} %broadcast_in_dim.34), calls=%async_computation.1 | async-start | bytes 786432 | tf_op jit(solution)/shard_map/all_to_all | solution.py:18
  46.4 7.7 %copy-start.3 = (f32[512]{0:T(512)S(1)}, f32[512]{0:T(512)}, u32[]{:S(2)}) copy-start(f32[512]{0:T(512)} %param.20) | copy-start | bytes 6148
  46.4 7.7 %copy-start.4 = (f32[512]{0:T(512)S(1)}, f32[512]{0:T(512)}, u32[]{:S(2)}) copy-start(f32[512]{0:T(512)} %param.18) | copy-start | bytes 6148
  46.5 7.7 %copy-start.5 = (f32[512]{0:T(512)S(1)}, f32[512]{0:T(512)}, u32[]{:S(2)}) copy-start(f32[512]{0:T(512)} %param.19) | copy-start | bytes 6148
  46.5 7.7 %copy-start.6 = (f32[512]{0:T(512)S(1)}, f32[512]{0:T(512)}, u32[]{:S(2)}) copy-start(f32[512]{0:T(512)} %param.17) | copy-start | bytes 6148
  47.5 21.7 %all-to-all-start.2 = ((f16[4,200,384]{2,1,0:T(8,128)(2,1)}), f16[4,200,384]{2,1,0:T(8,128)(2,1)S(1)}, u32[]{:S(2)}, u32[]{:S(2)}) async-start(f16[4,200,384]{2,1,0:T(8,128)(2,1)} %pad_maximum_fusion.1), calls=%async_computation.2 | async-start | bytes 1228800 | tf_op jit(solution)/shard_map/all_to_all | solution.py:18
  69.4 6.3 %collective-permute-start.1 = (f16[136,384]{1,0:T(8,128)(2,1)S(1)}, f16[136,384]{1,0:T(8,128)(2,1)S(1)}, u32[]{:S(2)}, u32[]{:S(2)}) collective-permute-start(f16[136,384]{1,0:T(8,128)(2,1)S(1)} %pad_maximum_fusion.12), channel_id=1, source_target_pairs={{0,32},{32,0},{1,33},{33,1},{2,34},{34,2},{3,35},{35,3},{4,36},{36... | collective-permute-start | bytes 313352 | tf_op jit(solution)/shard_map/ppermute | solution.py:57
  76.9 18.4 %all-to-all-start.3 = ((f16[4,136,384]{2,1,0:T(8,128)(2,1)}), f16[4,136,384]{2,1,0:T(8,128)(2,1)S(1)}, u32[]{:S(2)}, u32[]{:S(2)}) async-start(f16[4,136,384]{2,1,0:T(8,128)(2,1)} %broadcast_in_dim.39), calls=%async_computation.3 | async-start | bytes 835584 | tf_op jit(solution)/shard_map/all_to_all | solution.py:18
  85.3 13.5 %collective-permute-start.2 = (bf16[256,384]{1,0:T(8,128)(2,1)S(1)}, bf16[256,384]{1,0:T(8,128)(2,1)S(1)}, u32[]{:S(2)}, u32[]{:S(2)}) collective-permute-start(bf16[256,384]{1,0:T(8,128)(2,1)S(1)} %bitcast.92), channel_id=1, source_target_pairs={{0,32},{32,0},{1,33},{33,1},{2,34},{34,2},{3,35},{35,3},{4,36},{36... | collective-permute-start | bytes 589832 | tf_op jit(solution)/shard_map/ppermute | solution.py:57
  100.1 6.4 %collective-permute-start.3 = (f32[384,512]{1,0:T(8,128)S(1)}, f32[384,512]{1,0:T(8,128)S(1)}, u32[]{:S(2)}, u32[]{:S(2)}) collective-permute-start(f32[384,512]{1,0:T(8,128)S(1)} %constant_dynamic-slice_fusion), channel_id=1, source_target_pairs={{0,1},{1,0},{2,3},{3,2},{4,5},{5,4},{6,7},{7,6},{8,9},{9,8},{10,11... | collective-permute-start | bytes 2359304 | tf_op jit(solution)/shard_map/ppermute | solution.py:57
  117.6 9.5 %collective-permute-start.4 = (f16[104,512]{1,0:T(8,128)(2,1)S(1)}, f16[104,512]{1,0:T(8,128)(2,1)S(1)}, u32[]{:S(2)}, u32[]{:S(2)}) collective-permute-start(f16[104,512]{1,0:T(8,128)(2,1)S(1)} %pad_maximum_fusion.9), channel_id=1, source_target_pairs={{0,2},{2,0},{1,3},{3,1},{4,6},{6,4},{5,7},{7,5},{8,10},{10,8},{9,1... | collective-permute-start | bytes 319496 | tf_op jit(solution)/shard_map/ppermute | solution.py:57
  128.1 8.3 %all-to-all-start.5 = ((f16[4,104,512]{2,1,0:T(8,128)(2,1)}), f16[4,104,512]{2,1,0:T(8,128)(2,1)S(1)}, u32[]{:S(2)}, u32[]{:S(2)}) async-start(f16[4,104,512]{2,1,0:T(8,128)(2,1)} %broadcast_in_dim.44), calls=%async_computation.5 | async-start | bytes 851968 | tf_op jit(solution)/shard_map/all_to_all | solution.py:18
  137.5 9.8 %all-to-all-start.6 = ((f16[4,104,512]{2,1,0:T(8,128)(2,1)}), f16[4,104,512]{2,1,0:T(8,128)(2,1)S(1)}, u32[]{:S(2)}, u32[]{:S(2)}) async-start(f16[4,104,512]{2,1,0:T(8,128)(2,1)} %broadcast_in_dim.51), calls=%async_computation.6 | async-start | bytes 851968 | tf_op jit(solution)/shard_map/all_to_all | solution.py:18
  155.8 1.3 copy-start.7
  158.9 12.2 %all-to-all-start.7 = ((f16[4,200,384]{2,1,0:T(8,128)(2,1)}), f16[4,200,384]{2,1,0:T(8,128)(2,1)S(1)}, u32[]{:S(2)}, u32[]{:S(2)}) async-start(f16[4,200,384]{2,1,0:T(8,128)(2,1)} %pad_maximum_fusion.2), calls=%async_computation.7 | async-start | bytes 1228800 | tf_op jit(solution)/shard_map/all_to_all | solution.py:18
  171.2 0.9 copy-start.2
  171.2 1.7 copy-start

commit v14 on v13

--- a/solution.py
+++ b/solution.py
@@ -23,16 +23,8 @@
     return high.astype(jnp.bfloat16), (wide - high).astype(jnp.bfloat16)
 
 
-def dot_wide_left(wide, narrow, dims):
-    high, low = halves(wide)
-    dot = lambda part: lax.dot_general(part, narrow, (dims, ((), ())), preferred_element_type=jnp.float32)
-    return dot(high) + dot(low)
-
-
-def dot_wide_right(narrow, wide, dims):
-    high, low = halves(wide)
-    dot = lambda part: lax.dot_general(narrow, part, (dims, ((), ())), preferred_element_type=jnp.float32)
-    return dot(high) + dot(low)
+def dot(left, right, dims):
+    return lax.dot_general(left, right, (dims, ((), ())), preferred_element_type=jnp.float32)
 
 
 def pack(values):
@@ -122,9 +114,10 @@
     right = (got[:, 136:].reshape(256, 384).astype(jnp.float32) * 2.0**-19).astype(jnp.bfloat16)
     right = jnp.concatenate([right, swap(right, "zp")], axis=0)
 
-    lifted = dot_wide_right(left, rows, ((0,), (0,)))
-    applied = gradient.astype(jnp.float32) / damp + lifted
-    cols = dot_wide_left(applied, right, ((1,), (1,)))
+    plain = dot(gradient, right, ((1,), (1,))) / damp
+    lifted = dot(jnp.concatenate([left, left], axis=0), jnp.concatenate(halves(rows), axis=0), ((0,), (0,)))
+    wide = jnp.concatenate([right, right], axis=1)
+    cols = plain + dot(jnp.concatenate(halves(lifted), axis=1), wide, ((1,), (1,)))
     cols = core_part(cols, core, True) + swap(core_part(cols, core, False), "c")
     cols = jnp.sum(unpack(exchange(pack(cols.reshape(4, 96, 512)), "x")), axis=0)
     cols = cols + unpack(swap(pack(cols), "zh"))
@@ -134,7 +127,8 @@
     cols = exchange(spread(pack(cols), 4), "x")
     cols = unpack(lax.all_gather(cols, "c", axis=0, tiled=True)).reshape(768, 512)
 
-    update = lifted / damp + dot_wide_left(cols * right_shift[None, :], right, ((1,), (0,)))
+    cols = jnp.concatenate(halves(cols * right_shift[None, :]), axis=1)
+    update = lifted / damp + dot(cols, jnp.concatenate([right, right], axis=0), ((1,), (0,)))
     update = unpack(exchange(pack(update.reshape(4, 192, 384)), QUAD))
     joined_update = jnp.concatenate([update[0], update[1], update[2]], axis=1) + joined_gradient.astype(jnp.float32) / damp / damp
     output_update = update[3] + output_gradient.astype(jnp.float32) / damp / damp

time: 175 us -> 179 us (1.023)
  waiting for transfers between devices: 56.5 us -> 59.1 us
  starting transfers between devices: 58.3 us -> 56.4 us
    ppermute x5, waiting for transfers between devices: 7.7 us -> 18.4 us  [swap(): return lax.ppermute(values, axis, [(0, 1), (1, 0)])]
    all_to_all x6, waiting for transfers between devices: 48.8 us -> 40.7 us  [exchange(): return lax.all_to_all(blocks, axes, 0, 0, tiled=True)]
    ppermute x5, starting transfers between devices: 28.8 us -> 27 us  [swap(): return lax.ppermute(values, axis, [(0, 1), (1, 0)])]
    dot_general x6 -> x4, matrix products: 4.62 us -> 5.59 us  [dot(): lax.dot_general(left, right, (dims, ((), ())), preferred_element_type=jnp...]
  transfers between devices with their start and end apart: 11 -> 11, of which waited for: 10 -> 9; matrix products, arithmetic and copies ran while one was open for 3% -> 2% of each run, Pallas kernels for 0% -> 0%
where the time goes in v14:
time: 179 us; the launch traced here: 178 us
  waiting for transfers between devices  59.1 us (33%)
  starting transfers between devices  56.4 us (32%)
  blocking collectives  37.2 us (21%)
  local copies, waits for them, and re-layouts  9.24 us (5%)
  other arithmetic  7.82 us (4%)
  matrix products  6.18 us (3%)
  between operations  1.98 us (1%)
    all_to_all x6, waiting for transfers between devices, exchange(): return lax.all_to_all(blocks, axes, 0, 0, tiled=True)  40.7 us
    all_to_all x6, starting transfers between devices, exchange(): return lax.all_to_all(blocks, axes, 0, 0, tiled=True)  29.5 us
    ppermute x5, starting transfers between devices, swap(): return lax.ppermute(values, axis, [(0, 1), (1, 0)])  27 us
    all_to_all x2, blocking collectives, exchange(): return lax.all_to_all(blocks, axes, 0, 0, tiled=True)  22.1 us
    ppermute x5, waiting for transfers between devices, swap(): return lax.ppermute(values, axis, [(0, 1), (1, 0)])  18.4 us
    all_gather x1, blocking collectives, local(): lax.all_gather(cols, 'c', axis=0, tiled=True)  9.01 us
    all_gather x1, blocking collectives, local(): left = lax.all_gather(left, 'c', axis=0, tiled=True)  6.09 us
    dot_general x4, matrix products, dot(): lax.dot_general(left, right, (dims, ((), ())), preferred_element_type=jnp...  5.59 us
  transfers between devices with their start and end apart: 11, of which 9 were waited for; matrix products, arithmetic and copies ran while one was open for 2% of the time, Pallas kernels for 0%

profile of v14, /device:TPU:1, one launch (start us, length us, event | category | flops | bytes accessed | tf_op | source)
XLA Modules:
  0.0 178.0 jit_solution(15001220017170511310)
XLA Ops:
  0.6 0.8 fusion.87
  1.5 11.5 %collective-permute-start = (bf16[32,384]{1,0:T(8,128)(2,1)S(1)}, bf16[32,384]{1,0:T(8,128)(2,1)S(1)}, u32[]{:S(2)}, u32[]{:S(2)}) collective-permute-start(bf16[32,384]{1,0:T(8,128)(2,1)S(1)} %maximum_maximum_fusion), channel_id=1, source_target_pairs={{0,2},{2,0},{1,3},{3,1},{4,6},{6,4},{5,7},{7,5},{8,10},{10,8},{9,1... | collective-permute-start | bytes 73736 | tf_op jit(solution)/shard_map/ppermute | solution.py:49
  12.9 1.1 fusion.84
  14.0 0.8 fusion.85
  14.8 1.0 maximum_bitcast_fusion
  15.8 0.1 fusion.42
  15.9 0.1 pad_maximum_fusion
  16.0 11.7 %all_to_all.40 = bf16[4,240,384]{2,1,0:T(8,128)(2,1)S(1)} all-to-all(bf16[4,240,384]{2,1,0:T(8,128)(2,1)S(1)} %pad_maximum_fusion), channel_id=1, replica_groups=mesh['yp'=4,'yb'=2,'zp'=2,'zb'=2,'x'=4,'zh'=2,'c'=2] {'yb','zb'}, dimensions={0} | all-to-all | bytes 1474560 | tf_op jit(solution)/shard_map/all_to_all | solution.py:18
  27.8 0.1 slice_bitcast_fusion.5
  27.9 0.1 pad_maximum_fusion.13
  28.0 0.8 broadcast_in_dim.34
  28.8 4.8 %all-to-all-start.1 = ((bf16[4,64,768]{2,1,0:T(8,128)(2,1)}), bf16[4,64,768]{2,1,0:T(8,128)(2,1)S(1)}, u32[]{:S(2)}, u32[]{:S(2)}) async-start(bf16[4,64,768]{2,1,0:T(8,128)(2,1)} %broadcast_in_dim.34), calls=%async_computation.1 | async-start | bytes 786432 | tf_op jit(solution)/shard_map/all_to_all | solution.py:18
  33.6 6.1 %all-to-all-done.1 = bf16[4,64,768]{2,1,0:T(8,128)(2,1)S(1)} async-done(((bf16[4,64,768]{2,1,0:T(8,128)(2,1)}), bf16[4,64,768]{2,1,0:T(8,128)(2,1)S(1)}, u32[]{:S(2)}, u32[]{:S(2)}) %all-to-all-start.1) | async-done | bytes 393248 | tf_op jit(solution)/shard_map/all_to_all | solution.py:18
  39.7 6.1 %all_gather.6 = bf16[512,768]{1,0:T(8,128)(2,1)S(1)} all-gather(bf16[256,768]{1,0:T(8,128)(2,1)S(1)} %bitcast.89), channel_id=1, replica_groups=mesh['yp'=4,'yb'=2,'zp'=2,'zb'=2,'x'=4,'zh'=2,'c'=2] {'c'}, dimensions={0}, use_global_device_ids=true | all-gather | bytes 1179648 | tf_op jit(solution)/shard_map/all_gather | solution.py:103
  45.8 0.6 abs_reduce_fusion.2
  46.6 1.0 pad_maximum_fusion.1
  47.6 5.9 %all-to-all-start.2 = ((f16[4,200,384]{2,1,0:T(8,128)(2,1)}), f16[4,200,384]{2,1,0:T(8,128)(2,1)S(1)}, u32[]{:S(2)}, u32[]{:S(2)}) async-start(f16[4,200,384]{2,1,0:T(8,128)(2,1)} %pad_maximum_fusion.1), calls=%async_computation.2 | async-start | bytes 1228800 | tf_op jit(solution)/shard_map/all_to_all | solution.py:18
  54.3 0.1 reshape.254
  54.4 15.0 %all-to-all-done.2 = f16[4,200,384]{2,1,0:T(8,128)(2,1)S(1)} async-done(((f16[4,200,384]{2,1,0:T(8,128)(2,1)}), f16[4,200,384]{2,1,0:T(8,128)(2,1)S(1)}, u32[]{:S(2)}, u32[]{:S(2)}) %all-to-all-start.2) | async-done | bytes 614432 | tf_op jit(solution)/shard_map/all_to_all | solution.py:18
  69.6 4.0 %collective-permute-start.1 = (f16[136,384]{1,0:T(8,128)(2,1)S(1)}, f16[136,384]{1,0:T(8,128)(2,1)S(1)}, u32[]{:S(2)}, u32[]{:S(2)}) collective-permute-start(f16[136,384]{1,0:T(8,128)(2,1)S(1)} %pad_maximum_fusion.11), channel_id=1, source_target_pairs={{0,32},{32,0},{1,33},{33,1},{2,34},{34,2},{3,35},{35,3},{4,36},{36... | collective-permute-start | bytes 313352 | tf_op jit(solution)/shard_map/ppermute | solution.py:49
  73.6 0.1 reshape.255
  73.8 2.1 %collective-permute-done.1 = f16[136,384]{1,0:T(8,128)(2,1)S(1)} collective-permute-done((f16[136,384]{1,0:T(8,128)(2,1)S(1)}, f16[136,384]{1,0:T(8,128)(2,1)S(1)}, u32[]{:S(2)}, u32[]{:S(2)}) %collective-permute-start.1) | collective-permute-done | bytes 104480 | tf_op jit(solution)/shard_map/ppermute | solution.py:49
  75.9 0.1 abs_reduce_fusion.6
  76.1 0.1 multiply_convert_fusion.7
  76.2 0.8 broadcast_in_dim.39
  77.0 8.3 %all-to-all-start.3 = ((f16[4,136,384]{2,1,0:T(8,128)(2,1)}), f16[4,136,384]{2,1,0:T(8,128)(2,1)S(1)}, u32[]{:S(2)}, u32[]{:S(2)}) async-start(f16[4,136,384]{2,1,0:T(8,128)(2,1)} %broadcast_in_dim.39), calls=%async_computation.3 | async-start | bytes 835584 | tf_op jit(solution)/shard_map/all_to_all | solution.py:18
  85.4 1.9 %collective-permute-start.2 = (bf16[256,384]{1,0:T(8,128)(2,1)S(1)}, bf16[256,384]{1,0:T(8,128)(2,1)S(1)}, u32[]{:S(2)}, u32[]{:S(2)}) collective-permute-start(bf16[256,384]{1,0:T(8,128)(2,1)S(1)} %bitcast.90), channel_id=1, source_target_pairs={{0,32},{32,0},{1,33},{33,1},{2,34},{34,2},{3,35},{35,3},{4,36},{36... | collective-permute-start | bytes 589832 | tf_op jit(solution)/shard_map/ppermute | solution.py:49
  87.3 11.5 %collective-permute-done.2 = bf16[256,384]{1,0:T(8,128)(2,1)S(1)} collective-permute-done((bf16[256,384]{1,0:T(8,128)(2,1)S(1)}, bf16[256,384]{1,0:T(8,128)(2,1)S(1)}, u32[]{:S(2)}, u32[]{:S(2)}) %collective-permute-start.2) | collective-permute-done | bytes 196640 | tf_op jit(solution)/shard_map/ppermute | solution.py:49
  98.9 1.7 fusion.37
  100.7 0.1 reduce-precision_convert_fusion.2
  100.8 2.0 %reduce-precision_convert_fusion.1 = (bf16[768,384]{1,0:T(8,128)(2,1)S(1)}, bf16[768,384]{1,0:T(8,128)(2,1)S(1)}, f32[768,384]{1,0:T(8,128)}) fusion(bf16[512,384]{1,0:T(8,128)(2,1)S(1)} %get-tuple-element.10, bf16[512,384]{1,0:T(8,128)(2,1)S(1)} %get-tuple-element.9, bf16[512,768]{1,0:T(8,128)(2,1)S(1)} %all_gather.6), kind=kOutput, calls=%fused_computation.3 | convolution fusion | flops 609878016 | bytes 3932160 | tf_op jit(solution)/shard_map/dot_general | solution.py:27
  102.9 0.8 divide_add_fusion
  103.7 0.9 constant_dynamic-slice_fusion
  104.7 2.8 %collective-permute-start.3 = (f32[384,512]{1,0:T(8,128)}, f32[384,512]{1,0:T(8,128)S(1)}, u32[]{:S(2)}, u32[]{:S(2)}) collective-permute-start(f32[384,512]{1,0:T(8,128)} %constant_dynamic-slice_fusion), channel_id=1, source_target_pairs={{0,1},{1,0},{2,3},{3,2},{4,5},{5,4},{6,7},{7,6},{8,9},{9,8},{10,11... | collective-permute-start | bytes 2359304 | tf_op jit(solution)/shard_map/ppermute | solution.py:49
  107.4 2.1 %collective-permute-done.3 = f32[384,512]{1,0:T(8,128)S(1)} collective-permute-done((f32[384,512]{1,0:T(8,128)}, f32[384,512]{1,0:T(8,128)S(1)}, u32[]{:S(2)}, u32[]{:S(2)}) %collective-permute-start.3) | collective-permute-done | bytes 786464 | tf_op jit(solution)/shard_map/ppermute | solution.py:49
  109.5 0.1 dynamic-slice_add_fusion
  109.7 0.1 abs_reduce_fusion.1
  109.8 0.1 multiply_convert_fusion.1
  109.9 0.1 pad_maximum_fusion.3
  110.0 10.4 %all_to_all.41 = f16[4,104,512]{2,1,0:T(8,128)(2,1)S(1)} all-to-all(f16[4,104,512]{2,1,0:T(8,128)(2,1)S(1)} %pad_maximum_fusion.3), channel_id=1, replica_groups=mesh['yp'=4,'yb'=2,'zp'=2,'zb'=2,'x'=4,'zh'=2,'c'=2] {'x'}, dimensions={0} | all-to-all | bytes 851968 | tf_op jit(solution)/shard_map/all_to_all | solution.py:18
  120.6 6.8 %collective-permute-start.4 = (f16[104,512]{1,0:T(8,128)(2,1)S(1)}, f16[104,512]{1,0:T(8,128)(2,1)S(1)}, u32[]{:S(2)}, u32[]{:S(2)}) collective-permute-start(f16[104,512]{1,0:T(8,128)(2,1)S(1)} %pad_maximum_fusion.8), channel_id=1, source_target_pairs={{0,2},{2,0},{1,3},{3,1},{4,6},{6,4},{5,7},{7,5},{8,10},{10,8},{9,1... | collective-permute-start | bytes 319496 | tf_op jit(solution)/shard_map/ppermute | solution.py:49
  127.5 2.6 %collective-permute-done.4 = f16[104,512]{1,0:T(8,128)(2,1)S(1)} collective-permute-done((f16[104,512]{1,0:T(8,128)(2,1)S(1)}, f16[104,512]{1,0:T(8,128)(2,1)S(1)}, u32[]{:S(2)}, u32[]{:S(2)}) %collective-permute-start.4) | collective-permute-done | bytes 106528 | tf_op jit(solution)/shard_map/ppermute | solution.py:49
  130.3 0.8 broadcast_in_dim.44
  131.1 3.5 %all-to-all-start.5 = ((f16[4,104,512]{2,1,0:T(8,128)(2,1)}), f16[4,104,512]{2,1,0:T(8,128)(2,1)S(1)}, u32[]{:S(2)}, u32[]{:S(2)}) async-start(f16[4,104,512]{2,1,0:T(8,128)(2,1)} %broadcast_in_dim.44), calls=%async_computation.5 | async-start | bytes 851968 | tf_op jit(solution)/shard_map/all_to_all | solution.py:18
  134.6 4.8 %all-to-all-done.5 = f16[4,104,512]{2,1,0:T(8,128)(2,1)S(1)} async-done(((f16[4,104,512]{2,1,0:T(8,128)(2,1)}), f16[4,104,512]{2,1,0:T(8,128)(2,1)S(1)}, u32[]{:S(2)}, u32[]{:S(2)}) %all-to-all-start.5) | async-done | bytes 426016 | tf_op jit(solution)/shard_map/all_to_all | solution.py:18
  139.5 0.1 select_reduce_fusion
  139.7 0.8 broadcast_in_dim.51
  140.5 3.5 %all-to-all-start.6 = ((f16[4,104,512]{2,1,0:T(8,128)(2,1)}), f16[4,104,512]{2,1,0:T(8,128)(2,1)S(1)}, u32[]{:S(2)}, u32[]{:S(2)}) async-start(f16[4,104,512]{2,1,0:T(8,128)(2,1)} %broadcast_in_dim.51), calls=%async_computation.6 | async-start | bytes 851968 | tf_op jit(solution)/shard_map/all_to_all | solution.py:18
  144.0 0.1 reshape.259
  144.1 0.1 mul.237
  144.2 6.1 %all-to-all-done.6 = f16[4,104,512]{2,1,0:T(8,128)(2,1)S(1)} async-done(((f16[4,104,512]{2,1,0:T(8,128)(2,1)}), f16[4,104,512]{2,1,0:T(8,128)(2,1)S(1)}, u32[]{:S(2)}, u32[]{:S(2)}) %all-to-all-start.6) | async-done | bytes 426016 | tf_op jit(solution)/shard_map/all_to_all | solution.py:18
  150.3 9.0 %all_gather.7 = f16[8,104,512]{2,1,0:T(8,128)(2,1)S(1)} all-gather(f16[4,104,512]{2,1,0:T(8,128)(2,1)S(1)} %all-to-all-done.6), channel_id=1, replica_groups=mesh['yp'=4,'yb'=2,'zp'=2,'zb'=2,'x'=4,'zh'=2,'c'=2] {'c'}, dimensions={0}, use_global_device_ids=true | all-gather | bytes 1277952 | tf_op jit(solution)/shard_map/all_gather | solution.py:128
  159.4 0.2 convert_multiply_fusion
  159.6 0.3 reduce-precision_convert_fusion
  159.9 1.0 copy-done.7
  160.9 1.0 fusion.9
  162.0 0.1 multiply_convert_fusion
  162.1 1.0 pad_maximum_fusion.2
  163.1 3.5 %all-to-all-start.7 = ((f16[4,200,384]{2,1,0:T(8,128)(2,1)}), f16[4,200,384]{2,1,0:T(8,128)(2,1)S(1)}, u32[]{:S(2)}, u32[]{:S(2)}) async-start(f16[4,200,384]{2,1,0:T(8,128)(2,1)} %pad_maximum_fusion.2), calls=%async_computation.7 | async-start | bytes 1228800 | tf_op jit(solution)/shard_map/all_to_all | solution.py:18
  166.6 8.7 %all-to-all-done.7 = f16[4,200,384]{2,1,0:T(8,128)(2,1)S(1)} async-done(((f16[4,200,384]{2,1,0:T(8,128)(2,1)}), f16[4,200,384]{2,1,0:T(8,128)(2,1)S(1)}, u32[]{:S(2)}, u32[]{:S(2)}) %all-to-all-start.7) | async-done | bytes 614432 | tf_op jit(solution)/shard_map/all_to_all | solution.py:18
  175.3 0.1 convert_multiply_fusion.1
  175.5 0.7 copy-done.2
  176.2 0.7 fusion.41
  177.0 1.0 maximum_add_fusion
  (81 shorter events, 1.6 us)
Async XLA Ops:
  1.5 13.3 %collective-permute-start = (bf16[32,384]{1,0:T(8,128)(2,1)S(1)}, bf16[32,384]{1,0:T(8,128)(2,1)S(1)}, u32[]{:S(2)}, u32[]{:S(2)}) collective-permute-start(bf16[32,384]{1,0:T(8,128)(2,1)S(1)} %maximum_maximum_fusion), channel_id=1, source_target_pairs={{0,2},{2,0},{1,3},{3,1},{4,6},{6,4},{5,7},{7,5},{8,10},{10,8},{9,1... | collective-permute-start | bytes 73736 | tf_op jit(solution)/shard_map/ppermute | solution.py:49
  28.8 11.0 %all-to-all-start.1 = ((bf16[4,64,768]{2,1,0:T(8,128)(2,1)}), bf16[4,64,768]{2,1,0:T(8,128)(2,1)S(1)}, u32[]{:S(2)}, u32[]{:S(2)}) async-start(bf16[4,64,768]{2,1,0:T(8,128)(2,1)} %broadcast_in_dim.34), calls=%async_computation.1 | async-start | bytes 786432 | tf_op jit(solution)/shard_map/all_to_all | solution.py:18
  46.5 7.7 %copy-start.3 = (f32[512]{0:T(512)S(1)}, f32[512]{0:T(512)}, u32[]{:S(2)}) copy-start(f32[512]{0:T(512)} %param.19) | copy-start | bytes 6148
  46.6 7.7 %copy-start.4 = (f32[512]{0:T(512)S(1)}, f32[512]{0:T(512)}, u32[]{:S(2)}) copy-start(f32[512]{0:T(512)} %param.17) | copy-start | bytes 6148
  47.6 21.7 %all-to-all-start.2 = ((f16[4,200,384]{2,1,0:T(8,128)(2,1)}), f16[4,200,384]{2,1,0:T(8,128)(2,1)S(1)}, u32[]{:S(2)}, u32[]{:S(2)}) async-start(f16[4,200,384]{2,1,0:T(8,128)(2,1)} %pad_maximum_fusion.1), calls=%async_computation.2 | async-start | bytes 1228800 | tf_op jit(solution)/shard_map/all_to_all | solution.py:18
  69.6 6.3 %collective-permute-start.1 = (f16[136,384]{1,0:T(8,128)(2,1)S(1)}, f16[136,384]{1,0:T(8,128)(2,1)S(1)}, u32[]{:S(2)}, u32[]{:S(2)}) collective-permute-start(f16[136,384]{1,0:T(8,128)(2,1)S(1)} %pad_maximum_fusion.11), channel_id=1, source_target_pairs={{0,32},{32,0},{1,33},{33,1},{2,34},{34,2},{3,35},{35,3},{4,36},{36... | collective-permute-start | bytes 313352 | tf_op jit(solution)/shard_map/ppermute | solution.py:49
  77.0 23.6 %all-to-all-start.3 = ((f16[4,136,384]{2,1,0:T(8,128)(2,1)}), f16[4,136,384]{2,1,0:T(8,128)(2,1)S(1)}, u32[]{:S(2)}, u32[]{:S(2)}) async-start(f16[4,136,384]{2,1,0:T(8,128)(2,1)} %broadcast_in_dim.39), calls=%async_computation.3 | async-start | bytes 835584 | tf_op jit(solution)/shard_map/all_to_all | solution.py:18
  85.4 13.5 %collective-permute-start.2 = (bf16[256,384]{1,0:T(8,128)(2,1)S(1)}, bf16[256,384]{1,0:T(8,128)(2,1)S(1)}, u32[]{:S(2)}, u32[]{:S(2)}) collective-permute-start(bf16[256,384]{1,0:T(8,128)(2,1)S(1)} %bitcast.90), channel_id=1, source_target_pairs={{0,32},{32,0},{1,33},{33,1},{2,34},{34,2},{3,35},{35,3},{4,36},{36... | collective-permute-start | bytes 589832 | tf_op jit(solution)/shard_map/ppermute | solution.py:49
  100.8 2.1 %copy-start.1 = (f32[768,512]{1,0:T(8,128)S(1)}, f32[768,512]{1,0:T(8,128)}, u32[]{:S(2)}) copy-start(f32[768,512]{1,0:T(8,128)} %fusion.37) | copy-start | bytes 4718596
  104.7 4.9 %collective-permute-start.3 = (f32[384,512]{1,0:T(8,128)}, f32[384,512]{1,0:T(8,128)S(1)}, u32[]{:S(2)}, u32[]{:S(2)}) collective-permute-start(f32[384,512]{1,0:T(8,128)} %constant_dynamic-slice_fusion), channel_id=1, source_target_pairs={{0,1},{1,0},{2,3},{3,2},{4,5},{5,4},{6,7},{7,6},{8,9},{9,8},{10,11... | collective-permute-start | bytes 2359304 | tf_op jit(solution)/shard_map/ppermute | solution.py:49
  120.6 9.5 %collective-permute-start.4 = (f16[104,512]{1,0:T(8,128)(2,1)S(1)}, f16[104,512]{1,0:T(8,128)(2,1)S(1)}, u32[]{:S(2)}, u32[]{:S(2)}) collective-permute-start(f16[104,512]{1,0:T(8,128)(2,1)S(1)} %pad_maximum_fusion.8), channel_id=1, source_target_pairs={{0,2},{2,0},{1,3},{3,1},{4,6},{6,4},{5,7},{7,5},{8,10},{10,8},{9,1... | collective-permute-start | bytes 319496 | tf_op jit(solution)/shard_map/ppermute | solution.py:49
  131.1 8.3 %all-to-all-start.5 = ((f16[4,104,512]{2,1,0:T(8,128)(2,1)}), f16[4,104,512]{2,1,0:T(8,128)(2,1)S(1)}, u32[]{:S(2)}, u32[]{:S(2)}) async-start(f16[4,104,512]{2,1,0:T(8,128)(2,1)} %broadcast_in_dim.44), calls=%async_computation.5 | async-start | bytes 851968 | tf_op jit(solution)/shard_map/all_to_all | solution.py:18
  134.5 9.4 %copy-start.5 = (f32[512]{0:T(512)S(1)}, f32[512]{0:T(512)}, u32[]{:S(2)}) copy-start(f32[512]{0:T(512)} %param.20) | copy-start | bytes 6148
  134.6 9.4 %copy-start.6 = (f32[512]{0:T(512)S(1)}, f32[512]{0:T(512)}, u32[]{:S(2)}) copy-start(f32[512]{0:T(512)} %param.18) | copy-start | bytes 6148
  140.5 9.8 %all-to-all-start.6 = ((f16[4,104,512]{2,1,0:T(8,128)(2,1)}), f16[4,104,512]{2,1,0:T(8,128)(2,1)S(1)}, u32[]{:S(2)}, u32[]{:S(2)}) async-start(f16[4,104,512]{2,1,0:T(8,128)(2,1)} %broadcast_in_dim.51), calls=%async_computation.6 | async-start | bytes 851968 | tf_op jit(solution)/shard_map/all_to_all | solution.py:18
  159.6 1.3 copy-start.7
  163.1 12.2 %all-to-all-start.7 = ((f16[4,200,384]{2,1,0:T(8,128)(2,1)}), f16[4,200,384]{2,1,0:T(8,128)(2,1)S(1)}, u32[]{:S(2)}, u32[]{:S(2)}) async-start(f16[4,200,384]{2,1,0:T(8,128)(2,1)} %pad_maximum_fusion.2), calls=%async_computation.7 | async-start | bytes 1228800 | tf_op jit(solution)/shard_map/all_to_all | solution.py:18
  175.3 0.9 copy-start.2
  175.4 1.6 copy-start

commit v15 on v12

--- a/solution.py
+++ b/solution.py
@@ -82,13 +82,14 @@
     damp = damping[0]
     quad = lax.axis_index("yb") * 2 + lax.axis_index("zb")
     level = lax.axis_index("yp")
+    octant = level * 2 + lax.axis_index("zp")
     core = lax.axis_index("c")
     is_output = quad == 3
     left_shift = shifted(jnp.where(is_output, output_left_eigen, joined_left_eigen), damp)
     right_shift = shifted(jnp.where(is_output, output_right_eigen, joined_right_eigen), damp)
     left_shift = left_shift.reshape(4, 2, 2, 32).transpose(2, 0, 1, 3)
     left_shift = jnp.where(lax.axis_index("zh") == 1, left_shift[:, :, ::-1], left_shift).reshape(512)
-    own_shift = lax.dynamic_slice_in_dim(left_shift, level * 128, 128, 0)
+    own_shift = lax.dynamic_slice_in_dim(left_shift, octant * 64, 64, 0)
     right_shift = right_shift.reshape(4, 2, 2, 2, 16).transpose(0, 2, 1, 3, 4).reshape(4, 2, 64)[::-1]
     right_shift = jnp.where(lax.axis_index("zp") == 1, right_shift[:, ::-1], right_shift)
     right_shift = jnp.concatenate([right_shift, right_shift], axis=0)
@@ -122,9 +123,9 @@
     right = jnp.concatenate([right, other], axis=0)
 
     rows = jnp.dot(left, gradient, preferred_element_type=jnp.float32)
-    rows = jnp.sum(unpack(exchange(pack(rows.reshape(4, 128, 384)), "yp")), axis=0)
-    rows = (rows + unpack(swap(pack(rows, there), "zp"))) * own_shift[:, None]
-    rows = unpack(exchange(spread(pack(rows), 4), "yp")).reshape(512, 384)
+    rows = jnp.sum(unpack(exchange(pack(rows.reshape(8, 64, 384)), OCT)), axis=0)
+    rows = pack(rows * own_shift[:, None], there)
+    rows = unpack(exchange(spread(rows, 8), OCT)).reshape(512, 384)
     right = jnp.concatenate([right] + [around(right, "yp", 4, step) for step in (1, 2, 3)], axis=0)
 
     lifted = dot_wide_right(left, rows, ((0,), (0,)))

time: 178 us -> 178 us (level)
    ppermute x5 -> x4, starting transfers between devices: 30.2 us -> 25.4 us  [swap(): return lax.ppermute(values, axis, [(0, 1), (1, 0)])]
    all_to_all x6, starting transfers between devices: 27.5 us -> 30.8 us  [exchange(): return lax.all_to_all(blocks, axes, 0, 0, tiled=True)]
    ppermute x5 -> x4, waiting for transfers between devices: 7.73 us -> 4.49 us  [swap(): return lax.ppermute(values, axis, [(0, 1), (1, 0)])]
    ppermute x3, waiting for transfers between devices: 5.53 us -> 7.53 us  [around(): lax.ppermute(values, axis, [(i, (i + step) % size) for i in range(size)])]
  transfers between devices with their start and end apart: 14 -> 13, of which waited for: 9 -> 9; matrix products, arithmetic and copies ran while one was open for 2% -> 2% of each run, Pallas kernels for 0% -> 0%
where the time goes in v15:
time: 178 us; the launch traced here: 177 us
  starting transfers between devices  69.7 us (39%)
  waiting for transfers between devices  47 us (26%)
  blocking collectives  36.9 us (21%)
  local copies, waits for them, and re-layouts  8.39 us (5%)
  other arithmetic  7.3 us (4%)
  matrix products  5.2 us (3%)
  between operations  2 us (1%)
    all_to_all x6, waiting for transfers between devices, exchange(): return lax.all_to_all(blocks, axes, 0, 0, tiled=True)  35 us
    all_to_all x6, starting transfers between devices, exchange(): return lax.all_to_all(blocks, axes, 0, 0, tiled=True)  30.8 us
    ppermute x4, starting transfers between devices, swap(): return lax.ppermute(values, axis, [(0, 1), (1, 0)])  25.4 us
    all_to_all x2, blocking collectives, exchange(): return lax.all_to_all(blocks, axes, 0, 0, tiled=True)  22.1 us
    ppermute x3, starting transfers between devices, around(): lax.ppermute(values, axis, [(i, (i + step) % size) for i in range(size)])  13.5 us
    all_gather x1, blocking collectives, local(): lax.all_gather(cols, 'c', axis=0, tiled=True)  8.71 us
    ppermute x3, waiting for transfers between devices, around(): lax.ppermute(values, axis, [(i, (i + step) % size) for i in range(size)])  7.53 us
    all_gather x1, blocking collectives, local(): left = lax.all_gather(left, 'c', axis=0, tiled=True)  6.09 us
  transfers between devices with their start and end apart: 13, of which 9 were waited for; matrix products, arithmetic and copies ran while one was open for 2% of the time, Pallas kernels for 0%

profile of v15, /device:TPU:1, one launch (start us, length us, event | category | flops | bytes accessed | tf_op | source)
XLA Modules:
  0.0 176.5 jit_solution(5552061106805352064)
XLA Ops:
  0.6 0.8 fusion.39
  1.5 11.5 %collective-permute-start = (bf16[32,384]{1,0:T(8,128)(2,1)S(1)}, bf16[32,384]{1,0:T(8,128)(2,1)S(1)}, u32[]{:S(2)}, u32[]{:S(2)}) collective-permute-start(bf16[32,384]{1,0:T(8,128)(2,1)S(1)} %maximum_maximum_fusion), channel_id=1, source_target_pairs={{0,2},{2,0},{1,3},{3,1},{4,6},{6,4},{5,7},{7,5},{8,10},{10,8},{9,1... | collective-permute-start | bytes 73736 | tf_op jit(solution)/shard_map/ppermute | solution.py:57
  13.0 1.1 fusion.36
  14.1 0.8 fusion.37
  14.8 0.8 maximum_bitcast_fusion
  15.7 0.1 pad_maximum_fusion
  15.8 11.7 %all_to_all.40 = bf16[4,240,384]{2,1,0:T(8,128)(2,1)S(1)} all-to-all(bf16[4,240,384]{2,1,0:T(8,128)(2,1)S(1)} %pad_maximum_fusion), channel_id=1, replica_groups=mesh['yp'=4,'yb'=2,'zp'=2,'zb'=2,'x'=4,'zh'=2,'c'=2] {'yb','zb'}, dimensions={0} | all-to-all | bytes 1474560 | tf_op jit(solution)/shard_map/all_to_all | solution.py:18
  27.6 0.1 slice_bitcast_fusion.5
  27.7 0.1 pad_maximum_fusion.11
  27.8 0.8 broadcast_in_dim.32
  28.6 4.8 %all-to-all-start.1 = ((bf16[4,64,768]{2,1,0:T(8,128)(2,1)}), bf16[4,64,768]{2,1,0:T(8,128)(2,1)S(1)}, u32[]{:S(2)}, u32[]{:S(2)}) async-start(bf16[4,64,768]{2,1,0:T(8,128)(2,1)} %broadcast_in_dim.32), calls=%async_computation.1 | async-start | bytes 786432 | tf_op jit(solution)/shard_map/all_to_all | solution.py:18
  33.4 6.2 %all-to-all-done.1 = bf16[4,64,768]{2,1,0:T(8,128)(2,1)S(1)} async-done(((bf16[4,64,768]{2,1,0:T(8,128)(2,1)}), bf16[4,64,768]{2,1,0:T(8,128)(2,1)S(1)}, u32[]{:S(2)}, u32[]{:S(2)}) %all-to-all-start.1) | async-done | bytes 393248 | tf_op jit(solution)/shard_map/all_to_all | solution.py:18
  39.6 6.1 %all_gather.6 = bf16[512,768]{1,0:T(8,128)(2,1)S(1)} all-gather(bf16[256,768]{1,0:T(8,128)(2,1)S(1)} %bitcast.94), channel_id=1, replica_groups=mesh['yp'=4,'yb'=2,'zp'=2,'zb'=2,'x'=4,'zh'=2,'c'=2] {'c'}, dimensions={0}, use_global_device_ids=true | all-gather | bytes 1179648 | tf_op jit(solution)/shard_map/all_gather | solution.py:118
  45.7 0.6 abs_reduce_fusion.2
  46.5 0.9 pad_maximum_fusion.2
  47.3 7.8 %all-to-all-start.2 = ((f16[8,72,384]{2,1,0:T(8,128)(2,1)}), f16[8,72,384]{2,1,0:T(8,128)(2,1)S(1)}, u32[]{:S(2)}, u32[]{:S(2)}) async-start(f16[8,72,384]{2,1,0:T(8,128)(2,1)} %pad_maximum_fusion.2), calls=%async_computation.2 | async-start | bytes 884736 | tf_op jit(solution)/shard_map/all_to_all | solution.py:18
  55.8 0.1 reshape.237
  55.9 0.1 reshape.238
  56.1 4.3 %collective-permute-start.1 = (bf16[64,384]{1,0:T(8,128)(2,1)S(1)}, bf16[64,384]{1,0:T(8,128)(2,1)S(1)}, u32[]{:S(2)}, u32[]{:S(2)}) collective-permute-start(bf16[64,384]{1,0:T(8,128)(2,1)S(1)} %bitcast.96), channel_id=1, source_target_pairs={{0,32},{32,0},{1,33},{33,1},{2,34},{34,2},{3,35},{35,3},{4,36},{36... | collective-permute-start | bytes 147464 | tf_op jit(solution)/shard_map/ppermute | solution.py:57
  60.4 8.5 %all-to-all-done.2 = f16[8,72,384]{2,1,0:T(8,128)(2,1)S(1)} async-done(((f16[8,72,384]{2,1,0:T(8,128)(2,1)}), f16[8,72,384]{2,1,0:T(8,128)(2,1)S(1)}, u32[]{:S(2)}, u32[]{:S(2)}) %all-to-all-start.2) | async-done | bytes 442400 | tf_op jit(solution)/shard_map/all_to_all | solution.py:18
  69.0 0.1 abs_reduce_fusion.6
  69.1 0.1 multiply_convert_fusion.6
  69.3 0.8 broadcast_in_dim.36
  70.1 7.5 %all-to-all-start.3 = ((f16[8,72,384]{2,1,0:T(8,128)(2,1)}), f16[8,72,384]{2,1,0:T(8,128)(2,1)S(1)}, u32[]{:S(2)}, u32[]{:S(2)}) async-start(f16[8,72,384]{2,1,0:T(8,128)(2,1)} %broadcast_in_dim.36), calls=%async_computation.3 | async-start | bytes 884736 | tf_op jit(solution)/shard_map/all_to_all | solution.py:18
  77.6 5.5 %collective-permute-start.4 = (bf16[128,384]{1,0:T(8,128)(2,1)S(1)}, bf16[128,384]{1,0:T(8,128)(2,1)S(1)}, u32[]{:S(2)}, u32[]{:S(2)}) collective-permute-start(bf16[128,384]{1,0:T(8,128)(2,1)S(1)} %pad_maximum_fusion.12), channel_id=1, source_target_pairs={{0,384},{128,0},{256,128},{384,256},{1,385},{129,1},{257,129},{385... | collective-permute-start | bytes 294920 | tf_op jit(solution)/shard_map/ppermute | solution.py:61
  83.1 4.0 %collective-permute-start.3 = (bf16[128,384]{1,0:T(8,128)(2,1)S(1)}, bf16[128,384]{1,0:T(8,128)(2,1)S(1)}, u32[]{:S(2)}, u32[]{:S(2)}) collective-permute-start(bf16[128,384]{1,0:T(8,128)(2,1)S(1)} %pad_maximum_fusion.12), channel_id=1, source_target_pairs={{0,256},{128,384},{256,0},{384,128},{1,257},{129,385},{257,1},{385... | collective-permute-start | bytes 294920 | tf_op jit(solution)/shard_map/ppermute | solution.py:61
  87.1 4.0 %collective-permute-start.2 = (bf16[128,384]{1,0:T(8,128)(2,1)S(1)}, bf16[128,384]{1,0:T(8,128)(2,1)S(1)}, u32[]{:S(2)}, u32[]{:S(2)}) collective-permute-start(bf16[128,384]{1,0:T(8,128)(2,1)S(1)} %pad_maximum_fusion.12), channel_id=1, source_target_pairs={{0,128},{128,256},{256,384},{384,0},{1,129},{129,257},{257,385},{3... | collective-permute-start | bytes 294920 | tf_op jit(solution)/shard_map/ppermute | solution.py:61
  91.1 6.7 %collective-permute-done.2 = bf16[128,384]{1,0:T(8,128)(2,1)S(1)} collective-permute-done((bf16[128,384]{1,0:T(8,128)(2,1)S(1)}, bf16[128,384]{1,0:T(8,128)(2,1)S(1)}, u32[]{:S(2)}, u32[]{:S(2)}) %collective-permute-start.2) | collective-permute-done | bytes 98336 | tf_op jit(solution)/shard_map/ppermute | solution.py:61
  97.9 0.8 collective-permute-done.4
  98.9 0.1 fusion.3
  99.0 0.6 fusion.41
  99.6 1.6 divide_add_fusion
  101.2 0.6 fusion.4
  101.8 0.6 convolution_add_fusion
  102.5 2.8 %collective-permute-start.5 = (f32[384,512]{1,0:T(8,128)S(1)}, f32[384,512]{1,0:T(8,128)S(1)}, u32[]{:S(2)}, u32[]{:S(2)}) collective-permute-start(f32[384,512]{1,0:T(8,128)S(1)} %constant_dynamic-slice_fusion), channel_id=1, source_target_pairs={{0,1},{1,0},{2,3},{3,2},{4,5},{5,4},{6,7},{7,6},{8,9},{9,8},{10,11... | collective-permute-start | bytes 2359304 | tf_op jit(solution)/shard_map/ppermute | solution.py:57
  105.3 1.9 %collective-permute-done.5 = f32[384,512]{1,0:T(8,128)S(1)} collective-permute-done((f32[384,512]{1,0:T(8,128)S(1)}, f32[384,512]{1,0:T(8,128)S(1)}, u32[]{:S(2)}, u32[]{:S(2)}) %collective-permute-start.5) | collective-permute-done | bytes 786464 | tf_op jit(solution)/shard_map/ppermute | solution.py:57
  107.2 0.1 dynamic-slice_add_fusion
  107.5 0.1 multiply_convert_fusion.1
  107.6 0.1 pad_maximum_fusion.3
  107.7 10.4 %all_to_all.41 = f16[4,104,512]{2,1,0:T(8,128)(2,1)S(1)} all-to-all(f16[4,104,512]{2,1,0:T(8,128)(2,1)S(1)} %pad_maximum_fusion.3), channel_id=1, replica_groups=mesh['yp'=4,'yb'=2,'zp'=2,'zb'=2,'x'=4,'zh'=2,'c'=2] {'x'}, dimensions={0} | all-to-all | bytes 851968 | tf_op jit(solution)/shard_map/all_to_all | solution.py:18
  118.4 6.8 %collective-permute-start.6 = (f16[104,512]{1,0:T(8,128)(2,1)S(1)}, f16[104,512]{1,0:T(8,128)(2,1)S(1)}, u32[]{:S(2)}, u32[]{:S(2)}) collective-permute-start(f16[104,512]{1,0:T(8,128)(2,1)S(1)} %pad_maximum_fusion.8), channel_id=1, source_target_pairs={{0,2},{2,0},{1,3},{3,1},{4,6},{6,4},{5,7},{7,5},{8,10},{10,8},{9,1... | collective-permute-start | bytes 319496 | tf_op jit(solution)/shard_map/ppermute | solution.py:57
  125.2 2.6 %collective-permute-done.6 = f16[104,512]{1,0:T(8,128)(2,1)S(1)} collective-permute-done((f16[104,512]{1,0:T(8,128)(2,1)S(1)}, f16[104,512]{1,0:T(8,128)(2,1)S(1)}, u32[]{:S(2)}, u32[]{:S(2)}) %collective-permute-start.6) | collective-permute-done | bytes 106528 | tf_op jit(solution)/shard_map/ppermute | solution.py:57
  128.0 0.8 broadcast_in_dim.45
  128.8 3.9 %all-to-all-start.5 = ((f16[4,104,512]{2,1,0:T(8,128)(2,1)}), f16[4,104,512]{2,1,0:T(8,128)(2,1)S(1)}, u32[]{:S(2)}, u32[]{:S(2)}) async-start(f16[4,104,512]{2,1,0:T(8,128)(2,1)} %broadcast_in_dim.45), calls=%async_computation.5 | async-start | bytes 851968 | tf_op jit(solution)/shard_map/all_to_all | solution.py:18
  132.7 0.1 reshape.243
  132.8 0.1 reshape.244
  132.9 5.4 %all-to-all-done.5 = f16[4,104,512]{2,1,0:T(8,128)(2,1)S(1)} async-done(((f16[4,104,512]{2,1,0:T(8,128)(2,1)}), f16[4,104,512]{2,1,0:T(8,128)(2,1)S(1)}, u32[]{:S(2)}, u32[]{:S(2)}) %all-to-all-start.5) | async-done | bytes 426016 | tf_op jit(solution)/shard_map/all_to_all | solution.py:18
  138.3 0.1 select_reduce_fusion
  138.6 0.8 broadcast_in_dim.48
  139.4 3.5 %all-to-all-start.6 = ((f16[4,104,512]{2,1,0:T(8,128)(2,1)}), f16[4,104,512]{2,1,0:T(8,128)(2,1)S(1)}, u32[]{:S(2)}, u32[]{:S(2)}) async-start(f16[4,104,512]{2,1,0:T(8,128)(2,1)} %broadcast_in_dim.48), calls=%async_computation.6 | async-start | bytes 851968 | tf_op jit(solution)/shard_map/all_to_all | solution.py:18
  143.0 6.2 %all-to-all-done.6 = f16[4,104,512]{2,1,0:T(8,128)(2,1)S(1)} async-done(((f16[4,104,512]{2,1,0:T(8,128)(2,1)}), f16[4,104,512]{2,1,0:T(8,128)(2,1)S(1)}, u32[]{:S(2)}, u32[]{:S(2)}) %all-to-all-start.6) | async-done | bytes 426016 | tf_op jit(solution)/shard_map/all_to_all | solution.py:18
  149.2 8.7 %all_gather.7 = f16[8,104,512]{2,1,0:T(8,128)(2,1)S(1)} all-gather(f16[4,104,512]{2,1,0:T(8,128)(2,1)S(1)} %all-to-all-done.6), channel_id=1, replica_groups=mesh['yp'=4,'yb'=2,'zp'=2,'zb'=2,'x'=4,'zh'=2,'c'=2] {'c'}, dimensions={0}, use_global_device_ids=true | all-gather | bytes 1277952 | tf_op jit(solution)/shard_map/all_gather | solution.py:141
  158.0 0.2 convert_multiply_fusion
  158.2 0.3 reduce-precision_convert_fusion
  158.5 0.6 fusion.42
  159.1 0.7 copy-done.7
  159.7 0.6 fusion.1
  160.4 0.1 multiply_convert_fusion
  160.6 1.0 pad_maximum_fusion.1
  161.6 3.5 %all-to-all-start.7 = ((f16[4,200,384]{2,1,0:T(8,128)(2,1)}), f16[4,200,384]{2,1,0:T(8,128)(2,1)S(1)}, u32[]{:S(2)}, u32[]{:S(2)}) async-start(f16[4,200,384]{2,1,0:T(8,128)(2,1)} %pad_maximum_fusion.1), calls=%async_computation.7 | async-start | bytes 1228800 | tf_op jit(solution)/shard_map/all_to_all | solution.py:18
  165.1 8.7 %all-to-all-done.7 = f16[4,200,384]{2,1,0:T(8,128)(2,1)S(1)} async-done(((f16[4,200,384]{2,1,0:T(8,128)(2,1)}), f16[4,200,384]{2,1,0:T(8,128)(2,1)S(1)}, u32[]{:S(2)}, u32[]{:S(2)}) %all-to-all-start.7) | async-done | bytes 614432 | tf_op jit(solution)/shard_map/all_to_all | solution.py:18
  174.0 0.8 copy-done.2
  174.8 0.7 fusion.6
  175.5 1.0 maximum_add_fusion
  (88 shorter events, 2.0 us)
Async XLA Ops:
  0.6 14.2 %copy-start.1 = (bf16[192,384]{1,0:T(8,128)(2,1)S(1)}, bf16[192,384]{1,0:T(8,128)(2,1)}, u32[]{:S(2)}) copy-start(bf16[192,384]{1,0:T(8,128)(2,1)} %param.12) | copy-start | bytes 442372
  1.5 13.3 %collective-permute-start = (bf16[32,384]{1,0:T(8,128)(2,1)S(1)}, bf16[32,384]{1,0:T(8,128)(2,1)S(1)}, u32[]{:S(2)}, u32[]{:S(2)}) collective-permute-start(bf16[32,384]{1,0:T(8,128)(2,1)S(1)} %maximum_maximum_fusion), channel_id=1, source_target_pairs={{0,2},{2,0},{1,3},{3,1},{4,6},{6,4},{5,7},{7,5},{8,10},{10,8},{9,1... | collective-permute-start | bytes 73736 | tf_op jit(solution)/shard_map/ppermute | solution.py:57
  28.6 11.0 %all-to-all-start.1 = ((bf16[4,64,768]{2,1,0:T(8,128)(2,1)}), bf16[4,64,768]{2,1,0:T(8,128)(2,1)S(1)}, u32[]{:S(2)}, u32[]{:S(2)}) async-start(bf16[4,64,768]{2,1,0:T(8,128)(2,1)} %broadcast_in_dim.32), calls=%async_computation.1 | async-start | bytes 786432 | tf_op jit(solution)/shard_map/all_to_all | solution.py:18
  46.4 9.4 %copy-start.3 = (f32[512]{0:T(512)S(1)}, f32[512]{0:T(512)}, u32[]{:S(2)}) copy-start(f32[512]{0:T(512)} %param.20) | copy-start | bytes 6148
  46.4 9.4 %copy-start.4 = (f32[512]{0:T(512)S(1)}, f32[512]{0:T(512)}, u32[]{:S(2)}) copy-start(f32[512]{0:T(512)} %param.18) | copy-start | bytes 6148
  46.4 9.4 %copy-start.5 = (f32[512]{0:T(512)S(1)}, f32[512]{0:T(512)}, u32[]{:S(2)}) copy-start(f32[512]{0:T(512)} %param.19) | copy-start | bytes 6148
  46.4 9.4 %copy-start.6 = (f32[512]{0:T(512)S(1)}, f32[512]{0:T(512)}, u32[]{:S(2)}) copy-start(f32[512]{0:T(512)} %param.17) | copy-start | bytes 6148
  47.3 21.6 %all-to-all-start.2 = ((f16[8,72,384]{2,1,0:T(8,128)(2,1)}), f16[8,72,384]{2,1,0:T(8,128)(2,1)S(1)}, u32[]{:S(2)}, u32[]{:S(2)}) async-start(f16[8,72,384]{2,1,0:T(8,128)(2,1)} %pad_maximum_fusion.2), calls=%async_computation.2 | async-start | bytes 884736 | tf_op jit(solution)/shard_map/all_to_all | solution.py:18
  56.1 13.1 %collective-permute-start.1 = (bf16[64,384]{1,0:T(8,128)(2,1)S(1)}, bf16[64,384]{1,0:T(8,128)(2,1)S(1)}, u32[]{:S(2)}, u32[]{:S(2)}) collective-permute-start(bf16[64,384]{1,0:T(8,128)(2,1)S(1)} %bitcast.96), channel_id=1, source_target_pairs={{0,32},{32,0},{1,33},{33,1},{2,34},{34,2},{3,35},{35,3},{4,36},{36... | collective-permute-start | bytes 147464 | tf_op jit(solution)/shard_map/ppermute | solution.py:57
  70.1 28.6 %all-to-all-start.3 = ((f16[8,72,384]{2,1,0:T(8,128)(2,1)}), f16[8,72,384]{2,1,0:T(8,128)(2,1)S(1)}, u32[]{:S(2)}, u32[]{:S(2)}) async-start(f16[8,72,384]{2,1,0:T(8,128)(2,1)} %broadcast_in_dim.36), calls=%async_computation.3 | async-start | bytes 884736 | tf_op jit(solution)/shard_map/all_to_all | solution.py:18
  77.6 21.1 %collective-permute-start.4 = (bf16[128,384]{1,0:T(8,128)(2,1)S(1)}, bf16[128,384]{1,0:T(8,128)(2,1)S(1)}, u32[]{:S(2)}, u32[]{:S(2)}) collective-permute-start(bf16[128,384]{1,0:T(8,128)(2,1)S(1)} %pad_maximum_fusion.12), channel_id=1, source_target_pairs={{0,384},{128,0},{256,128},{384,256},{1,385},{129,1},{257,129},{385... | collective-permute-start | bytes 294920 | tf_op jit(solution)/shard_map/ppermute | solution.py:61
  83.1 14.8 %collective-permute-start.3 = (bf16[128,384]{1,0:T(8,128)(2,1)S(1)}, bf16[128,384]{1,0:T(8,128)(2,1)S(1)}, u32[]{:S(2)}, u32[]{:S(2)}) collective-permute-start(bf16[128,384]{1,0:T(8,128)(2,1)S(1)} %pad_maximum_fusion.12), channel_id=1, source_target_pairs={{0,256},{128,384},{256,0},{384,128},{1,257},{129,385},{257,1},{385... | collective-permute-start | bytes 294920 | tf_op jit(solution)/shard_map/ppermute | solution.py:61
  87.1 10.7 %collective-permute-start.2 = (bf16[128,384]{1,0:T(8,128)(2,1)S(1)}, bf16[128,384]{1,0:T(8,128)(2,1)S(1)}, u32[]{:S(2)}, u32[]{:S(2)}) collective-permute-start(bf16[128,384]{1,0:T(8,128)(2,1)S(1)} %pad_maximum_fusion.12), channel_id=1, source_target_pairs={{0,128},{128,256},{256,384},{384,0},{1,129},{129,257},{257,385},{3... | collective-permute-start | bytes 294920 | tf_op jit(solution)/shard_map/ppermute | solution.py:61
  102.5 4.7 %collective-permute-start.5 = (f32[384,512]{1,0:T(8,128)S(1)}, f32[384,512]{1,0:T(8,128)S(1)}, u32[]{:S(2)}, u32[]{:S(2)}) collective-permute-start(f32[384,512]{1,0:T(8,128)S(1)} %constant_dynamic-slice_fusion), channel_id=1, source_target_pairs={{0,1},{1,0},{2,3},{3,2},{4,5},{5,4},{6,7},{7,6},{8,9},{9,8},{10,11... | collective-permute-start | bytes 2359304 | tf_op jit(solution)/shard_map/ppermute | solution.py:57
  118.4 9.5 %collective-permute-start.6 = (f16[104,512]{1,0:T(8,128)(2,1)S(1)}, f16[104,512]{1,0:T(8,128)(2,1)S(1)}, u32[]{:S(2)}, u32[]{:S(2)}) collective-permute-start(f16[104,512]{1,0:T(8,128)(2,1)S(1)} %pad_maximum_fusion.8), channel_id=1, source_target_pairs={{0,2},{2,0},{1,3},{3,1},{4,6},{6,4},{5,7},{7,5},{8,10},{10,8},{9,1... | collective-permute-start | bytes 319496 | tf_op jit(solution)/shard_map/ppermute | solution.py:57
  128.8 9.5 %all-to-all-start.5 = ((f16[4,104,512]{2,1,0:T(8,128)(2,1)}), f16[4,104,512]{2,1,0:T(8,128)(2,1)S(1)}, u32[]{:S(2)}, u32[]{:S(2)}) async-start(f16[4,104,512]{2,1,0:T(8,128)(2,1)} %broadcast_in_dim.45), calls=%async_computation.5 | async-start | bytes 851968 | tf_op jit(solution)/shard_map/all_to_all | solution.py:18
  139.4 9.8 %all-to-all-start.6 = ((f16[4,104,512]{2,1,0:T(8,128)(2,1)}), f16[4,104,512]{2,1,0:T(8,128)(2,1)S(1)}, u32[]{:S(2)}, u32[]{:S(2)}) async-start(f16[4,104,512]{2,1,0:T(8,128)(2,1)} %broadcast_in_dim.48), calls=%async_computation.6 | async-start | bytes 851968 | tf_op jit(solution)/shard_map/all_to_all | solution.py:18
  158.5 1.3 copy-start.7
  161.6 12.2 %all-to-all-start.7 = ((f16[4,200,384]{2,1,0:T(8,128)(2,1)}), f16[4,200,384]{2,1,0:T(8,128)(2,1)S(1)}, u32[]{:S(2)}, u32[]{:S(2)}) async-start(f16[4,200,384]{2,1,0:T(8,128)(2,1)} %pad_maximum_fusion.1), calls=%async_computation.7 | async-start | bytes 1228800 | tf_op jit(solution)/shard_map/all_to_all | solution.py:18
  173.9 0.9 copy-start.2
  173.9 1.7 copy-start
